TPU v7x, 32 devices: a whole 2x2x4 slice. The times are simulated.
32 devices in a mesh: ctx: 16 (over z, x, core), fsdp: 2 (over y).
Axes of the slice: x: 2, y: 2, z: 4, core: 2. Of those that a mesh axis runs over, the one named last changes fastest.
Arguments:
- inputs: bfloat16 [2, 2048, 2048], P('fsdp', 'ctx'), may hold values from -6 to 6
- w_query: bfloat16 [2048, 4096], P('fsdp'), may hold values from -0.125 to 0.125
- w_key: bfloat16 [2048, 512], P('fsdp'), may hold values from -0.125 to 0.125
- w_value: bfloat16 [2048, 512], P('fsdp'), may hold values from -0.125 to 0.125
- w_output: bfloat16 [4096, 2048], P('fsdp'), may hold values from -0.75 to 0.75
- norm_attn: bfloat16 [2048], P('fsdp'), may hold values from 0.5 to 1.5
- gain_query: bfloat16 [128], P('fsdp'), may hold values from 0.796875 to 1.59375
- gain_key: bfloat16 [128], P('fsdp'), may hold values from 0.796875 to 1.59375
- w_router: bfloat16 [2048, 16], P('fsdp'), may hold values from -0.0625 to 0.0625
- norm_moe: bfloat16 [2048], P('fsdp'), may hold values from 0.5 to 1.5
- w_gate: bfloat16 [16, 2048, 768], P('ctx', 'fsdp'), may hold values from -0.125 to 0.125
- w_up: bfloat16 [16, 2048, 768], P('ctx', 'fsdp'), may hold values from -0.125 to 0.125
- w_down: bfloat16 [16, 2048, 768], P('ctx', 'fsdp'), may hold values from -0.875 to 0.875
- lengths: int32 [2, 4], P('fsdp'), may hold values from 204 to 1280, as said below
- routes: int32 [2, 2048, 8], P('fsdp', 'ctx'), may hold values from 0 to 15, all different within a row
- pair_order: int32 [2, 16, 1024], P('fsdp', 'ctx'), may hold values from 0 to 1023, each once within a row
- cotangent: bfloat16 [2, 2048, 2048], P('fsdp', 'ctx'), may hold values from -6 to 6
Outputs:
- outputs: bfloat16 [2, 2048, 2048], P('fsdp', 'ctx')
- input_grad: bfloat16 [2, 2048, 2048], P('fsdp', 'ctx')
- grad_w_query: float32 [2048, 4096], P('fsdp')
- grad_w_key: float32 [2048, 512], P('fsdp')
- grad_w_value: float32 [2048, 512], P('fsdp')
- grad_w_output: float32 [4096, 2048], P('fsdp')
- grad_norm_attn: float32 [2048], P('fsdp')
- grad_gain_query: float32 [128], P('fsdp')
- grad_gain_key: float32 [128], P('fsdp')
- grad_w_router: float32 [2048, 16], P('fsdp')
- grad_norm_moe: float32 [2048], P('fsdp')
- grad_w_gate: float32 [16, 2048, 768], P('ctx', 'fsdp')
- grad_w_up: float32 [16, 2048, 768], P('ctx', 'fsdp')
- grad_w_down: float32 [16, 2048, 768], P('ctx', 'fsdp')
Inputs may be any that keep to these rules, and one draw needn't show every extreme that they name: Each sequence holds, in an order drawn from the seed, one document of 1280 tokens, one of 204 tokens and two of 204 tokens or more; a sequence's lengths sum to 2048. `routes`: a token's 8 experts differ. `pair_order`: each device's row holds every number below 1024 once.
All inputs are finite; a program needn't handle non-finite values.
Results may differ from a plain program's by a relative error of at most 0.025.
Values may be sent and summed in bfloat16 or wider, within the bound.
No kernel may reach another device: no remote copies, remote signals or barrier semaphores. Data moves between devices by JAX's collectives and lax.ppermute only.
A program may use at most 256 MiB of HBM per device.

v0:
```python
import jax
import jax.numpy as jnp
from jax import lax
from jax.sharding import PartitionSpec as P

H = 32
KVH = 4
HD = 128
TOPK = 8


EPS = 1e-06
THETA = 1000000.0
HIGH = lax.Precision.HIGHEST


def rms_scale(values):
    return lax.rsqrt(jnp.mean(values * values, axis=-1, keepdims=True) + EPS)


def rotary_tables(positions, width):
    half = width // 2
    steps = jnp.arange(half, dtype=jnp.int32).astype(jnp.float32)
    inverse = jnp.exp(steps * (-2.0 * jnp.log(THETA) / width))
    angles = positions.astype(jnp.float32)[:, None] * inverse[None, :]
    return (jnp.cos(angles), jnp.sin(angles))


def rotate(values, cosine, sine):
    half = values.shape[-1] // 2
    first = values[..., :half]
    second = values[..., half:]
    return jnp.concatenate(
        [first * cosine - second * sine, second * cosine + first * sine], axis=-1
    )


def rotate_back(grad, cosine, sine):
    half = grad.shape[-1] // 2
    first = grad[..., :half]
    second = grad[..., half:]
    return jnp.concatenate(
        [first * cosine + second * sine, second * cosine - first * sine], axis=-1
    )


def documents(positions, lengths_row):
    ends = jnp.cumsum(lengths_row)
    return jnp.sum((positions[:, None] >= ends[None, :]).astype(jnp.int32), axis=1)


def placements(route_row, order_row, experts):
    ranked = jnp.zeros_like(route_row).at[order_row].set(route_row)
    table = (ranked[:, None] == jnp.arange(experts, dtype=jnp.int32)[None, :]).astype(jnp.int32)
    running = jnp.cumsum(table, axis=0)
    return (jnp.sum(running * table, axis=1) - 1)[order_row]


def norm_back(values, scale, gain, grad):
    scaled = grad * gain
    inner = jnp.mean(scaled * values, axis=-1, keepdims=True)
    return (scale * scaled - values * scale * scale * scale * inner, grad * values * scale)


def head_rows(values, kv_heads):
    count, heads, width = values.shape
    group = heads // kv_heads
    return (
        values.reshape(count, kv_heads, group, width)
        .transpose(1, 2, 0, 3)
        .reshape(kv_heads, group * count, width)
    )


def token_rows(values, count):
    kv_heads, rows, width = values.shape
    group = rows // count
    return (
        values.reshape(kv_heads, group, count, width)
        .transpose(2, 0, 1, 3)
        .reshape(count, kv_heads * group * width)
    )


def gather_keys(keys, values):
    return (
        lax.all_gather(keys, "ctx", axis=0, tiled=True),
        lax.all_gather(values, "ctx", axis=0, tiled=True),
    )


def masked_scores(query_rows, key_block, start, row_pos, row_seg, lengths_row, scale):
    width = key_block.shape[0]
    scores = (
        jnp.einsum("hrd,khd->hrk", query_rows, key_block, preferred_element_type=jnp.float32)
        * scale
    )
    key_pos = start + jnp.arange(width, dtype=jnp.int32)
    key_seg = documents(key_pos, lengths_row)
    allowed = (key_pos[None, :] <= row_pos[:, None]) & (key_seg[None, :] == row_seg[:, None])
    return (scores, allowed[None])


def local(
    inputs,
    w_query,
    w_key,
    w_value,
    w_output,
    norm_attn,
    gain_query,
    gain_key,
    w_router,
    norm_moe,
    w_gate,
    w_up,
    w_down,
    lengths,
    routes,
    pair_order,
    cotangent,
):
    n_ctx = lax.axis_size("ctx")
    count = inputs.shape[1]
    width = inputs.shape[2]
    length = count * n_ctx
    group = H // KVH
    scale = HD ** (-0.5)
    block = min(512, length)
    key_blocks = length // block
    query_all, key_weight, value_weight, output_all, attn_gain, query_gain, key_gain = (
        lax.all_gather(w_query, "fsdp", axis=0, tiled=True),
        lax.all_gather(w_key, "fsdp", axis=0, tiled=True),
        lax.all_gather(w_value, "fsdp", axis=0, tiled=True),
        lax.all_gather(w_output, "fsdp", axis=0, tiled=True),
        lax.all_gather(norm_attn, "fsdp", axis=0, tiled=True),
        lax.all_gather(gain_query, "fsdp", axis=0, tiled=True),
        lax.all_gather(gain_key, "fsdp", axis=0, tiled=True),
    )
    lengths_row = lengths[0]
    positions = lax.axis_index("ctx") * count + jnp.arange(count, dtype=jnp.int32)
    cosine, sine = rotary_tables(positions, HD)
    cosine = cosine[:, None, :]
    sine = sine[:, None, :]
    inputs_f = inputs[0].astype(jnp.float32)
    attn_scale = rms_scale(inputs_f)
    normed = (inputs_f * attn_scale * attn_gain.astype(jnp.float32)).astype(jnp.bfloat16)
    query_raw = jnp.dot(normed, query_all, preferred_element_type=jnp.float32).reshape(count, H, HD)
    key_raw = jnp.dot(normed, key_weight, preferred_element_type=jnp.float32).reshape(
        count, KVH, HD
    )
    value_raw = jnp.dot(normed, value_weight, preferred_element_type=jnp.float32)
    query_scale = rms_scale(query_raw)
    key_scale = rms_scale(key_raw)
    queries = rotate(query_raw * query_scale * query_gain.astype(jnp.float32), cosine, sine).astype(
        jnp.bfloat16
    )
    keys = rotate(key_raw * key_scale * key_gain.astype(jnp.float32), cosine, sine).astype(
        jnp.bfloat16
    )
    values = value_raw.astype(jnp.bfloat16)
    query_rows = head_rows(queries, KVH)
    row_pos = jnp.tile(positions, group)
    row_seg = documents(row_pos, lengths_row)
    flat_keys = keys.reshape(count, KVH * HD)
    key_all, value_all = gather_keys(flat_keys, values)
    row_count = query_rows.shape[1]

    def total_step(carry, number):
        best, total = carry
        start = number * block
        key_block = lax.dynamic_slice_in_dim(key_all, start, block, 0).reshape(block, KVH, HD)
        scores, allowed = masked_scores(
            query_rows, key_block, start, row_pos, row_seg, lengths_row, scale
        )
        scores = jnp.where(allowed, scores, -1e30)
        new_best = jnp.maximum(best, jnp.max(scores, axis=-1))
        total = total * jnp.exp(best - new_best) + jnp.sum(
            jnp.where(allowed, jnp.exp(scores - new_best[..., None]), 0.0), axis=-1
        )
        return ((new_best, total), None)

    start_best = jnp.full((KVH, row_count), -1e30, jnp.float32)
    start_total = jnp.zeros((KVH, row_count), jnp.float32)
    (best, total), unused = lax.scan(
        total_step, (start_best, start_total), jnp.arange(key_blocks, dtype=jnp.int32)
    )
    log_total = best + jnp.log(total)

    def output_step(carry, number):
        start = number * block
        key_block = lax.dynamic_slice_in_dim(key_all, start, block, 0).reshape(block, KVH, HD)
        value_block = lax.dynamic_slice_in_dim(value_all, start, block, 0).reshape(block, KVH, HD)
        scores, allowed = masked_scores(
            query_rows, key_block, start, row_pos, row_seg, lengths_row, scale
        )
        probs = jnp.where(allowed, jnp.exp(scores - log_total[..., None]), 0.0).astype(jnp.bfloat16)
        return (
            carry
            + jnp.einsum("hrk,khd->hrd", probs, value_block, preferred_element_type=jnp.float32),
            None,
        )

    mixed_rows, unused = lax.scan(
        output_step,
        jnp.zeros((KVH, row_count, HD), jnp.float32),
        jnp.arange(key_blocks, dtype=jnp.int32),
    )
    attended = token_rows(mixed_rows, count).astype(jnp.bfloat16)
    middle = inputs_f + jnp.dot(attended, output_all, preferred_element_type=jnp.float32)
    gate_all, up_all, down_all, router_all, moe_gain = (
        lax.all_gather(w_gate, "fsdp", axis=1, tiled=True),
        lax.all_gather(w_up, "fsdp", axis=1, tiled=True),
        lax.all_gather(w_down, "fsdp", axis=1, tiled=True),
        lax.all_gather(w_router, "fsdp", axis=0, tiled=True),
        lax.all_gather(norm_moe, "fsdp", axis=0, tiled=True),
    )
    moe_scale = rms_scale(middle)
    routed_in = (middle * moe_scale * moe_gain.astype(jnp.float32)).astype(jnp.bfloat16)
    n_exp = w_router.shape[1]
    capacity = 5 * count * TOPK // (4 * n_exp)
    pairs = count * TOPK
    total_slots = n_exp * capacity
    route_flat = routes[0].reshape(pairs)
    place = placements(route_flat, pair_order[0, 0], n_exp)
    kept = place < capacity
    pair_slot = jnp.where(kept, route_flat * capacity + place, total_slots)
    slot_pair = (
        jnp.full((total_slots,), pairs, jnp.int32)
        .at[pair_slot]
        .set(jnp.arange(pairs, dtype=jnp.int32), mode="drop")
    )
    slot_token = slot_pair // TOPK
    routed_pad = jnp.concatenate([routed_in, jnp.zeros((1, width), jnp.bfloat16)], axis=0)
    sending = routed_pad[slot_token].reshape(n_exp, capacity, width)
    received = lax.all_to_all(sending, "ctx", split_axis=0, concat_axis=1, tiled=True)
    gate_part = jnp.einsum("erd,edf->erf", received, gate_all, preferred_element_type=jnp.float32)
    up_part = jnp.einsum("erd,edf->erf", received, up_all, preferred_element_type=jnp.float32)
    sigma = jax.nn.sigmoid(gate_part)
    silu_gate = gate_part * sigma
    hidden = (silu_gate * up_part).astype(jnp.bfloat16)
    expert_out = jnp.einsum(
        "erf,edf->erd", hidden, down_all, preferred_element_type=jnp.float32
    ).astype(jnp.bfloat16)
    returned = lax.all_to_all(expert_out, "ctx", split_axis=1, concat_axis=0, tiled=True)
    returned_pad = jnp.concatenate(
        [returned.reshape(total_slots, width), jnp.zeros((1, width), jnp.bfloat16)], axis=0
    )
    per_pair = returned_pad[pair_slot].reshape(count, TOPK, width).astype(jnp.float32)
    onehot = (routes[0][:, :, None] == jnp.arange(n_exp, dtype=jnp.int32)[None, None, :]).astype(
        jnp.float32
    )
    logits = jnp.dot(routed_in, router_all, preferred_element_type=jnp.float32)
    chosen = jnp.einsum("tke,te->tk", onehot, logits, precision=HIGH)
    gates = jax.nn.softmax(chosen, axis=-1)
    kept_share = kept.reshape(count, TOPK).astype(jnp.float32)
    mixing = gates * kept_share
    moe = jnp.einsum("tk,tkd->td", mixing, per_pair, precision=HIGH)
    outputs = (middle + moe).astype(jnp.bfloat16)
    grad_out = cotangent[0].astype(jnp.float32)
    mixing_pad = jnp.concatenate([mixing.reshape(pairs), jnp.zeros((1,), jnp.float32)], axis=0)
    grad_pad = jnp.concatenate([grad_out, jnp.zeros((1, width), jnp.float32)], axis=0)
    pair_grad = (
        (mixing_pad[slot_pair][:, None] * grad_pad[slot_token])
        .astype(jnp.bfloat16)
        .reshape(n_exp, capacity, width)
    )
    gate_grad = jnp.einsum("tkd,td->tk", per_pair, grad_out, precision=HIGH) * kept_share
    received_grad = lax.all_to_all(pair_grad, "ctx", split_axis=0, concat_axis=1, tiled=True)
    hidden_grad = jnp.einsum(
        "erd,edf->erf", received_grad, down_all, preferred_element_type=jnp.float32
    )
    gate_part_grad = (hidden_grad * up_part * sigma * (1.0 + gate_part * (1.0 - sigma))).astype(
        jnp.bfloat16
    )
    up_part_grad = (hidden_grad * silu_gate).astype(jnp.bfloat16)
    grad_down_full = jnp.einsum(
        "erd,erf->edf", received_grad, hidden, preferred_element_type=jnp.float32
    )
    grad_gate_full = jnp.einsum(
        "erd,erf->edf", received, gate_part_grad, preferred_element_type=jnp.float32
    )
    grad_up_full = jnp.einsum(
        "erd,erf->edf", received, up_part_grad, preferred_element_type=jnp.float32
    )
    row_grad = jnp.einsum(
        "erf,edf->erd", gate_part_grad, gate_all, preferred_element_type=jnp.float32
    )
    row_grad = (
        row_grad
        + jnp.einsum("erf,edf->erd", up_part_grad, up_all, preferred_element_type=jnp.float32)
    ).astype(jnp.bfloat16)
    row_back = lax.all_to_all(row_grad, "ctx", split_axis=1, concat_axis=0, tiled=True)
    row_pad = jnp.concatenate(
        [row_back.reshape(total_slots, width), jnp.zeros((1, width), jnp.bfloat16)], axis=0
    )
    routed_grad = jnp.sum(
        row_pad[pair_slot].reshape(count, TOPK, width).astype(jnp.float32), axis=1
    )
    chosen_grad = gates * (gate_grad - jnp.sum(gates * gate_grad, axis=-1, keepdims=True))
    logit_grad = jnp.einsum("tk,tke->te", chosen_grad, onehot, precision=HIGH)
    routed_grad = routed_grad + jnp.dot(
        logit_grad, router_all.astype(jnp.float32).T, precision=HIGH
    )
    grad_router_full = jnp.dot(routed_in.astype(jnp.float32).T, logit_grad, precision=HIGH)
    moe_scaled = routed_grad * moe_gain.astype(jnp.float32)
    grad_moe_full = jnp.sum(routed_grad * middle * moe_scale, axis=0)
    middle_grad = (
        grad_out
        + moe_scale * moe_scaled
        - middle
        * moe_scale
        * moe_scale
        * moe_scale
        * jnp.mean(moe_scaled * middle, axis=-1, keepdims=True)
    )
    branch_grad = middle_grad.astype(jnp.bfloat16)
    grad_output_full = jnp.dot(attended.T, branch_grad, preferred_element_type=jnp.float32)
    attended_grad = jnp.dot(branch_grad, output_all.T, preferred_element_type=jnp.float32).astype(
        jnp.bfloat16
    )
    grad_rows = head_rows(attended_grad.reshape(count, H, HD), KVH)
    delta = jnp.sum(grad_rows.astype(jnp.float32) * mixed_rows, axis=-1)
    key_back, value_back = (key_all, value_all)

    def grad_step(carry, number):
        start = number * block
        key_block = lax.dynamic_slice_in_dim(key_back, start, block, 0).reshape(block, KVH, HD)
        value_block = lax.dynamic_slice_in_dim(value_back, start, block, 0).reshape(block, KVH, HD)
        scores, allowed = masked_scores(
            query_rows, key_block, start, row_pos, row_seg, lengths_row, scale
        )
        probs = jnp.where(allowed, jnp.exp(scores - log_total[..., None]), 0.0)
        value_grad = jnp.einsum(
            "hrk,hrd->khd",
            probs.astype(jnp.bfloat16),
            grad_rows,
            preferred_element_type=jnp.float32,
        )
        prob_grad = jnp.einsum(
            "hrd,khd->hrk", grad_rows, value_block, preferred_element_type=jnp.float32
        )
        score_grad = (probs * (prob_grad - delta[..., None])).astype(jnp.bfloat16)
        carry = (
            carry
            + jnp.einsum("hrk,khd->hrd", score_grad, key_block, preferred_element_type=jnp.float32)
            * scale
        )
        key_grad = (
            jnp.einsum("hrk,hrd->khd", score_grad, query_rows, preferred_element_type=jnp.float32)
            * scale
        )
        return (carry, (key_grad, value_grad))

    query_grad_rows, (key_grads, value_grads) = lax.scan(
        grad_step,
        jnp.zeros((KVH, row_count, HD), jnp.float32),
        jnp.arange(key_blocks, dtype=jnp.int32),
    )
    key_grad_all = key_grads.reshape(length, KVH * HD)
    value_grad_all = value_grads.reshape(length, KVH * HD)
    key_grad_own, value_grad_own = (
        lax.psum_scatter(
            key_grad_all.astype(jnp.bfloat16), "ctx", scatter_dimension=0, tiled=True
        ).astype(jnp.float32),
        lax.psum_scatter(
            value_grad_all.astype(jnp.bfloat16), "ctx", scatter_dimension=0, tiled=True
        ).astype(jnp.float32),
    )
    query_turned = rotate_back(
        token_rows(query_grad_rows, count).reshape(count, H, HD), cosine, sine
    )
    query_raw_grad, query_gain_terms = norm_back(
        query_raw, query_scale, query_gain.astype(jnp.float32), query_turned
    )
    key_turned = rotate_back(key_grad_own.reshape(count, KVH, HD), cosine, sine)
    key_raw_grad, key_gain_terms = norm_back(
        key_raw, key_scale, key_gain.astype(jnp.float32), key_turned
    )
    query_raw_b = query_raw_grad.reshape(count, H * HD).astype(jnp.bfloat16)
    key_raw_b = key_raw_grad.reshape(count, KVH * HD).astype(jnp.bfloat16)
    value_raw_b = value_grad_own.astype(jnp.bfloat16)
    grad_query_full = jnp.dot(normed.T, query_raw_b, preferred_element_type=jnp.float32)
    grad_key_full = jnp.dot(normed.T, key_raw_b, preferred_element_type=jnp.float32)
    grad_value_full = jnp.dot(normed.T, value_raw_b, preferred_element_type=jnp.float32)
    grad_qgain_full = jnp.sum(query_gain_terms, axis=(0, 1))
    grad_kgain_full = jnp.sum(key_gain_terms, axis=(0, 1))
    normed_grad = jnp.dot(query_raw_b, query_all.T, preferred_element_type=jnp.float32)
    normed_grad = normed_grad + jnp.dot(key_raw_b, key_weight.T, preferred_element_type=jnp.float32)
    normed_grad = normed_grad + jnp.dot(
        value_raw_b, value_weight.T, preferred_element_type=jnp.float32
    )
    attn_scaled = normed_grad * attn_gain.astype(jnp.float32)
    grad_attn_full = jnp.sum(normed_grad * inputs_f * attn_scale, axis=0)
    input_grad = (
        middle_grad
        + attn_scale * attn_scaled
        - inputs_f
        * attn_scale
        * attn_scale
        * attn_scale
        * jnp.mean(attn_scaled * inputs_f, axis=-1, keepdims=True)
    )
    parts = (
        lax.psum_scatter(
            grad_query_full.astype(jnp.bfloat16), "fsdp", scatter_dimension=0, tiled=True
        ).astype(jnp.float32),
        lax.psum_scatter(
            grad_key_full.astype(jnp.bfloat16), "fsdp", scatter_dimension=0, tiled=True
        ).astype(jnp.float32),
        lax.psum_scatter(
            grad_value_full.astype(jnp.bfloat16), "fsdp", scatter_dimension=0, tiled=True
        ).astype(jnp.float32),
        lax.psum_scatter(
            grad_output_full.astype(jnp.bfloat16), "fsdp", scatter_dimension=0, tiled=True
        ).astype(jnp.float32),
        lax.psum_scatter(
            grad_attn_full.astype(jnp.bfloat16), "fsdp", scatter_dimension=0, tiled=True
        ).astype(jnp.float32),
        lax.psum_scatter(
            grad_qgain_full.astype(jnp.bfloat16), "fsdp", scatter_dimension=0, tiled=True
        ).astype(jnp.float32),
        lax.psum_scatter(
            grad_kgain_full.astype(jnp.bfloat16), "fsdp", scatter_dimension=0, tiled=True
        ).astype(jnp.float32),
        lax.psum_scatter(
            grad_router_full.astype(jnp.bfloat16), "fsdp", scatter_dimension=0, tiled=True
        ).astype(jnp.float32),
        lax.psum_scatter(
            grad_moe_full.astype(jnp.bfloat16), "fsdp", scatter_dimension=0, tiled=True
        ).astype(jnp.float32),
        lax.psum_scatter(
            grad_gate_full.astype(jnp.bfloat16), "fsdp", scatter_dimension=1, tiled=True
        ).astype(jnp.float32),
        lax.psum_scatter(
            grad_up_full.astype(jnp.bfloat16), "fsdp", scatter_dimension=1, tiled=True
        ).astype(jnp.float32),
        lax.psum_scatter(
            grad_down_full.astype(jnp.bfloat16), "fsdp", scatter_dimension=1, tiled=True
        ).astype(jnp.float32),
    )
    (
        part_query,
        part_key,
        part_value,
        part_output,
        part_attn,
        part_qgain,
        part_kgain,
        part_router,
        part_moe,
        grad_w_gate,
        grad_w_up,
        grad_w_down,
    ) = parts
    shared = (
        lax.psum(part_query.astype(jnp.bfloat16), "ctx").astype(jnp.float32),
        lax.psum(part_key.astype(jnp.bfloat16), "ctx").astype(jnp.float32),
        lax.psum(part_value.astype(jnp.bfloat16), "ctx").astype(jnp.float32),
        lax.psum(part_output.astype(jnp.bfloat16), "ctx").astype(jnp.float32),
        lax.psum(part_attn.astype(jnp.bfloat16), "ctx").astype(jnp.float32),
        lax.psum(part_qgain.astype(jnp.bfloat16), "ctx").astype(jnp.float32),
        lax.psum(part_kgain.astype(jnp.bfloat16), "ctx").astype(jnp.float32),
        lax.psum(part_router.astype(jnp.bfloat16), "ctx").astype(jnp.float32),
        lax.psum(part_moe.astype(jnp.bfloat16), "ctx").astype(jnp.float32),
    )
    (
        grad_w_query,
        grad_w_key,
        grad_w_value,
        grad_w_output,
        grad_norm_attn,
        grad_gain_query,
        grad_gain_key,
        grad_w_router,
        grad_norm_moe,
    ) = shared
    return (
        outputs[None],
        input_grad.astype(jnp.bfloat16)[None],
        grad_w_query,
        grad_w_key,
        grad_w_value,
        grad_w_output,
        grad_norm_attn,
        grad_gain_query,
        grad_gain_key,
        grad_w_router,
        grad_norm_moe,
        grad_w_gate,
        grad_w_up,
        grad_w_down,
    )


def solution(mesh):
    in_specs = (
        P("fsdp", "ctx", None),
        P("fsdp", None),
        P("fsdp", None),
        P("fsdp", None),
        P("fsdp", None),
        P("fsdp"),
        P("fsdp"),
        P("fsdp"),
        P("fsdp", None),
        P("fsdp"),
        P("ctx", "fsdp", None),
        P("ctx", "fsdp", None),
        P("ctx", "fsdp", None),
        P("fsdp", None),
        P("fsdp", "ctx", None),
        P("fsdp", "ctx", None),
        P("fsdp", "ctx", None),
    )
    out_specs = (
        P("fsdp", "ctx", None),
        P("fsdp", "ctx", None),
        P("fsdp", None),
        P("fsdp", None),
        P("fsdp", None),
        P("fsdp", None),
        P("fsdp"),
        P("fsdp"),
        P("fsdp"),
        P("fsdp", None),
        P("fsdp"),
        P("ctx", "fsdp", None),
        P("ctx", "fsdp", None),
        P("ctx", "fsdp", None),
    )
    return jax.shard_map(local, mesh=mesh, in_specs=in_specs, out_specs=out_specs, check_vma=False)
```

profile of v0, /device:TPU:0, one launch (start us, length us, event | category | flops | bytes accessed | tf_op | source)
XLA Modules:
  0.0 2460.7 jit_solution(17383233619888262788)
XLA Ops:
  15.4 30.0 %all-gather.16.cloned.1.call-done = bf16[2048,512]{1,0:T(8,128)(2,1)} async-done(((bf16[1024,512]{1,0:T(8,128)(2,1)}), bf16[2048,512]{1,0:T(8,128)(2,1)}) %all-gather.16.cloned.1.call-update) | async-done | bytes 2097168 | tf_op jit(solution)/shard_map/all_gather | solution.py:134
  128.2 195.2 %all-gather.14.cloned.1.call-done = bf16[2048,4096]{1,0:T(8,128)(2,1)} async-done(((bf16[1024,4096]{1,0:T(8,128)(2,1)}), bf16[2048,4096]{1,0:T(8,128)(2,1)}) %all-gather.14.cloned.1.call-update) | async-done | bytes 16777232 | tf_op jit(solution)/shard_map/all_gather | solution.py:132
  367.2 55.5 %while.45 = (s32[]{:T(128)}, f32[4,1024]{1,0:T(4,128)S(1)}, f32[4,1024]{1,0:T(4,128)S(1)}, s32[4]{0:T(128)S(1)}, s32[1,4]{1,0:T(1,128)S(1)}, /*index=5*/s32[1024...) while((s32[]{:T(128)}, f32[4,1024]{1,0:T(4,128)S(1)}, ...), condition=%wide.region_10.11_spmd.clone, body=%wide.region_6.10_spmd.clone.sunk | while | flops 555247616 | bytes 21207776 | solution.py:185
  422.7 37.1 %while.46 = (s32[]{:T(128)}, f32[4,1024,128]{2,1,0:T(8,128)}, s32[4]{0:T(128)S(1)}, s32[1,4]{1,0:T(1,128)S(1)}, s32[1024]{0:T(1024)S(1)}, /*index=5*/bf16[2048,5...) while((s32[]{:T(128)}, f32[4,1024,128]{2,1,0:T(8,128)}, ...), condition=%wide.region_13.14_spmd.clone, body=%wide.region_11.13_spmd.clone.sunk | while | flops 1084758016 | bytes 9476841 | solution.py:204
  464.9 101.6 %all-gather.20.cloned.1.call-done = bf16[4096,2048]{1,0:T(8,128)(2,1)} async-done(((bf16[2048,2048]{1,0:T(8,128)(2,1)}), bf16[4096,2048]{1,0:T(8,128)(2,1)}) %all-gather.20.cloned.1.call-update) | async-done | bytes 16777232 | tf_op jit(solution)/shard_map/all_gather | solution.py:135
  616.8 67.0 %all-to-all-done = bf16[16,80,2048]{2,1,0:T(8,128)(2,1)} async-done(((bf16[16,80,2048]{2,1,0:T(8,128)(2,1)}), bf16[16,80,2048]{2,1,0:T(8,128)(2,1)}, u32[]{:S(2)}, u32[]{:S(2)}) %all-to-all-start) | async-done | bytes 5242912 | tf_op jit(solution)/shard_map/all_to_all | solution.py:236
  710.0 45.5 %all-gather.22.cloned.1.call-done = bf16[1,2048,768]{2,1,0:T(8,128)(2,1)} async-done(((bf16[1,1024,768]{2,1,0:T(8,128)(2,1)}), bf16[1,2048,768]{2,1,0:T(8,128)(2,1)}) %all-gather.22.cloned.1.call-update) | async-done | bytes 3145744 | tf_op jit(solution)/shard_map/all_gather | solution.py:212
  765.1 36.9 %all-gather.24.cloned.1.call-done = bf16[1,2048,768]{2,1,0:T(8,128)(2,1)} async-done(((bf16[1,1024,768]{2,1,0:T(8,128)(2,1)}), bf16[1,2048,768]{2,1,0:T(8,128)(2,1)}) %all-gather.24.cloned.1.call-update) | async-done | bytes 3145744 | tf_op jit(solution)/shard_map/all_gather | solution.py:213
  811.6 36.9 %all-gather.26.cloned.1.call-done = bf16[1,2048,768]{2,1,0:T(8,128)(2,1)} async-done(((bf16[1,1024,768]{2,1,0:T(8,128)(2,1)}), bf16[1,2048,768]{2,1,0:T(8,128)(2,1)}) %all-gather.26.cloned.1.call-update) | async-done | bytes 3145744 | tf_op jit(solution)/shard_map/all_gather | solution.py:214
  875.7 30.5 %copy.227 = bf16[1,1280,2048]{2,0,1:T(2,128)(2,1)} copy(bf16[1,1280,2048]{2,1,0:T(8,128)(2,1)S(1)} %fusion.37) | data formatting | bytes 10485760 | tf_op jit(solution)/shard_map/convert_element_type | solution.py:292
  906.7 32.9 %reduce = bf16[1280,2048]{1,0:T(8,128)(2,1)} reduce(bf16[1280,1,2048]{2,1,0:T(2,128)(2,1)} %bitcast.389, bf16[]{:T(256)} %broadcast.652), dimensions={1}, to_apply=%bitcast.307.reduce_sub_computation | reduce | bytes 10485762
  963.8 30.5 %copy.228 = bf16[1,1280,2048]{2,0,1:T(2,128)(2,1)} copy(bf16[1,1280,2048]{2,1,0:T(8,128)(2,1)S(1)} %fusion.36) | data formatting | bytes 10485760 | tf_op jit(solution)/shard_map/convert_element_type | solution.py:244
  994.3 32.9 %reduce.1 = bf16[1280,2048]{1,0:T(8,128)(2,1)} reduce(bf16[1280,1,2048]{2,1,0:T(2,128)(2,1)} %bitcast.390, bf16[]{:T(256)} %broadcast.652), dimensions={1}, to_apply=%bitcast.308.reduce_sub_computation | reduce | bytes 10485762
  1118.3 55.2 %all-to-all-done.1 = bf16[16,2,81920]{2,1,0:T(2,128)(2,1)} async-done(((bf16[16,2,81920]{2,1,0:T(2,128)(2,1)}), bf16[16,2,81920]{2,1,0:T(2,128)(2,1)}, u32[]{:S(2)}, u32[]{:S(2)}) %all-to-all-start.1) | async-done | bytes 5242912 | tf_op jit(solution)/shard_map/all_to_all | solution.py:245
  1236.5 100.2 %while.47 = (s32[]{:T(128)}, f32[4,1024,128]{2,1,0:T(8,128)}, bf16[4,512,4,128]{3,1,2,0:T(8,128)(2,1)}, bf16[4,512,4,128]{3,1,2,0:T(8,128)(2,1)}, s32[4]{0:T(128...) while((s32[]{:T(128)}, f32[4,1024,128]{2,1,0:T(8,128)}, ...), condition=%wide.region_28.29_spmd.clone, body=%wide.region_26.28_spmd.clone.sunk | while | flops 2708740096 | bytes 137436032 | solution.py:355
  1345.5 76.0 %reduce-scatter.11.cloned.1.call-done = bf16[128,512]{1,0:T(8,128)(2,1)} async-done(((bf16[2048,512]{1,0:T(8,128)(2,1)}), bf16[128,512]{1,0:T(8,128)(2,1)}) %reduce-scatter.11.cloned.1.call-update) | async-done | bytes 131088 | tf_op jit(solution)/shard_map/reduce_scatter | solution.py:363
  1425.1 61.8 %reduce-scatter.13.cloned.1.call-done = bf16[128,512]{1,0:T(8,128)(2,1)} async-done(((bf16[2048,512]{1,0:T(8,128)(2,1)}), bf16[128,512]{1,0:T(8,128)(2,1)}) %reduce-scatter.13.cloned.1.call-update) | async-done | bytes 131088 | tf_op jit(solution)/shard_map/reduce_scatter | solution.py:366
  1555.2 191.9 %reduce-scatter.15.cloned.1.call-done = bf16[1024,4096]{1,0:T(8,128)(2,1)} async-done(((bf16[2048,4096]{1,0:T(8,128)(2,1)}), bf16[1024,4096]{1,0:T(8,128)(2,1)}) %reduce-scatter.15.cloned.1.call-update) | async-done | bytes 8388624 | tf_op jit(solution)/shard_map/reduce_scatter | solution.py:405
  1747.1 192.0 %reduce-scatter.21.cloned.1.call-done = bf16[2048,2048]{1,0:T(8,128)(2,1)} async-done(((bf16[4096,2048]{1,0:T(8,128)(2,1)}), bf16[2048,2048]{1,0:T(8,128)(2,1)}) %reduce-scatter.21.cloned.1.call-update) | async-done | bytes 8388624 | tf_op jit(solution)/shard_map/reduce_scatter | solution.py:414
  1940.3 44.8 %reduce-scatter.25.cloned.1.call-done = bf16[1,1024,768]{2,1,0:T(8,128)(2,1)} async-done(((bf16[1,2048,768]{2,1,0:T(8,128)(2,1)}), bf16[1,1024,768]{2,1,0:T(8,128)(2,1)}) %reduce-scatter.25.cloned.1.call-update) | async-done | bytes 1572880 | tf_op jit(solution)/shard_map/reduce_scatter | solution.py:432
  1988.4 42.8 %reduce-scatter.27.cloned.1.call-done = bf16[1,1024,768]{2,1,0:T(8,128)(2,1)} async-done(((bf16[1,2048,768]{2,1,0:T(8,128)(2,1)}), bf16[1,1024,768]{2,1,0:T(8,128)(2,1)}) %reduce-scatter.27.cloned.1.call-update) | async-done | bytes 1572880 | tf_op jit(solution)/shard_map/reduce_scatter | solution.py:435
  2034.6 42.1 %reduce-scatter.29.cloned.1.call-done = bf16[1,1024,768]{2,1,0:T(8,128)(2,1)} async-done(((bf16[1,2048,768]{2,1,0:T(8,128)(2,1)}), bf16[1,1024,768]{2,1,0:T(8,128)(2,1)}) %reduce-scatter.29.cloned.1.call-update) | async-done | bytes 1572880 | tf_op jit(solution)/shard_map/reduce_scatter | solution.py:438
  2101.6 64.1 %all-reduce.10 = (bf16[1024]{0:T(1024)(128)(2,1)S(1)}, bf16[64]{0:T(256)(128)(2,1)S(1)}, bf16[64]{0:T(256)(128)(2,1)S(1)}, bf16[1024,16]{0,1:T(8,128)(2,1)S(1)}, bf16[1024]{0:T(1024)(128)(2,1)S(1)}) all-reduce(bf16[1024]{0:T(1024)(128)(2,1)S(1)} %dynamic-slice.3, ...), channel_id=1, replica_groups=mesh['ctx'=16,'fsdp'=2] {'ctx'}, use_global_device_ids=true, to_apply=%region_44.45 | all-reduce | flops 18560 | bytes 74240 | tf_op jit(solution)/shard_map/psum | solution.py:461
  2169.7 256.9 %all-reduce.16.cloned.1.call-done = (bf16[1024,4096]{1,0:T(8,128)(2,1)}, bf16[1024,512]{1,0:T(8,128)(2,1)}, bf16[1024,512]{1,0:T(8,128)(2,1)}, bf16[2048,2048]{1,0:T(8,128)(2,1)}) async-done(((bf16[1024,4096]{1,0:T(8,128)(2,1)}, bf16[1024,512]{1,0:T(8,128)(2,1)}, bf16[1024,512]{1,0:T(8,128)(2,1)}, bf16[2048,2048]{1,0:T(8,128)(2,1)}), (bf16[1024,4096]{1,0:T(8,128)(2,1)}, bf16[1024,512]{1,0:T(8,128)(2,1)}, ...) | async-done | bytes 18874384 | tf_op jit(solution)/shard_map/psum | solution.py:457
  (545 shorter events, 766.5 us)
Async XLA Ops:
  7.2 38.2 %all-gather.16.cloned.1.call-start = ((), (), s32[]{:S(2)}) async-start(), calls=%async_computation.17 | async-start | bytes 3145728 | tf_op jit(solution)/shard_map/all_gather | solution.py:134
  7.9 72.2 %all-gather.10.cloned.1.call-start = ((), (), s32[]{:S(2)}) async-start(), calls=%async_computation.14 | async-start | bytes 3145728 | tf_op jit(solution)/shard_map/all_gather | solution.py:133
  8.7 115.6 %all-gather.18.cloned.1.call-start = ((), (), s32[]{:S(2)}) async-start(), calls=%async_computation.18 | async-start | bytes 2228224 | tf_op jit(solution)/shard_map/all_gather | solution.py:88
  48.4 275.0 %all-gather.14.cloned.1.call-start = ((), (), s32[]{:S(2)}) async-start(), calls=%async_computation.16 | async-start | bytes 25165824 | tf_op jit(solution)/shard_map/all_gather | solution.py:132
  49.0 318.2 %all-gather.12.cloned.1.call-start = ((), (), s32[]{:S(2)}) async-start(), calls=%async_computation.15 | async-start | bytes 2228224 | tf_op jit(solution)/shard_map/all_gather | solution.py:87
  88.0 478.6 %all-gather.20.cloned.1.call-start = ((), (), s32[]{:S(2)}) async-start(), calls=%async_computation.19 | async-start | bytes 25165824 | tf_op jit(solution)/shard_map/all_gather | solution.py:135
  582.1 101.7 %all-to-all-start = ((bf16[16,80,2048]{2,1,0:T(8,128)(2,1)}), bf16[16,80,2048]{2,1,0:T(8,128)(2,1)}, u32[]{:S(2)}, u32[]{:S(2)}) async-start(bf16[16,80,2048]{2,1,0:T(8,128)(2,1)} %bitcast.393), calls=%async_computation | async-start | bytes 10485760 | tf_op jit(solution)/shard_map/all_to_all | solution.py:236
  683.9 164.6 %all-to-all-start.2 = ((bf16[16,80,2048]{2,1,0:T(8,128)(2,1)}), bf16[16,80,2048]{2,1,0:T(8,128)(2,1)}, u32[]{:S(2)}, u32[]{:S(2)}) async-start(bf16[16,80,2048]{2,1,0:T(8,128)(2,1)} %multiply_convert_fusion), calls=%async_computation.2 | async-start | bytes 10485760 | tf_op jit(solution)/shard_map/all_to_all | solution.py:269
  707.8 47.7 %all-gather.22.cloned.1.call-start = ((), (), s32[]{:S(2)}) async-start(), calls=%async_computation.20 | async-start | bytes 4718592 | tf_op jit(solution)/shard_map/all_gather | solution.py:212
  708.5 93.5 %all-gather.24.cloned.1.call-start = ((), (), s32[]{:S(2)}) async-start(), calls=%async_computation.21 | async-start | bytes 4718592 | tf_op jit(solution)/shard_map/all_gather | solution.py:213
  709.3 139.2 %all-gather.26.cloned.1.call-start = ((), (), s32[]{:S(2)}) async-start(), calls=%async_computation.22 | async-start | bytes 4718592 | tf_op jit(solution)/shard_map/all_gather | solution.py:214
  951.8 101.9 %all-to-all-start.3 = ((bf16[16,2,81920]{2,1,0:T(2,128)(2,1)}), bf16[16,2,81920]{2,1,0:T(2,128)(2,1)}, u32[]{:S(2)}, u32[]{:S(2)}) async-start(bf16[16,2,81920]{2,1,0:T(2,128)(2,1)} %reshape.858), calls=%async_computation.3 | async-start | bytes 10485760 | tf_op jit(solution)/shard_map/all_to_all | solution.py:293
  1053.6 119.8 %all-to-all-start.1 = ((bf16[16,2,81920]{2,1,0:T(2,128)(2,1)}), bf16[16,2,81920]{2,1,0:T(2,128)(2,1)}, u32[]{:S(2)}, u32[]{:S(2)}) async-start(bf16[16,2,81920]{2,1,0:T(2,128)(2,1)} %reshape.856), calls=%async_computation.1 | async-start | bytes 10485760 | tf_op jit(solution)/shard_map/all_to_all | solution.py:245
  1077.5 344.0 %reduce-scatter.11.cloned.1.call-start = ((), (), s32[]{:S(2)}) async-start(), calls=%async_computation.23 | async-start | bytes 2228224 | tf_op jit(solution)/shard_map/reduce_scatter | solution.py:363
  1341.6 145.3 %reduce-scatter.13.cloned.1.call-start = ((), (), s32[]{:S(2)}) async-start(), calls=%async_computation.24 | async-start | bytes 2228224 | tf_op jit(solution)/shard_map/reduce_scatter | solution.py:366
  1345.4 199.3 %reduce-scatter.17.cloned.1.call-start = ((), (), s32[]{:S(2)}) async-start(), calls=%async_computation.26 | async-start | bytes 3145728 | tf_op jit(solution)/shard_map/reduce_scatter | solution.py:408
  1425.1 130.1 %reduce-scatter.19.cloned.1.call-start = ((), (), s32[]{:S(2)}) async-start(), calls=%async_computation.27 | async-start | bytes 3145728 | tf_op jit(solution)/shard_map/reduce_scatter | solution.py:411
  1490.0 257.1 %reduce-scatter.15.cloned.1.call-start = ((), (), s32[]{:S(2)}) async-start(), calls=%async_computation.25 | async-start | bytes 25165824 | tf_op jit(solution)/shard_map/reduce_scatter | solution.py:405
  1504.4 434.6 %reduce-scatter.21.cloned.1.call-start = ((), (), s32[]{:S(2)}) async-start(), calls=%async_computation.28 | async-start | bytes 25165824 | tf_op jit(solution)/shard_map/reduce_scatter | solution.py:414
  1514.5 470.7 %reduce-scatter.25.cloned.1.call-start = ((), (), s32[]{:S(2)}) async-start(), calls=%async_computation.30 | async-start | bytes 4718592 | tf_op jit(solution)/shard_map/reduce_scatter | solution.py:432
  1523.9 507.4 %reduce-scatter.27.cloned.1.call-start = ((), (), s32[]{:S(2)}) async-start(), calls=%async_computation.31 | async-start | bytes 4718592 | tf_op jit(solution)/shard_map/reduce_scatter | solution.py:435
  1533.1 543.6 %reduce-scatter.29.cloned.1.call-start = ((), (), s32[]{:S(2)}) async-start(), calls=%async_computation.32 | async-start | bytes 4718592 | tf_op jit(solution)/shard_map/reduce_scatter | solution.py:438
  1542.6 559.0 %reduce-scatter.23.cloned.1.call-start = ((), (), s32[]{:S(2)}) async-start(), calls=%async_computation.29 | async-start | bytes 98304 | tf_op jit(solution)/shard_map/reduce_scatter | solution.py:426
  1544.7 881.9 %all-reduce.16.cloned.1.call-start = ((), (), s32[]{:S(2)}) async-start(), calls=%async_computation.33 | async-start | bytes 37748736 | tf_op jit(solution)/shard_map/psum | solution.py:457
  (103 other events, 3885.8 us)
Sparse Core Ops, SparseCore 0:
  9.6 35.8 all-gather.15
  47.0 33.1 all-gather.9
  82.8 41.3 all-gather.17
  125.7 197.6 all-gather.13
  325.9 41.1 all-gather.11
  368.6 197.9 all-gather.19
  710.2 45.2 all-gather.21
  757.0 44.9 all-gather.23
  803.5 44.9 all-gather.25
  1341.7 79.7 reduce-scatter.10
  1426.3 60.6 reduce-scatter.12
  1489.6 30.7 reduce-scatter.16
  1523.3 31.8 reduce-scatter.18
  1557.9 189.1 reduce-scatter.14
  1749.9 189.1 reduce-scatter.20
  1941.7 43.3 reduce-scatter.24
  1987.9 43.3 reduce-scatter.26
  2033.4 43.3 reduce-scatter.28
  2079.6 9.8 reduce-scatter.22
  2094.5 332.0 all-reduce.15
where the time goes:
time: 2470 us; the launch traced here: 2460 us
  waiting for transfers between devices  1550 us (63%)
  local copies, waits for them, and re-layouts  284 us (11%)
  matrix products  283 us (11%)
  other arithmetic  166 us (7%)
  blocking collectives  88.5 us (4%)
  starting transfers between devices  61.3 us (2%)
    psum x1, waiting for transfers between devices, local(): lax.psum(part_query.astype(jnp.bfloat16), 'ctx').astype(jnp.float32)  257 us
    all_gather x1, waiting for transfers between devices, local(): lax.all_gather(w_query, 'fsdp', axis=0, tiled=True)  195 us
    reduce_scatter x1, waiting for transfers between devices, local(): lax.psum_scatter(grad_output_full.astype(jnp.bfloat16), 'fsdp', scatter_d...  192 us
    reduce_scatter x1, waiting for transfers between devices, local(): lax.psum_scatter(grad_query_full.astype(jnp.bfloat16), 'fsdp', scatter_di...  192 us
    all_gather x1, waiting for transfers between devices, local(): lax.all_gather(w_output, 'fsdp', axis=0, tiled=True)  102 us
    unnamed x195, local copies, waits for them, and re-layouts  82.7 us
    reduce_scatter x1, waiting for transfers between devices, local(): lax.psum_scatter(key_grad_all.astype(jnp.bfloat16), 'ctx', scatter_dimens...  76 us
    all_to_all x1, waiting for transfers between devices, local(): lax.all_to_all(sending, 'ctx', split_axis=0, concat_axis=1, tiled=True)  67 us
  transfers between devices with their start and end apart: 24, of which 21 were waited for; matrix products, arithmetic and copies ran while one was open for 17% of the time, Pallas kernels for 0%

commit v1 on v0

v1 whole, which is shorter than its diff:
```python
import functools

import jax
import jax.numpy as jnp
from jax import lax
from jax.experimental import pallas as pl
from jax.experimental.pallas import tpu as pltpu
from jax.sharding import PartitionSpec as P

H = 32
KVH = 4
HD = 128
TOPK = 8
EPS = 1e-06
THETA = 1000000.0
HIGH = lax.Precision.HIGHEST
LOG2E = 1.4426950408889634
F32 = jnp.float32
BF16 = jnp.bfloat16
ROWS_T = (((1,), (1,)), ((), ()))
COLS_T = (((0,), (0,)), ((), ()))
VMEM_LIMIT = 48 * 1024 * 1024


def dot(a, b, dims=(((1,), (0,)), ((), ()))):
    return lax.dot_general(a, b, dims, preferred_element_type=F32)


def params(limit=VMEM_LIMIT):
    return pltpu.CompilerParams(vmem_limit_bytes=limit)


def cost(flops, moved, transcendentals=0):
    return pl.CostEstimate(
        flops=int(flops), bytes_accessed=int(moved), transcendentals=int(transcendentals)
    )


def flip(n_ctx, bit):
    return [(i, i ^ bit) for i in range(n_ctx)]


def ring(n_ctx, step):
    return [(i, (i + step) % n_ctx) for i in range(n_ctx)]


def block_order(n_ctx):
    c = lax.axis_index("ctx")
    nz = n_ctx // 4
    z, x, core = c // 4, (c // 2) % 2, c % 2
    table = []
    for dc in range(2):
        for k in range(nz):
            for dx in range(2):
                table.append(lax.rem(z + nz - k, nz) * 4 + (x ^ dx) * 2 + (core ^ dc))
    return jnp.stack(table).astype(jnp.int32)


def gather_ctx(piece, n_ctx):
    nz = n_ctx // 4
    pieces = []
    current = piece
    for k in range(nz):
        following = lax.ppermute(current, "ctx", ring(n_ctx, 4)) if k < nz - 1 else None
        pieces += [current, lax.ppermute(current, "ctx", flip(n_ctx, 2))]
        current = following
    mine = jnp.stack(pieces)
    return mine, lax.ppermute(mine, "ctx", flip(n_ctx, 1))


def scatter_ctx(mine, others, n_ctx):
    nz = n_ctx // 4
    arrived = lax.ppermute(others, "ctx", flip(n_ctx, 1))
    both = (mine.astype(F32) + arrived.astype(F32)).astype(BF16)
    carry = None
    for k in reversed(range(nz)):
        other = lax.ppermute(both[2 * k + 1], "ctx", flip(n_ctx, 2))
        total = both[2 * k].astype(F32) + other.astype(F32)
        if carry is not None:
            total = total + carry.astype(F32)
        if k > 0:
            carry = lax.ppermute(total.astype(BF16), "ctx", ring(n_ctx, -4))
    return total


def gather_fsdp(part):
    n_f = lax.axis_size("fsdp")
    if n_f != 2:
        return lax.all_gather(part, "fsdp", axis=0, tiled=True)
    other = lax.ppermute(part, "fsdp", [(0, 1), (1, 0)])
    first = lax.axis_index("fsdp") == 0
    return jnp.concatenate([jnp.where(first, part, other), jnp.where(first, other, part)], axis=0)


def scatter_fsdp(full):
    n_f = lax.axis_size("fsdp")
    if n_f != 2:
        return lax.psum_scatter(
            full.astype(BF16), "fsdp", scatter_dimension=0, tiled=True
        ).astype(F32)
    rows = full.shape[0] // 2
    first = lax.axis_index("fsdp") == 0
    low, high = full[:rows], full[rows:]
    sent = jnp.where(first, high, low).astype(BF16)
    other = lax.ppermute(sent, "fsdp", [(0, 1), (1, 0)])
    return jnp.where(first, low, high).astype(F32) + other.astype(F32)


def rotary_tables(length):
    half = HD // 2
    steps = jnp.arange(half, dtype=jnp.int32).astype(F32)
    inverse = jnp.exp(steps * (-2.0 * jnp.log(THETA) / HD))
    angles = jnp.arange(length, dtype=jnp.int32).astype(F32)[:, None] * inverse[None, :]
    cosine, sine = jnp.cos(angles), jnp.sin(angles)
    return (
        jnp.concatenate([cosine, cosine], axis=1),
        jnp.concatenate([-sine, sine], axis=1),
    )


def half_turn(v):
    return pltpu.roll(v, HD // 2, 1)


def qkv_kernel(
    hpd, table, xa, xb, w, gain, gq, gk, cosine, sine, normed, raw, query, key, value
):
    r = pl.program_id(0)
    half = pl.num_programs(0) // 2

    def body(x_ref):
        x = x_ref[0].astype(F32)
        r1 = lax.rsqrt(jnp.mean(x * x, axis=-1, keepdims=True) + EPS)
        n = (x * r1 * gain[...]).astype(BF16)
        normed[0] = n
        out = dot(n, w[...])
        raw[0] = out
        cos, sin = cosine[...], sine[...]
        for j in range(3 * hpd):
            v = out[:, j * HD : (j + 1) * HD]
            if j >= 2 * hpd:
                value[j - 2 * hpd] = v.astype(BF16)
                continue
            scale = lax.rsqrt(jnp.mean(v * v, axis=-1, keepdims=True) + EPS)
            v = v * scale * (gq[...] if j < hpd else gk[...])
            v = (v * cos + half_turn(v) * sin).astype(BF16)
            if j < hpd:
                query[j] = v
            else:
                key[j - hpd] = v

    @pl.when(r < half)
    def _():
        body(xa)

    @pl.when(r >= half)
    def _():
        body(xb)


def project(xa, xb, w, gain, gq, gk, cosine, sine, table, hpd):
    half, count, width = xa.shape
    n = 2 * half
    length = n * count
    cols = w.shape[1]
    whole = lambda r, t: (0, 0)
    at = lambda r, t: (t[r], 0)
    head_at = lambda r, t: (0, t[r], 0)
    head = jax.ShapeDtypeStruct((hpd, length, HD), BF16)
    return pl.pallas_call(
        functools.partial(qkv_kernel, hpd),
        grid_spec=pltpu.PrefetchScalarGridSpec(
            num_scalar_prefetch=1,
            grid=(n,),
            in_specs=[
                pl.BlockSpec((1, count, width), lambda r, t: (jnp.minimum(r, half - 1), 0, 0)),
                pl.BlockSpec((1, count, width), lambda r, t: (jnp.maximum(r - half, 0), 0, 0)),
                pl.BlockSpec((width, cols), whole),
                pl.BlockSpec((1, width), whole),
                pl.BlockSpec((1, HD), whole),
                pl.BlockSpec((1, HD), whole),
                pl.BlockSpec((count, HD), at),
                pl.BlockSpec((count, HD), at),
            ],
            out_specs=[
                pl.BlockSpec((1, count, width), lambda r, t: (r, 0, 0)),
                pl.BlockSpec((1, count, cols), lambda r, t: (r, 0, 0)),
                pl.BlockSpec((hpd, count, HD), head_at),
                pl.BlockSpec((hpd, count, HD), head_at),
                pl.BlockSpec((hpd, count, HD), head_at),
            ],
        ),
        out_shape=[
            jax.ShapeDtypeStruct((n, count, width), BF16),
            jax.ShapeDtypeStruct((n, count, cols), F32),
            head,
            head,
            head,
        ],
        compiler_params=params(),
        cost_estimate=cost(2 * length * width * cols, 4 * length * width + 8 * length * cols),
        name="project",
    )(table, xa, xb, w, gain, gq, gk, cosine, sine)


def qkv_back_kernel(hpd, table, dq, dk, dv, raw, cosine, sine, gq, gk, out, gains):
    r = pl.program_id(0)

    @pl.when(r == 0)
    def _():
        gains[...] = jnp.zeros_like(gains)

    cos, sin = cosine[...], sine[...]
    factor = HD**-0.5
    for j in range(2 * hpd):
        grad = (dq[j] if j < hpd else dk[j - hpd]) * factor
        gain = gq[...] if j < hpd else gk[...]
        v = raw[0, :, j * HD : (j + 1) * HD]
        scale = lax.rsqrt(jnp.mean(v * v, axis=-1, keepdims=True) + EPS)
        d = grad * cos - half_turn(grad) * sin
        u = d * gain
        inner = jnp.mean(u * v, axis=-1, keepdims=True)
        out[0, :, j * HD : (j + 1) * HD] = (
            scale * u - v * (scale * scale * scale * inner)
        ).astype(BF16)
        term = jnp.sum(d * v * scale, axis=0, keepdims=True)
        row = 0 if j < hpd else 1
        gains[row : row + 1, :] += term
    for j in range(hpd):
        out[0, :, (2 * hpd + j) * HD : (2 * hpd + j + 1) * HD] = dv[j].astype(BF16)


def qkv_back(dq, dk, dv, raw, cosine, sine, gq, gk, table, hpd):
    n, count, cols = raw.shape
    whole = lambda r, t: (0, 0)
    at = lambda r, t: (t[r], 0)
    head_at = lambda r, t: (0, t[r], 0)
    return pl.pallas_call(
        functools.partial(qkv_back_kernel, hpd),
        grid_spec=pltpu.PrefetchScalarGridSpec(
            num_scalar_prefetch=1,
            grid=(n,),
            in_specs=[
                pl.BlockSpec((hpd, count, HD), head_at),
                pl.BlockSpec((hpd, count, HD), head_at),
                pl.BlockSpec((hpd, count, HD), head_at),
                pl.BlockSpec((1, count, cols), lambda r, t: (r, 0, 0)),
                pl.BlockSpec((count, HD), at),
                pl.BlockSpec((count, HD), at),
                pl.BlockSpec((1, HD), whole),
                pl.BlockSpec((1, HD), whole),
            ],
            out_specs=[
                pl.BlockSpec((1, count, cols), lambda r, t: (r, 0, 0)),
                pl.BlockSpec((8, HD), whole),
            ],
        ),
        out_shape=[
            jax.ShapeDtypeStruct((n, count, cols), BF16),
            jax.ShapeDtypeStruct((8, HD), F32),
        ],
        compiler_params=params(),
        cost_estimate=cost(20 * n * count * cols, 10 * n * count * cols),
        name="qkv_back",
    )(table, dq, dk, dv, raw, cosine, sine, gq, gk)


def first_key(ends, docs, position):
    start = jnp.zeros_like(position)
    for d in range(docs):
        start = jnp.where(position >= ends[d], jnp.maximum(start, ends[d]), start)
    return start


def attend_kernel(docs, bq, bk, ends, query, key, value, mixed, total):
    i = pl.program_id(1)
    q = query[0]
    positions = i * bq + lax.broadcasted_iota(jnp.int32, (bq, 1), 0)
    starts = first_key(ends, docs, positions)
    low = lax.div(first_key(ends, docs, i * bq), bk)
    high = lax.div((i + 1) * bq - 1, bk) + 1

    def step(j, carry):
        acc, sums = carry
        rows = pl.ds(pl.multiple_of(j * bk, bk), bk)
        scores = dot(q, key[0, rows, :], ROWS_T)
        spots = j * bk + lax.broadcasted_iota(jnp.int32, (1, bk), 1)
        seen = (spots <= positions) & (spots >= starts)
        p = jnp.where(seen, jnp.exp2(scores * (LOG2E * HD**-0.5)), 0.0)
        return acc + dot(p.astype(BF16), value[0, rows, :]), sums + jnp.sum(
            p, axis=-1, keepdims=True
        )

    acc, sums = lax.fori_loop(
        low, high, step, (jnp.zeros((bq, HD), F32), jnp.zeros((bq, 1), F32))
    )
    mixed[0] = acc / sums
    total[0] = jnp.broadcast_to(jnp.log2(sums), (bq, HD))


def attend(query, key, value, ends, bq=256, bk=256):
    heads, length, _ = query.shape
    docs = ends.shape[0]
    block = pl.BlockSpec((1, bq, HD), lambda h, i, e: (h, i, 0))
    whole = pl.BlockSpec((1, length, HD), lambda h, i, e: (h, 0, 0))
    out = jax.ShapeDtypeStruct((heads, length, HD), F32)
    return pl.pallas_call(
        functools.partial(attend_kernel, docs, bq, bk),
        grid_spec=pltpu.PrefetchScalarGridSpec(
            num_scalar_prefetch=1,
            grid=(heads, length // bq),
            in_specs=[block, whole, whole],
            out_specs=[block, block],
        ),
        out_shape=[out, out],
        compiler_params=params(),
        cost_estimate=cost(
            heads * length * length * HD * 2, heads * length * HD * 14, heads * length * length // 2
        ),
        name="attend",
    )(ends, query, key, value)


def attend_back_kernel(docs, bq, bk, ends, query, grad, total, delta, key, value, dq, dk, dv):
    i = pl.program_id(1)

    @pl.when(i == 0)
    def _():
        dk[...] = jnp.zeros_like(dk)
        dv[...] = jnp.zeros_like(dv)

    q, g = query[0], grad[0]
    log_total, shift = total[0], delta[0]
    positions = i * bq + lax.broadcasted_iota(jnp.int32, (1, bq), 1)
    starts = first_key(ends, docs, positions)
    low = lax.div(first_key(ends, docs, i * bq), bk)
    high = lax.div((i + 1) * bq - 1, bk) + 1

    def step(j, acc):
        rows = pl.ds(pl.multiple_of(j * bk, bk), bk)
        k, v = key[0, rows, :], value[0, rows, :]
        scores = dot(k, q, ROWS_T)
        spots = j * bk + lax.broadcasted_iota(jnp.int32, (bk, 1), 0)
        seen = (spots <= positions) & (spots >= starts)
        p = jnp.where(seen, jnp.exp2(scores * (LOG2E * HD**-0.5) - log_total), 0.0)
        ds = (p * (dot(v, g, ROWS_T) - shift)).astype(BF16)
        dv[0, rows, :] += dot(p.astype(BF16), g)
        dk[0, rows, :] += dot(ds, q)
        return acc + dot(ds, k, COLS_T)

    dq[0] = lax.fori_loop(low, high, step, jnp.zeros((bq, HD), F32))


def attend_back(query, grad, total, delta, key, value, ends, bq=256, bk=256):
    heads, length, _ = query.shape
    docs = ends.shape[0]
    block = pl.BlockSpec((1, bq, HD), lambda h, i, e: (h, i, 0))
    line = pl.BlockSpec((1, 1, bq), lambda h, i, e: (h, 0, i))
    whole = pl.BlockSpec((1, length, HD), lambda h, i, e: (h, 0, 0))
    out = jax.ShapeDtypeStruct((heads, length, HD), F32)
    return pl.pallas_call(
        functools.partial(attend_back_kernel, docs, bq, bk),
        grid_spec=pltpu.PrefetchScalarGridSpec(
            num_scalar_prefetch=1,
            grid=(heads, length // bq),
            in_specs=[block, block, line, line, whole, whole],
            out_specs=[block, whole, whole],
        ),
        out_shape=[out, out, out],
        compiler_params=params(),
        cost_estimate=cost(
            heads * length * length * HD * 5, heads * length * HD * 20, heads * length * length // 2
        ),
        name="attend_back",
    )(ends, query, grad, total, delta, key, value)


def branch_kernel(hpd, table, mixed, w, out):
    total = None
    for j in range(hpd):
        part = dot(mixed[j].astype(BF16), w[j * HD : (j + 1) * HD, :])
        total = part if total is None else total + part
    out[0] = total.astype(BF16)


def branch_half(mixed, w, table, first, blocks):
    hpd, length, _ = mixed.shape
    count = length // (2 * blocks)
    width = w.shape[1]
    return pl.pallas_call(
        functools.partial(branch_kernel, hpd),
        grid_spec=pltpu.PrefetchScalarGridSpec(
            num_scalar_prefetch=1,
            grid=(blocks,),
            in_specs=[
                pl.BlockSpec((hpd, count, HD), lambda r, t: (0, t[r + first], 0)),
                pl.BlockSpec((hpd * HD, width), lambda r, t: (0, 0)),
            ],
            out_specs=pl.BlockSpec((1, count, width), lambda r, t: (r, 0, 0)),
        ),
        out_shape=jax.ShapeDtypeStruct((blocks, count, width), BF16),
        compiler_params=params(),
        cost_estimate=cost(length * hpd * HD * width, length * width),
        name="branch",
    )(table, mixed, w)


def branch_back_kernel(hpd, table, ga, gb, mixed, w, grad, dw):
    r = pl.program_id(0)
    half = pl.num_programs(0) // 2

    @pl.when(r == 0)
    def _():
        dw[...] = jnp.zeros_like(dw)

    def body(g_ref):
        g = g_ref[0]
        back = dot(g, w[...], ROWS_T)
        for j in range(hpd):
            grad[j] = back[:, j * HD : (j + 1) * HD].astype(BF16)
            dw[j * HD : (j + 1) * HD, :] += dot(mixed[j].astype(BF16), g, COLS_T)

    @pl.when(r < half)
    def _():
        body(ga)

    @pl.when(r >= half)
    def _():
        body(gb)


def branch_back(ga, gb, mixed, w, table):
    half, count, width = ga.shape
    hpd, length, _ = mixed.shape
    head_at = lambda r, t: (0, t[r], 0)
    return pl.pallas_call(
        functools.partial(branch_back_kernel, hpd),
        grid_spec=pltpu.PrefetchScalarGridSpec(
            num_scalar_prefetch=1,
            grid=(2 * half,),
            in_specs=[
                pl.BlockSpec((1, count, width), lambda r, t: (jnp.minimum(r, half - 1), 0, 0)),
                pl.BlockSpec((1, count, width), lambda r, t: (jnp.maximum(r - half, 0), 0, 0)),
                pl.BlockSpec((hpd, count, HD), head_at),
                pl.BlockSpec((hpd * HD, width), lambda r, t: (0, 0)),
            ],
            out_specs=[
                pl.BlockSpec((hpd, count, HD), head_at),
                pl.BlockSpec((hpd * HD, width), lambda r, t: (0, 0)),
            ],
        ),
        out_shape=[
            jax.ShapeDtypeStruct((hpd, length, HD), BF16),
            jax.ShapeDtypeStruct((hpd * HD, width), F32),
        ],
        compiler_params=params(),
        cost_estimate=cost(4 * length * hpd * HD * width, 2 * length * width),
        name="branch_back",
    )(table, ga, gb, mixed, w)


def slots_of(place, capacity):
    spots = lax.broadcasted_iota(jnp.int32, (capacity, place.shape[1]), 0)
    return spots == place


def take_rows_kernel(capacity, table, xa, xb, place, router, rows, logits):
    r = pl.program_id(0)
    half = pl.num_programs(0) // 2

    def body(x_ref):
        x = x_ref[0]
        chosen = slots_of(place[0], capacity).astype(BF16)
        rows[0] = dot(chosen, x).astype(BF16)
        logits[0] = dot(x, router[...])

    @pl.when(r < half)
    def _():
        body(xa)

    @pl.when(r >= half)
    def _():
        body(xb)


def take_rows(xa, xb, place, router, table, capacity):
    half, count, width = xa.shape
    n = 2 * half
    lanes = router.shape[1]
    at = lambda r, t: (t[r], 0, 0)
    return pl.pallas_call(
        functools.partial(take_rows_kernel, capacity),
        grid_spec=pltpu.PrefetchScalarGridSpec(
            num_scalar_prefetch=1,
            grid=(n,),
            in_specs=[
                pl.BlockSpec((1, count, width), lambda r, t: (jnp.minimum(r, half - 1), 0, 0)),
                pl.BlockSpec((1, count, width), lambda r, t: (jnp.maximum(r - half, 0), 0, 0)),
                pl.BlockSpec((1, 1, count), at),
                pl.BlockSpec((width, lanes), lambda r, t: (0, 0)),
            ],
            out_specs=[
                pl.BlockSpec((1, capacity, width), lambda r, t: (r, 0, 0)),
                pl.BlockSpec((1, count, lanes), at),
            ],
        ),
        out_shape=[
            jax.ShapeDtypeStruct((n, capacity, width), BF16),
            jax.ShapeDtypeStruct((n, count, lanes), F32),
        ],
        compiler_params=params(),
        cost_estimate=cost(4 * n * count * width * 128, 6 * n * count * width),
        name="take_rows",
    )(table, xa, xb, place, router)


def take_grads_kernel(capacity, table, grads, place, gates, rows, scaled, gate_rows):
    chosen = slots_of(place[0], capacity)
    picked = dot(chosen.astype(BF16), grads[0])
    rows[0] = picked.astype(BF16)
    gate = jnp.sum(jnp.where(chosen, gates[0], 0.0), axis=1, keepdims=True)
    scaled[0] = (picked * gate).astype(BF16)
    gate_rows[0] = jnp.broadcast_to(gate, gate_rows.shape[1:])


def take_grads(grads, place, gates, table, capacity):
    n, count, width = grads.shape
    at = lambda r, t: (t[r], 0, 0)
    own = lambda r, t: (r, 0, 0)
    return pl.pallas_call(
        functools.partial(take_grads_kernel, capacity),
        grid_spec=pltpu.PrefetchScalarGridSpec(
            num_scalar_prefetch=1,
            grid=(n,),
            in_specs=[
                pl.BlockSpec((1, count, width), at),
                pl.BlockSpec((1, 1, count), at),
                pl.BlockSpec((1, 1, count), at),
            ],
            out_specs=[
                pl.BlockSpec((1, capacity, width), own),
                pl.BlockSpec((1, capacity, width), own),
                pl.BlockSpec((1, capacity, 128), own),
            ],
        ),
        out_shape=[
            jax.ShapeDtypeStruct((n, capacity, width), BF16),
            jax.ShapeDtypeStruct((n, capacity, width), BF16),
            jax.ShapeDtypeStruct((n, capacity, 128), F32),
        ],
        compiler_params=params(),
        cost_estimate=cost(2 * n * count * width * 128, 6 * n * count * width),
        name="take_grads",
    )(table, grads, place, gates)


def give_results_kernel(capacity, table, results, grads, gate_rows, place, out, gate_grads):
    chosen = slots_of(place[0], capacity)
    result = results[0].astype(F32)
    scaled = (result * gate_rows[0][:, :1]).astype(BF16)
    out[0] = dot(chosen.astype(BF16), scaled, COLS_T).astype(BF16)
    inner = jnp.sum(result * grads[0].astype(F32), axis=1, keepdims=True)
    gate_grads[0] = jnp.sum(jnp.where(chosen, inner, 0.0), axis=0, keepdims=True)


def give_results(results, grads, gate_rows, place, table):
    n, capacity, width = results.shape
    count = place.shape[2]
    at = lambda r, t: (t[r], 0, 0)
    own = lambda r, t: (r, 0, 0)
    return pl.pallas_call(
        functools.partial(give_results_kernel, capacity),
        grid_spec=pltpu.PrefetchScalarGridSpec(
            num_scalar_prefetch=1,
            grid=(n,),
            in_specs=[
                pl.BlockSpec((1, capacity, width), own),
                pl.BlockSpec((1, capacity, width), own),
                pl.BlockSpec((1, capacity, 128), own),
                pl.BlockSpec((1, 1, count), at),
            ],
            out_specs=[
                pl.BlockSpec((1, count, width), at),
                pl.BlockSpec((1, 1, count), at),
            ],
        ),
        out_shape=[
            jax.ShapeDtypeStruct((n, count, width), BF16),
            jax.ShapeDtypeStruct((n, 1, count), F32),
        ],
        compiler_params=params(),
        cost_estimate=cost(2 * n * count * width * 128, 6 * n * count * width),
        name="give_results",
    )(table, results, grads, gate_rows, place)


def give_rows_kernel(capacity, table, rows, place, out):
    chosen = slots_of(place[0], capacity).astype(BF16)
    out[0] = dot(chosen, rows[0], COLS_T).astype(BF16)


def give_rows_half(rows, place, table, first, blocks):
    n, capacity, width = rows.shape
    count = place.shape[2]
    return pl.pallas_call(
        functools.partial(give_rows_kernel, capacity),
        grid_spec=pltpu.PrefetchScalarGridSpec(
            num_scalar_prefetch=1,
            grid=(blocks,),
            in_specs=[
                pl.BlockSpec((1, capacity, width), lambda r, t: (r + first, 0, 0)),
                pl.BlockSpec((1, 1, count), lambda r, t: (t[r + first], 0, 0)),
            ],
            out_specs=pl.BlockSpec((1, count, width), lambda r, t: (r, 0, 0)),
        ),
        out_shape=jax.ShapeDtypeStruct((blocks, count, width), BF16),
        compiler_params=params(),
        cost_estimate=cost(2 * blocks * count * width * 128, 4 * blocks * count * width),
        name="give_rows",
    )(table, rows, place)


def input_back_kernel(grads, w, x_ref, out, gain_grad):
    @pl.when(pl.program_id(0) == 0)
    def _():
        gain_grad[...] = jnp.zeros_like(gain_grad)

    back = dot(grads[0], w[...], ROWS_T)
    out[0] = back.astype(BF16)
    x = x_ref[0].astype(F32)
    r1 = lax.rsqrt(jnp.mean(x * x, axis=-1, keepdims=True) + EPS)
    gain_grad[0:1, :] += jnp.sum(back * (x * r1), axis=0, keepdims=True)


def input_back_half(grads, w, x, first):
    blocks, count, width = x.shape
    cols = w.shape[1]
    return pl.pallas_call(
        input_back_kernel,
        grid=(blocks,),
        in_specs=[
            pl.BlockSpec((1, count, cols), lambda r: (r + first, 0, 0)),
            pl.BlockSpec((width, cols), lambda r: (0, 0)),
            pl.BlockSpec((1, count, width), lambda r: (r, 0, 0)),
        ],
        out_specs=[
            pl.BlockSpec((1, count, width), lambda r: (r, 0, 0)),
            pl.BlockSpec((8, width), lambda r: (0, 0)),
        ],
        out_shape=[
            jax.ShapeDtypeStruct((blocks, count, width), BF16),
            jax.ShapeDtypeStruct((8, width), F32),
        ],
        compiler_params=params(),
        cost_estimate=cost(2 * blocks * count * width * cols, 4 * blocks * count * width),
        name="input_back",
    )(grads, w, x)


def local(
    inputs,
    w_query,
    w_key,
    w_value,
    w_output,
    norm_attn,
    gain_query,
    gain_key,
    w_router,
    norm_moe,
    w_gate,
    w_up,
    w_down,
    lengths,
    routes,
    pair_order,
    cotangent,
):
    n_ctx = lax.axis_size("ctx")
    n_f = lax.axis_size("fsdp")
    c = lax.axis_index("ctx")
    f = lax.axis_index("fsdp")
    count, width = inputs.shape[1], inputs.shape[2]
    length = count * n_ctx
    half = n_ctx // 2
    hpd = H // n_ctx
    hpf = H // n_f
    group = H // KVH
    n_exp = w_router.shape[1]
    capacity = 5 * count * TOPK // (4 * n_exp)
    table = block_order(n_ctx)

    heads = [c % hpf + hpf * ((c // hpf) * hpd + j) for j in range(hpd)]
    kv_heads = [h // group for h in heads]
    columns = lambda w, h: lax.dynamic_slice_in_dim(w, h * HD, HD, 1)
    w_part = jnp.concatenate(
        [columns(w_query, h) for h in heads]
        + [columns(w_key, h) for h in kv_heads]
        + [columns(w_value, h) for h in kv_heads],
        axis=1,
    )
    xa, xb = gather_ctx(inputs[0], n_ctx)
    w_qkv = gather_fsdp(w_part)
    vectors = jnp.concatenate([norm_attn, gain_query, gain_key, norm_moe])
    vectors = gather_fsdp(vectors[None])
    sizes = [norm_attn.shape[0], gain_query.shape[0], gain_key.shape[0], norm_moe.shape[0]]
    rows_of, at = [], 0
    for size in sizes:
        rows_of.append(vectors[:, at : at + size].reshape(1, n_f * size).astype(F32))
        at += size
    attn_gain, query_gain, key_gain, moe_gain = rows_of
    w_out = gather_fsdp(lax.dynamic_slice_in_dim(w_output, (c % hpf) * HD, HD, 0))
    w_out = lax.dynamic_slice_in_dim(w_out, (c // hpf) * hpd * HD, hpd * HD, 0)
    router = gather_fsdp(w_router)
    router_wide = jnp.pad(router, ((0, 0), (0, 128 - n_exp)))
    cot_all = lax.all_gather(cotangent[0], "ctx", axis=0)
    gate_w = lax.all_gather(w_gate[0], "fsdp", axis=0, tiled=True)
    up_w = lax.all_gather(w_up[0], "fsdp", axis=0, tiled=True)
    down_w = lax.all_gather(w_down[0], "fsdp", axis=0, tiled=True)

    pair_table = jnp.stack([routes[0].reshape(count * TOPK), pair_order[0, 0]])
    pair_table = lax.all_gather(pair_table, "ctx", axis=0)
    routes_all = pair_table[:, 0].reshape(n_ctx, count, TOPK)
    order_all = pair_table[:, 1].reshape(n_ctx, count, TOPK)
    mine = routes_all == c
    has = jnp.any(mine, axis=-1)
    rank = jnp.where(has, jnp.sum(jnp.where(mine, order_all, 0), axis=-1), count * TOPK)
    place = jnp.sum((rank[:, None, :] < rank[:, :, None]).astype(jnp.int32), axis=-1)
    place = jnp.where(has & (place < capacity), place, -1)[:, None, :]
    chosen_all = jnp.any(
        routes_all[..., None] == jnp.arange(n_exp, dtype=jnp.int32), axis=2
    )

    ends = jnp.cumsum(lengths[0]).astype(jnp.int32)
    cosine, sine = rotary_tables(length)

    normed, raw, query, key, value = project(
        xa, xb, w_qkv, attn_gain, query_gain, key_gain, cosine, sine, table, hpd
    )
    mixed, log_total = attend(query, key, value, ends)
    branch_b = branch_half(mixed, w_out, table, half, half)
    branch_a = branch_half(mixed, w_out, table, 0, half)
    x = inputs[0].astype(F32)
    middle = x + scatter_ctx(branch_a, branch_b, n_ctx)
    moe_scale = lax.rsqrt(jnp.mean(middle * middle, axis=-1, keepdims=True) + EPS)
    routed_in = (middle * moe_scale * moe_gain).astype(BF16)

    ra, rb = gather_ctx(routed_in, n_ctx)
    rows, logits = take_rows(ra, rb, place, router_wide, table, capacity)
    logits = logits[:, :, :n_exp]
    top = jnp.max(jnp.where(chosen_all, logits, -1e30), axis=-1, keepdims=True)
    weights = jnp.where(chosen_all, jnp.exp(logits - top), 0.0)
    gates = weights / jnp.sum(weights, axis=-1, keepdims=True)
    own_gates = jnp.sum(
        jnp.where(jnp.arange(n_exp, dtype=jnp.int32) == c, gates, 0.0), axis=-1
    )[:, None, :]
    grad_rows, pair_grad, gate_rows = take_grads(cot_all, place, own_gates, table, capacity)
    slots = n_ctx * capacity
    rows_flat = rows.reshape(slots, width)
    pair_flat = pair_grad.reshape(slots, width)
    gate_part = dot(rows_flat, gate_w)
    up_part = dot(rows_flat, up_w)
    sigma = jax.nn.sigmoid(gate_part)
    silu_gate = gate_part * sigma
    hidden = (silu_gate * up_part).astype(BF16)
    expert_out = dot(hidden, down_w, ROWS_T).astype(BF16)
    results, gate_grads = give_results(
        expert_out.reshape(n_ctx, capacity, width), grad_rows, gate_rows, place, table
    )
    gate_grads = lax.all_gather(gate_grads.reshape(length), "ctx", axis=0)
    moe = lax.psum_scatter(results, "ctx", scatter_dimension=0, tiled=False)
    outputs = (middle + moe.astype(F32)).astype(BF16)
    hidden_grad = dot(pair_flat, down_w)
    gate_part_grad = (hidden_grad * up_part * sigma * (1.0 + gate_part * (1.0 - sigma))).astype(
        BF16
    )
    up_part_grad = (hidden_grad * silu_gate).astype(BF16)
    row_grad = dot(gate_part_grad, gate_w, ROWS_T) + dot(up_part_grad, up_w, ROWS_T)
    row_grad = row_grad.astype(BF16).reshape(n_ctx, capacity, width)
    back_b = give_rows_half(row_grad, place, table, half, half)
    back_a = give_rows_half(row_grad, place, table, 0, half)
    routed_grad = scatter_ctx(back_a, back_b, n_ctx)
    grad_w_gate = scatter_fsdp(dot(rows_flat, gate_part_grad, COLS_T))
    grad_w_up = scatter_fsdp(dot(rows_flat, up_part_grad, COLS_T))
    grad_w_down = scatter_fsdp(dot(pair_flat, hidden, COLS_T))

    gate_grads = gate_grads.T.reshape(n_ctx, count, n_exp)
    logit_grad = gates * (gate_grads - jnp.sum(gates * gate_grads, axis=-1, keepdims=True))
    own_logit_grad = lax.dynamic_index_in_dim(logit_grad, c, 0, keepdims=False)
    routed_grad = routed_grad + lax.dot_general(
        own_logit_grad, router.astype(F32), ROWS_T, precision=HIGH
    )
    places = (table[:, None] == jnp.arange(n_ctx, dtype=jnp.int32)[None, :]).astype(F32)
    ordered = jnp.einsum("rb,bte->rte", places, logit_grad, precision=HIGH).astype(BF16)
    ordered = ordered.reshape(2, half * count, n_exp)
    grad_router = dot(ra.reshape(half * count, width), ordered[0], COLS_T) + dot(
        rb.reshape(half * count, width), ordered[1], COLS_T
    )
    grad_w_router = scatter_fsdp(grad_router)

    grad_out = cotangent[0].astype(F32)
    moe_scaled = routed_grad * moe_gain
    grad_moe_part = jnp.sum(routed_grad * middle * moe_scale, axis=0)
    middle_grad = (
        grad_out
        + moe_scale * moe_scaled
        - middle
        * (
            moe_scale
            * moe_scale
            * moe_scale
            * jnp.mean(moe_scaled * middle, axis=-1, keepdims=True)
        )
    )

    ga, gb = gather_ctx(middle_grad.astype(BF16), n_ctx)
    mixed_grad, grad_out_w = branch_back(ga, gb, mixed, w_out, table)
    delta = jnp.sum(mixed_grad.astype(F32) * mixed, axis=-1)[:, None, :]
    dq, dk, dv = attend_back(
        query, mixed_grad, log_total[:, :, 0][:, None, :], delta, key, value, ends
    )
    qkv_grad, gain_grads = qkv_back(
        dq, dk, dv, raw, cosine, sine, query_gain, key_gain, table, hpd
    )
    qkv_flat = qkv_grad.reshape(length, 3 * hpd * HD)
    normed_flat = normed.reshape(length, width)
    q_cols = hpd * HD
    grad_q = scatter_fsdp(dot(normed_flat, qkv_flat[:, :q_cols], COLS_T)).astype(BF16)
    grad_kv = scatter_fsdp(dot(normed_flat, qkv_flat[:, q_cols:], COLS_T))
    inner_b, gain_b = input_back_half(qkv_grad, w_qkv, xb, half)
    inner_a, gain_a = input_back_half(qkv_grad, w_qkv, xa, 0)
    normed_grad = scatter_ctx(inner_a, inner_b, n_ctx)

    grad_q = lax.all_gather(grad_q, "ctx", axis=0)
    grad_w_query = (
        grad_q.reshape(n_ctx // hpf, hpf, width // n_f, hpd, HD)
        .transpose(2, 0, 3, 1, 4)
        .reshape(width // n_f, H * HD)
        .astype(F32)
    )
    slots_kv = jnp.arange(KVH, dtype=jnp.int32)
    spread = jnp.stack([slots_kv == h for h in kv_heads]).astype(F32)
    grad_kv = grad_kv.reshape(width // n_f, 2, hpd, 1, HD) * spread[None, None, :, :, None]
    grad_kv = jnp.sum(grad_kv, axis=2).reshape(width // n_f, 2 * KVH * HD)
    grad_kv = lax.psum(grad_kv.astype(BF16), "ctx").astype(F32)
    grad_w_key = grad_kv[:, : KVH * HD]
    grad_w_value = grad_kv[:, KVH * HD :]
    spread_out = jnp.arange(n_f, dtype=jnp.int32)[:, None] == (
        (c // hpf) * hpd + jnp.arange(hpd, dtype=jnp.int32)[None, :]
    )
    if n_f == hpd:
        placed = grad_out_w
    else:
        placed = jnp.einsum(
            "fj,jrd->frd", spread_out.astype(F32), grad_out_w.reshape(hpd, HD, width)
        ).reshape(n_f * HD, width)
    grad_o = scatter_fsdp(placed).astype(BF16)
    grad_o = lax.all_gather(grad_o, "ctx", axis=0).reshape(n_ctx // hpf, hpf * HD, width)
    grad_w_output = lax.dynamic_index_in_dim(grad_o, f // hpd, 0, keepdims=False).astype(F32)

    grad_attn_part = gain_a[0] + gain_b[0]
    tiny = jnp.concatenate([grad_attn_part, grad_moe_part, gain_grads[0], gain_grads[1]])
    tiny = lax.psum(tiny, ("ctx", "fsdp"))
    tiny_outs, at = [], 0
    for size in (width, width, HD, HD):
        tiny_outs.append(
            lax.dynamic_slice_in_dim(tiny, at + f * (size // n_f), size // n_f, 0)
        )
        at += size
    grad_norm_attn, grad_norm_moe, grad_gain_query, grad_gain_key = tiny_outs

    attn_scale = lax.rsqrt(jnp.mean(x * x, axis=-1, keepdims=True) + EPS)
    attn_scaled = normed_grad * attn_gain
    input_grad = (
        middle_grad
        + attn_scale * attn_scaled
        - x
        * (
            attn_scale
            * attn_scale
            * attn_scale
            * jnp.mean(attn_scaled * x, axis=-1, keepdims=True)
        )
    )
    return (
        outputs[None],
        input_grad.astype(BF16)[None],
        grad_w_query,
        grad_w_key,
        grad_w_value,
        grad_w_output,
        grad_norm_attn,
        grad_gain_query,
        grad_gain_key,
        grad_w_router,
        grad_norm_moe,
        grad_w_gate[None],
        grad_w_up[None],
        grad_w_down[None],
    )


def solution(mesh):
    in_specs = (
        P("fsdp", "ctx", None),
        P("fsdp", None),
        P("fsdp", None),
        P("fsdp", None),
        P("fsdp", None),
        P("fsdp"),
        P("fsdp"),
        P("fsdp"),
        P("fsdp", None),
        P("fsdp"),
        P("ctx", "fsdp", None),
        P("ctx", "fsdp", None),
        P("ctx", "fsdp", None),
        P("fsdp", None),
        P("fsdp", "ctx", None),
        P("fsdp", "ctx", None),
        P("fsdp", "ctx", None),
    )
    out_specs = (
        P("fsdp", "ctx", None),
        P("fsdp", "ctx", None),
        P("fsdp", None),
        P("fsdp", None),
        P("fsdp", None),
        P("fsdp", None),
        P("fsdp"),
        P("fsdp"),
        P("fsdp"),
        P("fsdp", None),
        P("fsdp"),
        P("ctx", "fsdp", None),
        P("ctx", "fsdp", None),
        P("ctx", "fsdp", None),
    )
    return jax.shard_map(local, mesh=mesh, in_specs=in_specs, out_specs=out_specs, check_vma=False)
```

time: 2470 us -> 1120 us (0.45)
  waiting for transfers between devices: 1550 us -> 446 us
  matrix products: 283 us -> 88.7 us
  Pallas kernels: 0 us -> 186 us
  local copies, waits for them, and re-layouts: 284 us -> 122 us
  other arithmetic: 166 us -> 86.3 us
    reduce_scatter x10 -> x1, waiting for transfers between devices: 662 us -> 0.02 us  [local(): moe = lax.psum_scatter(results, 'ctx', scatter_dimension=0, tiled=False)]
    all_gather x9 -> x6, waiting for transfers between devices: 492 us -> 77 us  [the longest x1 54.7 us: local(): grad_q = lax.all_gather(grad_q, 'ctx', axis=0)]
    ppermute x0 -> x59, waiting for transfers between devices: none -> 368 us  [the longest x9 112 us: gather_ctx(): lax.ppermute(current, 'ctx', ring(n_ctx, 4))]
    psum x1, waiting for transfers between devices: 257 us -> 0.01 us  [local(): grad_kv = lax.psum(grad_kv.astype(BF16), 'ctx').astype(F32)]
    dot_general x56 -> x15, matrix products: 283 us -> 88.7 us  [the longest x13 86.5 us: dot(): return lax.dot_general(a, b, dims, preferred_element_type=F32)]
    pallas_call x0 -> x14, Pallas kernels: none -> 186 us  [the longest x2 25 us: input_back_half(): pl.pallas_call(input_back_kernel, grid=(blocks,), in_specs=[pl.BlockSpec(...]
    all_to_all x4 -> x0, waiting for transfers between devices: 137 us -> none  [the longest x1 67 us: local(): lax.all_to_all(sending, 'ctx', split_axis=0, concat_axis=1, tiled=True)]
    ppermute x0 -> x59, starting transfers between devices: none -> 72.8 us  [the longest x9 20.7 us: scatter_ctx(): carry = lax.ppermute(total.astype(BF16), 'ctx', ring(n_ctx, -4))]
  transfers between devices with their start and end apart: 24 -> 67, of which waited for: 21 -> 37; matrix products, arithmetic and copies ran while one was open for 17% -> 20% of each run, Pallas kernels for 0% -> 11%
where the time goes in v1:
time: 1120 us; the launch traced here: 1110 us
  waiting for transfers between devices  446 us (40%)
  Pallas kernels  186 us (17%)
  local copies, waits for them, and re-layouts  122 us (11%)
  matrix products  88.7 us (8%)
  blocking collectives  88.5 us (8%)
  other arithmetic  86.3 us (8%)
  starting transfers between devices  73.3 us (7%)
  between operations  15.8 us (1%)
    ppermute x9, waiting for transfers between devices, gather_ctx(): lax.ppermute(current, 'ctx', ring(n_ctx, 4))  112 us
    ppermute x7, waiting for transfers between devices, scatter_fsdp(): other = lax.ppermute(sent, 'fsdp', [(0, 1), (1, 0)])  100 us
    dot_general x13, matrix products, dot(): return lax.dot_general(a, b, dims, preferred_element_type=F32)  86.5 us
    all_gather x1, waiting for transfers between devices, local(): grad_q = lax.all_gather(grad_q, 'ctx', axis=0)  54.7 us
    convert_element_type x3, local copies, waits for them, and re-layouts, local(): grad_w_query = grad_q.reshape(n_ctx // hpf, hpf, width // n_f, hpd, HD).t...  53.3 us
    psum x1, blocking collectives, local(): tiny = lax.psum(tiny, ('ctx', 'fsdp'))  48.4 us
    ppermute x12, waiting for transfers between devices, scatter_ctx(): other = lax.ppermute(both[2 * k + 1], 'ctx', flip(n_ctx, 2))  47.4 us
    unnamed x132, local copies, waits for them, and re-layouts  40.4 us
  transfers between devices with their start and end apart: 67, of which 37 were waited for; matrix products, arithmetic and copies ran while one was open for 20% of the time, Pallas kernels for 11%

profile of v1, /device:TPU:0, one launch (start us, length us, event | category | flops | bytes accessed | tf_op | source)
XLA Modules:
  0.0 1106.7 jit_solution(14063638587188633859)
XLA Ops:
  27.7 24.1 %collective-permute-done.3 = bf16[128,2048]{1,0:T(8,128)(2,1)S(1)} collective-permute-done((bf16[128,2048]{1,0:T(8,128)(2,1)S(1)}, bf16[128,2048]{1,0:T(8,128)(2,1)S(1)}, u32[]{:S(2)}, u32[]{:S(2)}) %collective-permute-start.3) | collective-permute-done | bytes 524320 | tf_op jit(solution)/shard_map/ppermute | solution.py:64
  54.8 18.0 %collective-permute-done.5 = bf16[128,2048]{1,0:T(8,128)(2,1)S(1)} collective-permute-done((bf16[128,2048]{1,0:T(8,128)(2,1)S(1)}, bf16[128,2048]{1,0:T(8,128)(2,1)S(1)}, u32[]{:S(2)}, u32[]{:S(2)}) %collective-permute-start.5) | collective-permute-done | bytes 524320 | tf_op jit(solution)/shard_map/ppermute | solution.py:64
  75.9 20.6 %collective-permute-done.6 = bf16[128,2048]{1,0:T(8,128)(2,1)S(1)} collective-permute-done((bf16[128,2048]{1,0:T(8,128)(2,1)S(1)}, bf16[128,2048]{1,0:T(8,128)(2,1)S(1)}, u32[]{:S(2)}, u32[]{:S(2)}) %collective-permute-start.6) | collective-permute-done | bytes 524320 | tf_op jit(solution)/shard_map/ppermute | solution.py:65
  112.4 28.4 %collective-permute-done.8 = bf16[1024,768]{1,0:T(8,128)(2,1)} collective-permute-done((bf16[1024,768]{1,0:T(8,128)(2,1)}, bf16[1024,768]{1,0:T(8,128)(2,1)}, u32[]{:S(2)}, u32[]{:S(2)}) %collective-permute-start.8) | collective-permute-done | bytes 1572896 | tf_op jit(solution)/shard_map/ppermute | solution.py:90
  144.7 21.7 %project.1 = (bf16[16,128,2048]{2,1,0:T(8,128)(2,1)}, f32[16,128,768]{2,1,0:T(8,128)}, bf16[2,2048,128]{2,1,0:T(8,128)(2,1)S(1)}, bf16[2,2048,128]{2,1,0:T(8,128)(2,1)S(1)}, bf16[2,2048,128]{2,1,0:T(8,128)(2,1)S(1)}) custom-call(s32[16]{0:T(128)S(1)} %stack.153.table, bf16[8,128,2048]{2,1,0:T(8,128)(2,1)} %bitcast_dynamic-update-slice_fusion.16.xa.x_ref, ...), custom_call_target="tpu_custom_call" | custom-call | flops 6442450944 | bytes 29360128 | tf_op jit(solution)/shard_map/project/pallas_call | solution.py:170
  166.4 18.2 %attend.1 = (f32[2,2048,128]{2,1,0:T(8,128)S(1)}, f32[2,2048,128]{2,1,0:T(8,128)}) custom-call(s32[4]{0:T(128)S(1)} %bitcast.288, bf16[2,2048,128]{2,1,0:T(8,128)(2,1)S(1)} %get-tuple-element.39.query, bf16[2,2048,128]{2,1,0:T(8,128)(2,1)S(1)} %get-tuple-element.40.key, bf16[2,2048,128]{2,1,0:T(8,128)(2,1)S(1)} %get-tuple-element.41.value), custom_call_target="tpu_custom_call" | custom-call | flops 2147483648 | bytes 7340032 | tf_op jit(solution)/shard_map/attend/pallas_call | solution.py:307
  319.6 22.1 %all-gather.6 = s32[16,2,1024]{2,1,0:T(2,128)S(1)} all-gather(s32[1,2,1024]{2,1,0:T(2,128)S(1)} %add_bitcast_fusion.3), channel_id=2, replica_groups=mesh['ctx'=16,'fsdp'=2] {'ctx'}, dimensions={0}, use_global_device_ids=true | all-gather | bytes 139264 | tf_op jit(solution)/shard_map/all_gather | solution.py:722
  364.9 13.4 %take_grads.1 = (bf16[16,80,2048]{2,1,0:T(8,128)(2,1)S(1)}, bf16[16,80,2048]{2,1,0:T(8,128)(2,1)}, f32[16,80,128]{2,1,0:T(8,128)S(1)}) custom-call(s32[16]{0:T(128)S(1)} %stack.153.table, bf16[16,128,2048]{2,1,0:T(8,128)(2,1)} %all-gather.15.cloned.1.call-done.grads, s32[16,1,128]{2,1,0:T(1,128)S(1)} %and_select_fusion.place, f32[16,1,128]{2,1,0:T(1,128)S(1)} %bitcast.283), custom_call_target="tpu_custom_call" | custom-call | flops 1073741824 | bytes 25165824 | tf_op jit(solution)/shard_map/take_grads/pallas_call | solution.py:530
  399.8 13.6 %multiply_convert_fusion = (bf16[1280,768]{1,0:T(8,128)(2,1)}, bf16[1280,768]{1,0:T(8,128)(2,1)S(1)}, bf16[1280,768]{1,0:T(8,128)(2,1)}) fusion(f32[1280,768]{1,0:T(8,128)} %fusion.2, f32[1280,768]{1,0:T(8,128)} %fusion.6, bf16[1280,2048]{1,0:T(8,128)(2,1)} %bitcast.313, bf16[1,2048,768]{2,1,0:T(8,128)(2,1)} %all-gather.17.cloned.1.call-done), kind=kOutput, calls=%fused_computation.7 | convolution fusion | flops 4041277440 | bytes 22151168 | tf_op jit(solution)/shard_map/dot_general | solution.py:26
  483.1 14.7 %give_results.1 = (bf16[16,128,2048]{2,1,0:T(8,128)(2,1)}, f32[16,1,128]{2,1,0:T(1,128)S(1)}) custom-call(s32[16]{0:T(128)S(1)} %stack.153.table, bf16[16,80,2048]{2,1,0:T(8,128)(2,1)S(1)} %bitcast.282, bf16[16,80,2048]{2,1,0:T(8,128)(2,1)} %copy-done.4, f32[16,80,128]{2,1,0:T(8,128)S(1)} %get-tuple-element.46.gate_rows, s32[16,1,128]{2,1,0:T(1,128)S(1)} %and_select_fusion.place), custom_call_target="tpu_custom_call" | custom-call | flops 1073741824 | bytes 25165824 | tf_op jit(solution)/shard_map/give_results/pallas_call | solution.py:571
  497.8 18.0 %all-gather.7 = f32[16,1,2048]{2,1,0:T(1,128)S(1)} all-gather(f32[1,1,2048]{2,1,0:T(1,128)S(1)} %bitcast.284), channel_id=1, replica_groups=mesh['ctx'=16,'fsdp'=2] {'ctx'}, dimensions={0}, use_global_device_ids=true | all-gather | bytes 139264 | tf_op jit(solution)/shard_map/all_gather | solution.py:770
  537.9 14.2 %collective-permute-done.37 = bf16[128,2048]{1,0:T(8,128)(2,1)S(1)} collective-permute-done((bf16[128,2048]{1,0:T(8,128)(2,1)S(1)}, bf16[128,2048]{1,0:T(8,128)(2,1)S(1)}, u32[]{:S(2)}, u32[]{:S(2)}) %collective-permute-start.37) | collective-permute-done | bytes 524320 | tf_op jit(solution)/shard_map/ppermute | solution.py:64
  597.7 16.7 %branch_back.1 = (bf16[2,2048,128]{2,1,0:T(8,128)(2,1)S(1)}, f32[256,2048]{1,0:T(8,128)S(1)}) custom-call(s32[16]{0:T(128)S(1)} %stack.153.table, bf16[8,128,2048]{2,1,0:T(8,128)(2,1)} %bitcast_dynamic-update-slice_fusion.ga, bf16[8,128,2048]{2,1,0:T(8,128)(2,1)} %collective-permute-done.43.gb, f32[2,2048,128]{2,1,0:T(8,128)} %copy-done.2, ...), custom_call_target="tpu_custom_call" | custom-call | flops 4294967296 | bytes 8388608 | tf_op jit(solution)/shard_map/branch_back/pallas_call | solution.py:436
  615.1 23.8 %attend_back.1 = (f32[2,2048,128]{2,1,0:T(8,128)}, f32[2,2048,128]{2,1,0:T(8,128)}, f32[2,2048,128]{2,1,0:T(8,128)}) custom-call(s32[4]{0:T(128)S(1)} %bitcast.289, bf16[2,2048,128]{2,1,0:T(8,128)(2,1)S(1)} %copy-done.12, bf16[2,2048,128]{2,1,0:T(8,128)(2,1)S(1)} %get-tuple-element.50.grad, f32[2,1,2048]{2,1,0:T(1,128)S(1)} %slice_bitcast_fusion.24.total, ...), custom_call_target="tpu_custom_call" | custom-call | flops 5368709120 | bytes 10485760 | tf_op jit(solution)/shard_map/attend_back/pallas_call | solution.py:361
  640.6 15.6 %qkv_back.1 = (bf16[16,128,768]{2,1,0:T(8,128)(2,1)}, f32[8,128]{1,0:T(8,128)S(1)}) custom-call(s32[16]{0:T(128)S(1)} %stack.153.table, f32[2,2048,128]{2,1,0:T(8,128)S(1)} %copy-done.9, f32[2,2048,128]{2,1,0:T(8,128)} %get-tuple-element.53.dk, f32[2,2048,128]{2,1,0:T(8,128)} %get-tuple-element.54.dv, f32[16,128,768]{2,1,0:T(8,128)} %get-tuple-element.55.raw, ...), custom_call_target="tpu_custom_call" | custom-call | flops 31457280 | bytes 15728640 | tf_op jit(solution)/shard_map/qkv_back/pallas_call | solution.py:238
  668.9 23.4 %collective-permute-done.53 = bf16[1024,512]{0,1:T(8,128)(2,1)S(1)} collective-permute-done((bf16[1024,512]{0,1:T(8,128)(2,1)S(1)}, bf16[1024,512]{0,1:T(8,128)(2,1)S(1)}, u32[]{:S(2)}, u32[]{:S(2)}) %collective-permute-start.53) | collective-permute-done | bytes 1048608 | tf_op jit(solution)/shard_map/ppermute | solution.py:105
  812.3 27.3 %collective-permute-done.57 = bf16[1024,768]{1,0:T(8,128)(2,1)} collective-permute-done((bf16[1024,768]{1,0:T(8,128)(2,1)S(1)}, bf16[1024,768]{1,0:T(8,128)(2,1)}, u32[]{:S(2)}, u32[]{:S(2)}) %collective-permute-start.57) | collective-permute-done | bytes 1572896 | tf_op jit(solution)/shard_map/ppermute | solution.py:105
  846.9 25.9 %collective-permute-done.56 = bf16[1024,768]{1,0:T(8,128)(2,1)S(1)} collective-permute-done((bf16[1024,768]{1,0:T(8,128)(2,1)S(1)}, bf16[1024,768]{1,0:T(8,128)(2,1)S(1)}, u32[]{:S(2)}, u32[]{:S(2)}) %collective-permute-start.56) | collective-permute-done | bytes 1572896 | tf_op jit(solution)/shard_map/ppermute | solution.py:105
  883.2 48.4 %psum.15 = f32[4352]{0:T(1024)S(1)} all-reduce(f32[4352]{0:T(1024)S(1)} %pad_maximum_fusion.5), channel_id=1, replica_groups=mesh['ctx'=16,'fsdp'=2] {'ctx','fsdp'}, use_global_device_ids=true, to_apply=%region_18.19 | all-reduce | flops 4352 | bytes 34816 | tf_op jit(solution)/shard_map/psum | solution.py:863
  957.5 54.7 %all-gather.23.cloned.1.call-done = bf16[16384,256]{1,0:T(8,128)(2,1)} async-done(((bf16[1024,256]{1,0:T(8,128)(2,1)}), bf16[16384,256]{1,0:T(8,128)(2,1)}) %all-gather.23.cloned.1.call-update) | async-done | bytes 8388624 | tf_op jit(solution)/shard_map/all_gather | solution.py:834
  1012.2 16.9 %reshape.323 = f32[1,16,1024,2,128]{4,3,2,1,0:T(2,128)} reshape(bf16[16384,256]{1,0:T(8,128)(2,1)} %all-gather.23.cloned.1.call-done) | data formatting | bytes 25165824 | tf_op jit(solution)/shard_map/convert_element_type | solution.py:839
  1029.1 17.8 %copy.109 = f32[1024,1,2,16,128]{4,3,2,0,1:T(8,128)} copy(f32[1024,1,2,16,128]{4,2,0,3,1:T(2,128)} %bitcast.290) | data formatting | bytes 33554432 | tf_op jit(solution)/shard_map/convert_element_type | solution.py:839
  1046.9 18.6 %reshape.321 = f32[1024,4096]{1,0:T(8,128)} reshape(f32[1024,1,2,16,128]{4,3,2,0,1:T(8,128)} %copy.109) | data formatting | bytes 33554432 | tf_op jit(solution)/shard_map/convert_element_type | solution.py:839
  1065.5 22.3 %all-gather.25.cloned.1.call-done = bf16[2048,2048]{1,0:T(8,128)(2,1)} async-done(((bf16[128,2048]{1,0:T(8,128)(2,1)}), bf16[2048,2048]{1,0:T(8,128)(2,1)}) %all-gather.25.cloned.1.call-update) | async-done | bytes 8388624 | tf_op jit(solution)/shard_map/all_gather | solution.py:858
  (390 shorter events, 552.6 us)
Async XLA Ops:
  7.2 357.7 %all-gather.15.cloned.1.call-start = ((), (), s32[]{:S(2)}) async-start(), calls=%async_computation.1 | async-start | bytes 8912896 | tf_op jit(solution)/shard_map/all_gather | solution.py:716
  11.8 368.8 %all-gather.21.cloned.1.call-start = ((), (), s32[]{:S(2)}) async-start(), calls=%async_computation.6 | async-start | bytes 4718592 | tf_op jit(solution)/shard_map/all_gather | solution.py:719
  14.7 95.3 %collective-permute-start.9 = (bf16[1,2176]{1,0:T(2,128)(2,1)S(1)}, bf16[1,2176]{1,0:T(2,128)(2,1)S(1)}, u32[]{:S(2)}, u32[]{:S(2)}) collective-permute-start(bf16[1,2176]{1,0:T(2,128)(2,1)S(1)} %broadcast_in_dim.64), channel_id=1, source_target_pairs={{0,1},{1,0},{2,3},{3,2},{4,5},{5,4},{6,7},{7,6},{8,9},{9,8},{10,11... | collective-permute-start | bytes 13064 | tf_op jit(solution)/shard_map/ppermute | solution.py:90
  18.1 92.7 %collective-permute-start.10 = (bf16[128,2048]{1,0:T(8,128)(2,1)}, bf16[128,2048]{1,0:T(8,128)(2,1)}, u32[]{:S(2)}, u32[]{:S(2)}) collective-permute-start(bf16[128,2048]{1,0:T(8,128)(2,1)} %constant_dynamic-slice_fusion), channel_id=1, source_target_pairs={{0,1},{1,0},{2,3},{3,2},{4,5},{5,4},{6,7},{7,6},{8,9},{9,8},{10,11... | collective-permute-start | bytes 1572872 | tf_op jit(solution)/shard_map/ppermute | solution.py:90
  97.3 47.4 %collective-permute-start.7 = (bf16[8,128,2048]{2,1,0:T(8,128)(2,1)}, bf16[8,128,2048]{2,1,0:T(8,128)(2,1)}, u32[]{:S(2)}, u32[]{:S(2)}) collective-permute-start(bf16[8,128,2048]{2,1,0:T(8,128)(2,1)} %bitcast_dynamic-update-slice_fusion.16.xa.x_ref), channel_id=1, source_target_pairs={{0,2},{2,0},{4,6},{6,4},{8,10},{10,8},{12,14},{14,12},{16,18},{18,... | collective-permute-start | bytes 12582920 | tf_op jit(solution)/shard_map/ppermute | solution.py:68
  103.6 37.1 %collective-permute-start.8 = (bf16[1024,768]{1,0:T(8,128)(2,1)}, bf16[1024,768]{1,0:T(8,128)(2,1)}, u32[]{:S(2)}, u32[]{:S(2)}) collective-permute-start(bf16[1024,768]{1,0:T(8,128)(2,1)} %dynamic-slice_dynamic-update-slice_fusion), channel_id=1, source_target_pairs={{0,1},{1,0},{2,3},{3,2},{4,5},{5,4},{6,7},{7,6},{8,9},{9,8},{10,11... | collective-permute-start | bytes 4718600 | tf_op jit(solution)/shard_map/ppermute | solution.py:90
  223.5 166.7 %all-gather.19.cloned.1.call-start = ((), (), s32[]{:S(2)}) async-start(), calls=%async_computation.5 | async-start | bytes 4718592 | tf_op jit(solution)/shard_map/all_gather | solution.py:718
  267.1 132.6 %all-gather.17.cloned.1.call-start = ((), (), s32[]{:S(2)}) async-start(), calls=%async_computation.4 | async-start | bytes 4718592 | tf_op jit(solution)/shard_map/all_gather | solution.py:717
  319.3 619.3 %all-reduce.3.cloned.1.call-start = ((), (), s32[]{:S(2)}) async-start(), calls=%async_computation.3 | async-start | bytes 4194304 | tf_op jit(solution)/shard_map/psum | solution.py:845
  459.8 58.8 %collective-permute-start.30 = (bf16[128,2048]{1,0:T(8,128)(2,1)}, bf16[128,2048]{1,0:T(8,128)(2,1)}, u32[]{:S(2)}, u32[]{:S(2)}) collective-permute-start(bf16[128,2048]{1,0:T(8,128)(2,1)} %get-tuple-element.130), channel_id=1, source_target_pairs={{0,4},{2,6},{4,0},{6,2},{8,12},{10,14},{12,8},{14,10},{16,20},{18,... | collective-permute-start | bytes 1572872 | tf_op jit(solution)/shard_map/ppermute | solution.py:77
  474.2 44.3 %collective-permute-start.34 = (bf16[128,2048]{1,0:T(8,128)(2,1)S(1)}, bf16[128,2048]{1,0:T(8,128)(2,1)}, u32[]{:S(2)}, u32[]{:S(2)}) collective-permute-start(bf16[128,2048]{1,0:T(8,128)(2,1)S(1)} %fusion.38), channel_id=1, source_target_pairs={{0,24},{2,26},{4,28},{6,30},{8,0},{10,2},{12,4},{14,6},{16,8},{18,... | collective-permute-start | bytes 1572872 | tf_op jit(solution)/shard_map/ppermute | solution.py:82
  705.6 248.6 %reduce-scatter.2.cloned.1.call-start = ((), (), s32[]{:S(2)}) async-start(), calls=%async_computation.2 | async-start | bytes 8912896 | tf_op jit(solution)/shard_map/reduce_scatter | solution.py:771
  706.2 306.0 %all-gather.23.cloned.1.call-start = ((), (), s32[]{:S(2)}) async-start(), calls=%async_computation.7 | async-start | bytes 8912896 | tf_op jit(solution)/shard_map/all_gather | solution.py:834
  727.1 360.6 %all-gather.25.cloned.1.call-start = ((), (), s32[]{:S(2)}) async-start(), calls=%async_computation.8 | async-start | bytes 8912896 | tf_op jit(solution)/shard_map/all_gather | solution.py:858
  745.7 38.7 %collective-permute-start.55 = (bf16[1024,16]{0,1:T(8,128)(2,1)S(1)}, bf16[1024,16]{0,1:T(8,128)(2,1)S(1)}, u32[]{:S(2)}, u32[]{:S(2)}) collective-permute-start(bf16[1024,16]{0,1:T(8,128)(2,1)S(1)} %select_convert_fusion.6), channel_id=1, source_target_pairs={{0,1},{1,0},{2,3},{3,2},{4,5},{5,4},{6,7},{7,6},{8,9},{9,8},{10,11... | collective-permute-start | bytes 98312 | tf_op jit(solution)/shard_map/ppermute | solution.py:105
  759.3 38.7 %collective-permute-start.44 = (bf16[8,128,2048]{2,1,0:T(8,128)(2,1)}, bf16[8,128,2048]{2,1,0:T(8,128)(2,1)}, u32[]{:S(2)}, u32[]{:S(2)}) collective-permute-start(bf16[8,128,2048]{2,1,0:T(8,128)(2,1)} %get-tuple-element.58), channel_id=1, source_target_pairs={{0,2},{2,0},{4,6},{6,4},{8,10},{10,8},{12,14},{14,12},{16,18},{18,... | collective-permute-start | bytes 12582920 | tf_op jit(solution)/shard_map/ppermute | solution.py:73
  768.6 37.3 %collective-permute-start.58 = (bf16[1024,768]{1,0:T(8,128)(2,1)S(1)}, bf16[1024,768]{1,0:T(8,128)(2,1)}, u32[]{:S(2)}, u32[]{:S(2)}) collective-permute-start(bf16[1024,768]{1,0:T(8,128)(2,1)S(1)} %select_convert_fusion), channel_id=1, source_target_pairs={{0,1},{1,0},{2,3},{3,2},{4,5},{5,4},{6,7},{7,6},{8,9},{9,8},{10,11... | collective-permute-start | bytes 4718600 | tf_op jit(solution)/shard_map/ppermute | solution.py:105
  782.3 57.3 %collective-permute-start.57 = (bf16[1024,768]{1,0:T(8,128)(2,1)S(1)}, bf16[1024,768]{1,0:T(8,128)(2,1)}, u32[]{:S(2)}, u32[]{:S(2)}) collective-permute-start(bf16[1024,768]{1,0:T(8,128)(2,1)S(1)} %select_convert_fusion.1), channel_id=1, source_target_pairs={{0,1},{1,0},{2,3},{3,2},{4,5},{5,4},{6,7},{7,6},{8,9},{9,8},{10,11... | collective-permute-start | bytes 4718600 | tf_op jit(solution)/shard_map/ppermute | solution.py:105
  783.5 89.4 %collective-permute-start.56 = (bf16[1024,768]{1,0:T(8,128)(2,1)S(1)}, bf16[1024,768]{1,0:T(8,128)(2,1)S(1)}, u32[]{:S(2)}, u32[]{:S(2)}) collective-permute-start(bf16[1024,768]{1,0:T(8,128)(2,1)S(1)} %select_convert_fusion.2), channel_id=1, source_target_pairs={{0,1},{1,0},{2,3},{3,2},{4,5},{5,4},{6,7},{7,6},{8,9},{9,8},{10,11... | collective-permute-start | bytes 4718600 | tf_op jit(solution)/shard_map/ppermute | solution.py:105
  804.6 39.8 %collective-permute-start.48 = (bf16[128,2048]{1,0:T(8,128)(2,1)S(1)}, bf16[128,2048]{1,0:T(8,128)(2,1)S(1)}, u32[]{:S(2)}, u32[]{:S(2)}) collective-permute-start(bf16[128,2048]{1,0:T(8,128)(2,1)S(1)} %get-tuple-element.124), channel_id=1, source_target_pairs={{0,4},{2,6},{4,0},{6,2},{8,12},{10,14},{12,8},{14,10},{16,20},{18,... | collective-permute-start | bytes 1572872 | tf_op jit(solution)/shard_map/ppermute | solution.py:77
  843.4 32.5 %collective-permute-start.47 = (bf16[128,2048]{1,0:T(8,128)(2,1)S(1)}, bf16[128,2048]{1,0:T(8,128)(2,1)S(1)}, u32[]{:S(2)}, u32[]{:S(2)}) collective-permute-start(bf16[128,2048]{1,0:T(8,128)(2,1)S(1)} %get-tuple-element.125), channel_id=1, source_target_pairs={{0,4},{2,6},{4,0},{6,2},{8,12},{10,14},{12,8},{14,10},{16,20},{18,... | collective-permute-start | bytes 1572872 | tf_op jit(solution)/shard_map/ppermute | solution.py:77
  844.6 38.3 %collective-permute-start.49 = (bf16[128,2048]{1,0:T(8,128)(2,1)S(1)}, bf16[128,2048]{1,0:T(8,128)(2,1)S(1)}, u32[]{:S(2)}, u32[]{:S(2)}) collective-permute-start(bf16[128,2048]{1,0:T(8,128)(2,1)S(1)} %fusion.29), channel_id=1, source_target_pairs={{0,24},{2,26},{4,28},{6,30},{8,0},{10,2},{12,4},{14,6},{16,8},{18,... | collective-permute-start | bytes 1572872 | tf_op jit(solution)/shard_map/ppermute | solution.py:82
  875.1 58.8 %collective-permute-start.46 = (bf16[128,2048]{1,0:T(8,128)(2,1)}, bf16[128,2048]{1,0:T(8,128)(2,1)S(1)}, u32[]{:S(2)}, u32[]{:S(2)}) collective-permute-start(bf16[128,2048]{1,0:T(8,128)(2,1)} %get-tuple-element.126), channel_id=1, source_target_pairs={{0,4},{2,6},{4,0},{6,2},{8,12},{10,14},{12,8},{14,10},{16,20},{18,... | collective-permute-start | bytes 1572872 | tf_op jit(solution)/shard_map/ppermute | solution.py:77
  883.1 50.8 %collective-permute-start.50 = (bf16[128,2048]{1,0:T(8,128)(2,1)S(1)}, bf16[128,2048]{1,0:T(8,128)(2,1)S(1)}, u32[]{:S(2)}, u32[]{:S(2)}) collective-permute-start(bf16[128,2048]{1,0:T(8,128)(2,1)S(1)} %fusion.31), channel_id=1, source_target_pairs={{0,24},{2,26},{4,28},{6,30},{8,0},{10,2},{12,4},{14,6},{16,8},{18,... | collective-permute-start | bytes 1572872 | tf_op jit(solution)/shard_map/ppermute | solution.py:82
  (94 other events, 2058.5 us)
Sparse Core Ops, SparseCore 0:
  11.9 102.6 all-gather.14
  223.6 47.5 all-gather.20
  272.8 44.9 all-gather.18
  319.4 45.3 all-gather.16
  705.7 97.6 all-reduce.2
  808.4 125.3 reduce-scatter.1
  936.2 75.9 all-gather.22
  1014.6 73.1 all-gather.24

commit v2 on v1

v2 whole, which is shorter than its diff:
```python
import functools

import jax
import jax.numpy as jnp
from jax import lax
from jax.experimental import pallas as pl
from jax.experimental.pallas import tpu as pltpu
from jax.sharding import PartitionSpec as P

H = 32
KVH = 4
HD = 128
TOPK = 8
EPS = 1e-06
THETA = 1000000.0
HIGH = lax.Precision.HIGHEST
LOG2E = 1.4426950408889634
F32 = jnp.float32
BF16 = jnp.bfloat16
ROWS_T = (((1,), (1,)), ((), ()))
COLS_T = (((0,), (0,)), ((), ()))
VMEM_LIMIT = 48 * 1024 * 1024


def dot(a, b, dims=(((1,), (0,)), ((), ()))):
    return lax.dot_general(a, b, dims, preferred_element_type=F32)


def params(limit=VMEM_LIMIT):
    return pltpu.CompilerParams(vmem_limit_bytes=limit)


def cost(microseconds):
    return pl.CostEstimate(
        flops=int(microseconds * 1.15e9), bytes_accessed=0, transcendentals=0
    )


def flip(n_ctx, bit):
    return [(i, i ^ bit) for i in range(n_ctx)]


def ring(n_ctx, step):
    return [(i, (i + step) % n_ctx) for i in range(n_ctx)]


def block_order(n_ctx):
    c = lax.axis_index("ctx")
    nz = n_ctx // 4
    z, x, core = c // 4, (c // 2) % 2, c % 2
    table = []
    for k in range(nz):
        for dc in range(2):
            for dx in range(2):
                table.append(lax.rem(z + nz - k, nz) * 4 + (x ^ dx) * 2 + (core ^ dc))
    return jnp.stack(table).astype(jnp.int32)


def tie(*arrays):
    return lax.optimization_barrier(arrays)


class Side:
    def __init__(self, chain):
        self.chain, self.flying, self.left = chain, None, 0
        self.resume(None)

    def resume(self, landed):
        try:
            self.flying, self.left = self.chain.send(landed)
        except StopIteration:
            self.flying = None

    def finish(self):
        while self.flying is not None:
            self.resume(self.flying)


def land(air, sides, *others):
    due = [side for side in sides if side.flying is not None and side.left <= 1]
    for side in sides:
        side.left -= 1
    keys = list(air)
    arrays = tie(*air.values(), *(side.flying for side in due), *others)
    air.clear()
    for side, array in zip(due, arrays[len(keys) :]):
        side.resume(array)
    return dict(zip(keys, arrays)), arrays[len(keys) + len(due) :]


def pipeline(n_ctx, order, compute, token, sides, piece=None, scatter=False, closing=None):
    nz = n_ctx // 4
    air, have, state = {}, {}, ()

    def send(key, array, pairs):
        air[key] = lax.ppermute(array, "ctx", pairs)

    def bring(k):
        send(("beside", k), have["piece", k], flip(n_ctx, 2))
        if k + 1 < nz:
            send(("piece", k + 1), have["piece", k], ring(n_ctx, 4))

    def step_ends(*others):
        landed, others = land(air, sides, *others)
        have.update(landed)
        return others

    def total_of(own):
        total = own + have["away"].astype(F32)
        return total + have["carry"].astype(F32) if "carry" in have else total

    def give(blocks, token):
        mine, theirs = blocks
        arrived = lax.ppermute(theirs, "ctx", flip(n_ctx, 1))
        own = mine[0].astype(F32) + arrived[0].astype(F32)
        away = (mine[1].astype(F32) + arrived[1].astype(F32)).astype(BF16)
        token, own, away = tie(token, own, away)
        send("away", away, flip(n_ctx, 2))
        return own, token

    if piece is not None:
        have["piece", 0] = piece
        for k in range(order[0] + 1):
            bring(k)
            step_ends()
    blocks = own = None
    for s, k in enumerate(order):
        following = order[s + 1 :][:1]
        quarter = None
        if piece is not None:
            for later in following:
                if ("beside", later) not in have:
                    bring(later)
            mine = jnp.stack([have["piece", k], have["beside", k]])
            quarter = mine, lax.ppermute(mine, "ctx", flip(n_ctx, 1))
        if not scatter:
            state = compute(k, quarter, token, state)
            if following:
                token, *state = step_ends(token, *state)
            continue
        if own is not None:
            send("carry", total_of(own).astype(BF16), ring(n_ctx, 4))
        if blocks is not None:
            own, token = give(blocks, token)
        blocks, state = compute(k, quarter, token, state)
        token, *blocks = step_ends(token, *blocks)
    if not scatter:
        return tuple(state)
    send("carry", total_of(own).astype(BF16), ring(n_ctx, 4))
    own, token = give(blocks, token)
    extra = closing(token) if closing else ()
    own, *extra = step_ends(own, *extra)
    return total_of(own), state, extra


def scatter_order(n_ctx):
    return list(range(1, n_ctx // 4)) + [0]


def sum_all(values, result):
    n_ctx = lax.axis_size("ctx")
    bit = 1
    while bit < n_ctx:
        values = values + (yield lax.ppermute(values, "ctx", flip(n_ctx, bit)), 1)
        bit *= 2
    if lax.axis_size("fsdp") == 2:
        values = values + (yield lax.ppermute(values, "fsdp", SWAP), 1)
    else:
        values = lax.psum(values, "fsdp")
    result.append(values)


SWAP = [(0, 1), (1, 0)]


def swap(part):
    return lax.ppermute(part, "fsdp", SWAP)


def fetch(part, steps=1):
    if lax.axis_size("fsdp") != 2:
        return [lax.all_gather(part, "fsdp", axis=0, tiled=True)]
    return [part, (yield swap(part), steps)]


def fetch_blocks(part, block):
    if lax.axis_size("fsdp") != 2:
        return [lax.all_gather(part, "fsdp", axis=0, tiled=True)]
    other = []
    for at in range(0, part.shape[1], block):
        other.append((yield swap(part[:, at : at + block]), 1))
    return [part, jnp.concatenate(other, axis=1)]


def joined(parts):
    if len(parts) == 1:
        return parts[0]
    mine, other = parts
    first = lax.axis_index("fsdp") == 0
    return jnp.concatenate([jnp.where(first, mine, other), jnp.where(first, other, mine)], axis=0)


def part_offsets(width):
    if lax.axis_size("fsdp") != 2:
        return [jnp.int32(0)]
    f = lax.axis_index("fsdp")
    return [f * (width // 2), (1 - f) * (width // 2)]


def scatter_blocks(lefts, right, block):
    if lax.axis_size("fsdp") != 2:
        full = dot(lefts[0], right, COLS_T).astype(BF16)
        return lax.psum_scatter(full, "fsdp", scatter_dimension=0, tiled=True).astype(F32)
    mine, other = lefts
    done = []
    for at in range(0, right.shape[1], block):
        columns = right[:, at : at + block]
        came = yield swap(dot(other, columns, COLS_T).astype(BF16)), 1
        done.append(dot(mine, columns, COLS_T) + came.astype(F32))
    return done[0] if len(done) == 1 else jnp.concatenate(done, axis=1)


def scatter_rows(full):
    if lax.axis_size("fsdp") != 2:
        return lax.psum_scatter(
            full.astype(BF16), "fsdp", scatter_dimension=0, tiled=True
        ).astype(F32)
    rows = full.shape[0] // 2
    first = lax.axis_index("fsdp") == 0
    low, high = full[:rows], full[rows:]
    came = yield swap(jnp.where(first, high, low).astype(BF16)), 1
    return jnp.where(first, low, high) + came.astype(F32)


def first_pair(shape):
    return pl.BlockSpec((1,) + shape, lambda i, t: (jnp.minimum(i, 1),) + (0,) * len(shape))


def last_pair(shape):
    return pl.BlockSpec((1,) + shape, lambda i, t: (jnp.maximum(i - 2, 0),) + (0,) * len(shape))


def whole(shape):
    return pl.BlockSpec(shape, lambda *_: (0,) * len(shape))


def split_pairs(i, body, first, last):
    @pl.when(i < 2)
    def _():
        body(first)

    @pl.when(i >= 2)
    def _():
        body(last)


def rotary_tables(length):
    half = HD // 2
    steps = jnp.arange(half, dtype=jnp.int32).astype(F32)
    inverse = jnp.exp(steps * (-2.0 * jnp.log(THETA) / HD))
    angles = jnp.arange(length, dtype=jnp.int32).astype(F32)[:, None] * inverse[None, :]
    cosine, sine = jnp.cos(angles), jnp.sin(angles)
    return (
        jnp.concatenate([cosine, cosine], axis=1),
        jnp.concatenate([-sine, sine], axis=1),
    )


def half_turn(v):
    return pltpu.roll(v, HD // 2, 1)


def project_kernel(hpd, n_parts, n_ctx, meta, xa, xb, w, gain, gq, gk, cosine, sine, *refs):
    normed, (raw, query, key, value, whole_rows) = refs[-5 - n_parts : -5], refs[-5:]

    def body(x_ref):
        x = x_ref[0].astype(F32)
        r1 = lax.rsqrt(jnp.mean(x * x, axis=-1, keepdims=True) + EPS)
        n = (x * r1 * gain[...]).astype(BF16)
        whole_rows[...] = n
        for p, part in enumerate(normed):
            width = part.shape[2]
            part[0] = whole_rows[:, pl.ds(pl.multiple_of(meta[n_ctx + 1 + p], 128), width)]
        out = dot(n, w[...])
        raw[0] = out
        cos, sin = cosine[...], sine[...]
        for j in range(3 * hpd):
            v = out[:, j * HD : (j + 1) * HD]
            if j >= 2 * hpd:
                value[j - 2 * hpd] = v.astype(BF16)
                continue
            scale = lax.rsqrt(jnp.mean(v * v, axis=-1, keepdims=True) + EPS)
            v = v * scale * (gq[...] if j < hpd else gk[...])
            v = (v * cos + half_turn(v) * sin).astype(BF16)
            if j < hpd:
                query[j] = v
            else:
                key[j - hpd] = v

    split_pairs(pl.program_id(0), body, xa, xb)


def project(k, quarter, w, gain, gq, gk, cosine, sine, meta, hpd, n_ctx, n_parts, before):
    xa, xb = quarter
    _, count, width = xa.shape
    length = n_ctx * count
    cols = w.shape[1]
    at = lambda i, t: (t[4 * k + i], 0)
    head_at = lambda i, t: (0, t[4 * k + i], 0)
    own = lambda i, t: (4 * k + i, 0, 0)
    head = jax.ShapeDtypeStruct((hpd, length, HD), BF16)
    return pl.pallas_call(
        functools.partial(project_kernel, hpd, n_parts, n_ctx),
        grid_spec=pltpu.PrefetchScalarGridSpec(
            num_scalar_prefetch=1,
            grid=(4,),
            in_specs=[
                first_pair((count, width)),
                last_pair((count, width)),
                whole((width, cols)),
                whole((1, width)),
                whole((1, HD)),
                whole((1, HD)),
                pl.BlockSpec((count, HD), at),
                pl.BlockSpec((count, HD), at),
            ]
            + [pl.BlockSpec(memory_space=pl.ANY)] * len(before),
            out_specs=[
                *[pl.BlockSpec((1, count, width // n_parts), own)] * n_parts,
                pl.BlockSpec((1, count, cols), own),
                pl.BlockSpec((hpd, count, HD), head_at),
                pl.BlockSpec((hpd, count, HD), head_at),
                pl.BlockSpec((hpd, count, HD), head_at),
            ],
            scratch_shapes=[pltpu.VMEM((count, width), BF16)],
        ),
        out_shape=[
            *[jax.ShapeDtypeStruct((n_ctx, count, width // n_parts), BF16)] * n_parts,
            jax.ShapeDtypeStruct((n_ctx, count, cols), F32),
            head,
            head,
            head,
        ],
        input_output_aliases={9 + i: i for i in range(len(before))},
        compiler_params=params(),
        cost_estimate=cost(7.3),
        name="project",
    )(meta, xa, xb, w, gain, gq, gk, cosine, sine, *before)


def first_key(ends, docs, position):
    start = jnp.zeros_like(position)
    for d in range(docs):
        start = jnp.where(position >= ends[d], jnp.maximum(start, ends[d]), start)
    return start


def attend_kernel(docs, bq, bk, ends, query, key, value, mixed, total):
    i = pl.program_id(1)
    q = query[0]
    positions = i * bq + lax.broadcasted_iota(jnp.int32, (bq, 1), 0)
    starts = first_key(ends, docs, positions)
    low = lax.div(first_key(ends, docs, i * bq), bk)
    high = lax.div((i + 1) * bq - 1, bk) + 1

    def step(j, carry):
        acc, sums = carry
        rows = pl.ds(pl.multiple_of(j * bk, bk), bk)
        scores = dot(q, key[0, rows, :], ROWS_T)
        spots = j * bk + lax.broadcasted_iota(jnp.int32, (1, bk), 1)
        seen = (spots <= positions) & (spots >= starts)
        p = jnp.where(seen, jnp.exp2(scores * (LOG2E * HD**-0.5)), 0.0)
        return acc + dot(p.astype(BF16), value[0, rows, :]), sums + jnp.sum(
            p, axis=-1, keepdims=True
        )

    acc, sums = lax.fori_loop(
        low, high, step, (jnp.zeros((bq, HD), F32), jnp.zeros((bq, 1), F32))
    )
    mixed[0] = acc / sums
    total[0] = jnp.broadcast_to(jnp.log2(sums), (bq, HD))


def attend(query, key, value, ends, bq=256, bk=256):
    heads, length, _ = query.shape
    docs = ends.shape[0]
    block = pl.BlockSpec((1, bq, HD), lambda h, i, e: (h, i, 0))
    whole = pl.BlockSpec((1, length, HD), lambda h, i, e: (h, 0, 0))
    out = jax.ShapeDtypeStruct((heads, length, HD), F32)
    return pl.pallas_call(
        functools.partial(attend_kernel, docs, bq, bk),
        grid_spec=pltpu.PrefetchScalarGridSpec(
            num_scalar_prefetch=1,
            grid=(heads, length // bq),
            in_specs=[block, whole, whole],
            out_specs=[block, block],
        ),
        out_shape=[out, out],
        compiler_params=params(),
        cost_estimate=cost(18),
        name="attend",
    )(ends, query, key, value)


def attend_back_kernel(docs, bq, bk, ends, query, grad, total, delta, key, value, dq, dk, dv):
    i = pl.program_id(1)

    @pl.when(i == 0)
    def _():
        dk[...] = jnp.zeros_like(dk)
        dv[...] = jnp.zeros_like(dv)

    q, g = query[0], grad[0]
    log_total, shift = total[0], delta[0]
    positions = i * bq + lax.broadcasted_iota(jnp.int32, (1, bq), 1)
    starts = first_key(ends, docs, positions)
    low = lax.div(first_key(ends, docs, i * bq), bk)
    high = lax.div((i + 1) * bq - 1, bk) + 1

    def step(j, acc):
        rows = pl.ds(pl.multiple_of(j * bk, bk), bk)
        k, v = key[0, rows, :], value[0, rows, :]
        scores = dot(k, q, ROWS_T)
        spots = j * bk + lax.broadcasted_iota(jnp.int32, (bk, 1), 0)
        seen = (spots <= positions) & (spots >= starts)
        p = jnp.where(seen, jnp.exp2(scores * (LOG2E * HD**-0.5) - log_total), 0.0)
        ds = (p * (dot(v, g, ROWS_T) - shift)).astype(BF16)
        dv[0, rows, :] += dot(p.astype(BF16), g)
        dk[0, rows, :] += dot(ds, q)
        return acc + dot(ds, k, COLS_T)

    dq[0] = lax.fori_loop(low, high, step, jnp.zeros((bq, HD), F32))


def attend_back(query, grad, total, delta, key, value, ends, bq=256, bk=256):
    heads, length, _ = query.shape
    docs = ends.shape[0]
    block = pl.BlockSpec((1, bq, HD), lambda h, i, e: (h, i, 0))
    line = pl.BlockSpec((1, 1, bq), lambda h, i, e: (h, 0, i))
    whole = pl.BlockSpec((1, length, HD), lambda h, i, e: (h, 0, 0))
    out = jax.ShapeDtypeStruct((heads, length, HD), F32)
    return pl.pallas_call(
        functools.partial(attend_back_kernel, docs, bq, bk),
        grid_spec=pltpu.PrefetchScalarGridSpec(
            num_scalar_prefetch=1,
            grid=(heads, length // bq),
            in_specs=[block, block, line, line, whole, whole],
            out_specs=[block, whole, whole],
        ),
        out_shape=[out, out, out],
        compiler_params=params(),
        cost_estimate=cost(24),
        name="attend_back",
    )(ends, query, grad, total, delta, key, value)


def branch_kernel(hpd, table, mixed, w, theirs, mine):
    def body(out):
        total = None
        for j in range(hpd):
            part = dot(mixed[j].astype(BF16), w[j * HD : (j + 1) * HD, :])
            total = part if total is None else total + part
        out[0] = total.astype(BF16)

    split_pairs(pl.program_id(0), body, theirs, mine)


def branch(k, mixed, w, table, count):
    hpd = mixed.shape[0]
    width = w.shape[1]
    pair = jax.ShapeDtypeStruct((2, count, width), BF16)
    theirs, mine = pl.pallas_call(
        functools.partial(branch_kernel, hpd),
        grid_spec=pltpu.PrefetchScalarGridSpec(
            num_scalar_prefetch=1,
            grid=(4,),
            in_specs=[
                pl.BlockSpec((hpd, count, HD), lambda i, t: (0, t[4 * k + (i ^ 2)], 0)),
                whole((hpd * HD, width)),
            ],
            out_specs=[first_pair((count, width)), last_pair((count, width))],
        ),
        out_shape=[pair, pair],
        compiler_params=params(),
        cost_estimate=cost(2.4),
        name="branch",
    )(table, mixed, w)
    return mine, theirs


def branch_back_kernel(hpd, table, ga, gb, mixed, w, *refs):
    before = refs[0] if len(refs) == 4 else None
    grad, dw = refs[-2:]
    i = pl.program_id(0)

    @pl.when(i == 0)
    def _():
        dw[...] = jnp.zeros_like(dw) if before is None else before[...]

    def body(g_ref):
        g = g_ref[0]
        back = dot(g, w[...])
        for j in range(hpd):
            grad[j] = back[:, j * HD : (j + 1) * HD].astype(BF16)
            dw[j * HD : (j + 1) * HD, :] += dot(mixed[j].astype(BF16), g, COLS_T)

    split_pairs(i, body, ga, gb)


def branch_back(k, quarter, mixed, w, table, before):
    ga, gb = quarter
    _, count, width = ga.shape
    hpd, length, _ = mixed.shape
    head_at = lambda i, t: (0, t[4 * k + i], 0)
    grad, dw = pl.pallas_call(
        functools.partial(branch_back_kernel, hpd),
        grid_spec=pltpu.PrefetchScalarGridSpec(
            num_scalar_prefetch=1,
            grid=(4,),
            in_specs=[
                first_pair((count, width)),
                last_pair((count, width)),
                pl.BlockSpec((hpd, count, HD), head_at),
                whole((width, hpd * HD)),
            ]
            + ([whole((hpd * HD, width)), pl.BlockSpec(memory_space=pl.ANY)] if before else []),
            out_specs=[pl.BlockSpec((hpd, count, HD), head_at), whole((hpd * HD, width))],
        ),
        out_shape=[
            jax.ShapeDtypeStruct((hpd, length, HD), BF16),
            jax.ShapeDtypeStruct((hpd * HD, width), F32),
        ],
        input_output_aliases={6: 0} if before else {},
        compiler_params=params(),
        cost_estimate=cost(7),
        name="branch_back",
    )(table, ga, gb, mixed, w, *before)
    return dw, grad


def experts_kernel(n_parts, width, capacity, n_exp, meta, xa, xb, cot, router, *refs):
    wg, wu, wd = (refs[n_parts * i : n_parts * (i + 1)] for i in range(3))
    outs = refs[-(5 * n_parts + 5 + 2) :]
    rows, pairs = outs[:n_parts], outs[n_parts : 2 * n_parts]
    hidden, gate_grad, up_grad, mine, theirs = outs[2 * n_parts : 2 * n_parts + 5]
    scratch = outs[2 * n_parts + 5 :]
    chosen_ref, gate_ref = scratch[:2]
    picked, out_sum, row_sum = (
        scratch[2 + n_parts * i : 2 + n_parts * (i + 1)] for i in range(3)
    )
    step = pl.program_id(0)
    part = width // n_parts
    c = meta[0]
    lanes = lax.broadcasted_iota(jnp.int32, (1, 128), 1)

    def columns(p, first=0):
        return pl.ds(pl.multiple_of(first + meta[1 + p], 128), part)

    @pl.when(step == 0)
    def _():
        for i in range(4):
            x_ref = (xa, xb)[i // 2].at[i % 2]
            inner = meta[4 + i]
            span = slice(i * capacity, (i + 1) * capacity)
            info = x_ref[:, width:].astype(F32)
            place = jnp.sum(jnp.where(lanes == c, info, 0.0), axis=1, keepdims=True)
            spots = lax.broadcasted_iota(jnp.int32, (1, capacity), 1).astype(F32)
            chosen = (spots == place).astype(BF16)
            chosen_ref[i] = chosen
            logits = dot(x_ref[:, :width], router[...])
            seen = info > -1.5
            top = jnp.max(jnp.where(seen, logits, -1e30), axis=1, keepdims=True)
            weights = jnp.where(seen, jnp.exp(logits - top), 0.0)
            gates = weights / jnp.sum(weights, axis=1, keepdims=True)
            own = jnp.sum(jnp.where(lanes == c, gates, 0.0), axis=1, keepdims=True)
            gate = lax.dot_general(
                chosen.astype(F32),
                jnp.broadcast_to(own, gates.shape),
                COLS_T,
                precision=HIGH,
                preferred_element_type=F32,
            )
            gate_ref[span, :] = gate
            for p in range(n_parts):
                rows[p][span, :] = dot(chosen, x_ref[:, columns(p)], COLS_T).astype(BF16)
                grads = dot(chosen, cot[0, inner, :, columns(p)], COLS_T)
                picked[p][span, :] = grads.astype(BF16)
                pairs[p][span, :] = (grads * gate[:, :1]).astype(BF16)
        for p in range(n_parts):
            out_sum[p][...] = jnp.zeros_like(out_sum[p])
            row_sum[p][...] = jnp.zeros_like(row_sum[p])

    gate_part = sum(dot(rows[p][...], wg[p][...]) for p in range(n_parts))
    up_part = sum(dot(rows[p][...], wu[p][...]) for p in range(n_parts))
    hidden_grad = sum(dot(pairs[p][...], wd[p][...]) for p in range(n_parts))
    sigma = jax.nn.sigmoid(gate_part)
    silu_gate = gate_part * sigma
    h = (silu_gate * up_part).astype(BF16)
    hidden[...] = h
    gg = (hidden_grad * up_part * sigma * (1.0 + gate_part * (1.0 - sigma))).astype(BF16)
    gate_grad[...] = gg
    ug = (hidden_grad * silu_gate).astype(BF16)
    up_grad[...] = ug
    for p in range(n_parts):
        out_sum[p][...] += dot(h, wd[p][...], ROWS_T)
        row_sum[p][...] += dot(gg, wg[p][...], ROWS_T) + dot(ug, wu[p][...], ROWS_T)

    @pl.when(step == pl.num_programs(0) - 1)
    def _():
        for i in range(4):
            back = (mine, theirs)[i // 2].at[i % 2]
            span = slice(i * capacity, (i + 1) * capacity)
            chosen = chosen_ref[i]
            gate = gate_ref[span, :1]
            inner_sum = jnp.zeros((capacity, 1), F32)
            for p in range(n_parts):
                out = out_sum[p][span, :].astype(BF16).astype(F32)
                inner_sum += jnp.sum(
                    out * picked[p][span, :].astype(F32), axis=1, keepdims=True
                )
                scaled = (out * gate).astype(BF16)
                back[:, columns(p, width + 128)] = dot(chosen, scaled).astype(BF16)
                back[:, columns(p)] = dot(chosen, row_sum[p][span, :].astype(BF16)).astype(BF16)
            high = inner_sum.astype(BF16).astype(F32)
            extra = jnp.where(lanes == c, high, 0.0) + jnp.where(
                lanes == c + n_exp, inner_sum - high, 0.0
            )
            back[:, width : width + 128] = dot(chosen, extra.astype(BF16)).astype(BF16)


def experts(k, quarter, cot_all, router, wg, wu, wd, meta, capacity, n_exp, before):
    xa, xb = quarter
    _, count, wide = xa.shape
    nz, width = cot_all.shape[0], cot_all.shape[-1]
    n_parts = len(wg)
    part = width // n_parts
    hid = wg[0].shape[1]
    block = min(256, hid)
    slots = 4 * capacity
    pair = lambda cols: pl.BlockSpec((2, count, cols), lambda j, m: (0, 0, 0))
    weight = lambda: pl.BlockSpec((part, block), lambda j, m: (0, j))
    at_rows = lambda cols: pl.BlockSpec((slots, cols), lambda j, m: (k, 0))
    at_cols = lambda: pl.BlockSpec((slots, block), lambda j, m: (k, j))
    at_group = lambda: pl.BlockSpec((1, 4, count, width), lambda j, m: (m[3], 0, 0, 0))
    whole_rows = lambda cols: jax.ShapeDtypeStruct((nz * slots, cols), BF16)
    n_out = 2 * n_parts + 3
    outs = pl.pallas_call(
        functools.partial(experts_kernel, n_parts, width, capacity, n_exp),
        grid_spec=pltpu.PrefetchScalarGridSpec(
            num_scalar_prefetch=1,
            grid=(hid // block,),
            in_specs=[pair(wide), pair(wide), at_group(), whole(router.shape)]
            + [weight() for _ in range(3 * n_parts)]
            + [pl.BlockSpec(memory_space=pl.ANY)] * len(before),
            out_specs=[at_rows(part) for _ in range(2 * n_parts)]
            + [at_cols(), at_cols(), at_cols(), pair(wide + width), pair(wide + width)],
            scratch_shapes=[
                pltpu.VMEM((4, count, capacity), BF16),
                pltpu.VMEM((slots, 128), F32),
            ]
            + [pltpu.VMEM((slots, part), BF16)] * n_parts
            + [pltpu.VMEM((slots, part), F32)] * (2 * n_parts),
        ),
        out_shape=[whole_rows(part)] * (2 * n_parts)
        + [whole_rows(hid)] * 3
        + [jax.ShapeDtypeStruct((2, count, wide + width), BF16)] * 2,
        input_output_aliases={5 + 3 * n_parts + i: i for i in range(len(before))},
        compiler_params=params(60 * 1024 * 1024),
        cost_estimate=cost(20.5),
        name="experts",
    )(meta, xa, xb, cot_all, router, *wg, *wu, *wd, *before)
    return (outs[n_out], outs[n_out + 1]), outs[:n_out]


def head_back(grad, v, gain, cos, sin):
    scale = lax.rsqrt(jnp.mean(v * v, axis=-1, keepdims=True) + EPS)
    d = grad * cos - half_turn(grad) * sin
    u = d * gain
    inner = jnp.mean(u * v, axis=-1, keepdims=True)
    back = scale * u - v * (scale * scale * scale * inner)
    return back.astype(BF16), jnp.sum(d * v * scale, axis=0, keepdims=True)


def key_back_kernel(hpd, n_ctx, meta, dk, dv, raw, cosine, sine, gk, out, gains):
    @pl.when(pl.program_id(0) == 0)
    def _():
        gains[...] = jnp.zeros_like(gains)

    n_kv = dk.shape[0]
    for j in range(n_kv):
        at = (hpd + j) * HD
        v = raw[0, :, at : at + HD]
        if n_kv < hpd:
            v = jnp.where(meta[n_ctx] == 0, v, raw[0, :, at + HD : at + 2 * HD])
        back, gain = head_back(dk[j] * HD**-0.5, v, gk[...], cosine[...], sine[...])
        out[0, :, j * HD : (j + 1) * HD] = back
        gains[0:1, :] += gain
        out[0, :, (n_kv + j) * HD : (n_kv + j + 1) * HD] = dv[j].astype(BF16)


def key_back(dk, dv, raw, cosine, sine, gk, meta, hpd):
    n_kv = dk.shape[0]
    n_ctx, count, cols = raw.shape
    at = lambda i, t: (t[i], 0)
    head_at = lambda i, t: (0, t[i], 0)
    own = lambda i, t: (i, 0, 0)
    return pl.pallas_call(
        functools.partial(key_back_kernel, hpd, n_ctx),
        grid_spec=pltpu.PrefetchScalarGridSpec(
            num_scalar_prefetch=1,
            grid=(n_ctx,),
            in_specs=[
                pl.BlockSpec((n_kv, count, HD), head_at),
                pl.BlockSpec((n_kv, count, HD), head_at),
                pl.BlockSpec((1, count, cols), own),
                pl.BlockSpec((count, HD), at),
                pl.BlockSpec((count, HD), at),
                whole((1, HD)),
            ],
            out_specs=[pl.BlockSpec((1, count, 2 * n_kv * HD), own), whole((8, HD))],
        ),
        out_shape=[
            jax.ShapeDtypeStruct((n_ctx, count, 2 * n_kv * HD), BF16),
            jax.ShapeDtypeStruct((8, HD), F32),
        ],
        compiler_params=params(),
        cost_estimate=cost(6),
        name="key_back",
    )(meta, dk, dv, raw, cosine, sine, gk)


def input_back_kernel(hpd, meta, dq, kv, raw, cosine, sine, gq, w, xb, xa, *refs):
    grads, theirs, mine, gains, gain_grad = refs[-5:]
    i = pl.program_id(0)

    @pl.when(i == 0)
    def _():
        gains[...] = jnp.zeros_like(gains)
        gain_grad[...] = jnp.zeros_like(gain_grad)

    for j in range(hpd):
        at = slice(j * HD, (j + 1) * HD)
        back, gain = head_back(
            dq[j] * HD**-0.5, raw[0, :, at], gq[...], cosine[...], sine[...]
        )
        grads[0, :, at] = back
        gains[0:1, :] += gain
    back = dot(grads[0], w[: hpd * HD, :]) + dot(kv[0], w[hpd * HD :, :])

    def body(pair):
        out, x_ref = pair
        out[0] = back.astype(BF16)
        x = x_ref[0].astype(F32)
        r1 = lax.rsqrt(jnp.mean(x * x, axis=-1, keepdims=True) + EPS)
        gain_grad[0:1, :] += jnp.sum(back * (x * r1), axis=0, keepdims=True)

    split_pairs(i, body, (theirs, xb), (mine, xa))


def input_back(k, quarter, dq, kv, raw, cosine, sine, gq, w, meta, before):
    xa, xb = quarter
    _, count, width = xa.shape
    hpd = dq.shape[0]
    n_ctx, _, cols = raw.shape
    q_cols = hpd * HD
    at = lambda i, t: (t[4 * k + (i ^ 2)], 0)
    head_at = lambda i, t: (0, t[4 * k + (i ^ 2)], 0)
    own = lambda i, t: (4 * k + (i ^ 2), 0, 0)
    pair = jax.ShapeDtypeStruct((2, count, width), BF16)
    outs = pl.pallas_call(
        functools.partial(input_back_kernel, hpd),
        grid_spec=pltpu.PrefetchScalarGridSpec(
            num_scalar_prefetch=1,
            grid=(4,),
            in_specs=[
                pl.BlockSpec((hpd, count, HD), head_at),
                pl.BlockSpec((1, count, kv.shape[2]), own),
                pl.BlockSpec((1, count, q_cols), own),
                pl.BlockSpec((count, HD), at),
                pl.BlockSpec((count, HD), at),
                whole((1, HD)),
                whole(w.shape),
                first_pair((count, width)),
                last_pair((count, width)),
            ]
            + [pl.BlockSpec(memory_space=pl.ANY)] * len(before),
            out_specs=[
                pl.BlockSpec((1, count, q_cols), own),
                first_pair((count, width)),
                last_pair((count, width)),
                whole((8, HD)),
                whole((8, width)),
            ],
        ),
        out_shape=[
            jax.ShapeDtypeStruct((n_ctx, count, q_cols), BF16),
            pair,
            pair,
            jax.ShapeDtypeStruct((8, HD), F32),
            jax.ShapeDtypeStruct((8, width), F32),
        ],
        input_output_aliases={10: 0} if before else {},
        compiler_params=params(),
        cost_estimate=cost(7),
        name="input_back",
    )(meta, dq, kv, raw, cosine, sine, gq, w, xb, xa, *before)
    grads, theirs, mine, gains, gain_grad = outs
    return (mine, theirs), grads, gains, gain_grad


def place_kernel(parts, table, a, b, *refs):
    out = refs[-1]
    split_pairs(
        pl.program_id(0) // parts, lambda ref: out.__setitem__(..., ref[0].astype(F32)), a, b
    )


def place_columns(k, quarter, table, n_ctx, before):
    a, b = quarter
    _, rows, cols = a.shape
    parts = cols // HD
    return pl.pallas_call(
        functools.partial(place_kernel, parts),
        grid_spec=pltpu.PrefetchScalarGridSpec(
            num_scalar_prefetch=1,
            grid=(4 * parts,),
            in_specs=[
                pl.BlockSpec(
                    (1, rows, HD), lambda i, t: (jnp.minimum(i // parts, 1), 0, i % parts)
                ),
                pl.BlockSpec(
                    (1, rows, HD), lambda i, t: (jnp.maximum(i // parts - 2, 0), 0, i % parts)
                ),
            ]
            + [pl.BlockSpec(memory_space=pl.ANY)] * len(before),
            out_specs=pl.BlockSpec(
                (rows, HD), lambda i, t: (0, (i % parts) * n_ctx + t[4 * k + i // parts])
            ),
        ),
        out_shape=jax.ShapeDtypeStruct((rows, n_ctx * cols), F32),
        input_output_aliases={3: 0} if before else {},
        compiler_params=params(),
        cost_estimate=cost(4.6),
        name="place_columns",
    )(table, a, b, *before)


def place_heads_kernel(pieces, key, value):
    key[...] = pieces[0, :, :HD].astype(F32)
    value[...] = pieces[0, :, HD:].astype(F32)


def place_heads(pieces):
    n_ctx, rows, _ = pieces.shape
    at = lambda i: ((i // 2) % 2 * 2 + (i // 4) % 2, (i % 2) * 2 + i // 8)
    out = jax.ShapeDtypeStruct((4 * rows, KVH * HD), F32)
    return pl.pallas_call(
        place_heads_kernel,
        grid=(n_ctx,),
        in_specs=[pl.BlockSpec((1, rows, 2 * HD), lambda i: (i, 0, 0))],
        out_specs=[pl.BlockSpec((rows, HD), at)] * 2,
        out_shape=[out, out],
        compiler_params=params(),
        cost_estimate=cost(4),
        name="place_heads",
    )(pieces)


def widen_kernel(narrow, wide):
    wide[...] = narrow[0].astype(F32)


def widen(pieces):
    n, rows, cols = pieces.shape
    return pl.pallas_call(
        widen_kernel,
        grid=(n,),
        in_specs=[pl.BlockSpec((1, rows, cols), lambda i: (i, 0, 0))],
        out_specs=pl.BlockSpec((rows, cols), lambda i: (i, 0)),
        out_shape=jax.ShapeDtypeStruct((n * rows, cols), F32),
        compiler_params=params(),
        cost_estimate=cost(8),
        name="widen",
    )(pieces)


def local(
    inputs,
    w_query,
    w_key,
    w_value,
    w_output,
    norm_attn,
    gain_query,
    gain_key,
    w_router,
    norm_moe,
    w_gate,
    w_up,
    w_down,
    lengths,
    routes,
    pair_order,
    cotangent,
):
    n_ctx = lax.axis_size("ctx")
    n_f = lax.axis_size("fsdp")
    c = lax.axis_index("ctx")
    f = lax.axis_index("fsdp")
    count, width = inputs.shape[1], inputs.shape[2]
    length = count * n_ctx
    nz = n_ctx // 4
    later = scatter_order(n_ctx)
    hpd = H // n_ctx
    hpf = H // n_f
    group = H // KVH
    n_exp = w_router.shape[1]
    capacity = 5 * count * TOPK // (4 * n_exp)
    table = block_order(n_ctx)
    core = c % 2

    heads = [c % hpf + hpf * ((c // hpf) * hpd + j) for j in range(hpd)]
    kv_heads = [h // group for h in heads]
    columns = lambda w, h: lax.dynamic_slice_in_dim(w, h * HD, HD, 1)
    shared = n_f == 2 and hpd == 2
    if shared:
        kv_own = heads[0] // group + core * (KVH // 2)
        w_part = jnp.concatenate(
            [columns(w_query, h) for h in heads]
            + [columns(w_key, kv_own), columns(w_value, kv_own)],
            axis=1,
        )
    else:
        w_part = jnp.concatenate(
            [columns(w_query, h) for h in heads]
            + [columns(w_key, h) for h in kv_heads]
            + [columns(w_value, h) for h in kv_heads],
            axis=1,
        )
    vectors = jnp.concatenate([norm_attn, gain_query, gain_key, norm_moe])
    if n_f == 2:
        vectors = joined([vectors[None], swap(vectors[None])])
        router = joined([w_router, swap(w_router)])
    else:
        vectors = lax.all_gather(vectors, "fsdp", axis=0)
        router = lax.all_gather(w_router, "fsdp", axis=0, tiled=True)
    sizes = [norm_attn.shape[0], gain_query.shape[0], gain_key.shape[0], norm_moe.shape[0]]
    rows_of, at = [], 0
    for size in sizes:
        rows_of.append(vectors[:, at : at + size].reshape(1, n_f * size).astype(F32))
        at += size
    attn_gain, query_gain, key_gain, moe_gain = rows_of
    router_wide = jnp.pad(router, ((0, 0), (0, 128 - n_exp)))
    offsets = part_offsets(width)
    n_parts = len(offsets)
    meta_rows = jnp.concatenate([table, jnp.stack([core] + offsets).astype(jnp.int32)])
    q_cols = hpd * HD
    block = min(256, w_gate.shape[2])
    weights = {}

    def fetch_weights():
        w_qkv = joined((yield from fetch(w_part, 2)))
        weights["back"] = w_qkv.T
        if shared:
            kv_mine = w_qkv[:, q_cols:]
            kv_other = lax.ppermute(kv_mine, "ctx", flip(n_ctx, 1))
            low = jnp.where(core == 0, kv_mine, kv_other)
            high = jnp.where(core == 0, kv_other, kv_mine)
            w_qkv = jnp.concatenate(
                [w_qkv[:, :q_cols], low[:, :HD], high[:, :HD], low[:, HD:], high[:, HD:]], axis=1
            )
        weights["qkv"] = w_qkv
        own_rows = lax.dynamic_slice_in_dim(w_output, (c % hpf) * HD, HD, 0)
        w_out = joined((yield from fetch(own_rows)))
        w_out = lax.dynamic_slice_in_dim(w_out, (c // hpf) * hpd * HD, hpd * HD, 0)
        weights["out"], weights["out_back"] = w_out, w_out.T
        weights["gate"] = yield from fetch_blocks(w_gate[0], block)
        weights["up"] = yield from fetch_blocks(w_up[0], block)
        weights["down"] = yield from fetch_blocks(w_down[0], block)

    sides = [Side(fetch_weights())]

    experts_of = jnp.arange(n_exp, dtype=jnp.int32)
    picks = routes[0][:, :, None] == experts_of
    ranks = jnp.sum(
        jnp.where(picks, pair_order[0, 0].reshape(count, TOPK, 1), 0), axis=1
    )
    chosen = jnp.any(picks, axis=1)
    ranks = jnp.where(chosen, ranks, count * TOPK)
    place = jnp.sum((ranks[None, :, :] < ranks[:, None, :]).astype(jnp.int32), axis=1)
    place = jnp.where(chosen, jnp.where(place < capacity, place, -1), -2)
    place = jnp.pad(place, ((0, 0), (0, 128 - n_exp)), constant_values=-2).astype(BF16)

    ends = jnp.cumsum(lengths[0]).astype(jnp.int32)
    cosine, sine = rotary_tables(length)

    xs = {}

    def through_projection(k, quarter, token, before):
        xs[k] = quarter
        if k == 0:
            return ()
        if k == 1:
            before = projection(0, token, ())
        return projection(k, token, before)

    def projection(k, token, before):
        return project(
            k,
            xs[k],
            weights["qkv"],
            attn_gain,
            query_gain,
            key_gain,
            cosine,
            sine,
            token,
            hpd,
            n_ctx,
            n_parts,
            before,
        )

    straight = list(range(nz))
    *normed, raw, query, key, value = pipeline(
        n_ctx, straight, through_projection, meta_rows, sides, piece=inputs[0]
    )
    _, (query, cot) = land({}, sides, query, cotangent[0])
    gathered = {}

    def gather_cotangents():
        gathered["cot"] = yield lax.all_gather(cot, "ctx", axis=0), 5

    sides.append(Side(gather_cotangents()))
    mixed, log_total = attend(query, key, value, ends)
    _, (mixed,) = land({}, sides, mixed)
    x = inputs[0].astype(F32)
    branch_sum, _, _ = pipeline(
        n_ctx,
        later,
        lambda k, _, token, state: (branch(k, mixed, weights["out"], token, count), state),
        table,
        sides,
        scatter=True,
    )
    middle = x + branch_sum
    moe_scale = lax.rsqrt(jnp.mean(middle * middle, axis=-1, keepdims=True) + EPS)
    routed_in = (middle * moe_scale * moe_gain).astype(BF16)

    pad_offsets = (offsets + [jnp.int32(0)])[:2]

    def through_experts(k, quarter, token, before):
        blocks = token[4 * k : 4 * k + 4]
        meta = jnp.concatenate(
            [jnp.stack([c] + pad_offsets + [blocks[0] // 4]).astype(jnp.int32), blocks % 4]
        )
        return experts(
            k,
            quarter,
            gathered["cot"].reshape(nz, 4, count, width),
            router_wide,
            weights["gate"],
            weights["up"],
            weights["down"],
            meta,
            capacity,
            n_exp,
            before,
        )

    routed_grad, seen, _ = pipeline(
        n_ctx,
        later,
        through_experts,
        table,
        sides,
        piece=jnp.concatenate([routed_in, place], axis=1),
        scatter=True,
    )
    rows, pairs = seen[:n_parts], seen[n_parts : 2 * n_parts]
    hidden, gate_part_grad, up_part_grad = seen[2 * n_parts :]
    outputs = (middle + routed_grad[:, width + 128 :]).astype(BF16)

    gate_grad = routed_grad[:, width : width + n_exp] + routed_grad[
        :, width + n_exp : width + 2 * n_exp
    ]
    routed_grad = routed_grad[:, :width]
    logits = dot(routed_in, router)
    top = jnp.max(jnp.where(chosen, logits, -1e30), axis=-1, keepdims=True)
    shares = jnp.where(chosen, jnp.exp(logits - top), 0.0)
    gates = shares / jnp.sum(shares, axis=-1, keepdims=True)
    logit_grad = gates * (gate_grad - jnp.sum(gates * gate_grad, axis=-1, keepdims=True))
    routed_grad = routed_grad + lax.dot_general(
        logit_grad, router.astype(F32), ROWS_T, precision=HIGH
    )
    router_part = lax.dot_general(
        logit_grad, routed_in.astype(F32), COLS_T, precision=HIGH
    )

    grad_out = cotangent[0].astype(F32)
    moe_scaled = routed_grad * moe_gain
    moe_part = jnp.sum(routed_grad * middle * moe_scale, axis=0, keepdims=True)
    middle_grad = (
        grad_out
        + moe_scale * moe_scaled
        - middle
        * (
            moe_scale
            * moe_scale
            * moe_scale
            * jnp.mean(moe_scaled * middle, axis=-1, keepdims=True)
        )
    )

    grads, early, late = {}, [], []

    def scatter_grads():
        grads["gate"] = yield from scatter_blocks(rows, gate_part_grad, block)
        grads["up"] = yield from scatter_blocks(rows, up_part_grad, block)
        grads["down"] = yield from scatter_blocks(pairs, hidden, block)

    grads_side = Side(scatter_grads())
    sides = [
        grads_side,
        Side(sum_all(jnp.concatenate([router_part, moe_part], axis=0), early)),
    ]
    grad_out_w, mixed_grad = pipeline(
        n_ctx,
        straight,
        lambda k, quarter, token, before: branch_back(
            k, quarter, mixed, weights["out_back"], token, before
        ),
        table,
        sides,
        piece=middle_grad.astype(BF16),
    )
    _, (mixed_grad,) = land({}, sides, mixed_grad)

    def sum_out_grad():
        if n_f == hpd:
            placed = grad_out_w
        else:
            spread_out = jnp.arange(n_f, dtype=jnp.int32)[:, None] == (
                (c // hpf) * hpd + jnp.arange(hpd, dtype=jnp.int32)[None, :]
            )
            placed = jnp.einsum(
                "fj,jrd->frd", spread_out.astype(F32), grad_out_w.reshape(hpd, HD, width)
            ).reshape(n_f * HD, width)
        own = yield from scatter_rows(placed)
        whole_grad = yield lax.all_gather(own.astype(BF16), "ctx", axis=0), 5
        whole_grad = whole_grad.reshape(n_ctx // hpf, hpf, HD, width)
        grads["out"] = widen(lax.dynamic_index_in_dim(whole_grad, f // hpd, 0, keepdims=False))

    sides.append(Side(sum_out_grad()))
    delta = jnp.sum(mixed_grad.astype(F32) * mixed, axis=-1)[:, None, :]
    dq, dk, dv = attend_back(
        query, mixed_grad, log_total[:, :, 0][:, None, :], delta, key, value, ends
    )
    _, (dq, dk, dv) = land({}, sides, dq, dk, dv)
    if shared:
        own = lambda d: lax.dynamic_index_in_dim(d, core, 0, keepdims=True)
        away = lambda d: lax.dynamic_index_in_dim(d, 1 - core, 0, keepdims=True)
        sent = jnp.concatenate([away(dk), away(dv)]).astype(BF16)
        got = lax.ppermute(sent, "ctx", flip(n_ctx, 1)).astype(F32)
        dk, dv = own(dk) + got[:1], own(dv) + got[1:]
    kv_grad, key_gains = key_back(dk, dv, raw, cosine, sine, key_gain, meta_rows, hpd)
    normed_flat = [n.reshape(length, -1) for n in normed]

    def sum_key_grads():
        grad_kv = yield from scatter_blocks(
            normed_flat, kv_grad.reshape(length, -1), kv_grad.shape[-1]
        )
        if not shared:
            slots_kv = jnp.arange(KVH, dtype=jnp.int32)
            spread = jnp.stack([slots_kv == h for h in kv_heads]).astype(F32)
            grad_kv = grad_kv.reshape(width // n_f, 2, hpd, 1, HD) * spread[None, None, :, :, None]
            grad_kv = jnp.sum(grad_kv, axis=2).reshape(width // n_f, 2 * KVH * HD)
            grad_kv = lax.psum(grad_kv.astype(BF16), "ctx").astype(F32)
            grads["key"], grads["value"] = grad_kv[:, : KVH * HD], grad_kv[:, KVH * HD :]
            return
        for bit in (2, 4):
            rows_kept = grad_kv.shape[0] // 2
            side = (c // bit) % 2
            kept = lax.dynamic_slice_in_dim(grad_kv, side * rows_kept, rows_kept, 0)
            gone = lax.dynamic_slice_in_dim(grad_kv, (1 - side) * rows_kept, rows_kept, 0)
            got = yield lax.ppermute(gone.astype(BF16), "ctx", flip(n_ctx, bit)), 1
            grad_kv = kept + got.astype(F32)
        pieces = yield lax.all_gather(grad_kv.astype(BF16), "ctx", axis=0), 4
        grads["key"], grads["value"] = place_heads(pieces)

    sides.append(Side(sum_key_grads()))
    gain_parts, attn_parts = [], []

    def through_inputs(k, _, token, before):
        back, q_grad, gains, gain_grad = input_back(
            k,
            xs[k],
            dq,
            kv_grad,
            raw,
            cosine,
            sine,
            query_gain,
            weights["back"],
            token,
            before,
        )
        gain_parts.append(gains)
        attn_parts.append(gain_grad)
        if len(gain_parts) == nz:
            gain_rows = jnp.concatenate([sum(gain_parts)[:1], key_gains[:1]], axis=1)
            rows_last = jnp.concatenate([sum(attn_parts)[:1], gain_rows], axis=1)
            sides.append(Side(sum_all(rows_last.reshape(-1, 128), late)))
        return back, (q_grad,)

    q_grads = []

    def query_weights(token):
        q_flat = q_grads[0].reshape(length, -1)
        if n_f != 2:
            return (
                lax.psum_scatter(
                    dot(normed_flat[0], q_flat, COLS_T).astype(BF16),
                    "fsdp",
                    scatter_dimension=0,
                    tiled=True,
                ),
            )
        mine, other = normed_flat
        came = swap(dot(other, q_flat, COLS_T).astype(BF16))
        return dot(mine, q_flat, COLS_T), came

    def through_inputs_last(k, quarter, token, before):
        back, state = through_inputs(k, quarter, token, before)
        q_grads[:] = state
        return back, state

    normed_grad, _, grad_q = pipeline(
        n_ctx, later, through_inputs_last, meta_rows, sides, scatter=True, closing=query_weights
    )
    grad_q = sum(g.astype(F32) for g in grad_q).astype(BF16)

    if n_ctx == hpf:
        (grad_w_query,) = pipeline(
            n_ctx,
            straight,
            lambda k, quarter, token, before: (place_columns(k, quarter, token, n_ctx, before),),
            table,
            sides,
            piece=grad_q,
        )
    else:
        grad_w_query = (
            lax.all_gather(grad_q, "ctx", axis=0)
            .reshape(n_ctx // hpf, hpf, width // n_f, hpd, HD)
            .transpose(2, 0, 3, 1, 4)
            .reshape(width // n_f, H * HD)
            .astype(F32)
        )
    for side in sides:
        side.finish()
    early, late = early[0], late[0].reshape(-1)
    own_part = lambda v, size: lax.dynamic_slice_in_dim(v, f * (size // n_f), size // n_f, 0)
    grad_w_router = own_part(early[:n_exp].T, width)
    grad_norm_moe = own_part(early[n_exp], width)
    grad_norm_attn = own_part(late[:width], width)
    grad_gain_query = own_part(late[width : width + HD], HD)
    grad_gain_key = own_part(late[width + HD :], HD)

    attn_scale = lax.rsqrt(jnp.mean(x * x, axis=-1, keepdims=True) + EPS)
    attn_scaled = normed_grad * attn_gain
    input_grad = (
        middle_grad
        + attn_scale * attn_scaled
        - x
        * (
            attn_scale
            * attn_scale
            * attn_scale
            * jnp.mean(attn_scaled * x, axis=-1, keepdims=True)
        )
    )
    return (
        outputs[None],
        input_grad.astype(BF16)[None],
        grad_w_query,
        grads["key"],
        grads["value"],
        grads["out"],
        grad_norm_attn,
        grad_gain_query,
        grad_gain_key,
        grad_w_router,
        grad_norm_moe,
        grads["gate"][None],
        grads["up"][None],
        grads["down"][None],
    )


def solution(mesh):
    in_specs = (
        P("fsdp", "ctx", None),
        P("fsdp", None),
        P("fsdp", None),
        P("fsdp", None),
        P("fsdp", None),
        P("fsdp"),
        P("fsdp"),
        P("fsdp"),
        P("fsdp", None),
        P("fsdp"),
        P("ctx", "fsdp", None),
        P("ctx", "fsdp", None),
        P("ctx", "fsdp", None),
        P("fsdp", None),
        P("fsdp", "ctx", None),
        P("fsdp", "ctx", None),
        P("fsdp", "ctx", None),
    )
    out_specs = (
        P("fsdp", "ctx", None),
        P("fsdp", "ctx", None),
        P("fsdp", None),
        P("fsdp", None),
        P("fsdp", None),
        P("fsdp", None),
        P("fsdp"),
        P("fsdp"),
        P("fsdp"),
        P("fsdp", None),
        P("fsdp"),
        P("ctx", "fsdp", None),
        P("ctx", "fsdp", None),
        P("ctx", "fsdp", None),
    )
    return jax.shard_map(local, mesh=mesh, in_specs=in_specs, out_specs=out_specs, check_vma=False)
```

time: 1120 us -> 870 us (0.78)
  waiting for transfers between devices: 446 us -> 262 us
  Pallas kernels: 186 us -> 275 us
  blocking collectives: 88.5 us -> 0 us
  local copies, waits for them, and re-layouts: 122 us -> 72.2 us
  matrix products: 88.7 us -> 48.6 us
  starting transfers between devices: 73.3 us -> 97 us
    ppermute x59 -> x116, waiting for transfers between devices: 368 us -> 262 us  [the longest x49 142 us: send(): air[key] = lax.ppermute(array, 'ctx', pairs)]
    all_gather x6 -> x3, waiting for transfers between devices: 77 us -> 0.01 us  [the longest x1 0.01 us: gather_cotangents(): gathered['cot'] = (yield (lax.all_gather(cot, 'ctx', axis=0), 5))]
    pallas_call x11 -> x23, Pallas kernels: 128 us -> 199 us  [the longest x4 83 us: experts(): pl.pallas_call(functools.partial(experts_kernel, n_parts, width, capacity...]
    convert_element_type x4 -> x2, local copies, waits for them, and re-layouts: 57.2 us -> 0.06 us  [sum_key_grads(): got = (yield (lax.ppermute(gone.astype(BF16), 'ctx', flip(n_ctx, bit)), 1))]
    psum x1 -> x0, blocking collectives: 48.4 us -> none  [local(): tiny = lax.psum(tiny, ('ctx', 'fsdp'))]
    all_gather x2 -> x0, blocking collectives: 40.1 us -> none  [the longest x1 22.1 us: local(): pair_table = lax.all_gather(pair_table, 'ctx', axis=0)]
    dot_general x13 -> x23, matrix products: 86.5 us -> 47.2 us  [dot(): return lax.dot_general(a, b, dims, preferred_element_type=F32)]
    ppermute x59 -> x116, starting transfers between devices: 72.8 us -> 96.1 us  [the longest x49 56.3 us: send(): air[key] = lax.ppermute(array, 'ctx', pairs)]
  transfers between devices with their start and end apart: 67 -> 119, of which waited for: 37 -> 48; matrix products, arithmetic and copies ran while one was open for 20% -> 21% of each run, Pallas kernels for 11% -> 31%
where the time goes in v2:
time: 870 us; the launch traced here: 865 us
  Pallas kernels  275 us (32%)
  waiting for transfers between devices  262 us (30%)
  starting transfers between devices  97 us (11%)
  other arithmetic  87.9 us (10%)
  local copies, waits for them, and re-layouts  72.2 us (8%)
  matrix products  48.6 us (6%)
  between operations  21.8 us (3%)
    ppermute x49, waiting for transfers between devices, send(): air[key] = lax.ppermute(array, 'ctx', pairs)  142 us
    ppermute x25, waiting for transfers between devices, swap(): return lax.ppermute(part, 'fsdp', SWAP)  84.5 us
    pallas_call x4, Pallas kernels, experts(): pl.pallas_call(functools.partial(experts_kernel, n_parts, width, capacity...  83 us
    ppermute x49, starting transfers between devices, send(): air[key] = lax.ppermute(array, 'ctx', pairs)  56.3 us
    dot_general x23, matrix products, dot(): return lax.dot_general(a, b, dims, preferred_element_type=F32)  47.2 us
    pallas_call x4, Pallas kernels, project(): pl.pallas_call(functools.partial(project_kernel, hpd, n_parts, n_ctx), gr...  30.9 us
    pallas_call x1, Pallas kernels, attend_back(): pl.pallas_call(functools.partial(attend_back_kernel, docs, bq, bk), grid_...  28.7 us
    pallas_call x4, Pallas kernels, input_back(): pl.pallas_call(functools.partial(input_back_kernel, hpd), grid_spec=pltpu...  27.4 us
  transfers between devices with their start and end apart: 119, of which 48 were waited for; matrix products, arithmetic and copies ran while one was open for 21% of the time, Pallas kernels for 31%

profile of v2, /device:TPU:0, one launch (start us, length us, event | category | flops | bytes accessed | tf_op | source)
XLA Modules:
  0.0 864.7 jit_solution(16452602721756289596)
XLA Ops:
  32.4 8.1 collective-permute-done.6
  65.2 7.6 project.4
  72.8 8.1 project.5
  85.5 7.6 project.6
  102.0 7.6 project.7
  125.2 21.4 %attend.1 = (f32[2,2048,128]{2,1,0:T(8,128)S(1)}, f32[2,2048,128]{2,1,0:T(8,128)}) custom-call(s32[4]{0:T(128)S(1)} %bitcast.225, bf16[2,2048,128]{2,1,0:T(8,128)(2,1)S(1)} %copy-done.27, bf16[2,2048,128]{2,1,0:T(8,128)(2,1)S(1)} %copy-done.30, bf16[2,2048,128]{2,1,0:T(8,128)(2,1)S(1)} %copy-done.33), custom_call_target="tpu_custom_call" | custom-call | flops 20700000256 | tf_op jit(solution)/shard_map/attend/pallas_call | solution.py:390
  163.5 14.9 %collective-permute-done.20 = bf16[128,2048]{1,0:T(8,128)(2,1)S(1)} collective-permute-done((bf16[128,2048]{1,0:T(8,128)(2,1)S(1)}, bf16[128,2048]{1,0:T(8,128)(2,1)S(1)}, u32[]{:S(2)}, u32[]{:S(2)}) %collective-permute-start.20) | collective-permute-done | bytes 524320 | tf_op jit(solution)/shard_map/ppermute | solution.py:96
  192.7 12.5 %collective-permute-done.22 = bf16[128,2048]{1,0:T(8,128)(2,1)S(1)} collective-permute-done((bf16[128,2048]{1,0:T(8,128)(2,1)S(1)}, bf16[128,2048]{1,0:T(8,128)(2,1)S(1)}, u32[]{:S(2)}, u32[]{:S(2)}) %collective-permute-start.22) | collective-permute-done | bytes 524320 | tf_op jit(solution)/shard_map/ppermute | solution.py:96
  253.8 10.7 %collective-permute-done.36 = bf16[1024,256]{1,0:T(8,128)(2,1)S(1)} collective-permute-done((bf16[1024,256]{1,0:T(8,128)(2,1)S(1)}, bf16[1024,256]{1,0:T(8,128)(2,1)S(1)}, u32[]{:S(2)}, u32[]{:S(2)}) %collective-permute-start.36) | collective-permute-done | bytes 524320 | tf_op jit(solution)/shard_map/ppermute | solution.py:177
  269.1 11.0 %collective-permute-done.38 = bf16[128,2176]{1,0:T(8,128)(2,1)} collective-permute-done((bf16[128,2176]{1,0:T(8,128)(2,1)}, bf16[128,2176]{1,0:T(8,128)(2,1)}, u32[]{:S(2)}, u32[]{:S(2)}) %collective-permute-start.38) | collective-permute-done | bytes 557088 | tf_op jit(solution)/shard_map/ppermute | solution.py:96
  288.6 20.5 %experts.4 = (bf16[1280,1024]{1,0:T(8,128)(2,1)}, bf16[1280,1024]{1,0:T(8,128)(2,1)}, bf16[1280,1024]{1,0:T(8,128)(2,1)}, bf16[1280,1024]{1,0:T(8,128)(2,1)}, bf...) custom-call(s32[8]{0:T(128)} %concatenate.85.meta, ...), custom_call_target="tpu_custom_call" | custom-call | flops 23574999040 | tf_op jit(solution)/shard_map/experts/pallas_call | solution.py:647
  320.9 20.7 %experts.5 = (bf16[1280,1024]{1,0:T(8,128)(2,1)}, bf16[1280,1024]{1,0:T(8,128)(2,1)}, bf16[1280,1024]{1,0:T(8,128)(2,1)}, bf16[1280,1024]{1,0:T(8,128)(2,1)}, bf...) custom-call(s32[8]{0:T(128)} %concatenate.90.meta, ...), custom_call_target="tpu_custom_call", output_to_operand_aliasing={{0}: (11, {}), {1}: (12, {}), {2}: (13, {}), {3}: (14, {}),... | custom-call | flops 23574999040 | tf_op jit(solution)/shard_map/experts/pallas_call | solution.py:647
  361.3 20.8 %experts.6 = (bf16[1280,1024]{1,0:T(8,128)(2,1)}, bf16[1280,1024]{1,0:T(8,128)(2,1)}, bf16[1280,1024]{1,0:T(8,128)(2,1)}, bf16[1280,1024]{1,0:T(8,128)(2,1)}, bf...) custom-call(s32[8]{0:T(128)} %concatenate.91.meta, ...), custom_call_target="tpu_custom_call", output_to_operand_aliasing={{0}: (11, {}), {1}: (12, {}), {2}: (13, {}), {3}: (14, {}),... | custom-call | flops 23574999040 | tf_op jit(solution)/shard_map/experts/pallas_call | solution.py:647
  397.9 20.9 %experts.7 = (bf16[1280,1024]{1,0:T(8,128)(2,1)}, bf16[1280,1024]{1,0:T(8,128)(2,1)}, bf16[1280,1024]{1,0:T(8,128)(2,1)}, bf16[1280,1024]{1,0:T(8,128)(2,1)}, bf...) custom-call(s32[8]{0:T(128)} %concatenate.92.meta, ...), custom_call_target="tpu_custom_call", output_to_operand_aliasing={{0}: (11, {}), {1}: (12, {}), {2}: (13, {}), {3}: (14, {}),... | custom-call | flops 23574999040 | tf_op jit(solution)/shard_map/experts/pallas_call | solution.py:647
  436.5 17.0 %collective-permute-done.55 = bf16[128,4224]{1,0:T(8,128)(2,1)} collective-permute-done((bf16[128,4224]{1,0:T(8,128)(2,1)}, bf16[128,4224]{1,0:T(8,128)(2,1)}, u32[]{:S(2)}, u32[]{:S(2)}) %collective-permute-start.55) | collective-permute-done | bytes 1081376 | tf_op jit(solution)/shard_map/ppermute | solution.py:96
  464.3 10.5 %collective-permute-done.61 = bf16[128,2048]{1,0:T(8,128)(2,1)S(1)} collective-permute-done((bf16[128,2048]{1,0:T(8,128)(2,1)S(1)}, bf16[128,2048]{1,0:T(8,128)(2,1)S(1)}, u32[]{:S(2)}, u32[]{:S(2)}) %collective-permute-start.61) | collective-permute-done | bytes 524320 | tf_op jit(solution)/shard_map/ppermute | solution.py:96
  557.8 11.5 %collective-permute-done.80 = bf16[1024,256]{1,0:T(8,128)(2,1)} collective-permute-done((bf16[1024,256]{1,0:T(8,128)(2,1)}, bf16[1024,256]{1,0:T(8,128)(2,1)}, u32[]{:S(2)}, u32[]{:S(2)}) %collective-permute-start.80) | collective-permute-done | bytes 524320 | tf_op jit(solution)/shard_map/ppermute | solution.py:177
  576.3 28.7 %attend_back.1 = (f32[2,2048,128]{2,1,0:T(8,128)}, f32[2,2048,128]{2,1,0:T(8,128)}, f32[2,2048,128]{2,1,0:T(8,128)}) custom-call(s32[4]{0:T(128)S(1)} %bitcast.226, bf16[2,2048,128]{2,1,0:T(8,128)(2,1)S(1)} %copy-done.28, bf16[2,2048,128]{2,1,0:T(8,128)(2,1)S(1)} %copy-done.7, f32[2,1,2048]{2,1,0:T(1,128)S(1)} %slice_bitcast_fusion.total, ...), custom_call_target="tpu_custom_call" | custom-call | flops 27599998976 | tf_op jit(solution)/shard_map/attend_back/pallas_call | solution.py:442
  622.4 10.6 %key_back.1 = (bf16[16,128,256]{2,1,0:T(8,128)(2,1)S(1)}, f32[8,128]{1,0:T(8,128)S(1)}) custom-call(s32[19]{0:T(128)S(1)} %copy-done.14, f32[1,2048,128]{2,1,0:T(8,128)S(1)} %get-tuple-element.639.dk, f32[1,2048,128]{2,1,0:T(8,128)S(1)} %get-tuple-element.638.dv, f32[16,128,768]{2,1,0:T(8,128)} %get-tuple-element.517.raw, f32[2048,128]{1,0:T(8,128)S(1)} %copy-done.2, ...), custom_call_target="tpu_custom_call" | custom-call | flops 6899999744 | tf_op jit(solution)/shard_map/key_back/pallas_call | solution.py:707
  641.8 16.5 %collective-permute-done.83 = bf16[1024,256]{1,0:T(8,128)(2,1)S(1)} collective-permute-done((bf16[1024,256]{1,0:T(8,128)(2,1)S(1)}, bf16[1024,256]{1,0:T(8,128)(2,1)S(1)}, u32[]{:S(2)}, u32[]{:S(2)}) %collective-permute-start.83) | collective-permute-done | bytes 524320 | tf_op jit(solution)/shard_map/ppermute | solution.py:177
  673.4 10.7 %collective-permute-done.85 = bf16[128,2048]{1,0:T(8,128)(2,1)S(1)} collective-permute-done((bf16[128,2048]{1,0:T(8,128)(2,1)S(1)}, bf16[128,2048]{1,0:T(8,128)(2,1)S(1)}, u32[]{:S(2)}, u32[]{:S(2)}) %collective-permute-start.85) | collective-permute-done | bytes 524320 | tf_op jit(solution)/shard_map/ppermute | solution.py:96
  748.6 12.4 %copy.209 = bf16[2048,2048]{1,0:T(8,128)(2,1)} copy(bf16[2048,2048]{0,1:T(8,128)(2,1)} %all-gather.9.cloned.1.call-done) | data formatting | bytes 16777216 | tf_op jit(solution)/shard_map/all_gather | solution.py:1150
  772.1 8.4 collective-permute-done.104
  809.4 13.4 %widen.1 = f32[2048,2048]{1,0:T(8,128)} custom-call(bf16[16,128,2048]{2,1,0:T(8,128)(2,1)} %bitcast.227), custom_call_target="tpu_custom_call" | custom-call | flops 9200000000 | tf_op jit(solution)/shard_map/widen/pallas_call | solution.py:875
  (726 shorter events, 510.7 us)
Async XLA Ops:
  7.2 216.7 %all-gather.7.cloned.1.call-start = ((), (), s32[]{:S(2)}) async-start(), calls=%async_computation | async-start | bytes 8912896 | tf_op jit(solution)/shard_map/all_gather | solution.py:1032
  14.6 35.3 %collective-permute-start.13 = (bf16[1,2176]{1,0:T(2,128)(2,1)S(1)}, bf16[1,2176]{1,0:T(2,128)(2,1)S(1)}, u32[]{:S(2)}, u32[]{:S(2)}) collective-permute-start(bf16[1,2176]{1,0:T(2,128)(2,1)S(1)} %broadcast_in_dim.68), channel_id=1, source_target_pairs={{0,1},{1,0},{2,3},{3,2},{4,5},{5,4},{6,7},{7,6},{8,9},{9,8},{10,11... | collective-permute-start | bytes 13064 | tf_op jit(solution)/shard_map/ppermute | solution.py:177
  20.1 26.4 %collective-permute-start.7 = (bf16[1024,512]{0,1:T(8,128)(2,1)}, bf16[1024,512]{0,1:T(8,128)(2,1)}, u32[]{:S(2)}, u32[]{:S(2)}) collective-permute-start(bf16[1024,512]{0,1:T(8,128)(2,1)} %pad_maximum_fusion.5), channel_id=1, source_target_pairs={{0,1},{1,0},{2,3},{3,2},{4,5},{5,4},{6,7},{7,6},{8,9},{9,8},{10,11... | collective-permute-start | bytes 3145736 | tf_op jit(solution)/shard_map/ppermute | solution.py:177
  22.7 58.2 %collective-permute-start.10 = (bf16[128,2048]{0,1:T(8,128)(2,1)}, bf16[128,2048]{0,1:T(8,128)(2,1)}, u32[]{:S(2)}, u32[]{:S(2)}) collective-permute-start(bf16[128,2048]{0,1:T(8,128)(2,1)} %copy.238), channel_id=1, source_target_pairs={{0,1},{1,0},{2,3},{3,2},{4,5},{5,4},{6,7},{7,6},{8,9},{9,8},{10,11... | collective-permute-start | bytes 1572872 | tf_op jit(solution)/shard_map/ppermute | solution.py:177
  51.5 29.3 %collective-permute-start.9 = (bf16[128,2048]{1,0:T(8,128)(2,1)}, bf16[128,2048]{1,0:T(8,128)(2,1)}, u32[]{:S(2)}, u32[]{:S(2)}) collective-permute-start(bf16[128,2048]{1,0:T(8,128)(2,1)} %collective-permute-done.6), channel_id=1, source_target_pairs={{0,8},{2,10},{4,12},{6,14},{8,16},{10,18},{12,20},{14,22},{16,24},... | collective-permute-start | bytes 1572872 | tf_op jit(solution)/shard_map/ppermute | solution.py:96
  53.3 27.6 %collective-permute-start.8 = (bf16[128,2048]{1,0:T(8,128)(2,1)}, bf16[128,2048]{1,0:T(8,128)(2,1)}, u32[]{:S(2)}, u32[]{:S(2)}) collective-permute-start(bf16[128,2048]{1,0:T(8,128)(2,1)} %collective-permute-done.6), channel_id=1, source_target_pairs={{0,4},{2,6},{4,0},{6,2},{8,12},{10,14},{12,8},{14,10},{16,20},{18,... | collective-permute-start | bytes 1572872 | tf_op jit(solution)/shard_map/ppermute | solution.py:96
  114.5 634.2 %all-gather.9.cloned.1.call-start = ((), (), s32[]{:S(2)}) async-start(), calls=%async_computation.1 | async-start | bytes 8912896 | tf_op jit(solution)/shard_map/all_gather | solution.py:1150
  114.9 31.7 %collective-permute-start.1 = (bf16[1024,256]{1,0:T(8,128)(2,1)}, bf16[1024,256]{1,0:T(8,128)(2,1)}, u32[]{:S(2)}, u32[]{:S(2)}) collective-permute-start(bf16[1024,256]{1,0:T(8,128)(2,1)} %get-tuple-element.662), channel_id=1, source_target_pairs={{0,1},{1,0},{2,3},{3,2},{4,5},{5,4},{6,7},{7,6},{8,9},{9,8},{10,11... | collective-permute-start | bytes 1572872 | tf_op jit(solution)/shard_map/ppermute | solution.py:177
  117.7 31.3 %collective-permute-start = (bf16[1024,256]{1,0:T(8,128)(2,1)}, bf16[1024,256]{1,0:T(8,128)(2,1)}, u32[]{:S(2)}, u32[]{:S(2)}) collective-permute-start(bf16[1024,256]{1,0:T(8,128)(2,1)} %get-tuple-element.659), channel_id=1, source_target_pairs={{0,1},{1,0},{2,3},{3,2},{4,5},{5,4},{6,7},{7,6},{8,9},{9,8},{10,11... | collective-permute-start | bytes 1572872 | tf_op jit(solution)/shard_map/ppermute | solution.py:177
  178.5 26.7 %collective-permute-start.22 = (bf16[128,2048]{1,0:T(8,128)(2,1)S(1)}, bf16[128,2048]{1,0:T(8,128)(2,1)S(1)}, u32[]{:S(2)}, u32[]{:S(2)}) collective-permute-start(bf16[128,2048]{1,0:T(8,128)(2,1)S(1)} %add_convert_fusion.21), channel_id=1, source_target_pairs={{0,8},{2,10},{4,12},{6,14},{8,16},{10,18},{12,20},{14,22},{16,24},... | collective-permute-start | bytes 1572872 | tf_op jit(solution)/shard_map/ppermute | solution.py:96
  309.3 32.3 %collective-permute-start.44 = (bf16[128,2176]{1,0:T(8,128)(2,1)}, bf16[128,2176]{1,0:T(8,128)(2,1)}, u32[]{:S(2)}, u32[]{:S(2)}) collective-permute-start(bf16[128,2176]{1,0:T(8,128)(2,1)} %collective-permute-done.40), channel_id=1, source_target_pairs={{0,4},{2,6},{4,0},{6,2},{8,12},{10,14},{12,8},{14,10},{16,20},{18,... | collective-permute-start | bytes 1671176 | tf_op jit(solution)/shard_map/ppermute | solution.py:96
  318.9 28.8 %collective-permute-start.45 = (bf16[128,4224]{1,0:T(8,128)(2,1)}, bf16[128,4224]{1,0:T(8,128)(2,1)}, u32[]{:S(2)}, u32[]{:S(2)}) collective-permute-start(bf16[128,4224]{1,0:T(8,128)(2,1)} %get-tuple-element.420), channel_id=1, source_target_pairs={{0,4},{2,6},{4,0},{6,2},{8,12},{10,14},{12,8},{14,10},{16,20},{18,... | collective-permute-start | bytes 3244040 | tf_op jit(solution)/shard_map/ppermute | solution.py:96
  350.8 31.4 %collective-permute-start.47 = (bf16[128,4224]{1,0:T(8,128)(2,1)}, bf16[128,4224]{1,0:T(8,128)(2,1)}, u32[]{:S(2)}, u32[]{:S(2)}) collective-permute-start(bf16[128,4224]{1,0:T(8,128)(2,1)} %add_convert_fusion.5), channel_id=1, source_target_pairs={{0,8},{2,10},{4,12},{6,14},{8,16},{10,18},{12,20},{14,22},{16,24},... | collective-permute-start | bytes 3244040 | tf_op jit(solution)/shard_map/ppermute | solution.py:96
  359.3 26.5 %collective-permute-start.49 = (bf16[128,4224]{1,0:T(8,128)(2,1)}, bf16[128,4224]{1,0:T(8,128)(2,1)}, u32[]{:S(2)}, u32[]{:S(2)}) collective-permute-start(bf16[128,4224]{1,0:T(8,128)(2,1)} %get-tuple-element.436), channel_id=1, source_target_pairs={{0,4},{2,6},{4,0},{6,2},{8,12},{10,14},{12,8},{14,10},{16,20},{18,... | collective-permute-start | bytes 3244040 | tf_op jit(solution)/shard_map/ppermute | solution.py:96
  391.5 27.9 %collective-permute-start.52 = (bf16[128,4224]{1,0:T(8,128)(2,1)}, bf16[128,4224]{1,0:T(8,128)(2,1)}, u32[]{:S(2)}, u32[]{:S(2)}) collective-permute-start(bf16[128,4224]{1,0:T(8,128)(2,1)} %add_convert_fusion.2), channel_id=1, source_target_pairs={{0,8},{2,10},{4,12},{6,14},{8,16},{10,18},{12,20},{14,22},{16,24},... | collective-permute-start | bytes 3244040 | tf_op jit(solution)/shard_map/ppermute | solution.py:96
  425.3 28.2 %collective-permute-start.55 = (bf16[128,4224]{1,0:T(8,128)(2,1)}, bf16[128,4224]{1,0:T(8,128)(2,1)}, u32[]{:S(2)}, u32[]{:S(2)}) collective-permute-start(bf16[128,4224]{1,0:T(8,128)(2,1)} %add_convert_fusion.1), channel_id=1, source_target_pairs={{0,8},{2,10},{4,12},{6,14},{8,16},{10,18},{12,20},{14,22},{16,24},... | collective-permute-start | bytes 3244040 | tf_op jit(solution)/shard_map/ppermute | solution.py:96
  434.7 28.1 %collective-permute-start.62 = (bf16[1024,256]{1,0:T(8,128)(2,1)S(1)}, bf16[1024,256]{1,0:T(8,128)(2,1)S(1)}, u32[]{:S(2)}, u32[]{:S(2)}) collective-permute-start(bf16[1024,256]{1,0:T(8,128)(2,1)S(1)} %convolution_convert_fusion.6), channel_id=1, source_target_pairs={{0,1},{1,0},{2,3},{3,2},{4,5},{5,4},{6,7},{7,6},{8,9},{9,8},{10,11... | collective-permute-start | bytes 1572872 | tf_op jit(solution)/shard_map/ppermute | solution.py:177
  543.1 61.9 %collective-permute-start.59 = (bf16[1024,256]{1,0:T(8,128)(2,1)}, bf16[1024,256]{1,0:T(8,128)(2,1)}, u32[]{:S(2)}, u32[]{:S(2)}) collective-permute-start(bf16[1024,256]{1,0:T(8,128)(2,1)} %convolution_convert_fusion.7), channel_id=1, source_target_pairs={{0,1},{1,0},{2,3},{3,2},{4,5},{5,4},{6,7},{7,6},{8,9},{9,8},{10,11... | collective-permute-start | bytes 1572872 | tf_op jit(solution)/shard_map/ppermute | solution.py:177
  546.8 26.4 %collective-permute-start.81 = (f32[17,2048]{1,0:T(8,128)S(1)}, f32[17,2048]{1,0:T(8,128)}, u32[]{:S(2)}, u32[]{:S(2)}) collective-permute-start(f32[17,2048]{1,0:T(8,128)S(1)} %add.621), channel_id=1, source_target_pairs={{0,1},{1,0},{2,3},{3,2},{4,5},{5,4},{6,7},{7,6},{8,9},{9,8},{10,11... | collective-permute-start | bytes 417800 | tf_op jit(solution)/shard_map/ppermute | solution.py:167
  575.8 29.2 %collective-permute-start.79 = (bf16[128,2048]{0,1:T(8,128)(2,1)S(1)}, bf16[128,2048]{0,1:T(8,128)(2,1)S(1)}, u32[]{:S(2)}, u32[]{:S(2)}) collective-permute-start(bf16[128,2048]{0,1:T(8,128)(2,1)S(1)} %select_convert_fusion), channel_id=1, source_target_pairs={{0,1},{1,0},{2,3},{3,2},{4,5},{5,4},{6,7},{7,6},{8,9},{9,8},{10,11... | collective-permute-start | bytes 1572872 | tf_op jit(solution)/shard_map/ppermute | solution.py:177
  606.0 194.2 %all-gather.11.cloned.1.call-start = ((), (), s32[]{:S(2)}) async-start(), calls=%async_computation.2 | async-start | bytes 2228224 | tf_op jit(solution)/shard_map/all_gather | solution.py:1188
  611.3 30.5 %collective-permute-start.58 = (bf16[1024,256]{1,0:T(8,128)(2,1)S(1)}, bf16[1024,256]{1,0:T(8,128)(2,1)S(1)}, u32[]{:S(2)}, u32[]{:S(2)}) collective-permute-start(bf16[1024,256]{1,0:T(8,128)(2,1)S(1)} %convolution_convert_fusion.8), channel_id=1, source_target_pairs={{0,1},{1,0},{2,3},{3,2},{4,5},{5,4},{6,7},{7,6},{8,9},{9,8},{10,11... | collective-permute-start | bytes 1572872 | tf_op jit(solution)/shard_map/ppermute | solution.py:177
  615.0 58.4 %collective-permute-start.86 = (bf16[1024,256]{1,0:T(8,128)(2,1)}, bf16[1024,256]{1,0:T(8,128)(2,1)}, u32[]{:S(2)}, u32[]{:S(2)}) collective-permute-start(bf16[1024,256]{1,0:T(8,128)(2,1)} %convolution_convert_fusion.1), channel_id=1, source_target_pairs={{0,1},{1,0},{2,3},{3,2},{4,5},{5,4},{6,7},{7,6},{8,9},{9,8},{10,11... | collective-permute-start | bytes 1572872 | tf_op jit(solution)/shard_map/ppermute | solution.py:177
  617.1 80.4 %collective-permute-start.91 = (bf16[1024,256]{1,0:T(8,128)(2,1)}, bf16[1024,256]{1,0:T(8,128)(2,1)}, u32[]{:S(2)}, u32[]{:S(2)}) collective-permute-start(bf16[1024,256]{1,0:T(8,128)(2,1)} %convolution_convert_fusion), channel_id=1, source_target_pairs={{0,1},{1,0},{2,3},{3,2},{4,5},{5,4},{6,7},{7,6},{8,9},{9,8},{10,11... | collective-permute-start | bytes 1572872 | tf_op jit(solution)/shard_map/ppermute | solution.py:177
  (237 other events, 3180.8 us)
Sparse Core Ops, SparseCore 0:
  114.6 95.0 all-gather.6
  606.1 76.4 all-gather.8
  735.8 51.4 all-gather.10

commit v3 on v2

v3 whole, which is shorter than its diff:
```python
import functools

import jax
import jax.numpy as jnp
from jax import lax
from jax.experimental import pallas as pl
from jax.experimental.pallas import tpu as pltpu
from jax.sharding import PartitionSpec as P

H = 32
KVH = 4
HD = 128
TOPK = 8
EPS = 1e-06
THETA = 1000000.0
HIGH = lax.Precision.HIGHEST
LOG2E = 1.4426950408889634
F32 = jnp.float32
BF16 = jnp.bfloat16
ROWS_T = (((1,), (1,)), ((), ()))
COLS_T = (((0,), (0,)), ((), ()))


def dot(a, b, dims=(((1,), (0,)), ((), ()))):
    return lax.dot_general(a, b, dims, preferred_element_type=F32)


def params(mebibytes):
    return pltpu.CompilerParams(vmem_limit_bytes=mebibytes * 1024 * 1024)


def once(shape, index):
    return pl.BlockSpec(shape, index, pipeline_mode=pl.Buffered(1))


def cost(microseconds):
    return pl.CostEstimate(
        flops=int(microseconds * 1.15e9), bytes_accessed=0, transcendentals=0
    )


def flip(n_ctx, bit):
    return [(i, i ^ bit) for i in range(n_ctx)]


def ring(n_ctx, step):
    return [(i, (i + step) % n_ctx) for i in range(n_ctx)]


def block_order(n_ctx):
    c = lax.axis_index("ctx")
    nz = n_ctx // 4
    z, x, core = c // 4, (c // 2) % 2, c % 2
    table = []
    for k in range(nz):
        for dc in range(2):
            for dx in range(2):
                table.append(lax.rem(z + nz - k, nz) * 4 + (x ^ dx) * 2 + (core ^ dc))
    return jnp.stack(table).astype(jnp.int32)


def tie(*arrays):
    return lax.optimization_barrier(arrays)


class Side:
    def __init__(self, chain):
        self.chain, self.flying, self.left = chain, None, 0
        self.resume(None)

    def resume(self, landed):
        try:
            self.flying, self.left = self.chain.send(landed)
        except StopIteration:
            self.flying = None

    def finish(self):
        while self.flying is not None:
            self.resume(self.flying)


def land(air, sides, *others):
    due = [side for side in sides if side.flying is not None and side.left <= 1]
    for side in sides:
        side.left -= 1
    keys = list(air)
    flying = [array for side in due for array in side.flying]
    arrays = list(tie(*air.values(), *flying, *others))
    air.clear()
    landed = {key: arrays.pop(0) for key in keys}
    for side in due:
        side.resume([arrays.pop(0) for _ in side.flying])
    return landed, arrays


def pipeline(n_ctx, order, compute, token, sides, piece=None, scatter=False, closing=None):
    nz = n_ctx // 4
    air, have, state = {}, {}, ()

    def send(key, array, pairs):
        air[key] = lax.ppermute(array, "ctx", pairs)

    def bring(k):
        send(("beside", k), have["piece", k], flip(n_ctx, 2))
        if k + 1 < nz:
            send(("piece", k + 1), have["piece", k], ring(n_ctx, 4))

    def step_ends(*others):
        landed, others = land(air, sides, *others)
        have.update(landed)
        return others

    def total_of(own):
        parts = [*own, have["away"]] + ([have["carry"]] if "carry" in have else [])
        return sum(part.astype(F32) for part in parts)

    def give(blocks, token):
        mine, theirs = blocks
        arrived = lax.ppermute(theirs, "ctx", flip(n_ctx, 1))
        away = (mine[1].astype(F32) + arrived[1].astype(F32)).astype(BF16)
        token, away = tie(token, away)
        send("away", away, flip(n_ctx, 2))
        return (mine[0], arrived[0]), token

    if piece is not None:
        have["piece", 0] = piece
        for k in range(order[0] + 1):
            bring(k)
            step_ends()
    blocks = own = None
    for s, k in enumerate(order):
        following = order[s + 1 :][:1]
        quarter = None
        if piece is not None:
            for later in following:
                if ("beside", later) not in have:
                    bring(later)
            pair = [have["piece", k], have["beside", k]]
            quarter = pair + [lax.ppermute(array, "ctx", flip(n_ctx, 1)) for array in pair]
        if not scatter:
            state = compute(k, quarter, token, state)
            if following:
                token, *state = step_ends(token, *state)
            continue
        if own is not None:
            send("carry", total_of(own).astype(BF16), ring(n_ctx, 4))
        if blocks is not None:
            own, token = give(blocks, token)
        blocks, state = compute(k, quarter, token, state)
        token, *blocks = step_ends(token, *blocks)
    if not scatter:
        return tuple(state)
    send("carry", total_of(own).astype(BF16), ring(n_ctx, 4))
    own, token = give(blocks, token)
    extra = closing(token) if closing else ()
    extra = step_ends(*extra)
    return total_of(own), state, extra


def gather_quarters(piece, n_ctx):
    nz = n_ctx // 4
    along, beside, others = [piece], [], []
    core = lambda array: lax.ppermute(array, "ctx", flip(n_ctx, 1))
    for step in range(nz + 1):
        going = []
        if step + 1 < nz:
            going.append(lax.ppermute(along[step], "ctx", ring(n_ctx, 4)))
        if step > 0:
            going.append(lax.ppermute(along[step - 1], "ctx", flip(n_ctx, 2)))
        came = list((yield tuple(going), 1))
        if step + 1 < nz:
            along.append(came.pop(0))
        if step > 0:
            beside.append(came.pop(0))
    return [(a, b, core(a), core(b)) for a, b in zip(along, beside)]


def gather_blocks(piece, n_ctx, last):
    nz = n_ctx // 4
    core = lambda array: lax.ppermute(array, "ctx", flip(n_ctx, 1))
    hop = lambda array: lax.ppermute(array, "ctx", ring(n_ctx, 4))
    along = [piece]
    came, following = yield (lax.ppermute(piece, "ctx", flip(n_ctx, 2)), hop(piece)), 1
    beside = [came]
    along.append(following)
    for k in range(1, nz):
        if k > 1:
            along += yield (hop(along[k - 1]),), 1
        beside += yield (hop(beside[k - 1]),), last if k == nz - 1 else 1
    return [(a, b, core(a), core(b)) for a, b in zip(along, beside)]


def scatter_order(n_ctx):
    return list(range(1, n_ctx // 4)) + [0]


def sum_all(values, result):
    n_ctx = lax.axis_size("ctx")
    bit = 1
    while bit < n_ctx:
        (came,) = yield (lax.ppermute(values.astype(BF16), "ctx", flip(n_ctx, bit)),), 1
        values = values + came.astype(F32)
        bit *= 2
    if lax.axis_size("fsdp") == 2:
        (came,) = yield (swap(values.astype(BF16)),), 1
        values = values + came.astype(F32)
    else:
        values = lax.psum(values, "fsdp")
    result.append(values)


SWAP = [(0, 1), (1, 0)]


def swap(part):
    return lax.ppermute(part, "fsdp", SWAP)


def fetch(part, steps=1):
    if lax.axis_size("fsdp") != 2:
        return [lax.all_gather(part, "fsdp", axis=0, tiled=True)]
    (other,) = yield (swap(part),), steps
    return [part, other]


def fetch_thirds(part):
    if lax.axis_size("fsdp") != 2:
        return [lax.all_gather(part, "fsdp", axis=0, tiled=True)]
    step = (part.shape[0] // 3 + 31) // 32 * 32
    other = []
    for at in range(0, part.shape[0], step):
        rows = part[at : at + step]
        if other:
            other[-1], rows = tie(other[-1], rows)
        other += yield (swap(rows),), 1
    return [part, jnp.concatenate(other, axis=0)]


def joined(parts):
    if len(parts) == 1:
        return parts[0]
    mine, other = parts
    first = lax.axis_index("fsdp") == 0
    return jnp.concatenate([jnp.where(first, mine, other), jnp.where(first, other, mine)], axis=0)


def part_offsets(width):
    if lax.axis_size("fsdp") != 2:
        return [jnp.int32(0)]
    f = lax.axis_index("fsdp")
    return [f * (width // 2), (1 - f) * (width // 2)]


def scatter_blocks(lefts, right, block):
    if lax.axis_size("fsdp") != 2:
        full = dot(lefts[0], right, COLS_T).astype(BF16)
        return lax.psum_scatter(full, "fsdp", scatter_dimension=0, tiled=True).astype(F32)
    mine, other = lefts
    columns = [right[:, at : at + block] for at in range(0, right.shape[1], block)]
    product = lambda left, i: dot(left, columns[i], COLS_T)
    done, count = [], len(columns)
    sent = product(other, 0).astype(BF16)
    for i in range(count):
        ahead = [product(other, i + 1).astype(BF16)] if i + 1 < count else []
        fresh = [product(mine, i - 1) + came.astype(F32)] if i > 0 else []
        came, *worked = yield (swap(sent), *ahead, *fresh), 1
        if ahead:
            sent = worked.pop(0)
        done += worked
    done.append(product(mine, count - 1) + came.astype(F32))
    return done[0] if count == 1 else jnp.concatenate(done, axis=1)


def scatter_rows(full):
    if lax.axis_size("fsdp") != 2:
        return lax.psum_scatter(
            full.astype(BF16), "fsdp", scatter_dimension=0, tiled=True
        ).astype(F32)
    rows = full.shape[0] // 2
    first = lax.axis_index("fsdp") == 0
    low, high = full[:rows], full[rows:]
    (came,) = yield (swap(jnp.where(first, high, low).astype(BF16)),), 1
    return jnp.where(first, low, high) + came.astype(F32)


def group_of(k):
    return lambda t: lax.div(t[4 * k], 4)


def span(t, k, i, count):
    return pl.ds(pl.multiple_of(lax.rem(t[4 * k + i], 4) * count, count), count)


IN_HBM = pl.BlockSpec(memory_space=pltpu.HBM)


def whole(shape):
    return once(shape, lambda *_: (0,) * len(shape))


def first_pair(shape):
    return pl.BlockSpec((1,) + shape, lambda i, t: (jnp.minimum(i, 1),) + (0,) * len(shape))


def last_pair(shape):
    return pl.BlockSpec((1,) + shape, lambda i, t: (jnp.maximum(i - 2, 0),) + (0,) * len(shape))


def split_pairs(i, body, first, last):
    @pl.when(i < 2)
    def _():
        body(first)

    @pl.when(i >= 2)
    def _():
        body(last)


def rotary_table(length):
    half = HD // 2
    steps = jnp.arange(half, dtype=jnp.int32).astype(F32)
    inverse = jnp.exp(steps * (-2.0 * jnp.log(THETA) / HD))
    angles = jnp.arange(length, dtype=jnp.int32).astype(F32)[:, None] * inverse[None, :]
    return jnp.concatenate([jnp.cos(angles), jnp.sin(angles)], axis=1)


def turns(table):
    other = pltpu.roll(table, HD // 2, 1)
    first = lax.broadcasted_iota(jnp.int32, (1, HD), 1) < HD // 2
    return jnp.where(first, table, other), jnp.where(first, -other, table)


def half_turn(v):
    return pltpu.roll(v, HD // 2, 1)


def head_norm(v, gain):
    scale = lax.rsqrt(jnp.mean(v * v, axis=-1, keepdims=True) + EPS)
    return v * scale * gain


def project_kernel(k, hpd, n_kv, n_parts, n_ctx, meta, x0, x1, x2, x3, gain, gq, gk, turn, *refs):
    n_outs = n_parts + 5
    w, beside = refs[:n_parts], refs[n_parts : 2 * n_parts] if n_kv < hpd else ()
    outs, refs = refs[-(2 * n_outs + 2) : -(n_outs + 2)], refs[-(n_outs + 2) :]
    here, rows, sems = refs[:n_outs], refs[-2], refs[-1]
    normed, (raw, scales, query, key, value) = here[:n_parts], here[n_parts:]
    count = x0.shape[0]
    group = pl.ds(pl.multiple_of(lax.div(meta[4 * k], 4) * 4 * count, count), 4 * count)
    places = [pl.ds(4 * k, 4)] * (n_parts + 2) + [(slice(None), group)] * 3
    leaving = [
        pltpu.make_async_copy(here[i], outs[i].at[places[i]], sems.at[i]) for i in range(n_outs)
    ]
    for i, piece in enumerate((x0, x1, x2, x3)):
        x = piece[...].astype(F32)
        r1 = lax.rsqrt(jnp.mean(x * x, axis=-1, keepdims=True) + EPS)
        scales[i] = jnp.broadcast_to(r1, scales.shape[1:])
        rows[i * count : (i + 1) * count, :] = (x * r1 * gain[...]).astype(BF16)
        for p, part in enumerate(normed):
            at = pl.ds(pl.multiple_of(meta[n_ctx + 1 + p], 128), part.shape[2])
            part[i] = rows[i * count : (i + 1) * count, at]
    for copy in leaving[:n_parts]:
        copy.start()
    parts = [part[...].reshape(4 * count, part.shape[2]) for part in normed]
    out = sum(dot(n, w_p[...]) for n, w_p in zip(parts, w))
    other = sum(dot(n, w_p[...]) for n, w_p in zip(parts, beside)) if beside else None
    core = meta[n_ctx]
    for i in range(4):
        at = span(meta, k, i, count)
        cos, sin = turns(turn[at, :])
        block = out[i * count : (i + 1) * count, :]
        raw[i] = block[:, : (hpd + n_kv) * HD]

        def turned(v, gain):
            v = head_norm(v, gain[...])
            return (v * cos + half_turn(v) * sin).astype(BF16)

        for j in range(hpd):
            query[j, at, :] = turned(block[:, j * HD : (j + 1) * HD], gq)
        for j in range(n_kv):
            v = block[:, (hpd + j) * HD : (hpd + j + 1) * HD]
            u = block[:, (hpd + n_kv + j) * HD : (hpd + n_kv + j + 1) * HD]
            head = core if beside else j
            key[head, at, :] = turned(v, gk)
            value[head, at, :] = u.astype(BF16)
        if beside:
            block = other[i * count : (i + 1) * count, :]
            key[1 - core, at, :] = turned(block[:, :HD], gk)
            value[1 - core, at, :] = block[:, HD:].astype(BF16)
    for copy in leaving[n_parts:]:
        copy.start()
    for copy in leaving:
        copy.wait()


def project(k, quarter, w, beside, gain, gq, gk, turn, meta, hpd, n_ctx, before):
    count, width = quarter[0].shape
    length = n_ctx * count
    n_parts = len(w)
    n_kv = 1 if beside else hpd
    group = group_of(k)
    turn_at = once((4 * count, HD), lambda i, t: (group(t), 0))
    head = pltpu.HBM((hpd, length, HD), BF16)
    cols = (hpd + n_kv) * HD
    weights = [*w, *beside]
    return pl.pallas_call(
        functools.partial(project_kernel, k, hpd, n_kv, n_parts, n_ctx),
        grid_spec=pltpu.PrefetchScalarGridSpec(
            num_scalar_prefetch=1,
            grid=(1,),
            in_specs=[whole((count, width))] * 4
            + [whole((1, width)), whole((1, HD)), whole((1, HD)), turn_at]
            + [whole(array.shape) for array in weights]
            + [IN_HBM] * len(before),
            out_specs=[IN_HBM] * (n_parts + 5),
            scratch_shapes=[pltpu.VMEM((4, count, width // n_parts), BF16)] * n_parts
            + [pltpu.VMEM((4, count, cols), F32), pltpu.VMEM((4, count, HD), F32)]
            + [pltpu.VMEM((hpd, 4 * count, HD), BF16)] * 3
            + [pltpu.VMEM((4 * count, width), BF16), pltpu.SemaphoreType.DMA((n_parts + 5,))],
        ),
        out_shape=[pltpu.HBM((n_ctx, count, width // n_parts), BF16)] * n_parts
        + [
            pltpu.HBM((n_ctx, count, cols), F32),
            pltpu.HBM((n_ctx, count, HD), F32),
            head,
            head,
            head,
        ],
        input_output_aliases={9 + len(weights) + i: i for i in range(len(before))},
        compiler_params=params(18),
        cost_estimate=cost(6),
        name="project",
    )(meta, *quarter, gain, gq, gk, turn, *weights, *before)


def first_key(ends, docs, position):
    start = jnp.zeros_like(position)
    for d in range(docs):
        start = jnp.where(position >= ends[d], jnp.maximum(start, ends[d]), start)
    return start


def attend_kernel(docs, heads, bq, bk, ends, query, key, value, mixed, total):
    i = pl.program_id(0)
    positions = i * bq + lax.broadcasted_iota(jnp.int32, (bq, 1), 0)
    starts = first_key(ends, docs, positions)
    low = lax.div(first_key(ends, docs, i * bq), bk)
    high = lax.div((i + 1) * bq - 1, bk) + 1

    def step(j, carry):
        rows = pl.ds(pl.multiple_of(j * bk, bk), bk)
        spots = j * bk + lax.broadcasted_iota(jnp.int32, (1, bk), 1)
        seen = (spots <= positions) & (spots >= starts)
        sums = []
        for h, (acc, norm) in enumerate(carry):
            scores = dot(query[h], key[h, rows, :], ROWS_T)
            p = jnp.where(seen, jnp.exp2(scores * (LOG2E * HD**-0.5)), 0.0)
            acc = acc + dot(p.astype(BF16), value[h, rows, :])
            sums.append((acc, norm + jnp.sum(p, axis=-1, keepdims=True)))
        return tuple(sums)

    start = (jnp.zeros((bq, HD), F32), jnp.zeros((bq, 1), F32))
    first_lane = lax.broadcasted_iota(jnp.int32, (1, HD), 1) == 0
    for h, (acc, norm) in enumerate(lax.fori_loop(low, high, step, (start,) * heads)):
        mixed[h] = acc / norm
        column = jnp.where(first_lane, jnp.log2(norm), 0.0)
        total[h] = row_sums(column)


def row_sums(values):
    return lax.dot_general(
        jnp.ones((8, values.shape[1]), F32),
        values,
        ROWS_T,
        precision=HIGH,
        preferred_element_type=F32,
    )


def attend(query, key, value, ends, bq=256, bk=512):
    heads, length, _ = query.shape
    docs = ends.shape[0]
    block = pl.BlockSpec((heads, bq, HD), lambda i, e: (0, i, 0))
    keys = once((heads, length, HD), lambda i, e: (0, 0, 0))
    line = pl.BlockSpec((heads, 8, bq), lambda i, e: (0, 0, i))
    return pl.pallas_call(
        functools.partial(attend_kernel, docs, heads, bq, bk),
        grid_spec=pltpu.PrefetchScalarGridSpec(
            num_scalar_prefetch=1,
            grid=(length // bq,),
            in_specs=[block, keys, keys],
            out_specs=[block, line],
        ),
        out_shape=[
            jax.ShapeDtypeStruct((heads, length, HD), F32),
            jax.ShapeDtypeStruct((heads, 8, length), F32),
        ],
        compiler_params=params(14),
        cost_estimate=cost(12.5),
        name="attend",
    )(ends, query, key, value)


def attend_back_kernel(
    docs, heads, bq, bk, ends, query, grad, total, delta, key, value, dq, dk, dv, *away
):
    i = pl.program_id(0)

    @pl.when(i == 0)
    def _():
        dk[...] = jnp.zeros_like(dk)
        dv[...] = jnp.zeros_like(dv)

    positions = i * bq + lax.broadcasted_iota(jnp.int32, (1, bq), 1)
    starts = first_key(ends, docs, positions)
    low = lax.div(first_key(ends, docs, i * bq), bk)
    high = lax.div((i + 1) * bq - 1, bk) + 1

    def step(j, sums):
        rows = pl.ds(pl.multiple_of(j * bk, bk), bk)
        spots = j * bk + lax.broadcasted_iota(jnp.int32, (bk, 1), 0)
        seen = (spots <= positions) & (spots >= starts)
        out = []
        for h in range(heads):
            q, g, k = query[h], grad[h], key[h, rows, :]
            scores = dot(k, q, ROWS_T)
            p = jnp.exp2(scores * (LOG2E * HD**-0.5) - total[h, 0:1, :])
            p = jnp.where(seen, p, 0.0)
            ds = (p * (dot(value[h, rows, :], g, ROWS_T) - delta[h, 0:1, :])).astype(BF16)
            dv[h, rows, :] += dot(p.astype(BF16), g)
            dk[h, rows, :] += dot(ds, q)
            out.append(sums[h] + dot(ds, k, COLS_T))
        return tuple(out)

    sums = lax.fori_loop(low, high, step, (jnp.zeros((bq, HD), F32),) * heads)
    for h in range(heads):
        dq[h] = sums[h]

    if away:

        @pl.when(i == pl.num_programs(0) - 1)
        def _():
            other = 1 - ends[docs]
            away[0][0] = dk[other].astype(BF16)
            away[0][1] = dv[other].astype(BF16)


def attend_back(query, grad, total, delta, key, value, ends, shared, bq=256, bk=512):
    heads, length, _ = query.shape
    docs = ends.shape[0] - 1
    block = pl.BlockSpec((heads, bq, HD), lambda i, e: (0, i, 0))
    line = pl.BlockSpec((heads, 8, bq), lambda i, e: (0, 0, i))
    keys = once((heads, length, HD), lambda i, e: (0, 0, 0))
    out = jax.ShapeDtypeStruct((heads, length, HD), F32)
    return pl.pallas_call(
        functools.partial(attend_back_kernel, docs, heads, bq, bk),
        grid_spec=pltpu.PrefetchScalarGridSpec(
            num_scalar_prefetch=1,
            grid=(length // bq,),
            in_specs=[block, block, line, line, keys, keys],
            out_specs=[block, keys, keys] + [whole((2, length, HD))] * shared,
        ),
        out_shape=[out, out, out] + [jax.ShapeDtypeStruct((2, length, HD), BF16)] * shared,
        compiler_params=params(24),
        cost_estimate=cost(17),
        name="attend_back",
    )(ends, query, grad, total, delta, key, value)


def branch_kernel(hpd, table, mixed, w, theirs, mine):
    def body(out):
        total = None
        for j in range(hpd):
            part = dot(mixed[j].astype(BF16), w[j * HD : (j + 1) * HD, :])
            total = part if total is None else total + part
        out[0] = total.astype(BF16)

    split_pairs(pl.program_id(0), body, theirs, mine)


def branch(k, mixed, w, table, count):
    hpd = mixed.shape[0]
    width = w.shape[1]
    pair = jax.ShapeDtypeStruct((2, count, width), BF16)
    theirs, mine = pl.pallas_call(
        functools.partial(branch_kernel, hpd),
        grid_spec=pltpu.PrefetchScalarGridSpec(
            num_scalar_prefetch=1,
            grid=(4,),
            in_specs=[
                pl.BlockSpec((hpd, count, HD), lambda i, t: (0, t[4 * k + (i ^ 2)], 0)),
                whole((hpd * HD, width)),
            ],
            out_specs=[first_pair((count, width)), last_pair((count, width))],
        ),
        out_shape=[pair, pair],
        compiler_params=params(10),
        cost_estimate=cost(2.4),
        name="branch",
    )(table, mixed, w)
    return mine, theirs


def branch_back_kernel(k, hpd, meta, g0, g1, g2, g3, mixed, w, *refs):
    grad, delta, dw = refs[-3:]
    pieces = (g0, g1, g2, g3)
    count = g0.shape[0]
    g = jnp.concatenate([piece[...] for piece in pieces], axis=0)
    back = dot(g, w[...], ROWS_T).astype(BF16)
    for j in range(hpd):
        heads = []
        for i in range(4):
            at = span(meta, k, i, count)
            own = back[i * count : (i + 1) * count, j * HD : (j + 1) * HD]
            out = mixed[j, at, :]
            grad[j, at, :] = own
            delta[j, :, at] = row_sums(own.astype(F32) * out)
            heads.append(out.astype(BF16))
        part = dot(jnp.concatenate(heads, axis=0), g, COLS_T)
        rows = slice(j * HD, (j + 1) * HD)
        dw[rows, :] = part if len(refs) == 3 else refs[0][rows, :] + part


def branch_back(k, quarter, mixed, w, table, before):
    count, width = quarter[0].shape
    hpd, length, _ = mixed.shape
    group = group_of(k)
    head_at = once((hpd, 4 * count, HD), lambda i, t: (0, group(t), 0))
    dw_at = whole((hpd * HD, width))
    grad, delta, dw = pl.pallas_call(
        functools.partial(branch_back_kernel, k, hpd),
        grid_spec=pltpu.PrefetchScalarGridSpec(
            num_scalar_prefetch=1,
            grid=(1,),
            in_specs=[whole((count, width))] * 4
            + [head_at, whole((hpd * HD, width))]
            + ([dw_at] + [pl.BlockSpec(memory_space=pl.ANY)] * 2 if before else []),
            out_specs=[
                head_at,
                once((hpd, 8, 4 * count), lambda i, t: (0, 0, group(t))),
                dw_at,
            ],
        ),
        out_shape=[
            jax.ShapeDtypeStruct((hpd, length, HD), BF16),
            jax.ShapeDtypeStruct((hpd, 8, length), F32),
            jax.ShapeDtypeStruct((hpd * HD, width), F32),
        ],
        input_output_aliases={8: 0, 9: 1} if before else {},
        compiler_params=params(20),
        cost_estimate=cost(6),
        name="branch_back",
    )(table, *quarter, mixed, w, *before)
    return dw, grad, delta


def experts_kernel(
    k, n_parts, width, capacity, n_exp, meta, x0, x1, x2, x3, g0, g1, g2, g3, router, *refs
):
    n = n_parts
    w_from = refs[: 3 * n]
    refs = refs[-(2 * n + 5 + 6 * n + 3 + 3) :]
    outs, (mine, theirs) = refs[: 2 * n + 3], refs[2 * n + 3 : 2 * n + 5]
    refs = refs[2 * n + 5 :]
    w_here, refs = refs[: 3 * n], refs[3 * n :]
    rows, pairs, picked, refs = refs[:n], refs[n : 2 * n], refs[2 * n : 3 * n], refs[3 * n :]
    hidden, gate_grad, up_grad, chosen_ref, gate_ref, sems = refs
    slots = 4 * capacity
    part = width // n
    c = meta[0]
    lanes = lax.broadcasted_iota(jnp.int32, (1, 128), 1)
    pieces = (x0, x1, x2, x3)
    arrivals = [
        pltpu.make_async_copy(w_from[i], w_here[i], sems.at[i]) for i in range(3 * n)
    ]
    for copy in arrivals:
        copy.start()
    here = [*rows, *pairs, hidden, gate_grad, up_grad]
    leaving = [
        pltpu.make_async_copy(
            here[i], outs[i].at[pl.ds(k * slots, slots), :], sems.at[3 * n + i]
        )
        for i in range(2 * n + 3)
    ]

    def columns(p, first=0):
        return pl.ds(pl.multiple_of(first + meta[1 + p], 128), part)

    for i, x_ref in enumerate(pieces):
        cot = (g0, g1, g2, g3)[i]
        at = slice(i * capacity, (i + 1) * capacity)
        info = x_ref[:, width:].astype(F32)
        place = jnp.sum(jnp.where(lanes == c, info, 0.0), axis=1, keepdims=True)
        spots = lax.broadcasted_iota(jnp.int32, (1, capacity), 1).astype(F32)
        chosen = (spots == place).astype(BF16)
        chosen_ref[i] = chosen
        logits = dot(x_ref[:, :width], router[...])
        seen = info > -1.5
        top = jnp.max(jnp.where(seen, logits, -1e30), axis=1, keepdims=True)
        shares = jnp.where(seen, jnp.exp(logits - top), 0.0)
        gates = shares / jnp.sum(shares, axis=1, keepdims=True)
        own = jnp.sum(jnp.where(lanes == c, gates, 0.0), axis=1, keepdims=True)
        gate = lax.dot_general(
            chosen.astype(F32),
            jnp.broadcast_to(own, gates.shape),
            COLS_T,
            precision=HIGH,
            preferred_element_type=F32,
        )
        gate_ref[at, :] = gate
        for p in range(n):
            rows[p][at, :] = dot(chosen, x_ref[:, columns(p)], COLS_T).astype(BF16)
            grads = dot(chosen, cot[:, columns(p)], COLS_T)
            picked[p][at, :] = grads.astype(BF16)
            pairs[p][at, :] = (grads * gate[:, :1]).astype(BF16)
    for copy in leaving[: 2 * n]:
        copy.start()
    for copy in arrivals[: 2 * n]:
        copy.wait()
    wg, wu, wd = (w_here[n * i : n * (i + 1)] for i in range(3))
    gate_part = sum(dot(rows[p][...], wg[p][...]) for p in range(n))
    up_part = sum(dot(rows[p][...], wu[p][...]) for p in range(n))
    sigma = jax.nn.sigmoid(gate_part)
    silu_gate = gate_part * sigma
    h = (silu_gate * up_part).astype(BF16)
    hidden[...] = h
    leaving[2 * n].start()
    for copy in arrivals[2 * n :]:
        copy.wait()
    hidden_grad = sum(dot(pairs[p][...], wd[p][...]) for p in range(n))
    gg = (hidden_grad * up_part * sigma * (1.0 + gate_part * (1.0 - sigma))).astype(BF16)
    gate_grad[...] = gg
    leaving[2 * n + 1].start()
    ug = (hidden_grad * silu_gate).astype(BF16)
    up_grad[...] = ug
    leaving[2 * n + 2].start()
    inner_sum = jnp.zeros((slots, 1), F32)
    for p in range(n):
        out = dot(h, wd[p][...], ROWS_T).astype(BF16).astype(F32)
        inner_sum += jnp.sum(out * picked[p][...].astype(F32), axis=1, keepdims=True)
        scaled = (out * gate_ref[:, :1]).astype(BF16)
        row_sum = (dot(gg, wg[p][...], ROWS_T) + dot(ug, wu[p][...], ROWS_T)).astype(BF16)
        for i in range(4):
            back = (mine, theirs)[i // 2].at[i % 2]
            at = slice(i * capacity, (i + 1) * capacity)
            back[:, columns(p)] = dot(chosen_ref[i], row_sum[at, :]).astype(BF16)
            back[:, columns(p, width + 128)] = dot(chosen_ref[i], scaled[at, :]).astype(BF16)
    high = inner_sum.astype(BF16).astype(F32)
    extra = jnp.where(lanes == c, high, 0.0) + jnp.where(
        lanes == c + n_exp, inner_sum - high, 0.0
    )
    extra = extra.astype(BF16)
    for i in range(4):
        back = (mine, theirs)[i // 2].at[i % 2]
        at = slice(i * capacity, (i + 1) * capacity)
        back[:, width : width + 128] = dot(chosen_ref[i], extra[at, :]).astype(BF16)
    for copy in leaving:
        copy.wait()


def experts(k, quarter, cots, router, wg, wu, wd, meta, capacity, n_exp, before):
    count, wide = quarter[0].shape
    nz, width = len(cots), cots[k][0].shape[1]
    n_parts = len(wg)
    part = width // n_parts
    hid = wg[0].shape[1]
    slots = 4 * capacity
    anywhere = pl.BlockSpec(memory_space=pl.ANY)
    pair = once((2, count, wide + width), lambda i, m: (0, 0, 0))
    rows_all = lambda cols: pltpu.HBM((nz * slots, cols), BF16)
    n_out = 2 * n_parts + 3
    outs = pl.pallas_call(
        functools.partial(experts_kernel, k, n_parts, width, capacity, n_exp),
        grid_spec=pltpu.PrefetchScalarGridSpec(
            num_scalar_prefetch=1,
            grid=(1,),
            in_specs=[whole((count, wide))] * 4
            + [whole((count, width))] * 4
            + [whole(router.shape)]
            + [anywhere] * (3 * n_parts)
            + [IN_HBM] * len(before),
            out_specs=[IN_HBM] * n_out + [pair, pair],
            scratch_shapes=[pltpu.VMEM((part, hid), BF16)] * (3 * n_parts)
            + [pltpu.VMEM((slots, part), BF16)] * (3 * n_parts)
            + [pltpu.VMEM((slots, hid), BF16)] * 3
            + [
                pltpu.VMEM((4, count, capacity), BF16),
                pltpu.VMEM((slots, 128), F32),
                pltpu.SemaphoreType.DMA((5 * n_parts + 3,)),
            ],
        ),
        out_shape=[rows_all(part)] * (2 * n_parts)
        + [rows_all(hid)] * 3
        + [jax.ShapeDtypeStruct((2, count, wide + width), BF16)] * 2,
        input_output_aliases={10 + 3 * n_parts + i: i for i in range(len(before))},
        compiler_params=params(42),
        cost_estimate=cost(15),
        name="experts",
    )(meta, *quarter, *cots[k], router, *wg, *wu, *wd, *before)
    return (outs[n_out], outs[n_out + 1]), outs[:n_out]


def head_back(grad, v, gain, cos, sin):
    scale = lax.rsqrt(jnp.mean(v * v, axis=-1, keepdims=True) + EPS)
    d = grad * cos - half_turn(grad) * sin
    u = d * gain
    inner = jnp.mean(u * v, axis=-1, keepdims=True)
    back = scale * u - v * (scale * scale * scale * inner)
    return back.astype(BF16), jnp.sum(d * v * scale, axis=0, keepdims=True)


def key_back_kernel(meta, dk, dv, raw, turn, gk, *refs):
    out, gains = refs[-2:]
    came = refs[:-2]
    z = pl.program_id(0)

    @pl.when(z == 0)
    def _():
        gains[...] = jnp.zeros_like(gains)

    n_kv = dk.shape[0]
    count = raw.shape[1]
    for i in range(4):
        at = pl.ds(pl.multiple_of(lax.rem(meta[4 * z + i], 4) * count, count), count)
        for j in range(n_kv):
            v = raw[i, :, j * HD : (j + 1) * HD]
            key_grad, value_grad = dk[j, at, :], dv[j, at, :]
            if came:
                key_grad = key_grad + came[0][0, at, :].astype(F32)
                value_grad = value_grad + came[0][1, at, :].astype(F32)
            grad = key_grad * HD**-0.5
            back, gain = head_back(grad, v, gk[...], *turns(turn[at, :]))
            out[i, :, j * HD : (j + 1) * HD] = back
            gains[0:1, :] += gain
            out[i, :, (n_kv + j) * HD : (n_kv + j + 1) * HD] = value_grad.astype(BF16)


def key_back(dk, dv, came, raw, turn, gk, meta):
    hpd = dk.shape[0]
    n_kv = 1 if came else hpd
    n_ctx, count, _ = raw.shape
    group = lambda z, t: lax.div(t[4 * z], 4)
    head_at = pl.BlockSpec(
        (n_kv, 4 * count, HD), lambda z, t: (t[n_ctx] if came else 0, group(z, t), 0)
    )
    turn_at = pl.BlockSpec((4 * count, HD), lambda z, t: (group(z, t), 0))
    return pl.pallas_call(
        key_back_kernel,
        grid_spec=pltpu.PrefetchScalarGridSpec(
            num_scalar_prefetch=1,
            grid=(n_ctx // 4,),
            in_specs=[
                head_at,
                head_at,
                pl.BlockSpec((4, count, n_kv * HD), lambda z, t: (z, 0, hpd // n_kv)),
                turn_at,
                whole((1, HD)),
            ]
            + [pl.BlockSpec((2, 4 * count, HD), lambda z, t: (0, group(z, t), 0))] * len(came),
            out_specs=[
                pl.BlockSpec((4, count, 2 * n_kv * HD), lambda z, t: (z, 0, 0)),
                whole((8, HD)),
            ],
        ),
        out_shape=[
            jax.ShapeDtypeStruct((n_ctx, count, 2 * n_kv * HD), BF16),
            jax.ShapeDtypeStruct((8, HD), F32),
        ],
        compiler_params=params(14),
        cost_estimate=cost(5),
        name="key_back",
    )(meta, dk, dv, raw, turn, gk, *came)


def input_back_kernel(k, hpd, meta, dq, kv, raw, scales, turn, gq, w, *refs):
    x, (grads_out, theirs, mine, gains, gain_grad, rows, grads, sem) = refs[:4], refs[-8:]
    copy = pltpu.make_async_copy(grads, grads_out.at[pl.ds(4 * k, 4)], sem)
    count = raw.shape[1]
    q_cols = hpd * HD

    @pl.when(pl.program_id(0) == 0)
    def _():
        gains[...] = jnp.zeros_like(gains)
        for i in range(4):
            at = span(meta, k, i, count)
            for j in range(hpd):
                cols = slice(j * HD, (j + 1) * HD)
                grad = dq[j, at, :] * HD**-0.5
                back, gain = head_back(grad, raw[i, :, cols], gq[...], *turns(turn[at, :]))
                grads[i, :, cols] = back
                gains[0:1, :] += gain
            rows[i * count : (i + 1) * count, :q_cols] = grads[i]
            rows[i * count : (i + 1) * count, q_cols:] = kv[i]
        copy.start()

    @pl.when(pl.program_id(0) == pl.num_programs(0) - 1)
    def _():
        copy.wait()

    back = dot(rows[...], w[...], ROWS_T)
    total = None
    for i in range(4):
        block = back[i * count : (i + 1) * count, :]
        (mine, theirs)[i // 2][i % 2] = block.astype(BF16)
        term = jnp.sum(block * x[i][...].astype(F32) * scales[i, :, :1], axis=0, keepdims=True)
        total = term if total is None else total + term
    gain_grad[...] = jnp.broadcast_to(total, gain_grad.shape)


def input_back(k, quarter, dq, kv, raw, scales, turn, gq, w, meta, before):
    count, width = quarter[0].shape
    hpd = dq.shape[0]
    n_ctx = raw.shape[0]
    q_cols = hpd * HD
    chunk = width // 4
    group = group_of(k)
    turn_at = pl.BlockSpec((4 * count, HD), lambda i, t: (group(t), 0))
    own = lambda cols: pl.BlockSpec((4, count, cols), lambda i, t: (k, 0, 0))
    pair_at = pl.BlockSpec((2, count, chunk), lambda i, t: (0, 0, i))
    pair = jax.ShapeDtypeStruct((2, count, width), BF16)
    outs = pl.pallas_call(
        functools.partial(input_back_kernel, k, hpd),
        grid_spec=pltpu.PrefetchScalarGridSpec(
            num_scalar_prefetch=1,
            grid=(4,),
            in_specs=[
                pl.BlockSpec((hpd, 4 * count, HD), lambda i, t: (0, group(t), 0)),
                own(kv.shape[2]),
                own(q_cols),
                own(HD),
                turn_at,
                whole((1, HD)),
                pl.BlockSpec((chunk, w.shape[1]), lambda i, t: (i, 0)),
            ]
            + [pl.BlockSpec((count, chunk), lambda i, t: (0, i))] * 4
            + [IN_HBM] * len(before),
            out_specs=[
                IN_HBM,
                pair_at,
                pair_at,
                whole((8, HD)),
                pl.BlockSpec((8, chunk), lambda i, t: (0, i)),
            ],
            scratch_shapes=[
                pltpu.VMEM((4 * count, w.shape[1]), BF16),
                pltpu.VMEM((4, count, q_cols), BF16),
                pltpu.SemaphoreType.DMA(()),
            ],
        ),
        out_shape=[
            pltpu.HBM((n_ctx, count, q_cols), BF16),
            pair,
            pair,
            jax.ShapeDtypeStruct((8, HD), F32),
            jax.ShapeDtypeStruct((8, width), F32),
        ],
        input_output_aliases={12: 0} if before else {},
        compiler_params=params(18),
        cost_estimate=cost(6),
        name="input_back",
    )(meta, dq, kv, raw, scales, turn, gq, w, *quarter, *before)
    grads, theirs, mine, gains, gain_grad = outs
    return (mine, theirs), grads, gains, gain_grad


def place_kernel(parts, n_kv, table, *refs):
    columns, keys = refs[:4], refs[4 : 4 + n_kv]
    outs = refs[-3:] if n_kv else refs[-1:]
    for n in range(4):

        @pl.when(pl.program_id(0) // parts == n)
        def _():
            outs[0][...] = columns[n][...].astype(F32)
            if n_kv:
                outs[1][...] = keys[n][:, :HD].astype(F32)
                outs[2][...] = keys[n][:, HD:].astype(F32)


def place_columns(k, quarter, table, n_ctx, rows, before):
    all_rows, cols = quarter[0].shape
    parts = cols // HD
    kv_rows = all_rows - rows

    def piece_at(n):
        return lambda i, t: (0, jnp.clip(i - n * parts, 0, parts - 1))

    def head_at(i, t):
        c = t[4 * k + i // parts]
        rows_part = lax.rem(c // 2, 2) * 2 + lax.rem(c // 4, 2)
        return rows_part, lax.rem(c, 2) * 2 + c // 8

    out_specs = [
        pl.BlockSpec((rows, HD), lambda i, t: (0, (i % parts) * n_ctx + t[4 * k + i // parts]))
    ]
    out_shape = [jax.ShapeDtypeStruct((rows, n_ctx * cols), F32)]
    in_specs = [pl.BlockSpec((rows, HD), piece_at(n)) for n in range(4)]
    pieces = list(quarter)
    if kv_rows:
        in_specs += [once((kv_rows, cols), lambda i, t: (rows // kv_rows, 0))] * 4
        pieces += quarter
        out_specs += [pl.BlockSpec((kv_rows, HD), head_at)] * 2
        out_shape += [jax.ShapeDtypeStruct((rows, KVH * HD), F32)] * 2
    return pl.pallas_call(
        functools.partial(place_kernel, parts, len(pieces) - 4),
        grid_spec=pltpu.PrefetchScalarGridSpec(
            num_scalar_prefetch=1,
            grid=(4 * parts,),
            in_specs=in_specs + [pl.BlockSpec(memory_space=pl.ANY)] * len(before),
            out_specs=out_specs,
        ),
        out_shape=out_shape,
        input_output_aliases={1 + len(pieces) + i: i for i in range(len(before))},
        compiler_params=params(12),
        cost_estimate=cost(4.6),
        name="place_columns",
    )(table, *pieces, *before)


def place_rows_kernel(table, *refs):
    out = refs[-1]
    for n in range(len(refs) - 1):

        @pl.when(pl.program_id(0) == n)
        def _():
            out[...] = refs[n][...].astype(F32)


def place_rows(quarters, table):
    blocks = [block for quarter in quarters for block in quarter]
    rows, cols = blocks[0].shape
    return pl.pallas_call(
        place_rows_kernel,
        grid_spec=pltpu.PrefetchScalarGridSpec(
            num_scalar_prefetch=1,
            grid=(len(blocks),),
            in_specs=[whole((rows, cols))] * len(blocks),
            out_specs=pl.BlockSpec((rows, cols), lambda i, t: (t[i], 0)),
        ),
        out_shape=jax.ShapeDtypeStruct((len(blocks) * rows, cols), F32),
        compiler_params=params(16),
        cost_estimate=cost(8),
        name="place_rows",
    )(table, *blocks)


def local(
    inputs,
    w_query,
    w_key,
    w_value,
    w_output,
    norm_attn,
    gain_query,
    gain_key,
    w_router,
    norm_moe,
    w_gate,
    w_up,
    w_down,
    lengths,
    routes,
    pair_order,
    cotangent,
):
    n_ctx = lax.axis_size("ctx")
    n_f = lax.axis_size("fsdp")
    c = lax.axis_index("ctx")
    f = lax.axis_index("fsdp")
    count, width = inputs.shape[1], inputs.shape[2]
    length = count * n_ctx
    nz = n_ctx // 4
    later = scatter_order(n_ctx)
    hpd = H // n_ctx
    hpf = H // n_f
    group = H // KVH
    n_exp = w_router.shape[1]
    capacity = 5 * count * TOPK // (4 * n_exp)
    table = block_order(n_ctx)
    core = c % 2

    heads = [c % hpf + hpf * ((c // hpf) * hpd + j) for j in range(hpd)]
    kv_heads = [h // group for h in heads]
    columns = lambda w, h: lax.dynamic_slice_in_dim(w, h * HD, HD, 1)
    shared = n_f == 2 and hpd == 2
    if shared:
        kv_own = heads[0] // group + core * (KVH // 2)
        w_part = jnp.concatenate(
            [columns(w_query, h) for h in heads]
            + [columns(w_key, kv_own), columns(w_value, kv_own)],
            axis=1,
        )
    else:
        w_part = jnp.concatenate(
            [columns(w_query, h) for h in heads]
            + [columns(w_key, h) for h in kv_heads]
            + [columns(w_value, h) for h in kv_heads],
            axis=1,
        )
    w_part, norm_first = tie(w_part, norm_attn)
    vectors = jnp.concatenate([norm_first, gain_query, gain_key, norm_moe])
    if n_f == 2:
        vectors = joined([vectors[None], swap(vectors[None])])
        router = joined([w_router, swap(w_router)])
    else:
        vectors = lax.all_gather(vectors, "fsdp", axis=0)
        router = lax.all_gather(w_router, "fsdp", axis=0, tiled=True)
    sizes = [norm_attn.shape[0], gain_query.shape[0], gain_key.shape[0], norm_moe.shape[0]]
    rows_of, at = [], 0
    for size in sizes:
        rows_of.append(vectors[:, at : at + size].reshape(1, n_f * size).astype(F32))
        at += size
    attn_gain, query_gain, key_gain, moe_gain = rows_of
    router_wide = jnp.pad(router, ((0, 0), (0, 128 - n_exp)))
    offsets = part_offsets(width)
    n_parts = len(offsets)
    meta_rows = jnp.concatenate([table, jnp.stack([core] + offsets).astype(jnp.int32)])
    q_cols = hpd * HD
    block = w_gate.shape[2] // 3
    weights = {}

    def fetch_weights():
        parts = yield from fetch(w_part, 2)
        weights["qkv"], weights["beside"] = parts, []
        if shared:
            weights["beside"] = [
                lax.ppermute(part[:, q_cols:], "ctx", flip(n_ctx, 1)) for part in parts
            ]
        weights["back"] = joined(parts)
        own_rows = lax.dynamic_slice_in_dim(w_output, (c % hpf) * HD, HD, 0)
        w_out = joined((yield from fetch(own_rows)))
        weights["out"] = lax.dynamic_slice_in_dim(w_out, (c // hpf) * hpd * HD, hpd * HD, 0)
        weights["gate"] = yield from fetch_thirds(w_gate[0])
        weights["up"] = yield from fetch_thirds(w_up[0])
        weights["down"] = yield from fetch_thirds(w_down[0])

    gathered = {}

    def gather_cotangents():
        (cot,) = yield (cotangent[0],), 3
        gathered["cot"] = yield from gather_quarters(cot, n_ctx)

    sides = [Side(fetch_weights()), Side(gather_cotangents())]

    experts_of = jnp.arange(n_exp, dtype=jnp.int32)
    picks = routes[0][:, :, None] == experts_of
    ranks = jnp.sum(
        jnp.where(picks, pair_order[0, 0].reshape(count, TOPK, 1), 0), axis=1
    )
    chosen = jnp.any(picks, axis=1)
    ranks = jnp.where(chosen, ranks, count * TOPK)
    place = jnp.sum((ranks[None, :, :] < ranks[:, None, :]).astype(jnp.int32), axis=1)
    place = jnp.where(chosen, jnp.where(place < capacity, place, -1), -2)
    place = jnp.pad(place, ((0, 0), (0, 128 - n_exp)), constant_values=-2).astype(BF16)

    ends = jnp.cumsum(lengths[0]).astype(jnp.int32)
    turn = rotary_table(length)

    xs = {}

    def through_projection(k, quarter, token, before):
        xs[k] = quarter
        if k == 0:
            return ()
        if k == 1:
            before = projection(0, token, ())
        return projection(k, token, before)

    def projection(k, token, before):
        return project(
            k,
            xs[k],
            weights["qkv"],
            weights["beside"],
            attn_gain,
            query_gain,
            key_gain,
            turn,
            token,
            hpd,
            n_ctx,
            before,
        )

    straight = list(range(nz))
    *normed, raw, scales, query, key, value = pipeline(
        n_ctx, straight, through_projection, meta_rows, sides, piece=inputs[0]
    )
    _, (query,) = land({}, sides, query)
    mixed, log_total = attend(query, key, value, ends)
    _, (mixed,) = land({}, sides, mixed)
    x = inputs[0].astype(F32)
    branch_sum, _, _ = pipeline(
        n_ctx,
        later,
        lambda k, _, token, state: (branch(k, mixed, weights["out"], token, count), state),
        table,
        sides,
        scatter=True,
    )
    middle = x + branch_sum
    moe_scale = lax.rsqrt(jnp.mean(middle * middle, axis=-1, keepdims=True) + EPS)
    routed_in = (middle * moe_scale * moe_gain).astype(BF16)

    pad_offsets = (offsets + [jnp.int32(0)])[:2]
    head_meta = [jnp.stack([c] + pad_offsets).astype(jnp.int32)]
    expert_meta = jnp.concatenate(head_meta)

    def through_experts(k, quarter, token, before):
        return experts(
            k,
            quarter,
            gathered["cot"],
            router_wide,
            weights["gate"],
            weights["up"],
            weights["down"],
            token,
            capacity,
            n_exp,
            before,
        )

    routed_grad, seen, _ = pipeline(
        n_ctx,
        later,
        through_experts,
        expert_meta,
        sides,
        piece=jnp.concatenate([routed_in, place], axis=1),
        scatter=True,
    )
    rows, pairs = seen[:n_parts], seen[n_parts : 2 * n_parts]
    hidden, gate_part_grad, up_part_grad = seen[2 * n_parts :]
    outputs = (middle + routed_grad[:, width + 128 :]).astype(BF16)

    gate_grad = routed_grad[:, width : width + n_exp] + routed_grad[
        :, width + n_exp : width + 2 * n_exp
    ]
    routed_grad = routed_grad[:, :width]
    logits = dot(routed_in, router)
    top = jnp.max(jnp.where(chosen, logits, -1e30), axis=-1, keepdims=True)
    shares = jnp.where(chosen, jnp.exp(logits - top), 0.0)
    gates = shares / jnp.sum(shares, axis=-1, keepdims=True)
    logit_grad = gates * (gate_grad - jnp.sum(gates * gate_grad, axis=-1, keepdims=True))
    routed_grad = routed_grad + lax.dot_general(
        logit_grad, router.astype(F32), ROWS_T, precision=HIGH
    )
    router_part = lax.dot_general(
        logit_grad, routed_in.astype(F32), COLS_T, precision=HIGH
    )

    grad_out = cotangent[0].astype(F32)
    moe_scaled = routed_grad * moe_gain
    moe_part = jnp.sum(routed_grad * middle * moe_scale, axis=0, keepdims=True)
    middle_grad = (
        grad_out
        + moe_scale * moe_scaled
        - middle
        * (
            moe_scale
            * moe_scale
            * moe_scale
            * jnp.mean(moe_scaled * middle, axis=-1, keepdims=True)
        )
    )

    grads, sums = {}, []

    def scatter_grads():
        grads["gate"] = yield from scatter_blocks(rows, gate_part_grad, block)
        grads["up"] = yield from scatter_blocks(rows, up_part_grad, block)
        grads["down"] = yield from scatter_blocks(pairs, hidden, block)

    sides = [Side(scatter_grads())]
    grad_out_w, mixed_grad, delta = pipeline(
        n_ctx,
        straight,
        lambda k, quarter, token, before: branch_back(
            k, quarter, mixed, weights["out"], token, before
        ),
        table,
        sides,
        piece=middle_grad.astype(BF16),
    )
    def sum_out_grad():
        if n_f == hpd:
            placed = grad_out_w
        else:
            spread_out = jnp.arange(n_f, dtype=jnp.int32)[:, None] == (
                (c // hpf) * hpd + jnp.arange(hpd, dtype=jnp.int32)[None, :]
            )
            placed = jnp.einsum(
                "fj,jrd->frd", spread_out.astype(F32), grad_out_w.reshape(hpd, HD, width)
            ).reshape(n_f * HD, width)
        own = yield from scatter_rows(placed)
        own = own.astype(BF16)
        if n_ctx == hpf:
            grads["out"] = place_rows((yield from gather_blocks(own, n_ctx, 4)), table)
        else:
            whole_grad = lax.all_gather(own, "ctx", axis=0).reshape(-1, hpf * HD, width)
            mine = lax.dynamic_index_in_dim(whole_grad, f // hpd, 0, keepdims=False)
            grads["out"] = mine.astype(F32)

    sides.append(Side(sum_out_grad()))
    ends_and_core = jnp.concatenate([ends, core[None].astype(jnp.int32)])
    dq, dk, dv, *away = attend_back(
        query, mixed_grad, log_total, delta, key, value, ends_and_core, int(shared)
    )
    _, (dq, dk, dv, *away) = land({}, sides, dq, dk, dv, *away)
    came = [lax.ppermute(array, "ctx", flip(n_ctx, 1)) for array in away]
    kv_grad, key_gains = key_back(dk, dv, came, raw, turn, key_gain, meta_rows)
    normed_flat = [n.reshape(length, -1) for n in normed]

    def sum_key_grads():
        grad_kv = yield from scatter_blocks(
            normed_flat, kv_grad.reshape(length, -1), kv_grad.shape[-1]
        )
        if not shared:
            slots_kv = jnp.arange(KVH, dtype=jnp.int32)
            spread = jnp.stack([slots_kv == h for h in kv_heads]).astype(F32)
            grad_kv = grad_kv.reshape(width // n_f, 2, hpd, 1, HD) * spread[None, None, :, :, None]
            grad_kv = jnp.sum(grad_kv, axis=2).reshape(width // n_f, 2 * KVH * HD)
            grad_kv = lax.psum(grad_kv.astype(BF16), "ctx").astype(F32)
            grads["key"], grads["value"] = grad_kv[:, : KVH * HD], grad_kv[:, KVH * HD :]
            return
        for bit in (2, 4):
            rows_kept = grad_kv.shape[0] // 2
            side = (c // bit) % 2
            kept = lax.dynamic_slice_in_dim(grad_kv, side * rows_kept, rows_kept, 0)
            gone = lax.dynamic_slice_in_dim(grad_kv, (1 - side) * rows_kept, rows_kept, 0)
            (got,) = yield (lax.ppermute(gone.astype(BF16), "ctx", flip(n_ctx, bit)),), 1
            grad_kv = kept + got.astype(F32)
        grads["key_piece"] = grad_kv.astype(BF16)

    sides.append(Side(sum_key_grads()))
    gain_parts, attn_parts = [], []

    def through_inputs(k, _, token, before):
        back, q_grad, gains, gain_grad = input_back(
            k,
            xs[k],
            dq,
            kv_grad,
            raw,
            scales,
            turn,
            query_gain,
            weights["back"],
            token,
            before,
        )
        gain_parts.append(gains)
        attn_parts.append(gain_grad)
        if len(gain_parts) == nz:
            gain_rows = jnp.concatenate([sum(gain_parts)[:1], key_gains[:1]], axis=1)
            gain_rows = jnp.pad(gain_rows, ((0, 0), (0, width - 2 * HD)))
            rows_last = [router_part, moe_part, sum(attn_parts)[:1], gain_rows]
            sides.append(Side(sum_all(jnp.concatenate(rows_last, axis=0), sums)))
        return back, (q_grad,)

    q_grads = []

    def query_weights(token):
        q_flat = q_grads[0].reshape(length, -1)
        if n_f != 2:
            return (
                lax.psum_scatter(
                    dot(normed_flat[0], q_flat, COLS_T).astype(BF16),
                    "fsdp",
                    scatter_dimension=0,
                    tiled=True,
                ),
            )
        mine, other = normed_flat
        came = swap(dot(other, q_flat, COLS_T).astype(BF16))
        return dot(mine, q_flat, COLS_T), came

    def through_inputs_last(k, quarter, token, before):
        back, state = through_inputs(k, quarter, token, before)
        q_grads[:] = state
        return back, state

    normed_grad, _, grad_q = pipeline(
        n_ctx, later, through_inputs_last, meta_rows, sides, scatter=True, closing=query_weights
    )
    for side in sides[2:3]:
        side.finish()
    grad_q = sum(g.astype(F32) for g in grad_q).astype(BF16)
    q_rows = grad_q.shape[0]
    if shared:
        grad_q = jnp.concatenate([grad_q, grads["key_piece"]], axis=0)

    if n_ctx == hpf:
        placed = pipeline(
            n_ctx,
            straight,
            lambda k, quarter, token, before: place_columns(
                k, quarter, token, n_ctx, q_rows, before
            ),
            table,
            sides,
            piece=grad_q,
        )
        grad_w_query = placed[0]
        if shared:
            grads["key"], grads["value"] = placed[1:]
    else:
        grad_w_query = (
            lax.all_gather(grad_q, "ctx", axis=0)
            .reshape(n_ctx // hpf, hpf, width // n_f, hpd, HD)
            .transpose(2, 0, 3, 1, 4)
            .reshape(width // n_f, H * HD)
            .astype(F32)
        )
    for side in sides:
        side.finish()
    sums = sums[0]
    own_part = lambda v, size: lax.dynamic_slice_in_dim(v, f * (size // n_f), size // n_f, 0)
    grad_w_router = own_part(sums[:n_exp].T, width)
    grad_norm_moe = own_part(sums[n_exp], width)
    grad_norm_attn = own_part(sums[n_exp + 1], width)
    grad_gain_query = own_part(sums[n_exp + 2, :HD], HD)
    grad_gain_key = own_part(sums[n_exp + 2, HD : 2 * HD], HD)

    attn_scale = lax.rsqrt(jnp.mean(x * x, axis=-1, keepdims=True) + EPS)
    attn_scaled = normed_grad * attn_gain
    input_grad = (
        middle_grad
        + attn_scale * attn_scaled
        - x
        * (
            attn_scale
            * attn_scale
            * attn_scale
            * jnp.mean(attn_scaled * x, axis=-1, keepdims=True)
        )
    )
    return (
        outputs[None],
        input_grad.astype(BF16)[None],
        grad_w_query,
        grads["key"],
        grads["value"],
        grads["out"],
        grad_norm_attn,
        grad_gain_query,
        grad_gain_key,
        grad_w_router,
        grad_norm_moe,
        grads["gate"][None],
        grads["up"][None],
        grads["down"][None],
    )


def solution(mesh):
    in_specs = (
        P("fsdp", "ctx", None),
        P("fsdp", None),
        P("fsdp", None),
        P("fsdp", None),
        P("fsdp", None),
        P("fsdp"),
        P("fsdp"),
        P("fsdp"),
        P("fsdp", None),
        P("fsdp"),
        P("ctx", "fsdp", None),
        P("ctx", "fsdp", None),
        P("ctx", "fsdp", None),
        P("fsdp", None),
        P("fsdp", "ctx", None),
        P("fsdp", "ctx", None),
        P("fsdp", "ctx", None),
    )
    out_specs = (
        P("fsdp", "ctx", None),
        P("fsdp", "ctx", None),
        P("fsdp", None),
        P("fsdp", None),
        P("fsdp", None),
        P("fsdp", None),
        P("fsdp"),
        P("fsdp"),
        P("fsdp"),
        P("fsdp", None),
        P("fsdp"),
        P("ctx", "fsdp", None),
        P("ctx", "fsdp", None),
        P("ctx", "fsdp", None),
    )
    return jax.shard_map(local, mesh=mesh, in_specs=in_specs, out_specs=out_specs, check_vma=False)
```

time: 870 us -> 759 us (0.87)
  Pallas kernels: 275 us -> 200 us
  waiting for transfers between devices: 262 us -> 324 us
  other arithmetic: 87.9 us -> 50.9 us
  local copies, waits for them, and re-layouts: 72.2 us -> 37.1 us
  matrix products: 48.6 us -> 25.2 us
  between operations: 21.8 us -> 3.51 us
  starting transfers between devices: 97 us -> 109 us
    pallas_call x25 -> x24, Pallas kernels: 265 us -> 189 us  [the longest x4 60.5 us: experts(): pl.pallas_call(functools.partial(experts_kernel, k, n_parts, width, capac...]
    ppermute x30 -> x71, waiting for transfers between devices: 31.1 us -> 71.6 us  [the longest x4 33.8 us: sum_all(): lax.ppermute(values.astype(BF16), 'ctx', flip(n_ctx, bit))]
    ppermute x49, waiting for transfers between devices: 142 us -> 172 us  [send(): air[key] = lax.ppermute(array, 'ctx', pairs)]
    dot_general x23, matrix products: 47.2 us -> 23.8 us  [dot(): return lax.dot_general(a, b, dims, preferred_element_type=F32)]
    another operation x19 -> x3, other arithmetic: 15.2 us -> 0.27 us  [the longest x17 15 us: pipeline(): mine = jnp.stack([have['piece', k], have['beside', k]])]
    ppermute x25 -> x26, waiting for transfers between devices: 84.5 us -> 71.2 us  [swap(): return lax.ppermute(part, 'fsdp', SWAP)]
    all_gather x1 -> x0, local copies, waits for them, and re-layouts: 12.4 us -> none  [sum_out_grad(): whole_grad = (yield (lax.all_gather(own.astype(BF16), 'ctx', axis=0), 5))]
    ppermute x30 -> x71, starting transfers between devices: 17.3 us -> 28.9 us  [the longest x6 6.51 us: gather_blocks(): hop = lambda array: lax.ppermute(array, 'ctx', ring(n_ctx, 4))]
  transfers between devices with their start and end apart: 119 -> 158, of which waited for: 48 -> 58; matrix products, arithmetic and copies ran while one was open for 21% -> 13% of each run, Pallas kernels for 31% -> 26%
where the time goes in v3:
time: 759 us; the launch traced here: 750 us
  waiting for transfers between devices  324 us (43%)
  Pallas kernels  200 us (26%)
  starting transfers between devices  109 us (14%)
  other arithmetic  50.9 us (7%)
  local copies, waits for them, and re-layouts  37.1 us (5%)
  matrix products  25.2 us (3%)
    ppermute x49, waiting for transfers between devices, send(): air[key] = lax.ppermute(array, 'ctx', pairs)  172 us
    ppermute x26, waiting for transfers between devices, swap(): return lax.ppermute(part, 'fsdp', SWAP)  71.2 us
    pallas_call x4, Pallas kernels, experts(): pl.pallas_call(functools.partial(experts_kernel, k, n_parts, width, capac...  60.5 us
    ppermute x49, starting transfers between devices, send(): air[key] = lax.ppermute(array, 'ctx', pairs)  48.7 us
    ppermute x4, waiting for transfers between devices, sum_all(): lax.ppermute(values.astype(BF16), 'ctx', flip(n_ctx, bit))  33.8 us
    ppermute x26, starting transfers between devices, swap(): return lax.ppermute(part, 'fsdp', SWAP)  31.1 us
    pallas_call x4, Pallas kernels, project(): pl.pallas_call(functools.partial(project_kernel, k, hpd, n_kv, n_parts, n...  28.4 us
    dot_general x23, matrix products, dot(): return lax.dot_general(a, b, dims, preferred_element_type=F32)  23.8 us
  transfers between devices with their start and end apart: 158, of which 58 were waited for; matrix products, arithmetic and copies ran while one was open for 13% of the time, Pallas kernels for 26%

profile of v3, /device:TPU:0, one launch (start us, length us, event | category | flops | bytes accessed | tf_op | source)
XLA Modules:
  0.0 749.7 jit_solution(8402077254238677362)
XLA Ops:
  73.5 9.3 %collective-permute-done.17 = bf16[352,768]{1,0:T(8,128)(2,1)} collective-permute-done((bf16[352,768]{1,0:T(8,128)(2,1)}, bf16[352,768]{1,0:T(8,128)(2,1)}, u32[]{:S(2)}, u32[]{:S(2)}) %collective-permute-start.17) | collective-permute-done | bytes 540704 | tf_op jit(solution)/shard_map/ppermute | solution.py:216
  113.4 14.0 %attend.1 = (f32[2,2048,128]{2,1,0:T(8,128)S(1)}, f32[2,8,2048]{2,1,0:T(8,128)S(1)}) custom-call(s32[4]{0:T(128)S(1)} %bitcast.245, bf16[2,2048,128]{2,1,0:T(8,128)(2,1)S(1)} %copy-done.58, bf16[2,2048,128]{2,1,0:T(8,128)(2,1)S(1)} %copy-done.60, bf16[2,2048,128]{2,1,0:T(8,128)(2,1)S(1)} %copy-done.62), custom_call_target="tpu_custom_call" | custom-call | flops 14375000064 | tf_op jit(solution)/shard_map/attend/pallas_call | solution.py:486
  135.6 9.7 %collective-permute-done.33.g1 = bf16[128,2048]{1,0:T(8,128)(2,1)S(1)} collective-permute-done((bf16[128,2048]{1,0:T(8,128)(2,1)S(1)}, bf16[128,2048]{1,0:T(8,128)(2,1)S(1)}, u32[]{:S(2)}, u32[]{:S(2)}) %collective-permute-start.33) | collective-permute-done | bytes 524320 | tf_op jit(solution)/shard_map/ppermute | solution.py:169
  145.3 10.4 %collective-permute-done.31 = bf16[128,2048]{1,0:T(8,128)(2,1)S(1)} collective-permute-done((bf16[128,2048]{1,0:T(8,128)(2,1)S(1)}, bf16[128,2048]{1,0:T(8,128)(2,1)S(1)}, u32[]{:S(2)}, u32[]{:S(2)}) %collective-permute-start.31) | collective-permute-done | bytes 524320 | tf_op jit(solution)/shard_map/ppermute | solution.py:101
  164.1 9.1 %collective-permute-done.37 = bf16[320,768]{1,0:T(8,128)(2,1)S(1)} collective-permute-done((bf16[320,768]{1,0:T(8,128)(2,1)S(1)}, bf16[320,768]{1,0:T(8,128)(2,1)S(1)}, u32[]{:S(2)}, u32[]{:S(2)}) %collective-permute-start.37) | collective-permute-done | bytes 491552 | tf_op jit(solution)/shard_map/ppermute | solution.py:216
  205.6 9.7 %collective-permute-done.43 = bf16[128,2048]{1,0:T(8,128)(2,1)} collective-permute-done((bf16[128,2048]{1,0:T(8,128)(2,1)}, bf16[128,2048]{1,0:T(8,128)(2,1)}, u32[]{:S(2)}, u32[]{:S(2)}) %collective-permute-start.43) | collective-permute-done | bytes 524320 | tf_op jit(solution)/shard_map/ppermute | solution.py:101
  223.5 10.3 %collective-permute-done.57 = bf16[1024,16]{0,1:T(8,128)(2,1)S(1)} collective-permute-done((bf16[1024,16]{0,1:T(8,128)(2,1)S(1)}, bf16[1024,16]{0,1:T(8,128)(2,1)S(1)}, u32[]{:S(2)}, u32[]{:S(2)}) %collective-permute-start.57) | collective-permute-done | bytes 32800 | tf_op jit(solution)/shard_map/ppermute | solution.py:216
  254.5 15.6 %experts.4 = (bf16[1280,1024]{1,0:T(8,128)(2,1)}, bf16[1280,1024]{1,0:T(8,128)(2,1)}, bf16[1280,1024]{1,0:T(8,128)(2,1)}, bf16[1280,1024]{1,0:T(8,128)(2,1)}, bf...) custom-call(s32[3]{0:T(128)S(1)} %pad_add_fusion.meta, ...), custom_call_target="tpu_custom_call" | custom-call | flops 17250000896 | tf_op jit(solution)/shard_map/experts/pallas_call | solution.py:772
  280.8 15.7 %experts.5 = (bf16[1280,1024]{1,0:T(8,128)(2,1)}, bf16[1280,1024]{1,0:T(8,128)(2,1)}, bf16[1280,1024]{1,0:T(8,128)(2,1)}, bf16[1280,1024]{1,0:T(8,128)(2,1)}, bf...) custom-call(s32[3]{0:T(128)S(1)} %pad_add_fusion.meta, ...), custom_call_target="tpu_custom_call", output_to_operand_aliasing={{0}: (16, {}), {1}: (17, {}), {2}: (18, {}), {3}: (19, {}),... | custom-call | flops 17250000896 | tf_op jit(solution)/shard_map/experts/pallas_call | solution.py:772
  296.4 13.2 %collective-permute-done.60 = bf16[128,4224]{1,0:T(8,128)(2,1)S(1)} collective-permute-done((bf16[128,4224]{1,0:T(8,128)(2,1)S(1)}, bf16[128,4224]{1,0:T(8,128)(2,1)S(1)}, u32[]{:S(2)}, u32[]{:S(2)}) %collective-permute-start.60) | collective-permute-done | bytes 1081376 | tf_op jit(solution)/shard_map/ppermute | solution.py:101
  318.4 14.7 %experts.6 = (bf16[1280,1024]{1,0:T(8,128)(2,1)}, bf16[1280,1024]{1,0:T(8,128)(2,1)}, bf16[1280,1024]{1,0:T(8,128)(2,1)}, bf16[1280,1024]{1,0:T(8,128)(2,1)}, bf...) custom-call(s32[3]{0:T(128)S(1)} %pad_add_fusion.meta, ...), custom_call_target="tpu_custom_call", output_to_operand_aliasing={{0}: (16, {}), {1}: (17, {}), {2}: (18, {}), {3}: (19, {}),... | custom-call | flops 17250000896 | tf_op jit(solution)/shard_map/experts/pallas_call | solution.py:772
  333.2 8.4 %collective-permute-done.66 = bf16[128,4224]{1,0:T(8,128)(2,1)S(1)} collective-permute-done((bf16[128,4224]{1,0:T(8,128)(2,1)}, bf16[128,4224]{1,0:T(8,128)(2,1)S(1)}, u32[]{:S(2)}, u32[]{:S(2)}) %collective-permute-start.66) | collective-permute-done | bytes 1081376 | tf_op jit(solution)/shard_map/ppermute | solution.py:101
  352.4 14.5 %experts.7 = (bf16[1280,1024]{1,0:T(8,128)(2,1)}, bf16[1280,1024]{1,0:T(8,128)(2,1)}, bf16[1280,1024]{1,0:T(8,128)(2,1)}, bf16[1280,1024]{1,0:T(8,128)(2,1)}, bf...) custom-call(s32[3]{0:T(128)S(1)} %pad_add_fusion.meta, ...), custom_call_target="tpu_custom_call", output_to_operand_aliasing={{0}: (16, {}), {1}: (17, {}), {2}: (18, {}), {3}: (19, {}),... | custom-call | flops 17250000896 | tf_op jit(solution)/shard_map/experts/pallas_call | solution.py:772
  366.9 9.9 %collective-permute-done.72 = bf16[128,4224]{1,0:T(8,128)(2,1)S(1)} collective-permute-done((bf16[128,4224]{1,0:T(8,128)(2,1)S(1)}, bf16[128,4224]{1,0:T(8,128)(2,1)S(1)}, u32[]{:S(2)}, u32[]{:S(2)}) %collective-permute-start.72) | collective-permute-done | bytes 1081376 | tf_op jit(solution)/shard_map/ppermute | solution.py:101
  392.2 18.3 %collective-permute-done.80 = bf16[128,4224]{1,0:T(8,128)(2,1)S(1)} collective-permute-done((bf16[128,4224]{1,0:T(8,128)(2,1)S(1)}, bf16[128,4224]{1,0:T(8,128)(2,1)S(1)}, u32[]{:S(2)}, u32[]{:S(2)}) %collective-permute-start.80) | collective-permute-done | bytes 1081376 | tf_op jit(solution)/shard_map/ppermute | solution.py:101
  469.2 16.6 %collective-permute-done.92 = bf16[1024,256]{1,0:T(8,128)(2,1)S(1)} collective-permute-done((bf16[1024,256]{1,0:T(8,128)(2,1)S(1)}, bf16[1024,256]{1,0:T(8,128)(2,1)S(1)}, u32[]{:S(2)}, u32[]{:S(2)}) %collective-permute-start.92) | collective-permute-done | bytes 524320 | tf_op jit(solution)/shard_map/ppermute | solution.py:216
  492.8 8.7 %collective-permute-done.95.g1 = bf16[128,2048]{1,0:T(8,128)(2,1)S(1)} collective-permute-done((bf16[128,2048]{1,0:T(8,128)(2,1)S(1)}, bf16[128,2048]{1,0:T(8,128)(2,1)S(1)}, u32[]{:S(2)}, u32[]{:S(2)}) %collective-permute-start.95) | collective-permute-done | bytes 524320 | tf_op jit(solution)/shard_map/ppermute | solution.py:101
  509.5 15.0 %attend_back.1 = (f32[2,2048,128]{2,1,0:T(8,128)S(1)}, f32[2,2048,128]{2,1,0:T(8,128)S(1)}, f32[2,2048,128]{2,1,0:T(8,128)S(1)}, bf16[2,2048,128]{2,1,0:T(8,128)(2,1)S(1)}) custom-call(s32[5]{0:T(128)S(1)} %pad_add_fusion.1.ends, bf16[2,2048,128]{2,1,0:T(8,128)(2,1)S(1)} %copy-done.59, bf16[2,2048,128]{2,1,0:T(8,128)(2,1)S(1)} %get-tuple-element.572.grad, ...), custom_call_target="tpu_custom_call" | custom-call | flops 19549999104 | tf_op jit(solution)/shard_map/attend_back/pallas_call | solution.py:555
  547.6 10.2 %collective-permute-done.107 = bf16[1024,256]{1,0:T(8,128)(2,1)S(1)} collective-permute-done((bf16[1024,256]{1,0:T(8,128)(2,1)S(1)}, bf16[1024,256]{1,0:T(8,128)(2,1)S(1)}, u32[]{:S(2)}, u32[]{:S(2)}) %collective-permute-start.107) | collective-permute-done | bytes 524320 | tf_op jit(solution)/shard_map/ppermute | solution.py:216
  647.5 18.7 %collective-permute-done.133 = bf16[19,2048]{1,0:T(8,128)(2,1)S(1)} collective-permute-done((bf16[19,2048]{1,0:T(8,128)(2,1)S(1)}, bf16[19,2048]{1,0:T(8,128)(2,1)S(1)}, u32[]{:S(2)}, u32[]{:S(2)}) %collective-permute-start.133) | collective-permute-done | bytes 77856 | tf_op jit(solution)/shard_map/ppermute | solution.py:201
  674.5 15.1 %collective-permute-done.136 = bf16[19,2048]{1,0:T(8,128)(2,1)S(1)} collective-permute-done((bf16[19,2048]{1,0:T(8,128)(2,1)S(1)}, bf16[19,2048]{1,0:T(8,128)(2,1)S(1)}, u32[]{:S(2)}, u32[]{:S(2)}) %collective-permute-start.136) | collective-permute-done | bytes 77856 | tf_op jit(solution)/shard_map/ppermute | solution.py:201
  699.5 9.0 %collective-permute-done.139.refs_1_.refs_5_ = bf16[1280,256]{1,0:T(8,128)(2,1)S(1)} collective-permute-done((bf16[1280,256]{1,0:T(8,128)(2,1)S(1)}, bf16[1280,256]{1,0:T(8,128)(2,1)S(1)}, u32[]{:S(2)}, u32[]{:S(2)}) %collective-permute-start.139) | collective-permute-done | bytes 655392 | tf_op jit(solution)/shard_map/ppermute | solution.py:101
  719.3 8.1 %collective-permute-done.145.refs_13_ = bf16[128,2048]{1,0:T(8,128)(2,1)S(1)} collective-permute-done((bf16[128,2048]{1,0:T(8,128)(2,1)S(1)}, bf16[128,2048]{1,0:T(8,128)(2,1)S(1)}, u32[]{:S(2)}, u32[]{:S(2)}) %collective-permute-start.145) | collective-permute-done | bytes 524320 | tf_op jit(solution)/shard_map/ppermute | solution.py:181
  734.6 9.5 %place_rows.1 = f32[2048,2048]{1,0:T(8,128)} custom-call(s32[16]{0:T(128)S(1)} %stack.87.table.meta, bf16[128,2048]{1,0:T(8,128)(2,1)S(1)} %add_convert_fusion.9.refs_0_, bf16[128,2048]{1,0:T(8,128)(2,1)S(1)} %collective-permute-done.104.refs_1_, bf16[128,2048]{1,0:T(8,128)(2,1)S(1)} %collective-permute-done.150.refs_2_, ...), custom_call_target="tpu_custom_call" | custom-call | flops 9200000000 | tf_op jit(solution)/shard_map/place_rows/pallas_call | solution.py:1031
  (705 shorter events, 452.5 us)
Async XLA Ops:
  5.2 31.8 %collective-permute-start.14 = (bf16[128,2048]{1,0:T(8,128)(2,1)}, bf16[128,2048]{1,0:T(8,128)(2,1)}, u32[]{:S(2)}, u32[]{:S(2)}) collective-permute-start(bf16[128,2048]{1,0:T(8,128)(2,1)} %bitcast.226), channel_id=1, source_target_pairs={{0,2},{2,0},{4,6},{6,4},{8,10},{10,8},{12,14},{14,12},{16,18},{18,... | collective-permute-start | bytes 1572872 | tf_op jit(solution)/shard_map/ppermute | solution.py:139
  7.8 28.4 %collective-permute-start.11 = (bf16[1,2176]{1,0:T(2,128)(2,1)S(1)}, bf16[1,2176]{1,0:T(2,128)(2,1)S(1)}, u32[]{:S(2)}, u32[]{:S(2)}) collective-permute-start(bf16[1,2176]{1,0:T(2,128)(2,1)S(1)} %broadcast_in_dim.66), channel_id=1, source_target_pairs={{0,1},{1,0},{2,3},{3,2},{4,5},{5,4},{6,7},{7,6},{8,9},{9,8},{10,11... | collective-permute-start | bytes 13064 | tf_op jit(solution)/shard_map/ppermute | solution.py:216
  9.3 26.0 %collective-permute-start.5 = (bf16[1024,512]{1,0:T(8,128)(2,1)S(1)}, bf16[1024,512]{1,0:T(8,128)(2,1)S(1)}, u32[]{:S(2)}, u32[]{:S(2)}) collective-permute-start(bf16[1024,512]{1,0:T(8,128)(2,1)S(1)} %pad_maximum_fusion.1.refs_0_), channel_id=1, source_target_pairs={{0,1},{1,0},{2,3},{3,2},{4,5},{5,4},{6,7},{7,6},{8,9},{9,8},{10,11... | collective-permute-start | bytes 3145736 | tf_op jit(solution)/shard_map/ppermute | solution.py:216
  56.4 73.5 %collective-permute-start = (bf16[352,768]{1,0:T(8,128)(2,1)}, bf16[352,768]{1,0:T(8,128)(2,1)}, u32[]{:S(2)}, u32[]{:S(2)}) collective-permute-start(bf16[352,768]{1,0:T(8,128)(2,1)} %get-tuple-element.717), channel_id=1, source_target_pairs={{0,1},{1,0},{2,3},{3,2},{4,5},{5,4},{6,7},{7,6},{8,9},{9,8},{10,11... | collective-permute-start | bytes 1622024 | tf_op jit(solution)/shard_map/ppermute | solution.py:216
  60.9 26.4 %collective-permute-start.18 = (bf16[128,2048]{1,0:T(8,128)(2,1)S(1)}, bf16[128,2048]{1,0:T(8,128)(2,1)S(1)}, u32[]{:S(2)}, u32[]{:S(2)}) collective-permute-start(bf16[128,2048]{1,0:T(8,128)(2,1)S(1)} %bitcast.229), channel_id=1, source_target_pairs={{0,8},{2,10},{4,12},{6,14},{8,16},{10,18},{12,20},{14,22},{16,24},... | collective-permute-start | bytes 1572872 | tf_op jit(solution)/shard_map/ppermute | solution.py:167
  62.8 35.9 %collective-permute-start.23 = (bf16[128,2048]{1,0:T(8,128)(2,1)S(1)}, bf16[128,2048]{1,0:T(8,128)(2,1)S(1)}, u32[]{:S(2)}, u32[]{:S(2)}) collective-permute-start(bf16[128,2048]{1,0:T(8,128)(2,1)S(1)} %bitcast.230), channel_id=1, source_target_pairs={{0,4},{2,6},{4,0},{6,2},{8,12},{10,14},{12,8},{14,10},{16,20},{18,... | collective-permute-start | bytes 1572872 | tf_op jit(solution)/shard_map/ppermute | solution.py:169
  90.3 37.2 %collective-permute-start.29 = (bf16[128,2048]{1,0:T(8,128)(2,1)S(1)}, bf16[128,2048]{1,0:T(8,128)(2,1)S(1)}, u32[]{:S(2)}, u32[]{:S(2)}) collective-permute-start(bf16[128,2048]{1,0:T(8,128)(2,1)S(1)} %collective-permute-done.18.g0), channel_id=1, source_target_pairs={{0,4},{2,6},{4,0},{6,2},{8,12},{10,14},{12,8},{14,10},{16,20},{18,... | collective-permute-start | bytes 1572872 | tf_op jit(solution)/shard_map/ppermute | solution.py:169
  105.2 24.8 %collective-permute-start.26 = (bf16[128,2048]{1,0:T(8,128)(2,1)S(1)}, bf16[128,2048]{1,0:T(8,128)(2,1)S(1)}, u32[]{:S(2)}, u32[]{:S(2)}) collective-permute-start(bf16[128,2048]{1,0:T(8,128)(2,1)S(1)} %collective-permute-done.22.g0), channel_id=1, source_target_pairs={{0,4},{2,6},{4,0},{6,2},{8,12},{10,14},{12,8},{14,10},{16,20},{18,... | collective-permute-start | bytes 1572872 | tf_op jit(solution)/shard_map/ppermute | solution.py:169
  279.2 30.5 %collective-permute-start.60 = (bf16[128,4224]{1,0:T(8,128)(2,1)S(1)}, bf16[128,4224]{1,0:T(8,128)(2,1)S(1)}, u32[]{:S(2)}, u32[]{:S(2)}) collective-permute-start(bf16[128,4224]{1,0:T(8,128)(2,1)S(1)} %fusion.10), channel_id=1, source_target_pairs={{0,4},{2,6},{4,0},{6,2},{8,12},{10,14},{12,8},{14,10},{16,20},{18,... | collective-permute-start | bytes 3244040 | tf_op jit(solution)/shard_map/ppermute | solution.py:101
  313.7 27.8 %collective-permute-start.66 = (bf16[128,4224]{1,0:T(8,128)(2,1)}, bf16[128,4224]{1,0:T(8,128)(2,1)S(1)}, u32[]{:S(2)}, u32[]{:S(2)}) collective-permute-start(bf16[128,4224]{1,0:T(8,128)(2,1)} %fusion.3), channel_id=1, source_target_pairs={{0,8},{2,10},{4,12},{6,14},{8,16},{10,18},{12,20},{14,22},{16,24},... | collective-permute-start | bytes 3244040 | tf_op jit(solution)/shard_map/ppermute | solution.py:101
  316.8 26.2 %collective-permute-start.67 = (bf16[128,4224]{1,0:T(8,128)(2,1)S(1)}, bf16[128,4224]{1,0:T(8,128)(2,1)S(1)}, u32[]{:S(2)}, u32[]{:S(2)}) collective-permute-start(bf16[128,4224]{1,0:T(8,128)(2,1)S(1)} %fusion.11), channel_id=1, source_target_pairs={{0,4},{2,6},{4,0},{6,2},{8,12},{10,14},{12,8},{14,10},{16,20},{18,... | collective-permute-start | bytes 3244040 | tf_op jit(solution)/shard_map/ppermute | solution.py:101
  348.7 28.1 %collective-permute-start.72 = (bf16[128,4224]{1,0:T(8,128)(2,1)S(1)}, bf16[128,4224]{1,0:T(8,128)(2,1)S(1)}, u32[]{:S(2)}, u32[]{:S(2)}) collective-permute-start(bf16[128,4224]{1,0:T(8,128)(2,1)S(1)} %fusion.5), channel_id=1, source_target_pairs={{0,8},{2,10},{4,12},{6,14},{8,16},{10,18},{12,20},{14,22},{16,24},... | collective-permute-start | bytes 3244040 | tf_op jit(solution)/shard_map/ppermute | solution.py:101
  350.7 26.3 %collective-permute-start.74 = (bf16[128,4224]{1,0:T(8,128)(2,1)S(1)}, bf16[128,4224]{1,0:T(8,128)(2,1)S(1)}, u32[]{:S(2)}, u32[]{:S(2)}) collective-permute-start(bf16[128,4224]{1,0:T(8,128)(2,1)S(1)} %fusion.12), channel_id=1, source_target_pairs={{0,4},{2,6},{4,0},{6,2},{8,12},{10,14},{12,8},{14,10},{16,20},{18,... | collective-permute-start | bytes 3244040 | tf_op jit(solution)/shard_map/ppermute | solution.py:101
  382.3 28.2 %collective-permute-start.80 = (bf16[128,4224]{1,0:T(8,128)(2,1)S(1)}, bf16[128,4224]{1,0:T(8,128)(2,1)S(1)}, u32[]{:S(2)}, u32[]{:S(2)}) collective-permute-start(bf16[128,4224]{1,0:T(8,128)(2,1)S(1)} %fusion.1), channel_id=1, source_target_pairs={{0,8},{2,10},{4,12},{6,14},{8,16},{10,18},{12,20},{14,22},{16,24},... | collective-permute-start | bytes 3244040 | tf_op jit(solution)/shard_map/ppermute | solution.py:101
  384.8 26.0 %collective-permute-start.81 = (bf16[128,4224]{1,0:T(8,128)(2,1)S(1)}, bf16[128,4224]{1,0:T(8,128)(2,1)S(1)}, u32[]{:S(2)}, u32[]{:S(2)}) collective-permute-start(bf16[128,4224]{1,0:T(8,128)(2,1)S(1)} %fusion.13), channel_id=1, source_target_pairs={{0,4},{2,6},{4,0},{6,2},{8,12},{10,14},{12,8},{14,10},{16,20},{18,... | collective-permute-start | bytes 3244040 | tf_op jit(solution)/shard_map/ppermute | solution.py:101
  387.3 32.9 %collective-permute-start.84 = (bf16[1024,256]{1,0:T(8,128)(2,1)S(1)}, bf16[1024,256]{1,0:T(8,128)(2,1)S(1)}, u32[]{:S(2)}, u32[]{:S(2)}) collective-permute-start(bf16[1024,256]{1,0:T(8,128)(2,1)S(1)} %convolution_convert_fusion.8), channel_id=1, source_target_pairs={{0,1},{1,0},{2,3},{3,2},{4,5},{5,4},{6,7},{7,6},{8,9},{9,8},{10,11... | collective-permute-start | bytes 1572872 | tf_op jit(solution)/shard_map/ppermute | solution.py:216
  448.9 43.9 %collective-permute-start.96 = (bf16[1024,256]{1,0:T(8,128)(2,1)S(1)}, bf16[1024,256]{1,0:T(8,128)(2,1)S(1)}, u32[]{:S(2)}, u32[]{:S(2)}) collective-permute-start(bf16[1024,256]{1,0:T(8,128)(2,1)S(1)} %convolution_convert_fusion.5), channel_id=1, source_target_pairs={{0,1},{1,0},{2,3},{3,2},{4,5},{5,4},{6,7},{7,6},{8,9},{9,8},{10,11... | collective-permute-start | bytes 1572872 | tf_op jit(solution)/shard_map/ppermute | solution.py:216
  450.5 123.7 %collective-permute-start.110 = (bf16[1024,256]{1,0:T(8,128)(2,1)S(1)}, bf16[1024,256]{1,0:T(8,128)(2,1)S(1)}, u32[]{:S(2)}, u32[]{:S(2)}) collective-permute-start(bf16[1024,256]{1,0:T(8,128)(2,1)S(1)} %convolution_convert_fusion.2), channel_id=1, source_target_pairs={{0,1},{1,0},{2,3},{3,2},{4,5},{5,4},{6,7},{7,6},{8,9},{9,8},{10,11... | collective-permute-start | bytes 1572872 | tf_op jit(solution)/shard_map/ppermute | solution.py:216
  455.0 30.8 %collective-permute-start.92 = (bf16[1024,256]{1,0:T(8,128)(2,1)S(1)}, bf16[1024,256]{1,0:T(8,128)(2,1)S(1)}, u32[]{:S(2)}, u32[]{:S(2)}) collective-permute-start(bf16[1024,256]{1,0:T(8,128)(2,1)S(1)} %convolution_convert_fusion.6), channel_id=1, source_target_pairs={{0,1},{1,0},{2,3},{3,2},{4,5},{5,4},{6,7},{7,6},{8,9},{9,8},{10,11... | collective-permute-start | bytes 1572872 | tf_op jit(solution)/shard_map/ppermute | solution.py:216
  560.4 31.3 %collective-permute-start.117 = (bf16[128,2048]{1,0:T(8,128)(2,1)S(1)}, bf16[128,2048]{1,0:T(8,128)(2,1)S(1)}, u32[]{:S(2)}, u32[]{:S(2)}) collective-permute-start(bf16[128,2048]{1,0:T(8,128)(2,1)S(1)} %collective-permute-done.105.refs_4_), channel_id=1, source_target_pairs={{0,8},{2,10},{4,12},{6,14},{8,16},{10,18},{12,20},{14,22},{16,24},... | collective-permute-start | bytes 1572872 | tf_op jit(solution)/shard_map/ppermute | solution.py:181
  633.9 96.2 %collective-permute-start.150 = (bf16[128,2048]{1,0:T(8,128)(2,1)S(1)}, bf16[128,2048]{1,0:T(8,128)(2,1)S(1)}, u32[]{:S(2)}, u32[]{:S(2)}) collective-permute-start(bf16[128,2048]{1,0:T(8,128)(2,1)S(1)} %add_convert_fusion.9.refs_0_), channel_id=1, source_target_pairs={{0,2},{2,0},{4,6},{6,4},{8,10},{10,8},{12,14},{14,12},{16,18},{18,... | collective-permute-start | bytes 1572872 | tf_op jit(solution)/shard_map/ppermute | solution.py:180
  666.8 25.7 %collective-permute-start.142 = (bf16[1280,256]{1,0:T(8,128)(2,1)S(1)}, bf16[1280,256]{1,0:T(8,128)(2,1)S(1)}, u32[]{:S(2)}, u32[]{:S(2)}) collective-permute-start(bf16[1280,256]{1,0:T(8,128)(2,1)S(1)} %collective-permute-done.132.refs_0_.refs_4_), channel_id=1, source_target_pairs={{0,2},{2,0},{4,6},{6,4},{8,10},{10,8},{12,14},{14,12},{16,18},{18,... | collective-permute-start | bytes 1966088 | tf_op jit(solution)/shard_map/ppermute | solution.py:139
  692.5 38.0 %collective-permute-start.151 = (bf16[128,2048]{1,0:T(8,128)(2,1)S(1)}, bf16[128,2048]{1,0:T(8,128)(2,1)S(1)}, u32[]{:S(2)}, u32[]{:S(2)}) collective-permute-start(bf16[128,2048]{1,0:T(8,128)(2,1)S(1)} %collective-permute-done.104.refs_1_), channel_id=1, source_target_pairs={{0,2},{2,0},{4,6},{6,4},{8,10},{10,8},{12,14},{14,12},{16,18},{18,... | collective-permute-start | bytes 1572872 | tf_op jit(solution)/shard_map/ppermute | solution.py:180
  699.5 31.1 %collective-permute-start.152 = (bf16[128,2048]{1,0:T(8,128)(2,1)S(1)}, bf16[128,2048]{1,0:T(8,128)(2,1)S(1)}, u32[]{:S(2)}, u32[]{:S(2)}) collective-permute-start(bf16[128,2048]{1,0:T(8,128)(2,1)S(1)} %collective-permute-done.105.refs_4_), channel_id=1, source_target_pairs={{0,2},{2,0},{4,6},{6,4},{8,10},{10,8},{12,14},{14,12},{16,18},{18,... | collective-permute-start | bytes 1572872 | tf_op jit(solution)/shard_map/ppermute | solution.py:180
  (252 other events, 2904.0 us)

commit v4 on v3

--- a/solution.py
+++ b/solution.py
@@ -93,7 +93,9 @@
     return landed, arrays
 
 
-def pipeline(n_ctx, order, compute, token, sides, piece=None, scatter=False, closing=None):
+def pipeline(
+    n_ctx, order, compute, token, sides, piece=None, scatter=False, closing=None, along=False
+):
     nz = n_ctx // 4
     air, have, state = {}, {}, ()
 
@@ -101,7 +103,10 @@
         air[key] = lax.ppermute(array, "ctx", pairs)
 
     def bring(k):
-        send(("beside", k), have["piece", k], flip(n_ctx, 2))
+        if along and k + 1 == nz:
+            send(("beside", k), have["beside", k - 1], ring(n_ctx, 4))
+        else:
+            send(("beside", k), have["piece", k], flip(n_ctx, 2))
         if k + 1 < nz:
             send(("piece", k + 1), have["piece", k], ring(n_ctx, 4))
 
@@ -157,37 +162,40 @@
     return total_of(own), state, extra
 
 
-def gather_quarters(piece, n_ctx):
-    nz = n_ctx // 4
-    along, beside, others = [piece], [], []
+def gather_planned(piece, n_ctx, plan):
+    arrays = {("along", 0): piece}
+    plan = list(plan)
+    source = lambda kind, k: ("along", k) if kind == "across" else (kind, k - 1)
+    for i, (items, steps) in enumerate(plan):
+        going = [
+            lax.ppermute(
+                arrays[source(*item)], "ctx", flip(n_ctx, 2) if item[0] == "across" else ring(n_ctx, 4)
+            )
+            for item in items
+        ]
+        later = {source(*item) for item in plan[i + 1][0]} if i + 1 < len(plan) else set()
+        tied = sorted(key for key in later if key in arrays)
+        came = list((yield (*going, *(arrays[key] for key in tied)), steps))
+        for kind, k in items:
+            arrays["along" if kind == "along" else "beside", k] = came.pop(0)
+        arrays.update(zip(tied, came))
     core = lambda array: lax.ppermute(array, "ctx", flip(n_ctx, 1))
-    for step in range(nz + 1):
-        going = []
-        if step + 1 < nz:
-            going.append(lax.ppermute(along[step], "ctx", ring(n_ctx, 4)))
-        if step > 0:
-            going.append(lax.ppermute(along[step - 1], "ctx", flip(n_ctx, 2)))
-        came = list((yield tuple(going), 1))
-        if step + 1 < nz:
-            along.append(came.pop(0))
-        if step > 0:
-            beside.append(came.pop(0))
-    return [(a, b, core(a), core(b)) for a, b in zip(along, beside)]
-
-
-def gather_blocks(piece, n_ctx, last):
-    nz = n_ctx // 4
-    core = lambda array: lax.ppermute(array, "ctx", flip(n_ctx, 1))
-    hop = lambda array: lax.ppermute(array, "ctx", ring(n_ctx, 4))
-    along = [piece]
-    came, following = yield (lax.ppermute(piece, "ctx", flip(n_ctx, 2)), hop(piece)), 1
-    beside = [came]
-    along.append(following)
-    for k in range(1, nz):
-        if k > 1:
-            along += yield (hop(along[k - 1]),), 1
-        beside += yield (hop(beside[k - 1]),), last if k == nz - 1 else 1
-    return [(a, b, core(a), core(b)) for a, b in zip(along, beside)]
+    pairs = [(arrays["along", k], arrays["beside", k]) for k in range(n_ctx // 4)]
+    return [(a, b, core(a), core(b)) for a, b in pairs]
+
+
+COTANGENT_PLAN = [
+    ([("along", 1)], 1),
+    ([("along", 2), ("across", 0), ("across", 1)], 1),
+    ([("along", 3), ("across", 2)], 1),
+    ([("beside", 3)], 2),
+]
+OUTPUT_GRAD_PLAN = [
+    ([("along", 1), ("across", 0)], 1),
+    ([("along", 2)], 1),
+    ([("along", 3), ("across", 1)], 1),
+    ([("beside", 2), ("across", 3)], 1),
+]
 
 
 def scatter_order(n_ctx):
@@ -223,17 +231,18 @@
     return [part, other]
 
 
-def fetch_thirds(part):
+def fetch_thirds(part, after, first=1):
     if lax.axis_size("fsdp") != 2:
-        return [lax.all_gather(part, "fsdp", axis=0, tiled=True)]
+        return [lax.all_gather(part, "fsdp", axis=0, tiled=True)], after
     step = (part.shape[0] // 3 + 31) // 32 * 32
     other = []
     for at in range(0, part.shape[0], step):
-        rows = part[at : at + step]
+        after, rows = tie(after, part[at : at + step])
         if other:
-            other[-1], rows = tie(other[-1], rows)
-        other += yield (swap(rows),), 1
-    return [part, jnp.concatenate(other, axis=0)]
+            other[-1] = after
+        (after,) = yield (swap(rows),), 1 if other else first
+        other.append(after)
+    return [part, jnp.concatenate(other, axis=0)], after
 
 
 def joined(parts):
@@ -251,24 +260,32 @@
     return [f * (width // 2), (1 - f) * (width // 2)]
 
 
-def scatter_blocks(lefts, right, block):
+def scatter_products(pairs, block, steps=()):
     if lax.axis_size("fsdp") != 2:
-        full = dot(lefts[0], right, COLS_T).astype(BF16)
-        return lax.psum_scatter(full, "fsdp", scatter_dimension=0, tiled=True).astype(F32)
-    mine, other = lefts
-    columns = [right[:, at : at + block] for at in range(0, right.shape[1], block)]
-    product = lambda left, i: dot(left, columns[i], COLS_T)
-    done, count = [], len(columns)
-    sent = product(other, 0).astype(BF16)
-    for i in range(count):
-        ahead = [product(other, i + 1).astype(BF16)] if i + 1 < count else []
-        fresh = [product(mine, i - 1) + came.astype(F32)] if i > 0 else []
-        came, *worked = yield (swap(sent), *ahead, *fresh), 1
+        full = [dot(left[0], right, COLS_T).astype(BF16) for left, right in pairs]
+        return [
+            lax.psum_scatter(g, "fsdp", scatter_dimension=0, tiled=True).astype(F32) for g in full
+        ]
+    work = []
+    for left, right in pairs:
+        step = min(block, right.shape[1])
+        work += [(left, right[:, at : at + step]) for at in range(0, right.shape[1], step)]
+    product = lambda i, part: dot(work[i][0][part], work[i][1], COLS_T)
+    done, sent = [], product(0, 1).astype(BF16)
+    for i in range(len(work)):
+        ahead = [product(i + 1, 1).astype(BF16)] if i + 1 < len(work) else []
+        fresh = [product(i - 1, 0) + came.astype(F32)] if i > 0 else []
+        came, *worked = yield (swap(sent), *ahead, *fresh), steps[i] if steps else 1
         if ahead:
             sent = worked.pop(0)
         done += worked
-    done.append(product(mine, count - 1) + came.astype(F32))
-    return done[0] if count == 1 else jnp.concatenate(done, axis=1)
+    done.append(product(len(work) - 1, 0) + came.astype(F32))
+    sums = []
+    for _, right in pairs:
+        count = max(1, right.shape[1] // block)
+        sums.append(done[0] if count == 1 else jnp.concatenate(done[:count], axis=1))
+        done = done[count:]
+    return sums
 
 
 def scatter_rows(full):
@@ -986,7 +1003,7 @@
 
     def head_at(i, t):
         c = t[4 * k + i // parts]
-        rows_part = lax.rem(c // 2, 2) * 2 + lax.rem(c // 4, 2)
+        rows_part = lax.rem(c // 4, 2) * 2 + lax.rem(c // 2, 2)
         return rows_part, lax.rem(c, 2) * 2 + c // 8
 
     out_specs = [
@@ -1018,7 +1035,7 @@
 
 def place_rows_kernel(table, *refs):
     out = refs[-1]
-    for n in range(len(refs) - 1):
+    for n in range(4):
 
         @pl.when(pl.program_id(0) == n)
         def _():
@@ -1026,21 +1043,24 @@
 
 
 def place_rows(quarters, table):
-    blocks = [block for quarter in quarters for block in quarter]
-    rows, cols = blocks[0].shape
-    return pl.pallas_call(
-        place_rows_kernel,
-        grid_spec=pltpu.PrefetchScalarGridSpec(
-            num_scalar_prefetch=1,
-            grid=(len(blocks),),
-            in_specs=[whole((rows, cols))] * len(blocks),
-            out_specs=pl.BlockSpec((rows, cols), lambda i, t: (t[i], 0)),
-        ),
-        out_shape=jax.ShapeDtypeStruct((len(blocks) * rows, cols), F32),
-        compiler_params=params(16),
-        cost_estimate=cost(8),
-        name="place_rows",
-    )(table, *blocks)
+    rows, cols = quarters[0][0].shape
+    placed = ()
+    for k, quarter in enumerate(quarters):
+        placed = pl.pallas_call(
+            place_rows_kernel,
+            grid_spec=pltpu.PrefetchScalarGridSpec(
+                num_scalar_prefetch=1,
+                grid=(4,),
+                in_specs=[whole((rows, cols))] * 4 + [IN_HBM] * len(placed),
+                out_specs=[pl.BlockSpec((rows, cols), lambda i, t, k=k: (t[4 * k + i], 0))],
+            ),
+            out_shape=[pltpu.HBM((4 * len(quarters) * rows, cols), F32)],
+            input_output_aliases={5: 0} if placed else {},
+            compiler_params=params(10),
+            cost_estimate=cost(2.4),
+            name="place_rows",
+        )(table, *quarter, *placed)
+    return placed[0]
 
 
 def local(
@@ -1127,17 +1147,19 @@
             ]
         weights["back"] = joined(parts)
         own_rows = lax.dynamic_slice_in_dim(w_output, (c % hpf) * HD, HD, 0)
-        w_out = joined((yield from fetch(own_rows)))
+        rows_parts = yield from fetch(own_rows)
+        last = rows_parts[-1]
+        w_out = joined(rows_parts)
         weights["out"] = lax.dynamic_slice_in_dim(w_out, (c // hpf) * hpd * HD, hpd * HD, 0)
-        weights["gate"] = yield from fetch_thirds(w_gate[0])
-        weights["up"] = yield from fetch_thirds(w_up[0])
-        weights["down"] = yield from fetch_thirds(w_down[0])
+        weights["gate"], last = yield from fetch_thirds(w_gate[0], last)
+        weights["up"], last = yield from fetch_thirds(w_up[0], last, 2)
+        weights["down"], last = yield from fetch_thirds(w_down[0], last)
 
     gathered = {}
 
     def gather_cotangents():
         (cot,) = yield (cotangent[0],), 3
-        gathered["cot"] = yield from gather_quarters(cot, n_ctx)
+        gathered["cot"] = yield from gather_planned(cot, n_ctx, COTANGENT_PLAN)
 
     sides = [Side(fetch_weights()), Side(gather_cotangents())]
 
@@ -1228,6 +1250,7 @@
         sides,
         piece=jnp.concatenate([routed_in, place], axis=1),
         scatter=True,
+        along=True,
     )
     rows, pairs = seen[:n_parts], seen[n_parts : 2 * n_parts]
     hidden, gate_part_grad, up_part_grad = seen[2 * n_parts :]
@@ -1267,11 +1290,14 @@
     grads, sums = {}, []
 
     def scatter_grads():
-        grads["gate"] = yield from scatter_blocks(rows, gate_part_grad, block)
-        grads["up"] = yield from scatter_blocks(rows, up_part_grad, block)
-        grads["down"] = yield from scatter_blocks(pairs, hidden, block)
-
-    sides = [Side(scatter_grads())]
+        pairs_of = [(rows, gate_part_grad), (rows, up_part_grad), (pairs, hidden)]
+        sums_of = yield from scatter_products(pairs_of, block, (1, 1, 1, 1, 1, 2, 2, 1, 1))
+        grads["gate"], grads["up"], grads["down"] = sums_of
+
+    sides = [
+        Side(scatter_grads()),
+        Side(sum_all(jnp.concatenate([router_part, moe_part], axis=0), sums)),
+    ]
     grad_out_w, mixed_grad, delta = pipeline(
         n_ctx,
         straight,
@@ -1295,7 +1321,9 @@
         own = yield from scatter_rows(placed)
         own = own.astype(BF16)
         if n_ctx == hpf:
-            grads["out"] = place_rows((yield from gather_blocks(own, n_ctx, 4)), table)
+            grads["out"] = place_rows(
+                (yield from gather_planned(own, n_ctx, OUTPUT_GRAD_PLAN)), table
+            )
         else:
             whole_grad = lax.all_gather(own, "ctx", axis=0).reshape(-1, hpf * HD, width)
             mine = lax.dynamic_index_in_dim(whole_grad, f // hpd, 0, keepdims=False)
@@ -1312,8 +1340,8 @@
     normed_flat = [n.reshape(length, -1) for n in normed]
 
     def sum_key_grads():
-        grad_kv = yield from scatter_blocks(
-            normed_flat, kv_grad.reshape(length, -1), kv_grad.shape[-1]
+        (grad_kv,) = yield from scatter_products(
+            [(normed_flat, kv_grad.reshape(length, -1))], kv_grad.shape[-1]
         )
         if not shared:
             slots_kv = jnp.arange(KVH, dtype=jnp.int32)
@@ -1323,7 +1351,7 @@
             grad_kv = lax.psum(grad_kv.astype(BF16), "ctx").astype(F32)
             grads["key"], grads["value"] = grad_kv[:, : KVH * HD], grad_kv[:, KVH * HD :]
             return
-        for bit in (2, 4):
+        for bit in (4, 2):
             rows_kept = grad_kv.shape[0] // 2
             side = (c // bit) % 2
             kept = lax.dynamic_slice_in_dim(grad_kv, side * rows_kept, rows_kept, 0)
@@ -1354,7 +1382,7 @@
         if len(gain_parts) == nz:
             gain_rows = jnp.concatenate([sum(gain_parts)[:1], key_gains[:1]], axis=1)
             gain_rows = jnp.pad(gain_rows, ((0, 0), (0, width - 2 * HD)))
-            rows_last = [router_part, moe_part, sum(attn_parts)[:1], gain_rows]
+            rows_last = [sum(attn_parts)[:1], gain_rows]
             sides.append(Side(sum_all(jnp.concatenate(rows_last, axis=0), sums)))
         return back, (q_grad,)
 
@@ -1383,7 +1411,7 @@
     normed_grad, _, grad_q = pipeline(
         n_ctx, later, through_inputs_last, meta_rows, sides, scatter=True, closing=query_weights
     )
-    for side in sides[2:3]:
+    for side in sides[3:4]:
         side.finish()
     grad_q = sum(g.astype(F32) for g in grad_q).astype(BF16)
     q_rows = grad_q.shape[0]
@@ -1414,13 +1442,13 @@
         )
     for side in sides:
         side.finish()
-    sums = sums[0]
+    early, late = sums
     own_part = lambda v, size: lax.dynamic_slice_in_dim(v, f * (size // n_f), size // n_f, 0)
-    grad_w_router = own_part(sums[:n_exp].T, width)
-    grad_norm_moe = own_part(sums[n_exp], width)
-    grad_norm_attn = own_part(sums[n_exp + 1], width)
-    grad_gain_query = own_part(sums[n_exp + 2, :HD], HD)
-    grad_gain_key = own_part(sums[n_exp + 2, HD : 2 * HD], HD)
+    grad_w_router = own_part(early[:n_exp].T, width)
+    grad_norm_moe = own_part(early[n_exp], width)
+    grad_norm_attn = own_part(late[0], width)
+    grad_gain_query = own_part(late[1, :HD], HD)
+    grad_gain_key = own_part(late[1, HD : 2 * HD], HD)
 
     attn_scale = lax.rsqrt(jnp.mean(x * x, axis=-1, keepdims=True) + EPS)
     attn_scaled = normed_grad * attn_gain

time: 759 us -> 736 us (0.970)
  waiting for transfers between devices: 324 us -> 282 us
  starting transfers between devices: 109 us -> 120 us
    ppermute x49, waiting for transfers between devices: 172 us -> 131 us  [send(): air[key] = lax.ppermute(array, 'ctx', pairs)]
    ppermute x26 -> x27, waiting for transfers between devices: 71.2 us -> 48.4 us  [swap(): return lax.ppermute(part, 'fsdp', SWAP)]
    ppermute x30, waiting for transfers between devices: 27.1 us -> 38 us  [the longest x14 37.9 us: gather_planned(): lax.ppermute(arrays[source(*item)], 'ctx', flip(n_ctx, 2) if item[0] == '...]
    ppermute x2, waiting for transfers between devices: 7.45 us -> 17.4 us  [sum_key_grads(): lax.ppermute(gone.astype(BF16), 'ctx', flip(n_ctx, bit))]
    ppermute x4 -> x8, waiting for transfers between devices: 33.8 us -> 42 us  [sum_all(): lax.ppermute(values.astype(BF16), 'ctx', flip(n_ctx, bit))]
    unnamed x246 -> x268, local copies, waits for them, and re-layouts: 18.8 us -> 20.4 us
    ppermute x26 -> x27, starting transfers between devices: 31.1 us -> 31.9 us  [swap(): return lax.ppermute(part, 'fsdp', SWAP)]
  transfers between devices with their start and end apart: 158 -> 163, of which waited for: 58 -> 57; matrix products, arithmetic and copies ran while one was open for 13% -> 14% of each run, Pallas kernels for 26% -> 27%
where the time goes in v4:
time: 736 us; the launch traced here: 726 us
  waiting for transfers between devices  282 us (38%)
  Pallas kernels  204 us (28%)
  starting transfers between devices  120 us (16%)
  other arithmetic  50.2 us (7%)
  local copies, waits for them, and re-layouts  39.3 us (5%)
  matrix products  27.4 us (4%)
    ppermute x49, waiting for transfers between devices, send(): air[key] = lax.ppermute(array, 'ctx', pairs)  131 us
    pallas_call x4, Pallas kernels, experts(): pl.pallas_call(functools.partial(experts_kernel, k, n_parts, width, capac...  61.6 us
    ppermute x49, starting transfers between devices, send(): air[key] = lax.ppermute(array, 'ctx', pairs)  51.7 us
    ppermute x27, waiting for transfers between devices, swap(): return lax.ppermute(part, 'fsdp', SWAP)  48.4 us
    ppermute x8, waiting for transfers between devices, sum_all(): lax.ppermute(values.astype(BF16), 'ctx', flip(n_ctx, bit))  42 us
    ppermute x14, waiting for transfers between devices, gather_planned(): lax.ppermute(arrays[source(*item)], 'ctx', flip(n_ctx, 2) if item[0] == '...  37.9 us
    ppermute x27, starting transfers between devices, swap(): return lax.ppermute(part, 'fsdp', SWAP)  31.9 us
    pallas_call x4, Pallas kernels, project(): pl.pallas_call(functools.partial(project_kernel, k, hpd, n_kv, n_parts, n...  28.4 us
  transfers between devices with their start and end apart: 163, of which 57 were waited for; matrix products, arithmetic and copies ran while one was open for 14% of the time, Pallas kernels for 27%

profile of v4, /device:TPU:0, one launch (start us, length us, event | category | flops | bytes accessed | tf_op | source)
XLA Modules:
  0.0 726.4 jit_solution(15362925606811953353)
XLA Ops:
  94.6 9.6 %collective-permute-done.22.g1 = bf16[128,2048]{1,0:T(8,128)(2,1)} collective-permute-done((bf16[128,2048]{1,0:T(8,128)(2,1)S(1)}, bf16[128,2048]{1,0:T(8,128)(2,1)}, u32[]{:S(2)}, u32[]{:S(2)}) %collective-permute-start.22) | collective-permute-done | bytes 524320 | tf_op jit(solution)/shard_map/ppermute | solution.py:171
  110.7 14.0 %attend.1 = (f32[2,2048,128]{2,1,0:T(8,128)S(1)}, f32[2,8,2048]{2,1,0:T(8,128)S(1)}) custom-call(s32[4]{0:T(128)S(1)} %bitcast.245, bf16[2,2048,128]{2,1,0:T(8,128)(2,1)S(1)} %copy-done.62, bf16[2,2048,128]{2,1,0:T(8,128)(2,1)S(1)} %copy-done.64, bf16[2,2048,128]{2,1,0:T(8,128)(2,1)S(1)} %copy-done.66), custom_call_target="tpu_custom_call" | custom-call | flops 14375000064 | tf_op jit(solution)/shard_map/attend/pallas_call | solution.py:503
  135.0 10.7 %collective-permute-done.32.g1 = bf16[128,2048]{1,0:T(8,128)(2,1)S(1)} collective-permute-done((bf16[128,2048]{1,0:T(8,128)(2,1)S(1)}, bf16[128,2048]{1,0:T(8,128)(2,1)S(1)}, u32[]{:S(2)}, u32[]{:S(2)}) %collective-permute-start.32) | collective-permute-done | bytes 524320 | tf_op jit(solution)/shard_map/ppermute | solution.py:171
  152.6 10.5 %collective-permute-done.34 = bf16[128,2048]{1,0:T(8,128)(2,1)S(1)} collective-permute-done((bf16[128,2048]{1,0:T(8,128)(2,1)S(1)}, bf16[128,2048]{1,0:T(8,128)(2,1)S(1)}, u32[]{:S(2)}, u32[]{:S(2)}) %collective-permute-start.34) | collective-permute-done | bytes 524320 | tf_op jit(solution)/shard_map/ppermute | solution.py:103
  172.7 7.9 %collective-permute-done.40 = bf16[320,768]{1,0:T(8,128)(2,1)S(1)} collective-permute-done((bf16[320,768]{1,0:T(8,128)(2,1)S(1)}, bf16[320,768]{1,0:T(8,128)(2,1)S(1)}, u32[]{:S(2)}, u32[]{:S(2)}) %collective-permute-start.40) | collective-permute-done | bytes 491552 | tf_op jit(solution)/shard_map/ppermute | solution.py:224
  215.6 9.0 %collective-permute-done.47 = bf16[352,768]{1,0:T(8,128)(2,1)} collective-permute-done((bf16[352,768]{1,0:T(8,128)(2,1)S(1)}, bf16[352,768]{1,0:T(8,128)(2,1)}, u32[]{:S(2)}, u32[]{:S(2)}) %collective-permute-start.47) | collective-permute-done | bytes 540704 | tf_op jit(solution)/shard_map/ppermute | solution.py:224
  232.1 11.0 %collective-permute-done.50 = bf16[320,768]{1,0:T(8,128)(2,1)S(1)} collective-permute-done((bf16[320,768]{1,0:T(8,128)(2,1)}, bf16[320,768]{1,0:T(8,128)(2,1)S(1)}, u32[]{:S(2)}, u32[]{:S(2)}) %collective-permute-start.50) | collective-permute-done | bytes 491552 | tf_op jit(solution)/shard_map/ppermute | solution.py:224
  249.8 15.6 %experts.4 = (bf16[1280,1024]{1,0:T(8,128)(2,1)}, bf16[1280,1024]{1,0:T(8,128)(2,1)}, bf16[1280,1024]{1,0:T(8,128)(2,1)}, bf16[1280,1024]{1,0:T(8,128)(2,1)}, bf...) custom-call(s32[3]{0:T(128)S(1)} %pad_add_fusion.meta, ...), custom_call_target="tpu_custom_call" | custom-call | flops 17250000896 | tf_op jit(solution)/shard_map/experts/pallas_call | solution.py:789
  274.6 15.3 %experts.5 = (bf16[1280,1024]{1,0:T(8,128)(2,1)}, bf16[1280,1024]{1,0:T(8,128)(2,1)}, bf16[1280,1024]{1,0:T(8,128)(2,1)}, bf16[1280,1024]{1,0:T(8,128)(2,1)}, bf...) custom-call(s32[3]{0:T(128)S(1)} %pad_add_fusion.meta, ...), custom_call_target="tpu_custom_call", output_to_operand_aliasing={{0}: (16, {}), {1}: (17, {}), {2}: (18, {}), {3}: (19, {}),... | custom-call | flops 17250000896 | tf_op jit(solution)/shard_map/experts/pallas_call | solution.py:789
  290.7 9.1 %collective-permute-done.60 = bf16[128,4224]{1,0:T(8,128)(2,1)S(1)} collective-permute-done((bf16[128,4224]{1,0:T(8,128)(2,1)S(1)}, bf16[128,4224]{1,0:T(8,128)(2,1)S(1)}, u32[]{:S(2)}, u32[]{:S(2)}) %collective-permute-start.60) | collective-permute-done | bytes 1081376 | tf_op jit(solution)/shard_map/ppermute | solution.py:103
  312.2 14.2 %experts.6 = (bf16[1280,1024]{1,0:T(8,128)(2,1)}, bf16[1280,1024]{1,0:T(8,128)(2,1)}, bf16[1280,1024]{1,0:T(8,128)(2,1)}, bf16[1280,1024]{1,0:T(8,128)(2,1)}, bf...) custom-call(s32[3]{0:T(128)S(1)} %pad_add_fusion.meta, ...), custom_call_target="tpu_custom_call", output_to_operand_aliasing={{0}: (16, {}), {1}: (17, {}), {2}: (18, {}), {3}: (19, {}),... | custom-call | flops 17250000896 | tf_op jit(solution)/shard_map/experts/pallas_call | solution.py:789
  346.2 16.5 %experts.7 = (bf16[1280,1024]{1,0:T(8,128)(2,1)}, bf16[1280,1024]{1,0:T(8,128)(2,1)}, bf16[1280,1024]{1,0:T(8,128)(2,1)}, bf16[1280,1024]{1,0:T(8,128)(2,1)}, bf...) custom-call(s32[3]{0:T(128)S(1)} %pad_add_fusion.meta, ...), custom_call_target="tpu_custom_call", output_to_operand_aliasing={{0}: (16, {}), {1}: (17, {}), {2}: (18, {}), {3}: (19, {}),... | custom-call | flops 17250000896 | tf_op jit(solution)/shard_map/experts/pallas_call | solution.py:789
  384.7 20.9 %collective-permute-done.80 = bf16[128,4224]{1,0:T(8,128)(2,1)S(1)} collective-permute-done((bf16[128,4224]{1,0:T(8,128)(2,1)S(1)}, bf16[128,4224]{1,0:T(8,128)(2,1)S(1)}, u32[]{:S(2)}, u32[]{:S(2)}) %collective-permute-start.80) | collective-permute-done | bytes 1081376 | tf_op jit(solution)/shard_map/ppermute | solution.py:103
  411.6 9.9 %collective-permute-done.82.g1 = bf16[128,2048]{1,0:T(8,128)(2,1)S(1)} collective-permute-done((bf16[128,2048]{1,0:T(8,128)(2,1)S(1)}, bf16[128,2048]{1,0:T(8,128)(2,1)S(1)}, u32[]{:S(2)}, u32[]{:S(2)}) %collective-permute-start.82) | collective-permute-done | bytes 524320 | tf_op jit(solution)/shard_map/ppermute | solution.py:103
  449.1 9.2 %collective-permute-done.95 = bf16[17,2048]{1,0:T(8,128)(2,1)S(1)} collective-permute-done((bf16[17,2048]{1,0:T(8,128)(2,1)S(1)}, bf16[17,2048]{1,0:T(8,128)(2,1)S(1)}, u32[]{:S(2)}, u32[]{:S(2)}) %collective-permute-start.95) | collective-permute-done | bytes 69664 | tf_op jit(solution)/shard_map/ppermute | solution.py:209
  484.3 15.0 %attend_back.1 = (f32[2,2048,128]{2,1,0:T(8,128)S(1)}, f32[2,2048,128]{2,1,0:T(8,128)S(1)}, f32[2,2048,128]{2,1,0:T(8,128)S(1)}, bf16[2,2048,128]{2,1,0:T(8,128)(2,1)S(1)}) custom-call(s32[5]{0:T(128)S(1)} %pad_add_fusion.1.ends, bf16[2,2048,128]{2,1,0:T(8,128)(2,1)S(1)} %copy-done.63, bf16[2,2048,128]{2,1,0:T(8,128)(2,1)S(1)} %get-tuple-element.596.grad, ...), custom_call_target="tpu_custom_call" | custom-call | flops 19549999104 | tf_op jit(solution)/shard_map/attend_back/pallas_call | solution.py:572
  517.3 10.3 %collective-permute-done.111 = bf16[1024,256]{1,0:T(8,128)(2,1)S(1)} collective-permute-done((bf16[1024,256]{1,0:T(8,128)(2,1)S(1)}, bf16[1024,256]{1,0:T(8,128)(2,1)S(1)}, u32[]{:S(2)}, u32[]{:S(2)}) %collective-permute-start.111) | collective-permute-done | bytes 524320 | tf_op jit(solution)/shard_map/ppermute | solution.py:224
  542.8 8.4 %collective-permute-done.116 = bf16[512,256]{1,0:T(8,128)(2,1)S(1)} collective-permute-done((bf16[512,256]{1,0:T(8,128)(2,1)S(1)}, bf16[512,256]{1,0:T(8,128)(2,1)S(1)}, u32[]{:S(2)}, u32[]{:S(2)}) %collective-permute-start.116) | collective-permute-done | bytes 262176 | tf_op jit(solution)/shard_map/ppermute | solution.py:1359
  564.4 9.0 %collective-permute-done.122 = bf16[256,256]{1,0:T(8,128)(2,1)S(1)} collective-permute-done((bf16[256,256]{1,0:T(8,128)(2,1)S(1)}, bf16[256,256]{1,0:T(8,128)(2,1)S(1)}, u32[]{:S(2)}, u32[]{:S(2)}) %collective-permute-start.122) | collective-permute-done | bytes 131104 | tf_op jit(solution)/shard_map/ppermute | solution.py:1359
  604.2 8.0 %collective-permute-done.123 = bf16[128,2048]{1,0:T(8,128)(2,1)S(1)} collective-permute-done((bf16[128,2048]{1,0:T(8,128)(2,1)S(1)}, bf16[128,2048]{1,0:T(8,128)(2,1)S(1)}, u32[]{:S(2)}, u32[]{:S(2)}) %collective-permute-start.123) | collective-permute-done | bytes 524320 | tf_op jit(solution)/shard_map/ppermute | solution.py:103
  643.7 13.5 %collective-permute-done.139 = bf16[2,2048]{1,0:T(2,128)(2,1)S(1)} collective-permute-done((bf16[2,2048]{1,0:T(2,128)(2,1)S(1)}, bf16[2,2048]{1,0:T(2,128)(2,1)S(1)}, u32[]{:S(2)}, u32[]{:S(2)}) %collective-permute-start.139) | collective-permute-done | bytes 8224 | tf_op jit(solution)/shard_map/ppermute | solution.py:209
  664.9 8.5 %collective-permute-done.142 = bf16[2,2048]{1,0:T(2,128)(2,1)S(1)} collective-permute-done((bf16[2,2048]{1,0:T(2,128)(2,1)S(1)}, bf16[2,2048]{1,0:T(2,128)(2,1)S(1)}, u32[]{:S(2)}, u32[]{:S(2)}) %collective-permute-start.142) | collective-permute-done | bytes 8224 | tf_op jit(solution)/shard_map/ppermute | solution.py:209
  686.4 8.2 %collective-permute-done.145.refs_1_.refs_5_ = bf16[1280,256]{1,0:T(8,128)(2,1)S(1)} collective-permute-done((bf16[1280,256]{1,0:T(8,128)(2,1)S(1)}, bf16[1280,256]{1,0:T(8,128)(2,1)S(1)}, u32[]{:S(2)}, u32[]{:S(2)}) %collective-permute-start.145) | collective-permute-done | bytes 655392 | tf_op jit(solution)/shard_map/ppermute | solution.py:103
  709.5 9.2 %collective-permute-done.150.refs_1_.refs_5_ = bf16[1280,256]{1,0:T(8,128)(2,1)S(1)} collective-permute-done((bf16[1280,256]{1,0:T(8,128)(2,1)S(1)}, bf16[1280,256]{1,0:T(8,128)(2,1)S(1)}, u32[]{:S(2)}, u32[]{:S(2)}) %collective-permute-start.150) | collective-permute-done | bytes 655392 | tf_op jit(solution)/shard_map/ppermute | solution.py:103
  (748 shorter events, 449.3 us)
Async XLA Ops:
  5.2 31.8 %collective-permute-start.13 = (bf16[128,2048]{1,0:T(8,128)(2,1)}, bf16[128,2048]{1,0:T(8,128)(2,1)}, u32[]{:S(2)}, u32[]{:S(2)}) collective-permute-start(bf16[128,2048]{1,0:T(8,128)(2,1)} %bitcast.226), channel_id=1, source_target_pairs={{0,2},{2,0},{4,6},{6,4},{8,10},{10,8},{12,14},{14,12},{16,18},{18,... | collective-permute-start | bytes 1572872 | tf_op jit(solution)/shard_map/ppermute | solution.py:144
  7.8 28.4 %collective-permute-start.10 = (bf16[1,2176]{1,0:T(2,128)(2,1)S(1)}, bf16[1,2176]{1,0:T(2,128)(2,1)S(1)}, u32[]{:S(2)}, u32[]{:S(2)}) collective-permute-start(bf16[1,2176]{1,0:T(2,128)(2,1)S(1)} %broadcast_in_dim.66), channel_id=1, source_target_pairs={{0,1},{1,0},{2,3},{3,2},{4,5},{5,4},{6,7},{7,6},{8,9},{9,8},{10,11... | collective-permute-start | bytes 13064 | tf_op jit(solution)/shard_map/ppermute | solution.py:224
  9.3 26.0 %collective-permute-start.4 = (bf16[1024,512]{1,0:T(8,128)(2,1)S(1)}, bf16[1024,512]{1,0:T(8,128)(2,1)S(1)}, u32[]{:S(2)}, u32[]{:S(2)}) collective-permute-start(bf16[1024,512]{1,0:T(8,128)(2,1)S(1)} %pad_maximum_fusion.1.refs_0_), channel_id=1, source_target_pairs={{0,1},{1,0},{2,3},{3,2},{4,5},{5,4},{6,7},{7,6},{8,9},{9,8},{10,11... | collective-permute-start | bytes 3145736 | tf_op jit(solution)/shard_map/ppermute | solution.py:224
  78.8 25.4 %collective-permute-start.23 = (bf16[128,2048]{1,0:T(8,128)(2,1)S(1)}, bf16[128,2048]{1,0:T(8,128)(2,1)S(1)}, u32[]{:S(2)}, u32[]{:S(2)}) collective-permute-start(bf16[128,2048]{1,0:T(8,128)(2,1)S(1)} %collective-permute-done.17.g0), channel_id=1, source_target_pairs={{0,4},{2,6},{4,0},{6,2},{8,12},{10,14},{12,8},{14,10},{16,20},{18,... | collective-permute-start | bytes 1572872 | tf_op jit(solution)/shard_map/ppermute | solution.py:171
  181.4 34.2 %collective-permute-start.57 = (bf16[1024,16]{0,1:T(8,128)(2,1)S(1)}, bf16[1024,16]{0,1:T(8,128)(2,1)S(1)}, u32[]{:S(2)}, u32[]{:S(2)}) collective-permute-start(bf16[1024,16]{0,1:T(8,128)(2,1)S(1)} %copy-done.104), channel_id=1, source_target_pairs={{0,1},{1,0},{2,3},{3,2},{4,5},{5,4},{6,7},{7,6},{8,9},{9,8},{10,11... | collective-permute-start | bytes 98312 | tf_op jit(solution)/shard_map/ppermute | solution.py:224
  273.8 25.9 %collective-permute-start.60 = (bf16[128,4224]{1,0:T(8,128)(2,1)S(1)}, bf16[128,4224]{1,0:T(8,128)(2,1)S(1)}, u32[]{:S(2)}, u32[]{:S(2)}) collective-permute-start(bf16[128,4224]{1,0:T(8,128)(2,1)S(1)} %fusion.10), channel_id=1, source_target_pairs={{0,4},{2,6},{4,0},{6,2},{8,12},{10,14},{12,8},{14,10},{16,20},{18,... | collective-permute-start | bytes 3244040 | tf_op jit(solution)/shard_map/ppermute | solution.py:103
  304.9 28.0 %collective-permute-start.66 = (bf16[128,4224]{1,0:T(8,128)(2,1)S(1)}, bf16[128,4224]{1,0:T(8,128)(2,1)S(1)}, u32[]{:S(2)}, u32[]{:S(2)}) collective-permute-start(bf16[128,4224]{1,0:T(8,128)(2,1)S(1)} %fusion.3), channel_id=1, source_target_pairs={{0,8},{2,10},{4,12},{6,14},{8,16},{10,18},{12,20},{14,22},{16,24},... | collective-permute-start | bytes 3244040 | tf_op jit(solution)/shard_map/ppermute | solution.py:103
  308.3 26.3 %collective-permute-start.67 = (bf16[128,4224]{1,0:T(8,128)(2,1)S(1)}, bf16[128,4224]{1,0:T(8,128)(2,1)S(1)}, u32[]{:S(2)}, u32[]{:S(2)}) collective-permute-start(bf16[128,4224]{1,0:T(8,128)(2,1)S(1)} %fusion.11), channel_id=1, source_target_pairs={{0,4},{2,6},{4,0},{6,2},{8,12},{10,14},{12,8},{14,10},{16,20},{18,... | collective-permute-start | bytes 3244040 | tf_op jit(solution)/shard_map/ppermute | solution.py:103
  340.9 28.1 %collective-permute-start.72 = (bf16[128,4224]{1,0:T(8,128)(2,1)S(1)}, bf16[128,4224]{1,0:T(8,128)(2,1)S(1)}, u32[]{:S(2)}, u32[]{:S(2)}) collective-permute-start(bf16[128,4224]{1,0:T(8,128)(2,1)S(1)} %fusion.5), channel_id=1, source_target_pairs={{0,8},{2,10},{4,12},{6,14},{8,16},{10,18},{12,20},{14,22},{16,24},... | collective-permute-start | bytes 3244040 | tf_op jit(solution)/shard_map/ppermute | solution.py:103
  345.4 26.0 %collective-permute-start.74 = (bf16[128,4224]{1,0:T(8,128)(2,1)S(1)}, bf16[128,4224]{1,0:T(8,128)(2,1)S(1)}, u32[]{:S(2)}, u32[]{:S(2)}) collective-permute-start(bf16[128,4224]{1,0:T(8,128)(2,1)S(1)} %fusion.12), channel_id=1, source_target_pairs={{0,4},{2,6},{4,0},{6,2},{8,12},{10,14},{12,8},{14,10},{16,20},{18,... | collective-permute-start | bytes 3244040 | tf_op jit(solution)/shard_map/ppermute | solution.py:103
  377.5 28.1 %collective-permute-start.80 = (bf16[128,4224]{1,0:T(8,128)(2,1)S(1)}, bf16[128,4224]{1,0:T(8,128)(2,1)S(1)}, u32[]{:S(2)}, u32[]{:S(2)}) collective-permute-start(bf16[128,4224]{1,0:T(8,128)(2,1)S(1)} %fusion.1), channel_id=1, source_target_pairs={{0,8},{2,10},{4,12},{6,14},{8,16},{10,18},{12,20},{14,22},{16,24},... | collective-permute-start | bytes 3244040 | tf_op jit(solution)/shard_map/ppermute | solution.py:103
  379.0 26.7 %collective-permute-start.81 = (bf16[128,4224]{1,0:T(8,128)(2,1)S(1)}, bf16[128,4224]{1,0:T(8,128)(2,1)S(1)}, u32[]{:S(2)}, u32[]{:S(2)}) collective-permute-start(bf16[128,4224]{1,0:T(8,128)(2,1)S(1)} %fusion.13), channel_id=1, source_target_pairs={{0,4},{2,6},{4,0},{6,2},{8,12},{10,14},{12,8},{14,10},{16,20},{18,... | collective-permute-start | bytes 3244040 | tf_op jit(solution)/shard_map/ppermute | solution.py:103
  380.6 30.9 %collective-permute-start.84 = (bf16[1024,256]{1,0:T(8,128)(2,1)S(1)}, bf16[1024,256]{1,0:T(8,128)(2,1)S(1)}, u32[]{:S(2)}, u32[]{:S(2)}) collective-permute-start(bf16[1024,256]{1,0:T(8,128)(2,1)S(1)} %convolution_convert_fusion.8), channel_id=1, source_target_pairs={{0,1},{1,0},{2,3},{3,2},{4,5},{5,4},{6,7},{7,6},{8,9},{9,8},{10,11... | collective-permute-start | bytes 1572872 | tf_op jit(solution)/shard_map/ppermute | solution.py:224
  474.1 25.3 %collective-permute-start.105 = (bf16[1024,256]{1,0:T(8,128)(2,1)S(1)}, bf16[1024,256]{1,0:T(8,128)(2,1)S(1)}, u32[]{:S(2)}, u32[]{:S(2)}) collective-permute-start(bf16[1024,256]{1,0:T(8,128)(2,1)S(1)} %convolution_convert_fusion.4), channel_id=1, source_target_pairs={{0,1},{1,0},{2,3},{3,2},{4,5},{5,4},{6,7},{7,6},{8,9},{9,8},{10,11... | collective-permute-start | bytes 1572872 | tf_op jit(solution)/shard_map/ppermute | solution.py:224
  475.3 24.0 %collective-permute-start.106 = (bf16[17,2048]{1,0:T(8,128)(2,1)S(1)}, bf16[17,2048]{1,0:T(8,128)(2,1)S(1)}, u32[]{:S(2)}, u32[]{:S(2)}) collective-permute-start(bf16[17,2048]{1,0:T(8,128)(2,1)S(1)} %fusion.63), channel_id=1, source_target_pairs={{0,1},{1,0},{2,3},{3,2},{4,5},{5,4},{6,7},{7,6},{8,9},{9,8},{10,11... | collective-permute-start | bytes 208904 | tf_op jit(solution)/shard_map/ppermute | solution.py:224
  501.9 49.3 %collective-permute-start.161 = (bf16[128,2048]{1,0:T(8,128)(2,1)S(1)}, bf16[128,2048]{1,0:T(8,128)(2,1)S(1)}, u32[]{:S(2)}, u32[]{:S(2)}) collective-permute-start(bf16[128,2048]{1,0:T(8,128)(2,1)S(1)} %add_convert_fusion.9.refs_0_), channel_id=1, source_target_pairs={{0,2},{2,0},{4,6},{6,4},{8,10},{10,8},{12,14},{14,12},{16,18},{18,... | collective-permute-start | bytes 1572872 | tf_op jit(solution)/shard_map/ppermute | solution.py:182
  502.2 33.3 %collective-permute-start.114 = (bf16[1024,256]{1,0:T(8,128)(2,1)S(1)}, bf16[1024,256]{1,0:T(8,128)(2,1)S(1)}, u32[]{:S(2)}, u32[]{:S(2)}) collective-permute-start(bf16[1024,256]{1,0:T(8,128)(2,1)S(1)} %convolution_convert_fusion.3), channel_id=1, source_target_pairs={{0,1},{1,0},{2,3},{3,2},{4,5},{5,4},{6,7},{7,6},{8,9},{9,8},{10,11... | collective-permute-start | bytes 1572872 | tf_op jit(solution)/shard_map/ppermute | solution.py:224
  555.7 26.1 %collective-permute-start.120 = (bf16[128,2048]{1,0:T(8,128)(2,1)S(1)}, bf16[128,2048]{1,0:T(8,128)(2,1)S(1)}, u32[]{:S(2)}, u32[]{:S(2)}) collective-permute-start(bf16[128,2048]{1,0:T(8,128)(2,1)S(1)} %collective-permute-done.115.refs_0_), channel_id=1, source_target_pairs={{0,8},{2,10},{4,12},{6,14},{8,16},{10,18},{12,20},{14,22},{16,24},... | collective-permute-start | bytes 1572872 | tf_op jit(solution)/shard_map/ppermute | solution.py:171
  555.8 26.0 %collective-permute-start.121 = (bf16[128,2048]{1,0:T(8,128)(2,1)S(1)}, bf16[128,2048]{1,0:T(8,128)(2,1)S(1)}, u32[]{:S(2)}, u32[]{:S(2)}) collective-permute-start(bf16[128,2048]{1,0:T(8,128)(2,1)S(1)} %collective-permute-done.108.refs_0_), channel_id=1, source_target_pairs={{0,4},{2,6},{4,0},{6,2},{8,12},{10,14},{12,8},{14,10},{16,20},{18,... | collective-permute-start | bytes 1572872 | tf_op jit(solution)/shard_map/ppermute | solution.py:171
  558.1 25.7 %collective-permute-start.119 = (bf16[128,2048]{1,0:T(8,128)(2,1)S(1)}, bf16[128,2048]{1,0:T(8,128)(2,1)S(1)}, u32[]{:S(2)}, u32[]{:S(2)}) collective-permute-start(bf16[128,2048]{1,0:T(8,128)(2,1)S(1)} %fusion.56), channel_id=1, source_target_pairs={{0,4},{2,6},{4,0},{6,2},{8,12},{10,14},{12,8},{14,10},{16,20},{18,... | collective-permute-start | bytes 1572872 | tf_op jit(solution)/shard_map/ppermute | solution.py:103
  573.4 29.5 %collective-permute-start.126 = (bf16[1024,256]{1,0:T(8,128)(2,1)S(1)}, bf16[1024,256]{1,0:T(8,128)(2,1)S(1)}, u32[]{:S(2)}, u32[]{:S(2)}) collective-permute-start(bf16[1024,256]{1,0:T(8,128)(2,1)S(1)} %convolution_convert_fusion.2), channel_id=1, source_target_pairs={{0,1},{1,0},{2,3},{3,2},{4,5},{5,4},{6,7},{7,6},{8,9},{9,8},{10,11... | collective-permute-start | bytes 1572872 | tf_op jit(solution)/shard_map/ppermute | solution.py:224
  584.8 27.4 %collective-permute-start.127 = (bf16[128,2048]{1,0:T(8,128)(2,1)S(1)}, bf16[128,2048]{1,0:T(8,128)(2,1)S(1)}, u32[]{:S(2)}, u32[]{:S(2)}) collective-permute-start(bf16[128,2048]{1,0:T(8,128)(2,1)S(1)} %collective-permute-done.121.refs_1_), channel_id=1, source_target_pairs={{0,8},{2,10},{4,12},{6,14},{8,16},{10,18},{12,20},{14,22},{16,24},... | collective-permute-start | bytes 1572872 | tf_op jit(solution)/shard_map/ppermute | solution.py:171
  586.7 25.5 %collective-permute-start.123 = (bf16[128,2048]{1,0:T(8,128)(2,1)S(1)}, bf16[128,2048]{1,0:T(8,128)(2,1)S(1)}, u32[]{:S(2)}, u32[]{:S(2)}) collective-permute-start(bf16[128,2048]{1,0:T(8,128)(2,1)S(1)} %fusion.25), channel_id=1, source_target_pairs={{0,8},{2,10},{4,12},{6,14},{8,16},{10,18},{12,20},{14,22},{16,24},... | collective-permute-start | bytes 1572872 | tf_op jit(solution)/shard_map/ppermute | solution.py:103
  679.6 24.7 %collective-permute-start.151 = (bf16[1280,256]{1,0:T(8,128)(2,1)S(1)}, bf16[1280,256]{1,0:T(8,128)(2,1)S(1)}, u32[]{:S(2)}, u32[]{:S(2)}) collective-permute-start(bf16[1280,256]{1,0:T(8,128)(2,1)S(1)} %collective-permute-done.141.refs_0_.refs_4_), channel_id=1, source_target_pairs={{0,2},{2,0},{4,6},{6,4},{8,10},{10,8},{12,14},{14,12},{16,18},{18,... | collective-permute-start | bytes 1966088 | tf_op jit(solution)/shard_map/ppermute | solution.py:144
  (269 other events, 3328.2 us)

commit v5 on v4

--- a/solution.py
+++ b/solution.py
@@ -152,19 +152,25 @@
         if blocks is not None:
             own, token = give(blocks, token)
         blocks, state = compute(k, quarter, token, state)
-        token, *blocks = step_ends(token, *blocks)
+        extra = closing[0]() if closing and not following else ()
+        if piece is not None and s < 2:
+            token, *blocks = step_ends(token, *blocks)
+        else:
+            mine, theirs = blocks
+            token, mine, *extra = step_ends(token, mine, *extra)
+            blocks = mine, theirs
+        if extra:
+            closing[1](*extra)
     if not scatter:
         return tuple(state)
     send("carry", total_of(own).astype(BF16), ring(n_ctx, 4))
     own, token = give(blocks, token)
-    extra = closing(token) if closing else ()
-    extra = step_ends(*extra)
-    return total_of(own), state, extra
-
-
-def gather_planned(piece, n_ctx, plan):
-    arrays = {("along", 0): piece}
-    plan = list(plan)
+    step_ends()
+    return total_of(own), state
+
+
+def gather_planned(piece, n_ctx, plan, arrays):
+    arrays["along", 0] = piece
     source = lambda kind, k: ("along", k) if kind == "across" else (kind, k - 1)
     for i, (items, steps) in enumerate(plan):
         going = [
@@ -179,22 +185,31 @@
         for kind, k in items:
             arrays["along" if kind == "along" else "beside", k] = came.pop(0)
         arrays.update(zip(tied, came))
-    core = lambda array: lax.ppermute(array, "ctx", flip(n_ctx, 1))
-    pairs = [(arrays["along", k], arrays["beside", k]) for k in range(n_ctx // 4)]
-    return [(a, b, core(a), core(b)) for a, b in pairs]
+
+
+def planned_quarter(arrays, k, n_ctx):
+    pair = [arrays["along", k], arrays["beside", k]]
+    return pair + [lax.ppermute(array, "ctx", flip(n_ctx, 1)) for array in pair]
 
 
 COTANGENT_PLAN = [
     ([("along", 1)], 1),
     ([("along", 2), ("across", 0), ("across", 1)], 1),
+    ([("beside", 2)], 2),
+    ([("along", 3)], 6),
+    ([("beside", 3)], 1),
+]
+QUERY_GRAD_PLAN = [
+    ([("along", 1), ("across", 0)], 1),
+    ([("along", 2), ("across", 1)], 1),
     ([("along", 3), ("across", 2)], 1),
-    ([("beside", 3)], 2),
+    ([("across", 3)], 1),
 ]
 OUTPUT_GRAD_PLAN = [
     ([("along", 1), ("across", 0)], 1),
-    ([("along", 2)], 1),
-    ([("along", 3), ("across", 1)], 1),
-    ([("beside", 2), ("across", 3)], 1),
+    ([("along", 2), ("across", 1)], 1),
+    ([("along", 3), ("across", 2)], 1),
+    ([("across", 3)], 1),
 ]
 
 
@@ -231,18 +246,12 @@
     return [part, other]
 
 
-def fetch_thirds(part, after, first=1):
+def fetch_after(part, after, steps):
     if lax.axis_size("fsdp") != 2:
         return [lax.all_gather(part, "fsdp", axis=0, tiled=True)], after
-    step = (part.shape[0] // 3 + 31) // 32 * 32
-    other = []
-    for at in range(0, part.shape[0], step):
-        after, rows = tie(after, part[at : at + step])
-        if other:
-            other[-1] = after
-        (after,) = yield (swap(rows),), 1 if other else first
-        other.append(after)
-    return [part, jnp.concatenate(other, axis=0)], after
+    after, sent = tie(after, part)
+    (after,) = yield (swap(sent),), steps
+    return [part, after], after
 
 
 def joined(parts):
@@ -260,7 +269,7 @@
     return [f * (width // 2), (1 - f) * (width // 2)]
 
 
-def scatter_products(pairs, block, steps=()):
+def scatter_products(pairs, block, steps=(), pause=()):
     if lax.axis_size("fsdp") != 2:
         full = [dot(left[0], right, COLS_T).astype(BF16) for left, right in pairs]
         return [
@@ -275,6 +284,8 @@
     for i in range(len(work)):
         ahead = [product(i + 1, 1).astype(BF16)] if i + 1 < len(work) else []
         fresh = [product(i - 1, 0) + came.astype(F32)] if i > 0 else []
+        if i in pause:
+            (sent,) = yield (sent,), pause[i]
         came, *worked = yield (swap(sent), *ahead, *fresh), steps[i] if steps else 1
         if ahead:
             sent = worked.pop(0)
@@ -775,9 +786,9 @@
         copy.wait()
 
 
-def experts(k, quarter, cots, router, wg, wu, wd, meta, capacity, n_exp, before):
+def experts(k, quarter, cots, router, wg, wu, wd, meta, capacity, n_exp, nz, before):
     count, wide = quarter[0].shape
-    nz, width = len(cots), cots[k][0].shape[1]
+    width = cots[0].shape[1]
     n_parts = len(wg)
     part = width // n_parts
     hid = wg[0].shape[1]
@@ -813,7 +824,7 @@
         compiler_params=params(42),
         cost_estimate=cost(15),
         name="experts",
-    )(meta, *quarter, *cots[k], router, *wg, *wu, *wd, *before)
+    )(meta, *quarter, *cots, router, *wg, *wu, *wd, *before)
     return (outs[n_out], outs[n_out + 1]), outs[:n_out]
 
 
@@ -1151,15 +1162,15 @@
         last = rows_parts[-1]
         w_out = joined(rows_parts)
         weights["out"] = lax.dynamic_slice_in_dim(w_out, (c // hpf) * hpd * HD, hpd * HD, 0)
-        weights["gate"], last = yield from fetch_thirds(w_gate[0], last)
-        weights["up"], last = yield from fetch_thirds(w_up[0], last, 2)
-        weights["down"], last = yield from fetch_thirds(w_down[0], last)
+        weights["gate"], last = yield from fetch_after(w_gate[0], last, 2)
+        weights["up"], last = yield from fetch_after(w_up[0], last, 4)
+        weights["down"], last = yield from fetch_after(w_down[0], last, 3)
 
     gathered = {}
 
     def gather_cotangents():
         (cot,) = yield (cotangent[0],), 3
-        gathered["cot"] = yield from gather_planned(cot, n_ctx, COTANGENT_PLAN)
+        yield from gather_planned(cot, n_ctx, COTANGENT_PLAN, gathered)
 
     sides = [Side(fetch_weights()), Side(gather_cotangents())]
 
@@ -1207,11 +1218,10 @@
     *normed, raw, scales, query, key, value = pipeline(
         n_ctx, straight, through_projection, meta_rows, sides, piece=inputs[0]
     )
-    _, (query,) = land({}, sides, query)
     mixed, log_total = attend(query, key, value, ends)
     _, (mixed,) = land({}, sides, mixed)
     x = inputs[0].astype(F32)
-    branch_sum, _, _ = pipeline(
+    branch_sum, _ = pipeline(
         n_ctx,
         later,
         lambda k, _, token, state: (branch(k, mixed, weights["out"], token, count), state),
@@ -1231,7 +1241,7 @@
         return experts(
             k,
             quarter,
-            gathered["cot"],
+            planned_quarter(gathered, k, n_ctx),
             router_wide,
             weights["gate"],
             weights["up"],
@@ -1239,10 +1249,11 @@
             token,
             capacity,
             n_exp,
+            nz,
             before,
         )
 
-    routed_grad, seen, _ = pipeline(
+    routed_grad, seen = pipeline(
         n_ctx,
         later,
         through_experts,
@@ -1291,7 +1302,9 @@
 
     def scatter_grads():
         pairs_of = [(rows, gate_part_grad), (rows, up_part_grad), (pairs, hidden)]
-        sums_of = yield from scatter_products(pairs_of, block, (1, 1, 1, 1, 1, 2, 2, 1, 1))
+        sums_of = yield from scatter_products(
+            pairs_of, block, (1, 1, 1, 1, 1, 2, 1, 1, 1), {6: 3}
+        )
         grads["gate"], grads["up"], grads["down"] = sums_of
 
     sides = [
@@ -1321,9 +1334,10 @@
         own = yield from scatter_rows(placed)
         own = own.astype(BF16)
         if n_ctx == hpf:
-            grads["out"] = place_rows(
-                (yield from gather_planned(own, n_ctx, OUTPUT_GRAD_PLAN)), table
-            )
+            arrays = {}
+            yield from gather_planned(own, n_ctx, OUTPUT_GRAD_PLAN, arrays)
+            quarters = [planned_quarter(arrays, k, n_ctx) for k in range(nz)]
+            grads["out"] = place_rows(quarters, table)
         else:
             whole_grad = lax.all_gather(own, "ctx", axis=0).reshape(-1, hpf * HD, width)
             mine = lax.dynamic_index_in_dim(whole_grad, f // hpd, 0, keepdims=False)
@@ -1388,60 +1402,64 @@
 
     q_grads = []
 
-    def query_weights(token):
-        q_flat = q_grads[0].reshape(length, -1)
-        if n_f != 2:
-            return (
-                lax.psum_scatter(
-                    dot(normed_flat[0], q_flat, COLS_T).astype(BF16),
-                    "fsdp",
-                    scatter_dimension=0,
-                    tiled=True,
-                ),
-            )
-        mine, other = normed_flat
-        came = swap(dot(other, q_flat, COLS_T).astype(BF16))
-        return dot(mine, q_flat, COLS_T), came
-
     def through_inputs_last(k, quarter, token, before):
         back, state = through_inputs(k, quarter, token, before)
         q_grads[:] = state
         return back, state
 
-    normed_grad, _, grad_q = pipeline(
-        n_ctx, later, through_inputs_last, meta_rows, sides, scatter=True, closing=query_weights
-    )
-    for side in sides[3:4]:
-        side.finish()
-    grad_q = sum(g.astype(F32) for g in grad_q).astype(BF16)
-    q_rows = grad_q.shape[0]
-    if shared:
-        grad_q = jnp.concatenate([grad_q, grads["key_piece"]], axis=0)
-
-    if n_ctx == hpf:
-        placed = pipeline(
-            n_ctx,
-            straight,
-            lambda k, quarter, token, before: place_columns(
-                k, quarter, token, n_ctx, q_rows, before
-            ),
-            table,
-            sides,
-            piece=grad_q,
-        )
-        grad_w_query = placed[0]
-        if shared:
-            grads["key"], grads["value"] = placed[1:]
-    else:
-        grad_w_query = (
-            lax.all_gather(grad_q, "ctx", axis=0)
+    def query_products():
+        q_flat = q_grads[0].reshape(length, -1)
+        if n_f != 2:
+            full = dot(normed_flat[0], q_flat, COLS_T).astype(BF16)
+            return (lax.psum_scatter(full, "fsdp", scatter_dimension=0, tiled=True),)
+        mine, other = normed_flat
+        came = swap(dot(other, q_flat, COLS_T).astype(BF16))
+        return dot(mine, q_flat, COLS_T), came
+
+    def gather_query_grads(*products):
+        own = sum(product.astype(F32) for product in products).astype(BF16)
+        if n_ctx == hpf:
+            sides.append(Side(gather_columns(own)))
+            return
+        grads["query"] = (
+            lax.all_gather(own, "ctx", axis=0)
             .reshape(n_ctx // hpf, hpf, width // n_f, hpd, HD)
             .transpose(2, 0, 3, 1, 4)
             .reshape(width // n_f, H * HD)
             .astype(F32)
         )
-    for side in sides:
-        side.finish()
+
+    def gather_columns(own):
+        q_rows = own.shape[0]
+        if shared:
+            own = jnp.concatenate([own, grads["key_piece"]], axis=0)
+        arrays, placed = {}, ()
+        chain = gather_planned(own, n_ctx, QUERY_GRAD_PLAN, arrays)
+        going, steps = next(chain)
+        for k in range(nz):
+            landed = yield (*going, *placed), steps
+            placed = landed[len(going) :]
+            try:
+                going, steps = chain.send(landed[: len(going)])
+            except StopIteration:
+                going = ()
+            quarter = planned_quarter(arrays, k, n_ctx)
+            placed = place_columns(k, quarter, table, n_ctx, q_rows, placed)
+        grads["query"] = placed[0]
+        if shared:
+            grads["key"], grads["value"] = placed[1:]
+
+    normed_grad, _ = pipeline(
+        n_ctx,
+        later,
+        through_inputs_last,
+        meta_rows,
+        sides,
+        scatter=True,
+        closing=(query_products, gather_query_grads),
+    )
+    while any(side.flying is not None for side in sides):
+        land({}, sides)
     early, late = sums
     own_part = lambda v, size: lax.dynamic_slice_in_dim(v, f * (size // n_f), size // n_f, 0)
     grad_w_router = own_part(early[:n_exp].T, width)
@@ -1466,7 +1484,7 @@
     return (
         outputs[None],
         input_grad.astype(BF16)[None],
-        grad_w_query,
+        grads["query"],
         grads["key"],
         grads["value"],
         grads["out"],

time: 736 us -> 688 us (0.935)
  waiting for transfers between devices: 282 us -> 245 us
  local copies, waits for them, and re-layouts: 39.3 us -> 27.8 us
  Pallas kernels: 204 us -> 212 us
  starting transfers between devices: 120 us -> 112 us
    ppermute x14 -> x21, waiting for transfers between devices: 37.9 us -> 20.8 us  [gather_planned(): lax.ppermute(arrays[source(*item)], 'ctx', flip(n_ctx, 2) if item[0] == '...]
    ppermute x49 -> x42, starting transfers between devices: 51.7 us -> 37 us  [send(): air[key] = lax.ppermute(array, 'ctx', pairs)]
    ppermute x27 -> x21, waiting for transfers between devices: 48.4 us -> 38.5 us  [swap(): return lax.ppermute(part, 'fsdp', SWAP)]
    ppermute x2, waiting for transfers between devices: 17.4 us -> 7.51 us  [sum_key_grads(): lax.ppermute(gone.astype(BF16), 'ctx', flip(n_ctx, bit))]
    unnamed x268 -> x224, local copies, waits for them, and re-layouts: 20.4 us -> 15.9 us
    ppermute x49 -> x42, waiting for transfers between devices: 131 us -> 127 us  [send(): air[key] = lax.ppermute(array, 'ctx', pairs)]
    ppermute x27 -> x21, starting transfers between devices: 31.9 us -> 35.2 us  [swap(): return lax.ppermute(part, 'fsdp', SWAP)]
    ppermute x14 -> x21, starting transfers between devices: 17 us -> 17.1 us  [gather_planned(): lax.ppermute(arrays[source(*item)], 'ctx', flip(n_ctx, 2) if item[0] == '...]
  transfers between devices with their start and end apart: 163 -> 157, of which waited for: 57 -> 52; matrix products, arithmetic and copies ran while one was open for 14% -> 14% of each run, Pallas kernels for 27% -> 29%
where the time goes in v5:
time: 688 us; the launch traced here: 681 us
  waiting for transfers between devices  245 us (36%)
  Pallas kernels  212 us (31%)
  starting transfers between devices  112 us (16%)
  other arithmetic  53 us (8%)
  matrix products  28.9 us (4%)
  local copies, waits for them, and re-layouts  27.8 us (4%)
    ppermute x42, waiting for transfers between devices, send(): air[key] = lax.ppermute(array, 'ctx', pairs)  127 us
    pallas_call x4, Pallas kernels, experts(): pl.pallas_call(functools.partial(experts_kernel, k, n_parts, width, capac...  66.6 us
    ppermute x8, waiting for transfers between devices, sum_all(): lax.ppermute(values.astype(BF16), 'ctx', flip(n_ctx, bit))  41.2 us
    ppermute x21, waiting for transfers between devices, swap(): return lax.ppermute(part, 'fsdp', SWAP)  38.5 us
    ppermute x42, starting transfers between devices, send(): air[key] = lax.ppermute(array, 'ctx', pairs)  37 us
    ppermute x21, starting transfers between devices, swap(): return lax.ppermute(part, 'fsdp', SWAP)  35.2 us
    pallas_call x4, Pallas kernels, project(): pl.pallas_call(functools.partial(project_kernel, k, hpd, n_kv, n_parts, n...  28.4 us
    dot_general x23, matrix products, dot(): return lax.dot_general(a, b, dims, preferred_element_type=F32)  27.4 us
  transfers between devices with their start and end apart: 157, of which 52 were waited for; matrix products, arithmetic and copies ran while one was open for 14% of the time, Pallas kernels for 29%

profile of v5, /device:TPU:0, one launch (start us, length us, event | category | flops | bytes accessed | tf_op | source)
XLA Modules:
  0.0 681.1 jit_solution(5435594967852077440)
XLA Ops:
  9.8 5.9 collective-permute-done.x1.refs_1_
  40.4 6.8 project.4
  47.8 7.2 %project.5 = (bf16[16,128,1024]{2,1,0:T(8,128)(2,1)}, bf16[16,128,1024]{2,1,0:T(8,128)(2,1)}, f32[16,128,384]{2,1,0:T(8,128)}, f32[16,128,128]{2,1,0:T(8,128)}, ...) custom-call(s32[19]{0:T(128)S(1)} %concatenate.53.meta, ...), custom_call_target="tpu_custom_call", output_to_operand_aliasing={{0}: (13, {}), {1}: (14, {}), {2}: (15, {}), {3}: (16, {}),... | custom-call | flops 6899999744 | tf_op jit(solution)/shard_map/project/pallas_call | solution.py:434
  61.4 7.5 %project.6 = (bf16[16,128,1024]{2,1,0:T(8,128)(2,1)}, bf16[16,128,1024]{2,1,0:T(8,128)(2,1)}, f32[16,128,384]{2,1,0:T(8,128)}, f32[16,128,128]{2,1,0:T(8,128)}, ...) custom-call(s32[19]{0:T(128)S(1)} %concatenate.53.meta, ...), custom_call_target="tpu_custom_call", output_to_operand_aliasing={{0}: (13, {}), {1}: (14, {}), {2}: (15, {}), {3}: (16, {}),... | custom-call | flops 6899999744 | tf_op jit(solution)/shard_map/project/pallas_call | solution.py:434
  78.1 6.9 %project.7 = (bf16[16,128,1024]{2,1,0:T(8,128)(2,1)}, bf16[16,128,1024]{2,1,0:T(8,128)(2,1)}, f32[16,128,384]{2,1,0:T(8,128)}, f32[16,128,128]{2,1,0:T(8,128)}, ...) custom-call(s32[19]{0:T(128)S(1)} %concatenate.53.meta, ...), custom_call_target="tpu_custom_call", output_to_operand_aliasing={{0}: (13, {}), {1}: (14, {}), {2}: (15, {}), {3}: (16, {}),... | custom-call | flops 6899999744 | tf_op jit(solution)/shard_map/project/pallas_call | solution.py:434
  88.7 15.4 %attend.1 = (f32[2,2048,128]{2,1,0:T(8,128)S(1)}, f32[2,8,2048]{2,1,0:T(8,128)S(1)}) custom-call(s32[4]{0:T(128)S(1)} %bitcast.224, bf16[2,2048,128]{2,1,0:T(8,128)(2,1)S(1)} %copy-done.55, bf16[2,2048,128]{2,1,0:T(8,128)(2,1)S(1)} %copy-done.57, bf16[2,2048,128]{2,1,0:T(8,128)(2,1)S(1)} %copy-done.59), custom_call_target="tpu_custom_call" | custom-call | flops 14375000064 | tf_op jit(solution)/shard_map/attend/pallas_call | solution.py:514
  113.6 14.8 %collective-permute-done.27.g1 = bf16[128,2048]{1,0:T(8,128)(2,1)S(1)} collective-permute-done((bf16[128,2048]{1,0:T(8,128)(2,1)}, bf16[128,2048]{1,0:T(8,128)(2,1)S(1)}, u32[]{:S(2)}, u32[]{:S(2)}) %collective-permute-start.27) | collective-permute-done | bytes 524320 | tf_op jit(solution)/shard_map/ppermute | solution.py:177
  134.9 12.6 %collective-permute-done.29 = bf16[128,2048]{1,0:T(8,128)(2,1)S(1)} collective-permute-done((bf16[128,2048]{1,0:T(8,128)(2,1)S(1)}, bf16[128,2048]{1,0:T(8,128)(2,1)S(1)}, u32[]{:S(2)}, u32[]{:S(2)}) %collective-permute-start.29) | collective-permute-done | bytes 524320 | tf_op jit(solution)/shard_map/ppermute | solution.py:103
  157.8 12.3 %collective-permute-done.34.refs_3_ = bf16[1024,768]{1,0:T(8,128)(2,1)} collective-permute-done((bf16[1024,768]{1,0:T(8,128)(2,1)}, bf16[1024,768]{1,0:T(8,128)(2,1)}, u32[]{:S(2)}, u32[]{:S(2)}) %collective-permute-start.34) | collective-permute-done | bytes 1572896 | tf_op jit(solution)/shard_map/ppermute | solution.py:239
  182.7 6.7 collective-permute-done.36
  194.3 10.8 %collective-permute-done.38.x1 = bf16[128,2176]{1,0:T(8,128)(2,1)S(1)} collective-permute-done((bf16[128,2176]{1,0:T(8,128)(2,1)S(1)}, bf16[128,2176]{1,0:T(8,128)(2,1)S(1)}, u32[]{:S(2)}, u32[]{:S(2)}) %collective-permute-start.38) | collective-permute-done | bytes 557088 | tf_op jit(solution)/shard_map/ppermute | solution.py:103
  229.6 17.0 %experts.4 = (bf16[1280,1024]{1,0:T(8,128)(2,1)}, bf16[1280,1024]{1,0:T(8,128)(2,1)}, bf16[1280,1024]{1,0:T(8,128)(2,1)}, bf16[1280,1024]{1,0:T(8,128)(2,1)}, bf...) custom-call(s32[3]{0:T(128)S(1)} %pad_add_fusion.meta, ...), custom_call_target="tpu_custom_call" | custom-call | flops 17250000896 | tf_op jit(solution)/shard_map/experts/pallas_call | solution.py:800
  246.7 7.0 %collective-permute-done.44.x0 = bf16[128,2176]{1,0:T(8,128)(2,1)S(1)} collective-permute-done((bf16[128,2176]{1,0:T(8,128)(2,1)}, bf16[128,2176]{1,0:T(8,128)(2,1)S(1)}, u32[]{:S(2)}, u32[]{:S(2)}) %collective-permute-start.44) | collective-permute-done | bytes 557088 | tf_op jit(solution)/shard_map/ppermute | solution.py:103
  263.7 16.2 %experts.5 = (bf16[1280,1024]{1,0:T(8,128)(2,1)}, bf16[1280,1024]{1,0:T(8,128)(2,1)}, bf16[1280,1024]{1,0:T(8,128)(2,1)}, bf16[1280,1024]{1,0:T(8,128)(2,1)}, bf...) custom-call(s32[3]{0:T(128)S(1)} %pad_add_fusion.meta, ...), custom_call_target="tpu_custom_call", output_to_operand_aliasing={{0}: (16, {}), {1}: (17, {}), {2}: (18, {}), {3}: (19, {}),... | custom-call | flops 17250000896 | tf_op jit(solution)/shard_map/experts/pallas_call | solution.py:800
  283.0 6.0 collective-permute-done.53
  298.9 17.2 %experts.6 = (bf16[1280,1024]{1,0:T(8,128)(2,1)}, bf16[1280,1024]{1,0:T(8,128)(2,1)}, bf16[1280,1024]{1,0:T(8,128)(2,1)}, bf16[1280,1024]{1,0:T(8,128)(2,1)}, bf...) custom-call(s32[3]{0:T(128)S(1)} %pad_add_fusion.meta, ...), custom_call_target="tpu_custom_call", output_to_operand_aliasing={{0}: (16, {}), {1}: (17, {}), {2}: (18, {}), {3}: (19, {}),... | custom-call | flops 17250000896 | tf_op jit(solution)/shard_map/experts/pallas_call | solution.py:800
  330.3 16.1 %experts.7 = (bf16[1280,1024]{1,0:T(8,128)(2,1)}, bf16[1280,1024]{1,0:T(8,128)(2,1)}, bf16[1280,1024]{1,0:T(8,128)(2,1)}, bf16[1280,1024]{1,0:T(8,128)(2,1)}, bf...) custom-call(s32[3]{0:T(128)S(1)} %pad_add_fusion.meta, ...), custom_call_target="tpu_custom_call", output_to_operand_aliasing={{0}: (16, {}), {1}: (17, {}), {2}: (18, {}), {3}: (19, {}),... | custom-call | flops 17250000896 | tf_op jit(solution)/shard_map/experts/pallas_call | solution.py:800
  371.8 13.6 %collective-permute-done.74 = bf16[128,4224]{1,0:T(8,128)(2,1)S(1)} collective-permute-done((bf16[128,4224]{1,0:T(8,128)(2,1)S(1)}, bf16[128,4224]{1,0:T(8,128)(2,1)S(1)}, u32[]{:S(2)}, u32[]{:S(2)}) %collective-permute-start.74) | collective-permute-done | bytes 1081376 | tf_op jit(solution)/shard_map/ppermute | solution.py:103
  393.1 8.1 %collective-permute-done.76.g1 = bf16[128,2048]{1,0:T(8,128)(2,1)S(1)} collective-permute-done((bf16[128,2048]{1,0:T(8,128)(2,1)S(1)}, bf16[128,2048]{1,0:T(8,128)(2,1)S(1)}, u32[]{:S(2)}, u32[]{:S(2)}) %collective-permute-start.76) | collective-permute-done | bytes 524320 | tf_op jit(solution)/shard_map/ppermute | solution.py:103
  430.8 9.4 %collective-permute-done.89 = bf16[17,2048]{1,0:T(8,128)(2,1)S(1)} collective-permute-done((bf16[17,2048]{1,0:T(8,128)(2,1)S(1)}, bf16[17,2048]{1,0:T(8,128)(2,1)S(1)}, u32[]{:S(2)}, u32[]{:S(2)}) %collective-permute-start.89) | collective-permute-done | bytes 69664 | tf_op jit(solution)/shard_map/ppermute | solution.py:224
  465.5 17.3 %attend_back.1 = (f32[2,2048,128]{2,1,0:T(8,128)S(1)}, f32[2,2048,128]{2,1,0:T(8,128)S(1)}, f32[2,2048,128]{2,1,0:T(8,128)S(1)}, bf16[2,2048,128]{2,1,0:T(8,128)(2,1)S(1)}) custom-call(s32[5]{0:T(128)S(1)} %pad_add_fusion.1.ends, bf16[2,2048,128]{2,1,0:T(8,128)(2,1)S(1)} %copy-done.56, bf16[2,2048,128]{2,1,0:T(8,128)(2,1)S(1)} %get-tuple-element.543.grad, ...), custom_call_target="tpu_custom_call" | custom-call | flops 19549999104 | tf_op jit(solution)/shard_map/attend_back/pallas_call | solution.py:583
  543.1 7.5 %collective-permute-done.117 = bf16[256,256]{1,0:T(8,128)(2,1)S(1)} collective-permute-done((bf16[256,256]{1,0:T(8,128)(2,1)S(1)}, bf16[256,256]{1,0:T(8,128)(2,1)S(1)}, u32[]{:S(2)}, u32[]{:S(2)}) %collective-permute-start.117) | collective-permute-done | bytes 131104 | tf_op jit(solution)/shard_map/ppermute | solution.py:1373
  581.4 8.1 %collective-permute-done.120 = bf16[128,2048]{1,0:T(8,128)(2,1)S(1)} collective-permute-done((bf16[128,2048]{1,0:T(8,128)(2,1)S(1)}, bf16[128,2048]{1,0:T(8,128)(2,1)S(1)}, u32[]{:S(2)}, u32[]{:S(2)}) %collective-permute-start.120) | collective-permute-done | bytes 524320 | tf_op jit(solution)/shard_map/ppermute | solution.py:103
  599.3 19.7 %collective-permute-done.127 = bf16[2,2048]{1,0:T(2,128)(2,1)S(1)} collective-permute-done((bf16[2,2048]{1,0:T(2,128)(2,1)S(1)}, bf16[2,2048]{1,0:T(2,128)(2,1)S(1)}, u32[]{:S(2)}, u32[]{:S(2)}) %collective-permute-start.127) | collective-permute-done | bytes 8224 | tf_op jit(solution)/shard_map/ppermute | solution.py:224
  (683 shorter events, 407.8 us)
Async XLA Ops:
  5.2 31.8 %collective-permute-start.13 = (bf16[128,2048]{1,0:T(8,128)(2,1)}, bf16[128,2048]{1,0:T(8,128)(2,1)}, u32[]{:S(2)}, u32[]{:S(2)}) collective-permute-start(bf16[128,2048]{1,0:T(8,128)(2,1)} %bitcast.208), channel_id=1, source_target_pairs={{0,2},{2,0},{4,6},{6,4},{8,10},{10,8},{12,14},{14,12},{16,18},{18,... | collective-permute-start | bytes 1572872 | tf_op jit(solution)/shard_map/ppermute | solution.py:144
  7.8 28.4 %collective-permute-start.10 = (bf16[1,2176]{1,0:T(2,128)(2,1)S(1)}, bf16[1,2176]{1,0:T(2,128)(2,1)S(1)}, u32[]{:S(2)}, u32[]{:S(2)}) collective-permute-start(bf16[1,2176]{1,0:T(2,128)(2,1)S(1)} %broadcast_in_dim.66), channel_id=1, source_target_pairs={{0,1},{1,0},{2,3},{3,2},{4,5},{5,4},{6,7},{7,6},{8,9},{9,8},{10,11... | collective-permute-start | bytes 13064 | tf_op jit(solution)/shard_map/ppermute | solution.py:239
  9.3 26.0 %collective-permute-start.4 = (bf16[1024,512]{1,0:T(8,128)(2,1)S(1)}, bf16[1024,512]{1,0:T(8,128)(2,1)S(1)}, u32[]{:S(2)}, u32[]{:S(2)}) collective-permute-start(bf16[1024,512]{1,0:T(8,128)(2,1)S(1)} %pad_maximum_fusion.1.refs_0_), channel_id=1, source_target_pairs={{0,1},{1,0},{2,3},{3,2},{4,5},{5,4},{6,7},{7,6},{8,9},{9,8},{10,11... | collective-permute-start | bytes 3145736 | tf_op jit(solution)/shard_map/ppermute | solution.py:239
  57.9 46.2 %collective-permute-start.15 = (bf16[1024,768]{1,0:T(8,128)(2,1)}, bf16[1024,768]{1,0:T(8,128)(2,1)S(1)}, u32[]{:S(2)}, u32[]{:S(2)}) collective-permute-start(bf16[1024,768]{1,0:T(8,128)(2,1)} %bitcast.219), channel_id=1, source_target_pairs={{0,1},{1,0},{2,3},{3,2},{4,5},{5,4},{6,7},{7,6},{8,9},{9,8},{10,11... | collective-permute-start | bytes 4718600 | tf_op jit(solution)/shard_map/ppermute | solution.py:239
  75.9 28.1 %collective-permute-start.20 = (bf16[128,2048]{1,0:T(8,128)(2,1)}, bf16[128,2048]{1,0:T(8,128)(2,1)S(1)}, u32[]{:S(2)}, u32[]{:S(2)}) collective-permute-start(bf16[128,2048]{1,0:T(8,128)(2,1)} %collective-permute-done.17.g0), channel_id=1, source_target_pairs={{0,8},{2,10},{4,12},{6,14},{8,16},{10,18},{12,20},{14,22},{16,24},... | collective-permute-start | bytes 1572872 | tf_op jit(solution)/shard_map/ppermute | solution.py:177
  76.0 28.1 %collective-permute-start.22 = (bf16[128,2048]{1,0:T(8,128)(2,1)}, bf16[128,2048]{1,0:T(8,128)(2,1)}, u32[]{:S(2)}, u32[]{:S(2)}) collective-permute-start(bf16[128,2048]{1,0:T(8,128)(2,1)} %collective-permute-done.17.g0), channel_id=1, source_target_pairs={{0,4},{2,6},{4,0},{6,2},{8,12},{10,14},{12,8},{14,10},{16,20},{18,... | collective-permute-start | bytes 1572872 | tf_op jit(solution)/shard_map/ppermute | solution.py:177
  77.5 26.6 %collective-permute-start.21 = (bf16[128,2048]{1,0:T(8,128)(2,1)S(1)}, bf16[128,2048]{1,0:T(8,128)(2,1)}, u32[]{:S(2)}, u32[]{:S(2)}) collective-permute-start(bf16[128,2048]{1,0:T(8,128)(2,1)S(1)} %bitcast.212), channel_id=1, source_target_pairs={{0,4},{2,6},{4,0},{6,2},{8,12},{10,14},{12,8},{14,10},{16,20},{18,... | collective-permute-start | bytes 1572872 | tf_op jit(solution)/shard_map/ppermute | solution.py:177
  133.1 36.9 %collective-permute-start.34 = (bf16[1024,768]{1,0:T(8,128)(2,1)}, bf16[1024,768]{1,0:T(8,128)(2,1)}, u32[]{:S(2)}, u32[]{:S(2)}) collective-permute-start(bf16[1024,768]{1,0:T(8,128)(2,1)} %bitcast.29.refs_2_), channel_id=1, source_target_pairs={{0,1},{1,0},{2,3},{3,2},{4,5},{5,4},{6,7},{7,6},{8,9},{9,8},{10,11... | collective-permute-start | bytes 4718600 | tf_op jit(solution)/shard_map/ppermute | solution.py:239
  180.9 35.8 %collective-permute-start.42 = (bf16[1024,768]{1,0:T(8,128)(2,1)}, bf16[1024,768]{1,0:T(8,128)(2,1)S(1)}, u32[]{:S(2)}, u32[]{:S(2)}) collective-permute-start(bf16[1024,768]{1,0:T(8,128)(2,1)} %bitcast.240), channel_id=1, source_target_pairs={{0,1},{1,0},{2,3},{3,2},{4,5},{5,4},{6,7},{7,6},{8,9},{9,8},{10,11... | collective-permute-start | bytes 4718600 | tf_op jit(solution)/shard_map/ppermute | solution.py:239
  226.8 26.9 %collective-permute-start.44 = (bf16[128,2176]{1,0:T(8,128)(2,1)}, bf16[128,2176]{1,0:T(8,128)(2,1)S(1)}, u32[]{:S(2)}, u32[]{:S(2)}) collective-permute-start(bf16[128,2176]{1,0:T(8,128)(2,1)} %copy-done.28), channel_id=1, source_target_pairs={{0,8},{2,10},{4,12},{6,14},{8,16},{10,18},{12,20},{14,22},{16,24},... | collective-permute-start | bytes 1671176 | tf_op jit(solution)/shard_map/ppermute | solution.py:103
  254.2 28.0 %collective-permute-start.51 = (bf16[128,2176]{1,0:T(8,128)(2,1)S(1)}, bf16[128,2176]{1,0:T(8,128)(2,1)}, u32[]{:S(2)}, u32[]{:S(2)}) collective-permute-start(bf16[128,2176]{1,0:T(8,128)(2,1)S(1)} %collective-permute-done.43.x1), channel_id=1, source_target_pairs={{0,8},{2,10},{4,12},{6,14},{8,16},{10,18},{12,20},{14,22},{16,24},... | collective-permute-start | bytes 1671176 | tf_op jit(solution)/shard_map/ppermute | solution.py:103
  294.8 28.7 %collective-permute-start.60 = (bf16[128,4224]{1,0:T(8,128)(2,1)}, bf16[128,4224]{1,0:T(8,128)(2,1)}, u32[]{:S(2)}, u32[]{:S(2)}) collective-permute-start(bf16[128,4224]{1,0:T(8,128)(2,1)} %fusion.3), channel_id=1, source_target_pairs={{0,8},{2,10},{4,12},{6,14},{8,16},{10,18},{12,20},{14,22},{16,24},... | collective-permute-start | bytes 3244040 | tf_op jit(solution)/shard_map/ppermute | solution.py:103
  298.3 26.6 %collective-permute-start.61 = (bf16[128,4224]{1,0:T(8,128)(2,1)}, bf16[128,4224]{1,0:T(8,128)(2,1)}, u32[]{:S(2)}, u32[]{:S(2)}) collective-permute-start(bf16[128,4224]{1,0:T(8,128)(2,1)} %fusion.11), channel_id=1, source_target_pairs={{0,4},{2,6},{4,0},{6,2},{8,12},{10,14},{12,8},{14,10},{16,20},{18,... | collective-permute-start | bytes 3244040 | tf_op jit(solution)/shard_map/ppermute | solution.py:103
  327.8 28.1 %collective-permute-start.66 = (bf16[128,4224]{1,0:T(8,128)(2,1)S(1)}, bf16[128,4224]{1,0:T(8,128)(2,1)S(1)}, u32[]{:S(2)}, u32[]{:S(2)}) collective-permute-start(bf16[128,4224]{1,0:T(8,128)(2,1)S(1)} %fusion.5), channel_id=1, source_target_pairs={{0,8},{2,10},{4,12},{6,14},{8,16},{10,18},{12,20},{14,22},{16,24},... | collective-permute-start | bytes 3244040 | tf_op jit(solution)/shard_map/ppermute | solution.py:103
  329.7 26.3 %collective-permute-start.68 = (bf16[128,4224]{1,0:T(8,128)(2,1)S(1)}, bf16[128,4224]{1,0:T(8,128)(2,1)S(1)}, u32[]{:S(2)}, u32[]{:S(2)}) collective-permute-start(bf16[128,4224]{1,0:T(8,128)(2,1)S(1)} %fusion.12), channel_id=1, source_target_pairs={{0,4},{2,6},{4,0},{6,2},{8,12},{10,14},{12,8},{14,10},{16,20},{18,... | collective-permute-start | bytes 3244040 | tf_op jit(solution)/shard_map/ppermute | solution.py:103
  358.0 27.3 %collective-permute-start.74 = (bf16[128,4224]{1,0:T(8,128)(2,1)S(1)}, bf16[128,4224]{1,0:T(8,128)(2,1)S(1)}, u32[]{:S(2)}, u32[]{:S(2)}) collective-permute-start(bf16[128,4224]{1,0:T(8,128)(2,1)S(1)} %fusion.1), channel_id=1, source_target_pairs={{0,8},{2,10},{4,12},{6,14},{8,16},{10,18},{12,20},{14,22},{16,24},... | collective-permute-start | bytes 3244040 | tf_op jit(solution)/shard_map/ppermute | solution.py:103
  363.6 29.5 %collective-permute-start.78 = (bf16[1024,256]{1,0:T(8,128)(2,1)S(1)}, bf16[1024,256]{1,0:T(8,128)(2,1)S(1)}, u32[]{:S(2)}, u32[]{:S(2)}) collective-permute-start(bf16[1024,256]{1,0:T(8,128)(2,1)S(1)} %convolution_convert_fusion.8), channel_id=1, source_target_pairs={{0,1},{1,0},{2,3},{3,2},{4,5},{5,4},{6,7},{7,6},{8,9},{9,8},{10,11... | collective-permute-start | bytes 1572872 | tf_op jit(solution)/shard_map/ppermute | solution.py:239
  455.1 27.7 %collective-permute-start.99 = (bf16[1024,256]{1,0:T(8,128)(2,1)S(1)}, bf16[1024,256]{1,0:T(8,128)(2,1)S(1)}, u32[]{:S(2)}, u32[]{:S(2)}) collective-permute-start(bf16[1024,256]{1,0:T(8,128)(2,1)S(1)} %convolution_convert_fusion.4), channel_id=1, source_target_pairs={{0,1},{1,0},{2,3},{3,2},{4,5},{5,4},{6,7},{7,6},{8,9},{9,8},{10,11... | collective-permute-start | bytes 1572872 | tf_op jit(solution)/shard_map/ppermute | solution.py:239
  456.6 26.3 %collective-permute-start.100 = (bf16[17,2048]{1,0:T(8,128)(2,1)S(1)}, bf16[17,2048]{1,0:T(8,128)(2,1)S(1)}, u32[]{:S(2)}, u32[]{:S(2)}) collective-permute-start(bf16[17,2048]{1,0:T(8,128)(2,1)S(1)} %fusion.63), channel_id=1, source_target_pairs={{0,1},{1,0},{2,3},{3,2},{4,5},{5,4},{6,7},{7,6},{8,9},{9,8},{10,11... | collective-permute-start | bytes 208904 | tf_op jit(solution)/shard_map/ppermute | solution.py:239
  485.0 32.3 %collective-permute-start.155 = (bf16[128,2048]{1,0:T(8,128)(2,1)S(1)}, bf16[128,2048]{1,0:T(8,128)(2,1)S(1)}, u32[]{:S(2)}, u32[]{:S(2)}) collective-permute-start(bf16[128,2048]{1,0:T(8,128)(2,1)S(1)} %add_convert_fusion.9.refs_0_), channel_id=1, source_target_pairs={{0,2},{2,0},{4,6},{6,4},{8,10},{10,8},{12,14},{14,12},{16,18},{18,... | collective-permute-start | bytes 1572872 | tf_op jit(solution)/shard_map/ppermute | solution.py:192
  590.3 29.4 %collective-permute-start.128 = (bf16[1280,256]{1,0:T(8,128)(2,1)S(1)}, bf16[1280,256]{1,0:T(8,128)(2,1)S(1)}, u32[]{:S(2)}, u32[]{:S(2)}) collective-permute-start(bf16[1280,256]{1,0:T(8,128)(2,1)S(1)} %pad_maximum_fusion.4.refs_0_.refs_4_), channel_id=1, source_target_pairs={{0,8},{2,10},{4,12},{6,14},{8,16},{10,18},{12,20},{14,22},{16,24},... | collective-permute-start | bytes 1966088 | tf_op jit(solution)/shard_map/ppermute | solution.py:177
  591.9 27.8 %collective-permute-start.129 = (bf16[1280,256]{1,0:T(8,128)(2,1)S(1)}, bf16[1280,256]{1,0:T(8,128)(2,1)S(1)}, u32[]{:S(2)}, u32[]{:S(2)}) collective-permute-start(bf16[1280,256]{1,0:T(8,128)(2,1)S(1)} %pad_maximum_fusion.4.refs_0_.refs_4_), channel_id=1, source_target_pairs={{0,4},{2,6},{4,0},{6,2},{8,12},{10,14},{12,8},{14,10},{16,20},{18,... | collective-permute-start | bytes 1966088 | tf_op jit(solution)/shard_map/ppermute | solution.py:177
  592.7 26.9 %collective-permute-start.125 = (bf16[128,2048]{1,0:T(8,128)(2,1)S(1)}, bf16[128,2048]{1,0:T(8,128)(2,1)S(1)}, u32[]{:S(2)}, u32[]{:S(2)}) collective-permute-start(bf16[128,2048]{1,0:T(8,128)(2,1)S(1)} %fusion.20), channel_id=1, source_target_pairs={{0,8},{2,10},{4,12},{6,14},{8,16},{10,18},{12,20},{14,22},{16,24},... | collective-permute-start | bytes 1572872 | tf_op jit(solution)/shard_map/ppermute | solution.py:103
  593.1 26.5 %collective-permute-start.126 = (bf16[128,2048]{1,0:T(8,128)(2,1)S(1)}, bf16[128,2048]{1,0:T(8,128)(2,1)S(1)}, u32[]{:S(2)}, u32[]{:S(2)}) collective-permute-start(bf16[128,2048]{1,0:T(8,128)(2,1)S(1)} %fusion.58), channel_id=1, source_target_pairs={{0,4},{2,6},{4,0},{6,2},{8,12},{10,14},{12,8},{14,10},{16,20},{18,... | collective-permute-start | bytes 1572872 | tf_op jit(solution)/shard_map/ppermute | solution.py:103
  (244 other events, 3216.8 us)

commit v6 on v5

--- a/solution.py
+++ b/solution.py
@@ -821,7 +821,7 @@
         + [rows_all(hid)] * 3
         + [jax.ShapeDtypeStruct((2, count, wide + width), BF16)] * 2,
         input_output_aliases={10 + 3 * n_parts + i: i for i in range(len(before))},
-        compiler_params=params(42),
+        compiler_params=params(34),
         cost_estimate=cost(15),
         name="experts",
     )(meta, *quarter, *cots, router, *wg, *wu, *wd, *before)

time: 688 us -> 684 us (level)
  Pallas kernels: 212 us -> 198 us
  starting transfers between devices: 112 us -> 98.5 us
  local copies, waits for them, and re-layouts: 27.8 us -> 40.3 us
  waiting for transfers between devices: 245 us -> 253 us
    ppermute x21, starting transfers between devices: 35.2 us -> 22.2 us  [swap(): return lax.ppermute(part, 'fsdp', SWAP)]
    unnamed x224 -> x248, local copies, waits for them, and re-layouts: 15.9 us -> 28.4 us
    pallas_call x4, Pallas kernels: 66.6 us -> 56.6 us  [experts(): pl.pallas_call(functools.partial(experts_kernel, k, n_parts, width, capac...]
  transfers between devices with their start and end apart: 157 -> 157, of which waited for: 52 -> 58; matrix products, arithmetic and copies ran while one was open for 14% -> 14% of each run, Pallas kernels for 29% -> 28%
where the time goes in v6:
time: 684 us; the launch traced here: 673 us
  waiting for transfers between devices  253 us (37%)
  Pallas kernels  198 us (29%)
  starting transfers between devices  98.5 us (14%)
  other arithmetic  50.2 us (7%)
  local copies, waits for them, and re-layouts  40.3 us (6%)
  matrix products  29 us (4%)
    ppermute x42, waiting for transfers between devices, send(): air[key] = lax.ppermute(array, 'ctx', pairs)  126 us
    pallas_call x4, Pallas kernels, experts(): pl.pallas_call(functools.partial(experts_kernel, k, n_parts, width, capac...  56.6 us
    ppermute x8, waiting for transfers between devices, sum_all(): lax.ppermute(values.astype(BF16), 'ctx', flip(n_ctx, bit))  43.2 us
    ppermute x21, waiting for transfers between devices, swap(): return lax.ppermute(part, 'fsdp', SWAP)  40.8 us
    ppermute x42, starting transfers between devices, send(): air[key] = lax.ppermute(array, 'ctx', pairs)  36.5 us
    unnamed x248, local copies, waits for them, and re-layouts  28.4 us
    pallas_call x4, Pallas kernels, project(): pl.pallas_call(functools.partial(project_kernel, k, hpd, n_kv, n_parts, n...  28.3 us
    dot_general x23, matrix products, dot(): return lax.dot_general(a, b, dims, preferred_element_type=F32)  27.5 us
  transfers between devices with their start and end apart: 157, of which 58 were waited for; matrix products, arithmetic and copies ran while one was open for 14% of the time, Pallas kernels for 28%

profile of v6, /device:TPU:0, one launch (start us, length us, event | category | flops | bytes accessed | tf_op | source)
XLA Modules:
  0.0 672.6 jit_solution(10877648834897698236)
XLA Ops:
  40.4 6.7 %project.4 = (bf16[16,128,1024]{2,1,0:T(8,128)(2,1)}, bf16[16,128,1024]{2,1,0:T(8,128)(2,1)}, f32[16,128,384]{2,1,0:T(8,128)}, f32[16,128,128]{2,1,0:T(8,128)}, ...) custom-call(s32[19]{0:T(128)S(1)} %concatenate.53.meta, ...), custom_call_target="tpu_custom_call" | custom-call | flops 6899999744 | tf_op jit(solution)/shard_map/project/pallas_call | solution.py:434
  47.8 7.2 %project.5 = (bf16[16,128,1024]{2,1,0:T(8,128)(2,1)}, bf16[16,128,1024]{2,1,0:T(8,128)(2,1)}, f32[16,128,384]{2,1,0:T(8,128)}, f32[16,128,128]{2,1,0:T(8,128)}, ...) custom-call(s32[19]{0:T(128)S(1)} %concatenate.53.meta, ...), custom_call_target="tpu_custom_call", output_to_operand_aliasing={{0}: (13, {}), {1}: (14, {}), {2}: (15, {}), {3}: (16, {}),... | custom-call | flops 6899999744 | tf_op jit(solution)/shard_map/project/pallas_call | solution.py:434
  61.3 7.5 %project.6 = (bf16[16,128,1024]{2,1,0:T(8,128)(2,1)}, bf16[16,128,1024]{2,1,0:T(8,128)(2,1)}, f32[16,128,384]{2,1,0:T(8,128)}, f32[16,128,128]{2,1,0:T(8,128)}, ...) custom-call(s32[19]{0:T(128)S(1)} %concatenate.53.meta, ...), custom_call_target="tpu_custom_call", output_to_operand_aliasing={{0}: (13, {}), {1}: (14, {}), {2}: (15, {}), {3}: (16, {}),... | custom-call | flops 6899999744 | tf_op jit(solution)/shard_map/project/pallas_call | solution.py:434
  78.0 6.9 %project.7 = (bf16[16,128,1024]{2,1,0:T(8,128)(2,1)}, bf16[16,128,1024]{2,1,0:T(8,128)(2,1)}, f32[16,128,384]{2,1,0:T(8,128)}, f32[16,128,128]{2,1,0:T(8,128)}, ...) custom-call(s32[19]{0:T(128)S(1)} %concatenate.53.meta, ...), custom_call_target="tpu_custom_call", output_to_operand_aliasing={{0}: (13, {}), {1}: (14, {}), {2}: (15, {}), {3}: (16, {}),... | custom-call | flops 6899999744 | tf_op jit(solution)/shard_map/project/pallas_call | solution.py:434
  88.6 14.0 %attend.1 = (f32[2,2048,128]{2,1,0:T(8,128)S(1)}, f32[2,8,2048]{2,1,0:T(8,128)S(1)}) custom-call(s32[4]{0:T(128)S(1)} %bitcast.229, bf16[2,2048,128]{2,1,0:T(8,128)(2,1)S(1)} %copy-done.72, bf16[2,2048,128]{2,1,0:T(8,128)(2,1)S(1)} %copy-done.74, bf16[2,2048,128]{2,1,0:T(8,128)(2,1)S(1)} %copy-done.76), custom_call_target="tpu_custom_call" | custom-call | flops 14375000064 | tf_op jit(solution)/shard_map/attend/pallas_call | solution.py:514
  112.2 14.8 %collective-permute-done.27.g1 = bf16[128,2048]{1,0:T(8,128)(2,1)S(1)} collective-permute-done((bf16[128,2048]{1,0:T(8,128)(2,1)}, bf16[128,2048]{1,0:T(8,128)(2,1)S(1)}, u32[]{:S(2)}, u32[]{:S(2)}) %collective-permute-start.27) | collective-permute-done | bytes 524320 | tf_op jit(solution)/shard_map/ppermute | solution.py:177
  132.2 14.0 %collective-permute-done.29 = bf16[128,2048]{1,0:T(8,128)(2,1)S(1)} collective-permute-done((bf16[128,2048]{1,0:T(8,128)(2,1)S(1)}, bf16[128,2048]{1,0:T(8,128)(2,1)S(1)}, u32[]{:S(2)}, u32[]{:S(2)}) %collective-permute-start.29) | collective-permute-done | bytes 524320 | tf_op jit(solution)/shard_map/ppermute | solution.py:103
  156.4 11.9 %collective-permute-done.34.refs_3_ = bf16[1024,768]{1,0:T(8,128)(2,1)} collective-permute-done((bf16[1024,768]{1,0:T(8,128)(2,1)}, bf16[1024,768]{1,0:T(8,128)(2,1)}, u32[]{:S(2)}, u32[]{:S(2)}) %collective-permute-start.34) | collective-permute-done | bytes 1572896 | tf_op jit(solution)/shard_map/ppermute | solution.py:239
  179.9 8.1 %collective-permute-done.36 = bf16[128,2048]{1,0:T(8,128)(2,1)} collective-permute-done((bf16[128,2048]{1,0:T(8,128)(2,1)}, bf16[128,2048]{1,0:T(8,128)(2,1)}, u32[]{:S(2)}, u32[]{:S(2)}) %collective-permute-start.36) | collective-permute-done | bytes 524320 | tf_op jit(solution)/shard_map/ppermute | solution.py:103
  193.1 11.6 %collective-permute-done.38.x1 = bf16[128,2176]{1,0:T(8,128)(2,1)S(1)} collective-permute-done((bf16[128,2176]{1,0:T(8,128)(2,1)S(1)}, bf16[128,2176]{1,0:T(8,128)(2,1)S(1)}, u32[]{:S(2)}, u32[]{:S(2)}) %collective-permute-start.38) | collective-permute-done | bytes 557088 | tf_op jit(solution)/shard_map/ppermute | solution.py:103
  232.7 14.4 %experts.4 = (bf16[1280,1024]{1,0:T(8,128)(2,1)}, bf16[1280,1024]{1,0:T(8,128)(2,1)}, bf16[1280,1024]{1,0:T(8,128)(2,1)}, bf16[1280,1024]{1,0:T(8,128)(2,1)}, bf...) custom-call(s32[3]{0:T(128)S(1)} %pad_add_fusion.meta, ...), custom_call_target="tpu_custom_call" | custom-call | flops 17250000896 | tf_op jit(solution)/shard_map/experts/pallas_call | solution.py:800
  247.2 6.6 collective-permute-done.44.x0
  261.1 13.5 %experts.5 = (bf16[1280,1024]{1,0:T(8,128)(2,1)}, bf16[1280,1024]{1,0:T(8,128)(2,1)}, bf16[1280,1024]{1,0:T(8,128)(2,1)}, bf16[1280,1024]{1,0:T(8,128)(2,1)}, bf...) custom-call(s32[3]{0:T(128)S(1)} %pad_add_fusion.meta, ...), custom_call_target="tpu_custom_call", output_to_operand_aliasing={{0}: (16, {}), {1}: (17, {}), {2}: (18, {}), {3}: (19, {}),... | custom-call | flops 17250000896 | tf_op jit(solution)/shard_map/experts/pallas_call | solution.py:800
  276.0 6.3 collective-permute-done.54.g1
  299.7 14.6 %experts.6 = (bf16[1280,1024]{1,0:T(8,128)(2,1)}, bf16[1280,1024]{1,0:T(8,128)(2,1)}, bf16[1280,1024]{1,0:T(8,128)(2,1)}, bf16[1280,1024]{1,0:T(8,128)(2,1)}, bf...) custom-call(s32[3]{0:T(128)S(1)} %pad_add_fusion.meta, ...), custom_call_target="tpu_custom_call", output_to_operand_aliasing={{0}: (16, {}), {1}: (17, {}), {2}: (18, {}), {3}: (19, {}),... | custom-call | flops 17250000896 | tf_op jit(solution)/shard_map/experts/pallas_call | solution.py:800
  327.7 14.0 %experts.7 = (bf16[1280,1024]{1,0:T(8,128)(2,1)}, bf16[1280,1024]{1,0:T(8,128)(2,1)}, bf16[1280,1024]{1,0:T(8,128)(2,1)}, bf16[1280,1024]{1,0:T(8,128)(2,1)}, bf...) custom-call(s32[3]{0:T(128)S(1)} %pad_add_fusion.meta, ...), custom_call_target="tpu_custom_call", output_to_operand_aliasing={{0}: (16, {}), {1}: (17, {}), {2}: (18, {}), {3}: (19, {}),... | custom-call | flops 17250000896 | tf_op jit(solution)/shard_map/experts/pallas_call | solution.py:800
  364.5 16.3 %collective-permute-done.74 = bf16[128,4224]{1,0:T(8,128)(2,1)S(1)} collective-permute-done((bf16[128,4224]{1,0:T(8,128)(2,1)S(1)}, bf16[128,4224]{1,0:T(8,128)(2,1)S(1)}, u32[]{:S(2)}, u32[]{:S(2)}) %collective-permute-start.74) | collective-permute-done | bytes 1081376 | tf_op jit(solution)/shard_map/ppermute | solution.py:103
  389.1 7.1 %collective-permute-done.76.g1 = bf16[128,2048]{1,0:T(8,128)(2,1)S(1)} collective-permute-done((bf16[128,2048]{1,0:T(8,128)(2,1)S(1)}, bf16[128,2048]{1,0:T(8,128)(2,1)S(1)}, u32[]{:S(2)}, u32[]{:S(2)}) %collective-permute-start.76) | collective-permute-done | bytes 524320 | tf_op jit(solution)/shard_map/ppermute | solution.py:103
  423.6 9.4 %collective-permute-done.89 = bf16[17,2048]{1,0:T(8,128)(2,1)S(1)} collective-permute-done((bf16[17,2048]{1,0:T(8,128)(2,1)S(1)}, bf16[17,2048]{1,0:T(8,128)(2,1)S(1)}, u32[]{:S(2)}, u32[]{:S(2)}) %collective-permute-start.89) | collective-permute-done | bytes 69664 | tf_op jit(solution)/shard_map/ppermute | solution.py:224
  458.5 15.2 %attend_back.1 = (f32[2,2048,128]{2,1,0:T(8,128)S(1)}, f32[2,2048,128]{2,1,0:T(8,128)S(1)}, f32[2,2048,128]{2,1,0:T(8,128)S(1)}, bf16[2,2048,128]{2,1,0:T(8,128)(2,1)S(1)}) custom-call(s32[5]{0:T(128)S(1)} %pad_add_fusion.1.ends, bf16[2,2048,128]{2,1,0:T(8,128)(2,1)S(1)} %copy-done.73, bf16[2,2048,128]{2,1,0:T(8,128)(2,1)S(1)} %get-tuple-element.543.grad, ...), custom_call_target="tpu_custom_call" | custom-call | flops 19549999104 | tf_op jit(solution)/shard_map/attend_back/pallas_call | solution.py:583
  533.8 7.9 %collective-permute-done.117 = bf16[256,256]{1,0:T(8,128)(2,1)S(1)} collective-permute-done((bf16[256,256]{1,0:T(8,128)(2,1)S(1)}, bf16[256,256]{1,0:T(8,128)(2,1)S(1)}, u32[]{:S(2)}, u32[]{:S(2)}) %collective-permute-start.117) | collective-permute-done | bytes 131104 | tf_op jit(solution)/shard_map/ppermute | solution.py:1373
  572.4 8.3 %collective-permute-done.120 = bf16[128,2048]{1,0:T(8,128)(2,1)S(1)} collective-permute-done((bf16[128,2048]{1,0:T(8,128)(2,1)S(1)}, bf16[128,2048]{1,0:T(8,128)(2,1)S(1)}, u32[]{:S(2)}, u32[]{:S(2)}) %collective-permute-start.120) | collective-permute-done | bytes 524320 | tf_op jit(solution)/shard_map/ppermute | solution.py:103
  589.9 19.7 %collective-permute-done.127 = bf16[2,2048]{1,0:T(2,128)(2,1)S(1)} collective-permute-done((bf16[2,2048]{1,0:T(2,128)(2,1)S(1)}, bf16[2,2048]{1,0:T(2,128)(2,1)S(1)}, u32[]{:S(2)}, u32[]{:S(2)}) %collective-permute-start.127) | collective-permute-done | bytes 8224 | tf_op jit(solution)/shard_map/ppermute | solution.py:224
  656.4 6.1 collective-permute-done.143
  (707 shorter events, 407.1 us)
Async XLA Ops:
  5.2 31.8 %collective-permute-start.13 = (bf16[128,2048]{1,0:T(8,128)(2,1)}, bf16[128,2048]{1,0:T(8,128)(2,1)}, u32[]{:S(2)}, u32[]{:S(2)}) collective-permute-start(bf16[128,2048]{1,0:T(8,128)(2,1)} %bitcast.208), channel_id=1, source_target_pairs={{0,2},{2,0},{4,6},{6,4},{8,10},{10,8},{12,14},{14,12},{16,18},{18,... | collective-permute-start | bytes 1572872 | tf_op jit(solution)/shard_map/ppermute | solution.py:144
  7.8 28.4 %collective-permute-start.10 = (bf16[1,2176]{1,0:T(2,128)(2,1)S(1)}, bf16[1,2176]{1,0:T(2,128)(2,1)S(1)}, u32[]{:S(2)}, u32[]{:S(2)}) collective-permute-start(bf16[1,2176]{1,0:T(2,128)(2,1)S(1)} %broadcast_in_dim.66), channel_id=1, source_target_pairs={{0,1},{1,0},{2,3},{3,2},{4,5},{5,4},{6,7},{7,6},{8,9},{9,8},{10,11... | collective-permute-start | bytes 13064 | tf_op jit(solution)/shard_map/ppermute | solution.py:239
  9.3 26.0 %collective-permute-start.4 = (bf16[1024,512]{1,0:T(8,128)(2,1)S(1)}, bf16[1024,512]{1,0:T(8,128)(2,1)S(1)}, u32[]{:S(2)}, u32[]{:S(2)}) collective-permute-start(bf16[1024,512]{1,0:T(8,128)(2,1)S(1)} %pad_maximum_fusion.1.refs_0_), channel_id=1, source_target_pairs={{0,1},{1,0},{2,3},{3,2},{4,5},{5,4},{6,7},{7,6},{8,9},{9,8},{10,11... | collective-permute-start | bytes 3145736 | tf_op jit(solution)/shard_map/ppermute | solution.py:239
  57.8 44.8 %collective-permute-start.15 = (bf16[1024,768]{1,0:T(8,128)(2,1)}, bf16[1024,768]{1,0:T(8,128)(2,1)S(1)}, u32[]{:S(2)}, u32[]{:S(2)}) collective-permute-start(bf16[1024,768]{1,0:T(8,128)(2,1)} %bitcast.219), channel_id=1, source_target_pairs={{0,1},{1,0},{2,3},{3,2},{4,5},{5,4},{6,7},{7,6},{8,9},{9,8},{10,11... | collective-permute-start | bytes 4718600 | tf_op jit(solution)/shard_map/ppermute | solution.py:239
  75.8 26.8 %collective-permute-start.20 = (bf16[128,2048]{1,0:T(8,128)(2,1)}, bf16[128,2048]{1,0:T(8,128)(2,1)S(1)}, u32[]{:S(2)}, u32[]{:S(2)}) collective-permute-start(bf16[128,2048]{1,0:T(8,128)(2,1)} %collective-permute-done.17.g0), channel_id=1, source_target_pairs={{0,8},{2,10},{4,12},{6,14},{8,16},{10,18},{12,20},{14,22},{16,24},... | collective-permute-start | bytes 1572872 | tf_op jit(solution)/shard_map/ppermute | solution.py:177
  75.9 26.8 %collective-permute-start.22 = (bf16[128,2048]{1,0:T(8,128)(2,1)}, bf16[128,2048]{1,0:T(8,128)(2,1)}, u32[]{:S(2)}, u32[]{:S(2)}) collective-permute-start(bf16[128,2048]{1,0:T(8,128)(2,1)} %collective-permute-done.17.g0), channel_id=1, source_target_pairs={{0,4},{2,6},{4,0},{6,2},{8,12},{10,14},{12,8},{14,10},{16,20},{18,... | collective-permute-start | bytes 1572872 | tf_op jit(solution)/shard_map/ppermute | solution.py:177
  77.4 25.3 %collective-permute-start.21 = (bf16[128,2048]{1,0:T(8,128)(2,1)S(1)}, bf16[128,2048]{1,0:T(8,128)(2,1)}, u32[]{:S(2)}, u32[]{:S(2)}) collective-permute-start(bf16[128,2048]{1,0:T(8,128)(2,1)S(1)} %bitcast.212), channel_id=1, source_target_pairs={{0,4},{2,6},{4,0},{6,2},{8,12},{10,14},{12,8},{14,10},{16,20},{18,... | collective-permute-start | bytes 1572872 | tf_op jit(solution)/shard_map/ppermute | solution.py:177
  131.7 36.6 %collective-permute-start.34 = (bf16[1024,768]{1,0:T(8,128)(2,1)}, bf16[1024,768]{1,0:T(8,128)(2,1)}, u32[]{:S(2)}, u32[]{:S(2)}) collective-permute-start(bf16[1024,768]{1,0:T(8,128)(2,1)} %bitcast.29.refs_2_), channel_id=1, source_target_pairs={{0,1},{1,0},{2,3},{3,2},{4,5},{5,4},{6,7},{7,6},{8,9},{9,8},{10,11... | collective-permute-start | bytes 4718600 | tf_op jit(solution)/shard_map/ppermute | solution.py:239
  178.4 36.4 %collective-permute-start.42 = (bf16[1024,768]{1,0:T(8,128)(2,1)}, bf16[1024,768]{1,0:T(8,128)(2,1)S(1)}, u32[]{:S(2)}, u32[]{:S(2)}) collective-permute-start(bf16[1024,768]{1,0:T(8,128)(2,1)} %bitcast.224), channel_id=1, source_target_pairs={{0,1},{1,0},{2,3},{3,2},{4,5},{5,4},{6,7},{7,6},{8,9},{9,8},{10,11... | collective-permute-start | bytes 4718600 | tf_op jit(solution)/shard_map/ppermute | solution.py:239
  227.0 26.7 %collective-permute-start.44 = (bf16[128,2176]{1,0:T(8,128)(2,1)}, bf16[128,2176]{1,0:T(8,128)(2,1)S(1)}, u32[]{:S(2)}, u32[]{:S(2)}) collective-permute-start(bf16[128,2176]{1,0:T(8,128)(2,1)} %copy-done.43), channel_id=1, source_target_pairs={{0,8},{2,10},{4,12},{6,14},{8,16},{10,18},{12,20},{14,22},{16,24},... | collective-permute-start | bytes 1671176 | tf_op jit(solution)/shard_map/ppermute | solution.py:103
  254.3 28.0 %collective-permute-start.51 = (bf16[128,2176]{1,0:T(8,128)(2,1)S(1)}, bf16[128,2176]{1,0:T(8,128)(2,1)}, u32[]{:S(2)}, u32[]{:S(2)}) collective-permute-start(bf16[128,2176]{1,0:T(8,128)(2,1)S(1)} %collective-permute-done.43.x1), channel_id=1, source_target_pairs={{0,8},{2,10},{4,12},{6,14},{8,16},{10,18},{12,20},{14,22},{16,24},... | collective-permute-start | bytes 1671176 | tf_op jit(solution)/shard_map/ppermute | solution.py:103
  259.5 25.9 %collective-permute-start.53 = (bf16[128,4224]{1,0:T(8,128)(2,1)S(1)}, bf16[128,4224]{1,0:T(8,128)(2,1)S(1)}, u32[]{:S(2)}, u32[]{:S(2)}) collective-permute-start(bf16[128,4224]{1,0:T(8,128)(2,1)S(1)} %fusion.10), channel_id=1, source_target_pairs={{0,4},{2,6},{4,0},{6,2},{8,12},{10,14},{12,8},{14,10},{16,20},{18,... | collective-permute-start | bytes 3244040 | tf_op jit(solution)/shard_map/ppermute | solution.py:103
  291.0 28.6 %collective-permute-start.60 = (bf16[128,4224]{1,0:T(8,128)(2,1)}, bf16[128,4224]{1,0:T(8,128)(2,1)}, u32[]{:S(2)}, u32[]{:S(2)}) collective-permute-start(bf16[128,4224]{1,0:T(8,128)(2,1)} %fusion.3), channel_id=1, source_target_pairs={{0,8},{2,10},{4,12},{6,14},{8,16},{10,18},{12,20},{14,22},{16,24},... | collective-permute-start | bytes 3244040 | tf_op jit(solution)/shard_map/ppermute | solution.py:103
  294.4 26.5 %collective-permute-start.61 = (bf16[128,4224]{1,0:T(8,128)(2,1)}, bf16[128,4224]{1,0:T(8,128)(2,1)}, u32[]{:S(2)}, u32[]{:S(2)}) collective-permute-start(bf16[128,4224]{1,0:T(8,128)(2,1)} %fusion.11), channel_id=1, source_target_pairs={{0,4},{2,6},{4,0},{6,2},{8,12},{10,14},{12,8},{14,10},{16,20},{18,... | collective-permute-start | bytes 3244040 | tf_op jit(solution)/shard_map/ppermute | solution.py:103
  323.6 28.1 %collective-permute-start.66 = (bf16[128,4224]{1,0:T(8,128)(2,1)S(1)}, bf16[128,4224]{1,0:T(8,128)(2,1)S(1)}, u32[]{:S(2)}, u32[]{:S(2)}) collective-permute-start(bf16[128,4224]{1,0:T(8,128)(2,1)S(1)} %fusion.5), channel_id=1, source_target_pairs={{0,8},{2,10},{4,12},{6,14},{8,16},{10,18},{12,20},{14,22},{16,24},... | collective-permute-start | bytes 3244040 | tf_op jit(solution)/shard_map/ppermute | solution.py:103
  325.4 26.2 %collective-permute-start.68 = (bf16[128,4224]{1,0:T(8,128)(2,1)S(1)}, bf16[128,4224]{1,0:T(8,128)(2,1)S(1)}, u32[]{:S(2)}, u32[]{:S(2)}) collective-permute-start(bf16[128,4224]{1,0:T(8,128)(2,1)S(1)} %fusion.12), channel_id=1, source_target_pairs={{0,4},{2,6},{4,0},{6,2},{8,12},{10,14},{12,8},{14,10},{16,20},{18,... | collective-permute-start | bytes 3244040 | tf_op jit(solution)/shard_map/ppermute | solution.py:103
  353.5 27.3 %collective-permute-start.74 = (bf16[128,4224]{1,0:T(8,128)(2,1)S(1)}, bf16[128,4224]{1,0:T(8,128)(2,1)S(1)}, u32[]{:S(2)}, u32[]{:S(2)}) collective-permute-start(bf16[128,4224]{1,0:T(8,128)(2,1)S(1)} %fusion.1), channel_id=1, source_target_pairs={{0,8},{2,10},{4,12},{6,14},{8,16},{10,18},{12,20},{14,22},{16,24},... | collective-permute-start | bytes 3244040 | tf_op jit(solution)/shard_map/ppermute | solution.py:103
  358.7 30.5 %collective-permute-start.78 = (bf16[1024,256]{1,0:T(8,128)(2,1)S(1)}, bf16[1024,256]{1,0:T(8,128)(2,1)S(1)}, u32[]{:S(2)}, u32[]{:S(2)}) collective-permute-start(bf16[1024,256]{1,0:T(8,128)(2,1)S(1)} %convolution_convert_fusion.8), channel_id=1, source_target_pairs={{0,1},{1,0},{2,3},{3,2},{4,5},{5,4},{6,7},{7,6},{8,9},{9,8},{10,11... | collective-permute-start | bytes 1572872 | tf_op jit(solution)/shard_map/ppermute | solution.py:239
  476.6 31.9 %collective-permute-start.155 = (bf16[128,2048]{1,0:T(8,128)(2,1)S(1)}, bf16[128,2048]{1,0:T(8,128)(2,1)S(1)}, u32[]{:S(2)}, u32[]{:S(2)}) collective-permute-start(bf16[128,2048]{1,0:T(8,128)(2,1)S(1)} %add_convert_fusion.9.refs_0_), channel_id=1, source_target_pairs={{0,2},{2,0},{4,6},{6,4},{8,10},{10,8},{12,14},{14,12},{16,18},{18,... | collective-permute-start | bytes 1572872 | tf_op jit(solution)/shard_map/ppermute | solution.py:192
  524.5 25.4 %collective-permute-start.115 = (bf16[128,2048]{1,0:T(8,128)(2,1)S(1)}, bf16[128,2048]{1,0:T(8,128)(2,1)S(1)}, u32[]{:S(2)}, u32[]{:S(2)}) collective-permute-start(bf16[128,2048]{1,0:T(8,128)(2,1)S(1)} %collective-permute-done.109.refs_0_), channel_id=1, source_target_pairs={{0,8},{2,10},{4,12},{6,14},{8,16},{10,18},{12,20},{14,22},{16,24},... | collective-permute-start | bytes 1572872 | tf_op jit(solution)/shard_map/ppermute | solution.py:177
  581.4 29.1 %collective-permute-start.128 = (bf16[1280,256]{1,0:T(8,128)(2,1)S(1)}, bf16[1280,256]{1,0:T(8,128)(2,1)S(1)}, u32[]{:S(2)}, u32[]{:S(2)}) collective-permute-start(bf16[1280,256]{1,0:T(8,128)(2,1)S(1)} %pad_maximum_fusion.4.refs_0_.refs_4_), channel_id=1, source_target_pairs={{0,8},{2,10},{4,12},{6,14},{8,16},{10,18},{12,20},{14,22},{16,24},... | collective-permute-start | bytes 1966088 | tf_op jit(solution)/shard_map/ppermute | solution.py:177
  582.4 28.1 %collective-permute-start.129 = (bf16[1280,256]{1,0:T(8,128)(2,1)S(1)}, bf16[1280,256]{1,0:T(8,128)(2,1)S(1)}, u32[]{:S(2)}, u32[]{:S(2)}) collective-permute-start(bf16[1280,256]{1,0:T(8,128)(2,1)S(1)} %pad_maximum_fusion.4.refs_0_.refs_4_), channel_id=1, source_target_pairs={{0,4},{2,6},{4,0},{6,2},{8,12},{10,14},{12,8},{14,10},{16,20},{18,... | collective-permute-start | bytes 1966088 | tf_op jit(solution)/shard_map/ppermute | solution.py:177
  584.1 26.4 %collective-permute-start.125 = (bf16[128,2048]{1,0:T(8,128)(2,1)S(1)}, bf16[128,2048]{1,0:T(8,128)(2,1)S(1)}, u32[]{:S(2)}, u32[]{:S(2)}) collective-permute-start(bf16[128,2048]{1,0:T(8,128)(2,1)S(1)} %fusion.20), channel_id=1, source_target_pairs={{0,8},{2,10},{4,12},{6,14},{8,16},{10,18},{12,20},{14,22},{16,24},... | collective-permute-start | bytes 1572872 | tf_op jit(solution)/shard_map/ppermute | solution.py:103
  584.4 26.1 %collective-permute-start.126 = (bf16[128,2048]{1,0:T(8,128)(2,1)S(1)}, bf16[128,2048]{1,0:T(8,128)(2,1)S(1)}, u32[]{:S(2)}, u32[]{:S(2)}) collective-permute-start(bf16[128,2048]{1,0:T(8,128)(2,1)S(1)} %fusion.58), channel_id=1, source_target_pairs={{0,4},{2,6},{4,0},{6,2},{8,12},{10,14},{12,8},{14,10},{16,20},{18,... | collective-permute-start | bytes 1572872 | tf_op jit(solution)/shard_map/ppermute | solution.py:103
  (256 other events, 3212.0 us)

commit v7 on v6

--- a/solution.py
+++ b/solution.py
@@ -991,48 +991,50 @@
     return (mine, theirs), grads, gains, gain_grad
 
 
-def place_kernel(parts, n_kv, table, *refs):
-    columns, keys = refs[:4], refs[4 : 4 + n_kv]
+def place_kernel(parts, n, n_kv, table, *refs):
+    columns, keys = refs[:n], refs[n : n + n_kv]
     outs = refs[-3:] if n_kv else refs[-1:]
-    for n in range(4):
-
-        @pl.when(pl.program_id(0) // parts == n)
+    for i in range(n):
+
+        @pl.when(pl.program_id(0) // parts == i)
         def _():
-            outs[0][...] = columns[n][...].astype(F32)
+            outs[0][...] = columns[i][...].astype(F32)
             if n_kv:
-                outs[1][...] = keys[n][:, :HD].astype(F32)
-                outs[2][...] = keys[n][:, HD:].astype(F32)
-
-
-def place_columns(k, quarter, table, n_ctx, rows, before):
+                outs[1][...] = keys[i][:, :HD].astype(F32)
+                outs[2][...] = keys[i][:, HD:].astype(F32)
+
+
+def place_columns(k, quarter, table, n_ctx, rows, before, first=0, stride=1):
     all_rows, cols = quarter[0].shape
     parts = cols // HD
     kv_rows = all_rows - rows
+    pieces = list(quarter[first::stride])
+    count = len(pieces)
+    block_of = lambda i: 4 * k + first + stride * (i // parts)
 
     def piece_at(n):
         return lambda i, t: (0, jnp.clip(i - n * parts, 0, parts - 1))
 
     def head_at(i, t):
-        c = t[4 * k + i // parts]
+        c = t[block_of(i)]
         rows_part = lax.rem(c // 4, 2) * 2 + lax.rem(c // 2, 2)
         return rows_part, lax.rem(c, 2) * 2 + c // 8
 
     out_specs = [
-        pl.BlockSpec((rows, HD), lambda i, t: (0, (i % parts) * n_ctx + t[4 * k + i // parts]))
+        pl.BlockSpec((rows, HD), lambda i, t: (0, (i % parts) * n_ctx + t[block_of(i)]))
     ]
     out_shape = [jax.ShapeDtypeStruct((rows, n_ctx * cols), F32)]
-    in_specs = [pl.BlockSpec((rows, HD), piece_at(n)) for n in range(4)]
-    pieces = list(quarter)
+    in_specs = [pl.BlockSpec((rows, HD), piece_at(n)) for n in range(count)]
     if kv_rows:
-        in_specs += [once((kv_rows, cols), lambda i, t: (rows // kv_rows, 0))] * 4
-        pieces += quarter
+        in_specs += [once((kv_rows, cols), lambda i, t: (rows // kv_rows, 0))] * count
+        pieces += pieces
         out_specs += [pl.BlockSpec((kv_rows, HD), head_at)] * 2
         out_shape += [jax.ShapeDtypeStruct((rows, KVH * HD), F32)] * 2
     return pl.pallas_call(
-        functools.partial(place_kernel, parts, len(pieces) - 4),
+        functools.partial(place_kernel, parts, count, len(pieces) - count),
         grid_spec=pltpu.PrefetchScalarGridSpec(
             num_scalar_prefetch=1,
-            grid=(4 * parts,),
+            grid=(count * parts,),
             in_specs=in_specs + [pl.BlockSpec(memory_space=pl.ANY)] * len(before),
             out_specs=out_specs,
         ),
@@ -1444,7 +1446,12 @@
             except StopIteration:
                 going = ()
             quarter = planned_quarter(arrays, k, n_ctx)
-            placed = place_columns(k, quarter, table, n_ctx, q_rows, placed)
+            halves = {"first": 1, "stride": 2} if k == nz - 1 else {}
+            placed = place_columns(k, quarter, table, n_ctx, q_rows, placed, **halves)
+            if k == nz - 2:
+                along = arrays["along", nz - 1]
+                pair = [along, None, lax.ppermute(along, "ctx", flip(n_ctx, 1))]
+                placed = place_columns(nz - 1, pair, table, n_ctx, q_rows, placed, 0, 2)
         grads["query"] = placed[0]
         if shared:
             grads["key"], grads["value"] = placed[1:]

time: 684 us -> 681 us (level)
  starting transfers between devices: 98.5 us -> 89.3 us
    ppermute x21, starting transfers between devices: 22.2 us -> 12.8 us  [swap(): return lax.ppermute(part, 'fsdp', SWAP)]
    unnamed x248 -> x250, local copies, waits for them, and re-layouts: 28.4 us -> 30.5 us
    pallas_call x4 -> x5, Pallas kernels: 20.6 us -> 21.6 us  [place_columns(): pl.pallas_call(functools.partial(place_kernel, parts, count, len(pieces)...]
  transfers between devices with their start and end apart: 157 -> 157, of which waited for: 58 -> 58; matrix products, arithmetic and copies ran while one was open for 14% -> 14% of each run, Pallas kernels for 28% -> 29%
where the time goes in v7:
time: 681 us; the launch traced here: 673 us
  waiting for transfers between devices  256 us (38%)
  Pallas kernels  203 us (30%)
  starting transfers between devices  89.3 us (13%)
  other arithmetic  50.3 us (7%)
  local copies, waits for them, and re-layouts  42.4 us (6%)
  matrix products  29 us (4%)
    ppermute x42, waiting for transfers between devices, send(): air[key] = lax.ppermute(array, 'ctx', pairs)  129 us
    pallas_call x4, Pallas kernels, experts(): pl.pallas_call(functools.partial(experts_kernel, k, n_parts, width, capac...  56.6 us
    ppermute x8, waiting for transfers between devices, sum_all(): lax.ppermute(values.astype(BF16), 'ctx', flip(n_ctx, bit))  45.1 us
    ppermute x42, starting transfers between devices, send(): air[key] = lax.ppermute(array, 'ctx', pairs)  38.3 us
    ppermute x21, waiting for transfers between devices, swap(): return lax.ppermute(part, 'fsdp', SWAP)  38.2 us
    unnamed x250, local copies, waits for them, and re-layouts  30.5 us
    pallas_call x4, Pallas kernels, project(): pl.pallas_call(functools.partial(project_kernel, k, hpd, n_kv, n_parts, n...  28.3 us
    dot_general x23, matrix products, dot(): return lax.dot_general(a, b, dims, preferred_element_type=F32)  27.5 us
  transfers between devices with their start and end apart: 157, of which 58 were waited for; matrix products, arithmetic and copies ran while one was open for 14% of the time, Pallas kernels for 29%

profile of v7, /device:TPU:0, one launch (start us, length us, event | category | flops | bytes accessed | tf_op | source)
XLA Modules:
  0.0 673.0 jit_solution(464849882500430640)
XLA Ops:
  9.8 5.9 collective-permute-done.x1.refs_1_
  40.4 6.8 %project.4 = (bf16[16,128,1024]{2,1,0:T(8,128)(2,1)}, bf16[16,128,1024]{2,1,0:T(8,128)(2,1)}, f32[16,128,384]{2,1,0:T(8,128)}, f32[16,128,128]{2,1,0:T(8,128)}, ...) custom-call(s32[19]{0:T(128)S(1)} %concatenate.53.meta, ...), custom_call_target="tpu_custom_call" | custom-call | flops 6899999744 | tf_op jit(solution)/shard_map/project/pallas_call | solution.py:434
  47.8 7.2 %project.5 = (bf16[16,128,1024]{2,1,0:T(8,128)(2,1)}, bf16[16,128,1024]{2,1,0:T(8,128)(2,1)}, f32[16,128,384]{2,1,0:T(8,128)}, f32[16,128,128]{2,1,0:T(8,128)}, ...) custom-call(s32[19]{0:T(128)S(1)} %concatenate.53.meta, ...), custom_call_target="tpu_custom_call", output_to_operand_aliasing={{0}: (13, {}), {1}: (14, {}), {2}: (15, {}), {3}: (16, {}),... | custom-call | flops 6899999744 | tf_op jit(solution)/shard_map/project/pallas_call | solution.py:434
  61.3 7.5 %project.6 = (bf16[16,128,1024]{2,1,0:T(8,128)(2,1)}, bf16[16,128,1024]{2,1,0:T(8,128)(2,1)}, f32[16,128,384]{2,1,0:T(8,128)}, f32[16,128,128]{2,1,0:T(8,128)}, ...) custom-call(s32[19]{0:T(128)S(1)} %concatenate.53.meta, ...), custom_call_target="tpu_custom_call", output_to_operand_aliasing={{0}: (13, {}), {1}: (14, {}), {2}: (15, {}), {3}: (16, {}),... | custom-call | flops 6899999744 | tf_op jit(solution)/shard_map/project/pallas_call | solution.py:434
  78.0 6.9 %project.7 = (bf16[16,128,1024]{2,1,0:T(8,128)(2,1)}, bf16[16,128,1024]{2,1,0:T(8,128)(2,1)}, f32[16,128,384]{2,1,0:T(8,128)}, f32[16,128,128]{2,1,0:T(8,128)}, ...) custom-call(s32[19]{0:T(128)S(1)} %concatenate.53.meta, ...), custom_call_target="tpu_custom_call", output_to_operand_aliasing={{0}: (13, {}), {1}: (14, {}), {2}: (15, {}), {3}: (16, {}),... | custom-call | flops 6899999744 | tf_op jit(solution)/shard_map/project/pallas_call | solution.py:434
  88.6 15.4 %attend.1 = (f32[2,2048,128]{2,1,0:T(8,128)S(1)}, f32[2,8,2048]{2,1,0:T(8,128)S(1)}) custom-call(s32[4]{0:T(128)S(1)} %bitcast.229, bf16[2,2048,128]{2,1,0:T(8,128)(2,1)S(1)} %copy-done.72, bf16[2,2048,128]{2,1,0:T(8,128)(2,1)S(1)} %copy-done.74, bf16[2,2048,128]{2,1,0:T(8,128)(2,1)S(1)} %copy-done.76), custom_call_target="tpu_custom_call" | custom-call | flops 14375000064 | tf_op jit(solution)/shard_map/attend/pallas_call | solution.py:514
  113.6 14.8 %collective-permute-done.27.g1 = bf16[128,2048]{1,0:T(8,128)(2,1)S(1)} collective-permute-done((bf16[128,2048]{1,0:T(8,128)(2,1)}, bf16[128,2048]{1,0:T(8,128)(2,1)S(1)}, u32[]{:S(2)}, u32[]{:S(2)}) %collective-permute-start.27) | collective-permute-done | bytes 524320 | tf_op jit(solution)/shard_map/ppermute | solution.py:177
  133.1 14.4 %collective-permute-done.29 = bf16[128,2048]{1,0:T(8,128)(2,1)S(1)} collective-permute-done((bf16[128,2048]{1,0:T(8,128)(2,1)S(1)}, bf16[128,2048]{1,0:T(8,128)(2,1)S(1)}, u32[]{:S(2)}, u32[]{:S(2)}) %collective-permute-start.29) | collective-permute-done | bytes 524320 | tf_op jit(solution)/shard_map/ppermute | solution.py:103
  157.8 11.9 %collective-permute-done.34.refs_3_ = bf16[1024,768]{1,0:T(8,128)(2,1)} collective-permute-done((bf16[1024,768]{1,0:T(8,128)(2,1)}, bf16[1024,768]{1,0:T(8,128)(2,1)}, u32[]{:S(2)}, u32[]{:S(2)}) %collective-permute-start.34) | collective-permute-done | bytes 1572896 | tf_op jit(solution)/shard_map/ppermute | solution.py:239
  180.0 9.3 %collective-permute-done.36 = bf16[128,2048]{1,0:T(8,128)(2,1)} collective-permute-done((bf16[128,2048]{1,0:T(8,128)(2,1)}, bf16[128,2048]{1,0:T(8,128)(2,1)}, u32[]{:S(2)}, u32[]{:S(2)}) %collective-permute-start.36) | collective-permute-done | bytes 524320 | tf_op jit(solution)/shard_map/ppermute | solution.py:103
  194.4 11.6 %collective-permute-done.38.x1 = bf16[128,2176]{1,0:T(8,128)(2,1)S(1)} collective-permute-done((bf16[128,2176]{1,0:T(8,128)(2,1)S(1)}, bf16[128,2176]{1,0:T(8,128)(2,1)S(1)}, u32[]{:S(2)}, u32[]{:S(2)}) %collective-permute-start.38) | collective-permute-done | bytes 557088 | tf_op jit(solution)/shard_map/ppermute | solution.py:103
  234.1 14.4 %experts.4 = (bf16[1280,1024]{1,0:T(8,128)(2,1)}, bf16[1280,1024]{1,0:T(8,128)(2,1)}, bf16[1280,1024]{1,0:T(8,128)(2,1)}, bf16[1280,1024]{1,0:T(8,128)(2,1)}, bf...) custom-call(s32[3]{0:T(128)S(1)} %pad_add_fusion.meta, ...), custom_call_target="tpu_custom_call" | custom-call | flops 17250000896 | tf_op jit(solution)/shard_map/experts/pallas_call | solution.py:800
  248.5 6.6 collective-permute-done.44.x0
  262.5 13.6 %experts.5 = (bf16[1280,1024]{1,0:T(8,128)(2,1)}, bf16[1280,1024]{1,0:T(8,128)(2,1)}, bf16[1280,1024]{1,0:T(8,128)(2,1)}, bf16[1280,1024]{1,0:T(8,128)(2,1)}, bf...) custom-call(s32[3]{0:T(128)S(1)} %pad_add_fusion.meta, ...), custom_call_target="tpu_custom_call", output_to_operand_aliasing={{0}: (16, {}), {1}: (17, {}), {2}: (18, {}), {3}: (19, {}),... | custom-call | flops 17250000896 | tf_op jit(solution)/shard_map/experts/pallas_call | solution.py:800
  277.4 6.3 collective-permute-done.54.g1
  301.1 14.6 %experts.6 = (bf16[1280,1024]{1,0:T(8,128)(2,1)}, bf16[1280,1024]{1,0:T(8,128)(2,1)}, bf16[1280,1024]{1,0:T(8,128)(2,1)}, bf16[1280,1024]{1,0:T(8,128)(2,1)}, bf...) custom-call(s32[3]{0:T(128)S(1)} %pad_add_fusion.meta, ...), custom_call_target="tpu_custom_call", output_to_operand_aliasing={{0}: (16, {}), {1}: (17, {}), {2}: (18, {}), {3}: (19, {}),... | custom-call | flops 17250000896 | tf_op jit(solution)/shard_map/experts/pallas_call | solution.py:800
  329.1 14.0 %experts.7 = (bf16[1280,1024]{1,0:T(8,128)(2,1)}, bf16[1280,1024]{1,0:T(8,128)(2,1)}, bf16[1280,1024]{1,0:T(8,128)(2,1)}, bf16[1280,1024]{1,0:T(8,128)(2,1)}, bf...) custom-call(s32[3]{0:T(128)S(1)} %pad_add_fusion.meta, ...), custom_call_target="tpu_custom_call", output_to_operand_aliasing={{0}: (16, {}), {1}: (17, {}), {2}: (18, {}), {3}: (19, {}),... | custom-call | flops 17250000896 | tf_op jit(solution)/shard_map/experts/pallas_call | solution.py:800
  365.8 16.4 %collective-permute-done.74 = bf16[128,4224]{1,0:T(8,128)(2,1)S(1)} collective-permute-done((bf16[128,4224]{1,0:T(8,128)(2,1)S(1)}, bf16[128,4224]{1,0:T(8,128)(2,1)S(1)}, u32[]{:S(2)}, u32[]{:S(2)}) %collective-permute-start.74) | collective-permute-done | bytes 1081376 | tf_op jit(solution)/shard_map/ppermute | solution.py:103
  391.0 7.1 %collective-permute-done.76.g1 = bf16[128,2048]{1,0:T(8,128)(2,1)S(1)} collective-permute-done((bf16[128,2048]{1,0:T(8,128)(2,1)S(1)}, bf16[128,2048]{1,0:T(8,128)(2,1)S(1)}, u32[]{:S(2)}, u32[]{:S(2)}) %collective-permute-start.76) | collective-permute-done | bytes 524320 | tf_op jit(solution)/shard_map/ppermute | solution.py:103
  425.1 9.7 %collective-permute-done.89 = bf16[17,2048]{1,0:T(8,128)(2,1)S(1)} collective-permute-done((bf16[17,2048]{1,0:T(8,128)(2,1)S(1)}, bf16[17,2048]{1,0:T(8,128)(2,1)S(1)}, u32[]{:S(2)}, u32[]{:S(2)}) %collective-permute-start.89) | collective-permute-done | bytes 69664 | tf_op jit(solution)/shard_map/ppermute | solution.py:224
  460.1 17.2 %attend_back.1 = (f32[2,2048,128]{2,1,0:T(8,128)S(1)}, f32[2,2048,128]{2,1,0:T(8,128)S(1)}, f32[2,2048,128]{2,1,0:T(8,128)S(1)}, bf16[2,2048,128]{2,1,0:T(8,128)(2,1)S(1)}) custom-call(s32[5]{0:T(128)S(1)} %pad_add_fusion.1.ends, bf16[2,2048,128]{2,1,0:T(8,128)(2,1)S(1)} %copy-done.73, bf16[2,2048,128]{2,1,0:T(8,128)(2,1)S(1)} %get-tuple-element.546.grad, ...), custom_call_target="tpu_custom_call" | custom-call | flops 19549999104 | tf_op jit(solution)/shard_map/attend_back/pallas_call | solution.py:583
  535.9 7.6 %collective-permute-done.117 = bf16[256,256]{1,0:T(8,128)(2,1)S(1)} collective-permute-done((bf16[256,256]{1,0:T(8,128)(2,1)S(1)}, bf16[256,256]{1,0:T(8,128)(2,1)S(1)}, u32[]{:S(2)}, u32[]{:S(2)}) %collective-permute-start.117) | collective-permute-done | bytes 131104 | tf_op jit(solution)/shard_map/ppermute | solution.py:1375
  573.8 8.7 %collective-permute-done.120 = bf16[128,2048]{1,0:T(8,128)(2,1)S(1)} collective-permute-done((bf16[128,2048]{1,0:T(8,128)(2,1)S(1)}, bf16[128,2048]{1,0:T(8,128)(2,1)S(1)}, u32[]{:S(2)}, u32[]{:S(2)}) %collective-permute-start.120) | collective-permute-done | bytes 524320 | tf_op jit(solution)/shard_map/ppermute | solution.py:103
  592.2 19.7 %collective-permute-done.127 = bf16[2,2048]{1,0:T(2,128)(2,1)S(1)} collective-permute-done((bf16[2,2048]{1,0:T(2,128)(2,1)S(1)}, bf16[2,2048]{1,0:T(2,128)(2,1)S(1)}, u32[]{:S(2)}, u32[]{:S(2)}) %collective-permute-start.127) | collective-permute-done | bytes 8224 | tf_op jit(solution)/shard_map/ppermute | solution.py:224
  (710 shorter events, 402.1 us)
Async XLA Ops:
  5.2 31.8 %collective-permute-start.13 = (bf16[128,2048]{1,0:T(8,128)(2,1)}, bf16[128,2048]{1,0:T(8,128)(2,1)}, u32[]{:S(2)}, u32[]{:S(2)}) collective-permute-start(bf16[128,2048]{1,0:T(8,128)(2,1)} %bitcast.208), channel_id=1, source_target_pairs={{0,2},{2,0},{4,6},{6,4},{8,10},{10,8},{12,14},{14,12},{16,18},{18,... | collective-permute-start | bytes 1572872 | tf_op jit(solution)/shard_map/ppermute | solution.py:144
  7.8 28.4 %collective-permute-start.10 = (bf16[1,2176]{1,0:T(2,128)(2,1)S(1)}, bf16[1,2176]{1,0:T(2,128)(2,1)S(1)}, u32[]{:S(2)}, u32[]{:S(2)}) collective-permute-start(bf16[1,2176]{1,0:T(2,128)(2,1)S(1)} %broadcast_in_dim.66), channel_id=1, source_target_pairs={{0,1},{1,0},{2,3},{3,2},{4,5},{5,4},{6,7},{7,6},{8,9},{9,8},{10,11... | collective-permute-start | bytes 13064 | tf_op jit(solution)/shard_map/ppermute | solution.py:239
  9.3 26.0 %collective-permute-start.4 = (bf16[1024,512]{1,0:T(8,128)(2,1)S(1)}, bf16[1024,512]{1,0:T(8,128)(2,1)S(1)}, u32[]{:S(2)}, u32[]{:S(2)}) collective-permute-start(bf16[1024,512]{1,0:T(8,128)(2,1)S(1)} %pad_maximum_fusion.1.refs_0_), channel_id=1, source_target_pairs={{0,1},{1,0},{2,3},{3,2},{4,5},{5,4},{6,7},{7,6},{8,9},{9,8},{10,11... | collective-permute-start | bytes 3145736 | tf_op jit(solution)/shard_map/ppermute | solution.py:239
  57.8 46.2 %collective-permute-start.15 = (bf16[1024,768]{1,0:T(8,128)(2,1)}, bf16[1024,768]{1,0:T(8,128)(2,1)S(1)}, u32[]{:S(2)}, u32[]{:S(2)}) collective-permute-start(bf16[1024,768]{1,0:T(8,128)(2,1)} %bitcast.219), channel_id=1, source_target_pairs={{0,1},{1,0},{2,3},{3,2},{4,5},{5,4},{6,7},{7,6},{8,9},{9,8},{10,11... | collective-permute-start | bytes 4718600 | tf_op jit(solution)/shard_map/ppermute | solution.py:239
  75.8 28.2 %collective-permute-start.20 = (bf16[128,2048]{1,0:T(8,128)(2,1)}, bf16[128,2048]{1,0:T(8,128)(2,1)S(1)}, u32[]{:S(2)}, u32[]{:S(2)}) collective-permute-start(bf16[128,2048]{1,0:T(8,128)(2,1)} %collective-permute-done.17.g0), channel_id=1, source_target_pairs={{0,8},{2,10},{4,12},{6,14},{8,16},{10,18},{12,20},{14,22},{16,24},... | collective-permute-start | bytes 1572872 | tf_op jit(solution)/shard_map/ppermute | solution.py:177
  75.9 28.2 %collective-permute-start.22 = (bf16[128,2048]{1,0:T(8,128)(2,1)}, bf16[128,2048]{1,0:T(8,128)(2,1)}, u32[]{:S(2)}, u32[]{:S(2)}) collective-permute-start(bf16[128,2048]{1,0:T(8,128)(2,1)} %collective-permute-done.17.g0), channel_id=1, source_target_pairs={{0,4},{2,6},{4,0},{6,2},{8,12},{10,14},{12,8},{14,10},{16,20},{18,... | collective-permute-start | bytes 1572872 | tf_op jit(solution)/shard_map/ppermute | solution.py:177
  77.3 26.7 %collective-permute-start.21 = (bf16[128,2048]{1,0:T(8,128)(2,1)S(1)}, bf16[128,2048]{1,0:T(8,128)(2,1)}, u32[]{:S(2)}, u32[]{:S(2)}) collective-permute-start(bf16[128,2048]{1,0:T(8,128)(2,1)S(1)} %bitcast.212), channel_id=1, source_target_pairs={{0,4},{2,6},{4,0},{6,2},{8,12},{10,14},{12,8},{14,10},{16,20},{18,... | collective-permute-start | bytes 1572872 | tf_op jit(solution)/shard_map/ppermute | solution.py:177
  133.1 36.6 %collective-permute-start.34 = (bf16[1024,768]{1,0:T(8,128)(2,1)}, bf16[1024,768]{1,0:T(8,128)(2,1)}, u32[]{:S(2)}, u32[]{:S(2)}) collective-permute-start(bf16[1024,768]{1,0:T(8,128)(2,1)} %bitcast.29.refs_2_), channel_id=1, source_target_pairs={{0,1},{1,0},{2,3},{3,2},{4,5},{5,4},{6,7},{7,6},{8,9},{9,8},{10,11... | collective-permute-start | bytes 4718600 | tf_op jit(solution)/shard_map/ppermute | solution.py:239
  179.7 36.4 %collective-permute-start.42 = (bf16[1024,768]{1,0:T(8,128)(2,1)}, bf16[1024,768]{1,0:T(8,128)(2,1)S(1)}, u32[]{:S(2)}, u32[]{:S(2)}) collective-permute-start(bf16[1024,768]{1,0:T(8,128)(2,1)} %bitcast.224), channel_id=1, source_target_pairs={{0,1},{1,0},{2,3},{3,2},{4,5},{5,4},{6,7},{7,6},{8,9},{9,8},{10,11... | collective-permute-start | bytes 4718600 | tf_op jit(solution)/shard_map/ppermute | solution.py:239
  228.4 26.7 %collective-permute-start.44 = (bf16[128,2176]{1,0:T(8,128)(2,1)}, bf16[128,2176]{1,0:T(8,128)(2,1)S(1)}, u32[]{:S(2)}, u32[]{:S(2)}) collective-permute-start(bf16[128,2176]{1,0:T(8,128)(2,1)} %copy-done.43), channel_id=1, source_target_pairs={{0,8},{2,10},{4,12},{6,14},{8,16},{10,18},{12,20},{14,22},{16,24},... | collective-permute-start | bytes 1671176 | tf_op jit(solution)/shard_map/ppermute | solution.py:103
  255.7 28.0 %collective-permute-start.51 = (bf16[128,2176]{1,0:T(8,128)(2,1)S(1)}, bf16[128,2176]{1,0:T(8,128)(2,1)}, u32[]{:S(2)}, u32[]{:S(2)}) collective-permute-start(bf16[128,2176]{1,0:T(8,128)(2,1)S(1)} %collective-permute-done.43.x1), channel_id=1, source_target_pairs={{0,8},{2,10},{4,12},{6,14},{8,16},{10,18},{12,20},{14,22},{16,24},... | collective-permute-start | bytes 1671176 | tf_op jit(solution)/shard_map/ppermute | solution.py:103
  292.4 28.6 %collective-permute-start.60 = (bf16[128,4224]{1,0:T(8,128)(2,1)}, bf16[128,4224]{1,0:T(8,128)(2,1)}, u32[]{:S(2)}, u32[]{:S(2)}) collective-permute-start(bf16[128,4224]{1,0:T(8,128)(2,1)} %fusion.3), channel_id=1, source_target_pairs={{0,8},{2,10},{4,12},{6,14},{8,16},{10,18},{12,20},{14,22},{16,24},... | collective-permute-start | bytes 3244040 | tf_op jit(solution)/shard_map/ppermute | solution.py:103
  295.8 26.5 %collective-permute-start.61 = (bf16[128,4224]{1,0:T(8,128)(2,1)}, bf16[128,4224]{1,0:T(8,128)(2,1)}, u32[]{:S(2)}, u32[]{:S(2)}) collective-permute-start(bf16[128,4224]{1,0:T(8,128)(2,1)} %fusion.11), channel_id=1, source_target_pairs={{0,4},{2,6},{4,0},{6,2},{8,12},{10,14},{12,8},{14,10},{16,20},{18,... | collective-permute-start | bytes 3244040 | tf_op jit(solution)/shard_map/ppermute | solution.py:103
  324.9 28.1 %collective-permute-start.66 = (bf16[128,4224]{1,0:T(8,128)(2,1)S(1)}, bf16[128,4224]{1,0:T(8,128)(2,1)S(1)}, u32[]{:S(2)}, u32[]{:S(2)}) collective-permute-start(bf16[128,4224]{1,0:T(8,128)(2,1)S(1)} %fusion.5), channel_id=1, source_target_pairs={{0,8},{2,10},{4,12},{6,14},{8,16},{10,18},{12,20},{14,22},{16,24},... | collective-permute-start | bytes 3244040 | tf_op jit(solution)/shard_map/ppermute | solution.py:103
  326.8 26.2 %collective-permute-start.68 = (bf16[128,4224]{1,0:T(8,128)(2,1)S(1)}, bf16[128,4224]{1,0:T(8,128)(2,1)S(1)}, u32[]{:S(2)}, u32[]{:S(2)}) collective-permute-start(bf16[128,4224]{1,0:T(8,128)(2,1)S(1)} %fusion.12), channel_id=1, source_target_pairs={{0,4},{2,6},{4,0},{6,2},{8,12},{10,14},{12,8},{14,10},{16,20},{18,... | collective-permute-start | bytes 3244040 | tf_op jit(solution)/shard_map/ppermute | solution.py:103
  354.9 27.3 %collective-permute-start.74 = (bf16[128,4224]{1,0:T(8,128)(2,1)S(1)}, bf16[128,4224]{1,0:T(8,128)(2,1)S(1)}, u32[]{:S(2)}, u32[]{:S(2)}) collective-permute-start(bf16[128,4224]{1,0:T(8,128)(2,1)S(1)} %fusion.1), channel_id=1, source_target_pairs={{0,8},{2,10},{4,12},{6,14},{8,16},{10,18},{12,20},{14,22},{16,24},... | collective-permute-start | bytes 3244040 | tf_op jit(solution)/shard_map/ppermute | solution.py:103
  360.0 31.0 %collective-permute-start.78 = (bf16[1024,256]{1,0:T(8,128)(2,1)S(1)}, bf16[1024,256]{1,0:T(8,128)(2,1)S(1)}, u32[]{:S(2)}, u32[]{:S(2)}) collective-permute-start(bf16[1024,256]{1,0:T(8,128)(2,1)S(1)} %convolution_convert_fusion.8), channel_id=1, source_target_pairs={{0,1},{1,0},{2,3},{3,2},{4,5},{5,4},{6,7},{7,6},{8,9},{9,8},{10,11... | collective-permute-start | bytes 1572872 | tf_op jit(solution)/shard_map/ppermute | solution.py:239
  450.5 26.8 %collective-permute-start.99 = (bf16[1024,256]{1,0:T(8,128)(2,1)S(1)}, bf16[1024,256]{1,0:T(8,128)(2,1)S(1)}, u32[]{:S(2)}, u32[]{:S(2)}) collective-permute-start(bf16[1024,256]{1,0:T(8,128)(2,1)S(1)} %convolution_convert_fusion.4), channel_id=1, source_target_pairs={{0,1},{1,0},{2,3},{3,2},{4,5},{5,4},{6,7},{7,6},{8,9},{9,8},{10,11... | collective-permute-start | bytes 1572872 | tf_op jit(solution)/shard_map/ppermute | solution.py:239
  451.2 26.2 %collective-permute-start.100 = (bf16[17,2048]{1,0:T(8,128)(2,1)S(1)}, bf16[17,2048]{1,0:T(8,128)(2,1)S(1)}, u32[]{:S(2)}, u32[]{:S(2)}) collective-permute-start(bf16[17,2048]{1,0:T(8,128)(2,1)S(1)} %fusion.63), channel_id=1, source_target_pairs={{0,1},{1,0},{2,3},{3,2},{4,5},{5,4},{6,7},{7,6},{8,9},{9,8},{10,11... | collective-permute-start | bytes 208904 | tf_op jit(solution)/shard_map/ppermute | solution.py:239
  478.7 31.8 %collective-permute-start.155 = (bf16[128,2048]{1,0:T(8,128)(2,1)S(1)}, bf16[128,2048]{1,0:T(8,128)(2,1)S(1)}, u32[]{:S(2)}, u32[]{:S(2)}) collective-permute-start(bf16[128,2048]{1,0:T(8,128)(2,1)S(1)} %add_convert_fusion.9.refs_0_), channel_id=1, source_target_pairs={{0,2},{2,0},{4,6},{6,4},{8,10},{10,8},{12,14},{14,12},{16,18},{18,... | collective-permute-start | bytes 1572872 | tf_op jit(solution)/shard_map/ppermute | solution.py:192
  583.9 29.1 %collective-permute-start.128 = (bf16[1280,256]{1,0:T(8,128)(2,1)S(1)}, bf16[1280,256]{1,0:T(8,128)(2,1)S(1)}, u32[]{:S(2)}, u32[]{:S(2)}) collective-permute-start(bf16[1280,256]{1,0:T(8,128)(2,1)S(1)} %pad_maximum_fusion.4.refs_0_.refs_4_), channel_id=1, source_target_pairs={{0,8},{2,10},{4,12},{6,14},{8,16},{10,18},{12,20},{14,22},{16,24},... | collective-permute-start | bytes 1966088 | tf_op jit(solution)/shard_map/ppermute | solution.py:177
  584.7 28.3 %collective-permute-start.129 = (bf16[1280,256]{1,0:T(8,128)(2,1)S(1)}, bf16[1280,256]{1,0:T(8,128)(2,1)S(1)}, u32[]{:S(2)}, u32[]{:S(2)}) collective-permute-start(bf16[1280,256]{1,0:T(8,128)(2,1)S(1)} %pad_maximum_fusion.4.refs_0_.refs_4_), channel_id=1, source_target_pairs={{0,4},{2,6},{4,0},{6,2},{8,12},{10,14},{12,8},{14,10},{16,20},{18,... | collective-permute-start | bytes 1966088 | tf_op jit(solution)/shard_map/ppermute | solution.py:177
  586.3 26.7 %collective-permute-start.125 = (bf16[128,2048]{1,0:T(8,128)(2,1)S(1)}, bf16[128,2048]{1,0:T(8,128)(2,1)S(1)}, u32[]{:S(2)}, u32[]{:S(2)}) collective-permute-start(bf16[128,2048]{1,0:T(8,128)(2,1)S(1)} %fusion.20), channel_id=1, source_target_pairs={{0,8},{2,10},{4,12},{6,14},{8,16},{10,18},{12,20},{14,22},{16,24},... | collective-permute-start | bytes 1572872 | tf_op jit(solution)/shard_map/ppermute | solution.py:103
  586.6 26.4 %collective-permute-start.126 = (bf16[128,2048]{1,0:T(8,128)(2,1)S(1)}, bf16[128,2048]{1,0:T(8,128)(2,1)S(1)}, u32[]{:S(2)}, u32[]{:S(2)}) collective-permute-start(bf16[128,2048]{1,0:T(8,128)(2,1)S(1)} %fusion.58), channel_id=1, source_target_pairs={{0,4},{2,6},{4,0},{6,2},{8,12},{10,14},{12,8},{14,10},{16,20},{18,... | collective-permute-start | bytes 1572872 | tf_op jit(solution)/shard_map/ppermute | solution.py:103
  (257 other events, 3196.6 us)
